TPU v7x, 32 devices: a whole 2x2x4 slice. The times are simulated.
32 devices in a mesh: seq: 8 (over z, x), chan: 4 (over y, core).
Axes of the slice: x: 2, y: 2, z: 4, core: 2. Of those that a mesh axis runs over, the one named last changes fastest.
Arguments:
- tokens: bfloat16 [2048, 4096], P('seq', 'chan'), may hold values from -6 to 6
- in_weight: bfloat16 [4096, 3, 4096], P('seq', None, 'chan'), may hold values from -0.09375 to 0.09375
- short_taps: float32 [3, 3, 4096], P(None, None, 'chan'), may hold values from -3 to 3
- skip_gain: float32 [4096], P('chan'), may hold values from 0.5 to 1.5
- long_filter: bfloat16 [2048, 4096], P('seq', 'chan'), may hold values from -1.1 to 1.1
- out_weight: bfloat16 [4096, 4096], P('chan'), may hold values from -0.125 to 0.125
Outputs:
- mixed_out: bfloat16 [2048, 4096], P('seq', 'chan')
All inputs are finite; a program needn't handle non-finite values.
Results may differ from a plain program's by a relative error of at most 0.023.
Values may be sent and summed in bfloat16 or wider, within the bound.
No kernel may reach another device: no remote copies, remote signals or barrier semaphores. Data moves between devices by JAX's collectives and lax.ppermute only.
A program may use at most 128 MiB of HBM per device.

v0:
```python
import math

import jax
import jax.numpy as jnp
from jax import lax
from jax.sharding import PartitionSpec as P

exact_prec = lax.Precision.HIGHEST


def dft_tables(half_len, blocks):
    full_len = 2 * half_len
    full_size = full_len * blocks
    half_index = jnp.arange(half_len, dtype=jnp.int32)
    full_index = jnp.arange(full_len, dtype=jnp.int32)
    block_index = jnp.arange(blocks, dtype=jnp.int32)
    outer_angle = (half_index[:, None] * full_index[None, :] % full_len).astype(jnp.float32) * (
        2.0 * math.pi / full_len
    )
    inner_angle = (block_index[:, None] * block_index[None, :] % blocks).astype(jnp.float32) * (
        2.0 * math.pi / blocks
    )
    twist_angle = (full_index[:, None] * block_index[None, :] % full_size).astype(jnp.float32) * (
        2.0 * math.pi / full_size
    )
    return (
        jnp.cos(outer_angle),
        jnp.sin(outer_angle),
        jnp.cos(inner_angle),
        jnp.sin(inner_angle),
        jnp.cos(twist_angle),
        jnp.sin(twist_angle),
    )


def forward_dft(signal, tables):
    outer_cos, outer_sin, inner_cos, inner_sin, twist_cos, twist_sin = tables
    real_section = jnp.einsum("cmn,mk->ckn", signal, outer_cos, precision=exact_prec)
    imag_section = -jnp.einsum("cmn,mk->ckn", signal, outer_sin, precision=exact_prec)
    real_twist = real_section * twist_cos + imag_section * twist_sin
    imag_twist = imag_section * twist_cos - real_section * twist_sin
    real_freq = jnp.einsum("ckn,nj->ckj", real_twist, inner_cos, precision=exact_prec) + jnp.einsum(
        "ckn,nj->ckj", imag_twist, inner_sin, precision=exact_prec
    )
    imag_freq = jnp.einsum("ckn,nj->ckj", imag_twist, inner_cos, precision=exact_prec) - jnp.einsum(
        "ckn,nj->ckj", real_twist, inner_sin, precision=exact_prec
    )
    return (real_freq, imag_freq)


def inverse_real(spectrum_real, spectrum_imag, tables):
    outer_cos, outer_sin, inner_cos, inner_sin, twist_cos, twist_sin = tables
    full_size = outer_cos.shape[1] * inner_cos.shape[0]
    back_real = jnp.einsum(
        "ckj,jn->ckn", spectrum_real, inner_cos, precision=exact_prec
    ) - jnp.einsum("ckj,jn->ckn", spectrum_imag, inner_sin, precision=exact_prec)
    back_imag = jnp.einsum(
        "ckj,jn->ckn", spectrum_imag, inner_cos, precision=exact_prec
    ) + jnp.einsum("ckj,jn->ckn", spectrum_real, inner_sin, precision=exact_prec)
    turn_real = back_real * twist_cos - back_imag * twist_sin
    turn_imag = back_imag * twist_cos + back_real * twist_sin
    summed_real = jnp.einsum(
        "ckn,mk->cmn", turn_real, outer_cos, precision=exact_prec
    ) - jnp.einsum("ckn,mk->cmn", turn_imag, outer_sin, precision=exact_prec)
    return summed_real / full_size


def causal_conv(signal, kernel, blocks):
    channels, length = signal.shape
    half_len = length // blocks
    tables = dft_tables(half_len, blocks)
    stacked = jnp.concatenate([signal, kernel], 0).reshape(2 * channels, half_len, blocks)
    real_freq, imag_freq = forward_dft(stacked, tables)
    data_real, filter_real = (real_freq[:channels], real_freq[channels:])
    data_imag, filter_imag = (imag_freq[:channels], imag_freq[channels:])
    spectrum_real = data_real * filter_real - data_imag * filter_imag
    spectrum_imag = data_real * filter_imag + data_imag * filter_real
    return inverse_real(spectrum_real, spectrum_imag, tables).reshape(channels, length)


def body(tokens, in_weight, short_taps, skip_gain, long_filter, out_weight):
    row_count, chan_width = tokens.shape
    blocks = lax.axis_size("seq")
    part_width = chan_width // blocks
    flat_weight = in_weight.reshape(in_weight.shape[0], 3 * chan_width)
    whole = lax.all_gather(tokens, "chan", axis=1, tiled=True)
    projected = jnp.dot(
        whole,
        lax.all_gather(flat_weight, "seq", axis=0, tiled=True),
        preferred_element_type=jnp.float32,
    )
    projected = projected.astype(jnp.bfloat16).reshape(row_count, 3, chan_width)
    outgoing = jnp.transpose(projected, (1, 2, 0))
    filter_rows = jnp.transpose(long_filter)[None]
    channel_major, filter_major = (
        lax.all_to_all(outgoing, "seq", split_axis=1, concat_axis=2, tiled=True),
        lax.all_to_all(filter_rows, "seq", split_axis=1, concat_axis=2, tiled=True),
    )
    offset = lax.axis_index("seq") * part_width
    local_taps = lax.dynamic_slice_in_dim(short_taps, offset, part_width, 2)
    local_skip = lax.dynamic_slice_in_dim(skip_gain, offset, part_width, 0)
    values = channel_major.astype(jnp.float32)
    tap_count = short_taps.shape[1]
    length = values.shape[2]
    padded = jnp.pad(values, ((0, 0), (0, 0), (tap_count - 1, 0)))
    smoothed = jnp.zeros_like(values)
    for tap_index in range(tap_count):
        lag_start = tap_count - 1 - tap_index
        smoothed = (
            smoothed
            + local_taps[:, tap_index, :, None] * padded[:, :, lag_start : lag_start + length]
        )
    gate_query = smoothed[0]
    gated = smoothed[1] * smoothed[2]
    mixed_seq = (
        causal_conv(gated, filter_major[0].astype(jnp.float32), blocks)
        + local_skip[:, None] * gated
    )
    product = (mixed_seq * gate_query).astype(jnp.bfloat16)
    returned = lax.all_to_all(product, "seq", split_axis=1, concat_axis=0, tiled=True)
    summed = lax.psum_scatter(
        lax.dot_general(
            out_weight, returned, (((0,), (0,)), ((), ())), preferred_element_type=jnp.float32
        ).astype(jnp.bfloat16),
        "chan",
        scatter_dimension=0,
        tiled=True,
    ).astype(jnp.float32)
    return jnp.transpose(summed).astype(jnp.bfloat16)


def solution(mesh):
    in_specs = (
        P("seq", "chan"),
        P("seq", None, "chan"),
        P(None, None, "chan"),
        P("chan"),
        P("seq", "chan"),
        P("chan", None),
    )
    out_specs = P("seq", "chan")
    return jax.shard_map(body, mesh=mesh, in_specs=in_specs, out_specs=out_specs, check_vma=False)
```

profile of v0, /device:TPU:0, one launch (start us, length us, event | category | flops | bytes accessed | tf_op | source)
XLA Modules:
  0.0 736.9 jit_solution(13712866021294325164)
XLA Ops:
  7.3 4.7 copy.67
  14.5 3.8 reduce
  19.3 7.3 all-to-all-start.1
  26.5 7.7 %all-gather.3.cloned.1.call-done = bf16[256,4096]{1,0:T(8,128)(2,1)} async-done(((bf16[256,1024]{1,0:T(8,128)(2,1)}), bf16[256,4096]{1,0:T(8,128)(2,1)}) %all-gather.3.cloned.1.call-update) | async-done | bytes 2097168 | tf_op jit(solution)/shard_map/all_gather | solution.py:86
  34.2 482.0 %all-gather.5.cloned.1.call-done = bf16[4096,3072]{0,1:T(8,128)(2,1)} async-done(((bf16[512,3072]{0,1:T(8,128)(2,1)}), bf16[4096,3072]{0,1:T(8,128)(2,1)}) %all-gather.5.cloned.1.call-update) | async-done | bytes 25165840 | tf_op jit(solution)/shard_map/all_gather | solution.py:89
  516.2 13.1 %convolution_convert_fusion.1 = bf16[256,3072]{1,0:T(8,128)(2,1)} fusion(bf16[256,4096]{1,0:T(8,128)(2,1)} %all-gather.3.cloned.1.call-done, bf16[4096,3072]{0,1:T(8,128)(2,1)} %all-gather.5.cloned.1.call-done), kind=kOutput, calls=%fused_computation.4 | convolution fusion | flops 6443237376 | bytes 28835840 | tf_op jit(solution)/shard_map/dot_general | solution.py:87
  529.4 1.7 copy.68
  531.1 2.7 copy.69
  534.5 4.6 all-to-all-start
  540.9 2.4 reshape.92
  543.6 1.3 copy.75
  544.9 2.5 copy.77
  547.4 40.2 %all-to-all-done = bf16[3,1024,256]{2,0,1:T(4,128)(2,1)S(1)} async-done(((bf16[3,1024,256]{2,0,1:T(4,128)(2,1)}), bf16[3,1024,256]{2,0,1:T(4,128)(2,1)S(1)}, u32[]{:S(2)}, u32[]{:S(2)}) %all-to-all-start) | async-done | bytes 1572896 | tf_op jit(solution)/shard_map/all_to_all | solution.py:96
  587.8 2.0 convert_bitcast_fusion
  589.8 2.4 copy.71
  595.5 8.8 %fusion.5 = f32[512,256,8]{1,0,2:T(8,128)S(1)} fusion(f32[128,256,8]{1,0,2:T(8,128)S(1)} %copy-done.3, f32[128,256,8]{1,0,2:T(8,128)S(1)} %copy.76), kind=kOutput, calls=%fused_computation.18 | convolution fusion | flops 3223584768 | bytes 6291456 | tf_op jit(solution)/shard_map/cmn,mk->ckn/dot_general | solution.py:39
  604.3 12.3 %add_bitcast_fusion = (f32[256,512,8]{0,1,2:T(8,128)}, f32[256,512,8]{0,1,2:T(8,128)}) fusion(f32[512,256,8]{1,0,2:T(8,128)S(1)} %fusion.5, f32[512,8]{0,1:T(8,128)S(1)} %get-tuple-element.18, f32[512,8]{0,1:T(8,128)S(1)} %get-tuple-element.19, f32[128,256,8]{1,0,2:T(8,128)S(1)} %copy-done.3, f32[128,256,8]{1,0,2:T(8,128)S(1)} %copy.76), kind=kOutput, calls=%fused_computation.3 | convolution fusion | flops 3230924800 | bytes 14712832 | tf_op jit(solution)/shard_map/cmn,mk->ckn/dot_general | solution.py:38
  616.6 5.5 copy.80
  622.2 8.4 %fusion.55 = f32[256,512,8]{1,2,0:T(8,128)} fusion(f32[256,512,8]{1,2,0:T(8,128)} %copy.80), kind=kOutput, calls=%fused_computation.72 | convolution fusion | flops 100664192 | bytes 8388608 | tf_op jit(solution)/shard_map/ckn,nj->ckj/dot_general | solution.py:42
  630.6 5.6 copy.81
  636.2 5.9 fusion.53
  642.1 5.1 convolution_add_fusion
  647.3 5.1 convolution_subtract_fusion
  653.6 2.3 fusion.51
  655.9 2.0 fusion.49
  658.0 2.2 convolution_subtract_fusion.1
  660.2 2.7 multiply_subtract_fusion
  662.9 4.9 fusion.1
  667.8 4.6 fusion.13
  673.9 18.1 %all_to_all.34 = bf16[128,8,256]{0,2,1:T(8,128)(2,1)S(1)} all-to-all(bf16[128,8,256]{0,2,1:T(8,128)(2,1)S(1)} %fusion.17), channel_id=1, replica_groups=mesh['seq'=8,'chan'=4] {'seq'}, dimensions={1} | all-to-all | bytes 1048576 | tf_op jit(solution)/shard_map/all_to_all | solution.py:120
  692.2 7.1 fusion
  699.4 30.6 %reduce-scatter.2.cloned.1.call-done = bf16[1024,256]{0,1:T(8,128)(2,1)} async-done(((bf16[4096,256]{0,1:T(8,128)(2,1)}), bf16[1024,256]{0,1:T(8,128)(2,1)}) %reduce-scatter.2.cloned.1.call-update) | async-done | bytes 524304 | tf_op jit(solution)/shard_map/reduce_scatter | solution.py:121
  (40 shorter events, 13.4 us)
Async XLA Ops:
  6.5 27.7 %all-gather.3.cloned.1.call-start = ((), (), s32[]{:S(2)}) async-start(), calls=%async_computation.4 | async-start | bytes 2621440 | tf_op jit(solution)/shard_map/all_gather | solution.py:86
  7.3 509.0 %all-gather.5.cloned.1.call-start = ((), (), s32[]{:S(2)}) async-start(), calls=%async_computation.5 | async-start | bytes 28311552 | tf_op jit(solution)/shard_map/all_gather | solution.py:89
  12.0 1.0 copy-start.6
  19.3 514.5 %all-to-all-start.1 = ((bf16[8,2,16384]{2,1,0:T(2,128)(2,1)}), bf16[8,2,16384]{2,1,0:T(2,128)(2,1)S(1)}, u32[]{:S(2)}, u32[]{:S(2)}) async-start(bf16[8,2,16384]{2,1,0:T(2,128)(2,1)} %reshape.91), calls=%async_computation.1 | async-start | bytes 1048576 | tf_op jit(solution)/shard_map/all_to_all | solution.py:97
  533.7 0.8 copy-start.5
  534.5 53.0 %all-to-all-start = ((bf16[3,1024,256]{2,0,1:T(4,128)(2,1)}), bf16[3,1024,256]{2,0,1:T(4,128)(2,1)S(1)}, u32[]{:S(2)}, u32[]{:S(2)}) async-start(bf16[3,1024,256]{2,0,1:T(4,128)(2,1)} %copy.69), calls=%async_computation | async-start | bytes 4194304 | tf_op jit(solution)/shard_map/all_to_all | solution.py:96
  539.1 190.8 %reduce-scatter.2.cloned.1.call-start = ((), (), s32[]{:S(2)}) async-start(), calls=%async_computation.6 | async-start | bytes 2621440 | tf_op jit(solution)/shard_map/reduce_scatter | solution.py:121
  594.3 1.2 copy-start.3
  636.2 5.9 copy-start.1
  636.2 5.9 copy-start.2
  642.1 5.2 copy-start
  672.5 1.2 copy-start.4
Sparse Core Ops, SparseCore 0:
  8.9 25.2 all-gather.2
  35.8 480.4 all-gather.4
  699.5 30.4 reduce-scatter.1
where the time goes:
time: 745 us; the launch traced here: 737 us
  waiting for transfers between devices  561 us (75%)
  matrix products  84.7 us (11%)
  local copies, waits for them, and re-layouts  37.7 us (5%)
  blocking collectives  18.1 us (2%)
  between operations  13.8 us (2%)
  starting transfers between devices  11.9 us (2%)
  other arithmetic  9.52 us (1%)
    all_gather x1, waiting for transfers between devices, body(): lax.all_gather(flat_weight, 'seq', axis=0, tiled=True)  482 us
    all_to_all x1, waiting for transfers between devices, body(): lax.all_to_all(outgoing, 'seq', split_axis=1, concat_axis=2, tiled=True)  40.2 us
    reduce_scatter x1, waiting for transfers between devices, body(): lax.psum_scatter(lax.dot_general(out_weight, returned, (((0,), (0,)), (()...  30.6 us
    all_to_all x1, blocking collectives, body(): lax.all_to_all(product, 'seq', split_axis=1, concat_axis=0, tiled=True)  18.1 us
  transfers between devices with their start and end apart: 5, of which 4 were waited for; matrix products, arithmetic and copies ran while one was open for 5% of the time, Pallas kernels for 0%

commit v1 on v0

--- a/solution.py
+++ b/solution.py
@@ -1,11 +1,16 @@
+import functools
 import math
 
 import jax
 import jax.numpy as jnp
+import numpy as np
 from jax import lax
+from jax.experimental import pallas as pl
+from jax.experimental.pallas import tpu as pltpu
 from jax.sharding import PartitionSpec as P
 
 exact_prec = lax.Precision.HIGHEST
+inner_len = 64
 
 
 def dft_tables(half_len, blocks):
@@ -129,6 +134,367 @@
     return jnp.transpose(summed).astype(jnp.bfloat16)
 
 
+def wave_tables(length):
+    span = 2 * length
+    outer = span // inner_len
+    used, rows = outer // 2, outer // 2 + 1
+    padded_rows = -(-rows // 8) * 8
+    m, k = np.arange(used), np.arange(rows)
+    n, j = np.arange(inner_len), np.arange(inner_len)
+    angle = (2.0 * math.pi / outer) * (np.outer(k, m) % outer)
+    ahead = np.zeros((2, padded_rows, used))
+    ahead[0, :rows], ahead[1, :rows] = np.cos(angle), -np.sin(angle)
+    weight = np.where((k == 0) | (k == used), 1.0, 2.0) / span
+    back = np.zeros((used, 2, padded_rows))
+    back[:, 0, :rows] = (np.cos(angle) * weight[:, None]).T
+    back[:, 1, :rows] = (-np.sin(angle) * weight[:, None]).T
+    turn = n[None, None, :] * (k[:, None, None] + outer * j[None, :, None]) % span
+    cos, sin = np.cos(turn * (2.0 * math.pi / span)), np.sin(turn * (2.0 * math.pi / span))
+    middle = np.concatenate(
+        [np.concatenate([cos, sin], 2), np.concatenate([-sin, cos], 2)], 1
+    )
+    return tuple(
+        jnp.asarray(table, jnp.bfloat16)
+        for table in (
+            ahead.reshape(2 * padded_rows, used),
+            middle,
+            np.swapaxes(middle, 1, 2),
+            back.reshape(used, 2 * padded_rows),
+        )
+    )
+
+
+def project_kernel(where_ref, *refs):
+    groups, parts = refs[:16], refs[16:20]
+    own_ref, send_ref, held, weights, sems = refs[20:]
+    place, chan = where_ref[0], where_ref[1]
+    depth, side = place // 2, place % 2
+    weight_copies = [
+        pltpu.make_async_copy(parts[i], weights.at[i], sems.at[i]) for i in range(4)
+    ]
+    token_copies = [
+        pltpu.make_async_copy(groups[i], held.at[i], sems.at[4 + i]) for i in range(16)
+    ]
+    for copy in weight_copies + token_copies:
+        copy.start()
+    for copy in weight_copies:
+        copy.wait()
+    block = own_ref.shape[0] // 8
+    half = own_ref.shape[1]
+    for step in range(4):
+        total = None
+        for turn in range(4):
+            token_copies[4 * step + turn].wait()
+            slot = jnp.bitwise_xor(depth, jnp.bitwise_xor(chan, turn))
+            term = jnp.dot(
+                held[4 * step + turn], weights[slot], preferred_element_type=jnp.float32
+            )
+            total = term if total is None else total + term
+        low, high = total[:, :half], total[:, half:]
+        own = jnp.where(side == 0, low, high)
+        send = jnp.where(side == 0, high, low).astype(jnp.bfloat16)
+        for pair in range(2):
+            start = pl.multiple_of(jnp.bitwise_xor(place, 2 * step + pair) * block, block)
+            own_ref[pl.ds(start, block), :] = own[pair * block : (pair + 1) * block]
+            send_ref[pl.ds(start, block), :] = send[pair * block : (pair + 1) * block]
+
+
+def project(where, groups, parts, length):
+    width = parts[0].shape[1] // 2
+    depth = parts[0].shape[0]
+    return pl.pallas_call(
+        project_kernel,
+        out_shape=(
+            jax.ShapeDtypeStruct((length, width), jnp.float32),
+            jax.ShapeDtypeStruct((length, width), jnp.bfloat16),
+        ),
+        in_specs=[pl.BlockSpec(memory_space=pltpu.SMEM)]
+        + [pl.BlockSpec(memory_space=pl.ANY)] * 20,
+        out_specs=(
+            pl.BlockSpec(memory_space=pltpu.VMEM),
+            pl.BlockSpec(memory_space=pltpu.VMEM),
+        ),
+        scratch_shapes=[
+            pltpu.VMEM((16,) + groups[0].shape, jnp.bfloat16),
+            pltpu.VMEM((4,) + parts[0].shape, jnp.bfloat16),
+            pltpu.SemaphoreType.DMA((20,)),
+        ],
+        compiler_params=pltpu.CompilerParams(vmem_limit_bytes=24 * 2**20),
+        cost_estimate=pl.CostEstimate(
+            flops=2 * length * 4 * depth * 2 * width,
+            bytes_accessed=2 * length * 4 * depth,
+            transcendentals=0,
+        ),
+        name="project",
+    )(where, *groups, *parts)
+
+
+def smooth_into(padded, own_ref, recv_ref, taps_ref, branch, store):
+    length = own_ref.shape[0]
+    tap_count = taps_ref.shape[1]
+    block = length // 8
+    padded[0:8, :] = jnp.zeros((8, padded.shape[1]), jnp.float32)
+    for i in range(8):
+        rows = slice(i * block, (i + 1) * block)
+        padded[8 + i * block : 8 + (i + 1) * block, :] = own_ref[rows, :] + recv_ref[
+            rows, :
+        ].astype(jnp.float32)
+    for i in range(8):
+        total = None
+        for tap in range(tap_count):
+            start = 8 + i * block - tap
+            term = taps_ref[branch, tap : tap + 1, :] * padded[start : start + block, :]
+            total = term if total is None else total + term
+        store(slice(i * block, (i + 1) * block), total)
+
+
+def mix_kernel(
+    where_ref, own1, recv1, own2, recv2, taps_ref, skip_ref, ahead, middle, middle_back, back, *refs
+):
+    filters, mixed_ref = refs[:8], refs[8]
+    padded, gated, lags, waves, filter_waves, sums = refs[9:]
+    place = where_ref[0]
+    length, width = own1.shape
+    block = length // 8
+    rows, two = middle.shape[0], middle.shape[1]
+    padded_rows = ahead.shape[0] // 2
+    used = ahead.shape[1]
+    for i in range(8):
+        start = pl.multiple_of(jnp.bitwise_xor(place, i) * block, block)
+        lags[pl.ds(start, block), :] = filters[i][...].astype(jnp.float32)
+
+    def first(at, value):
+        gated[at, :] = value
+
+    def second(at, value):
+        gated[at, :] = gated[at, :] * value
+
+    smooth_into(padded, own1, recv1, taps_ref, 1, first)
+    smooth_into(padded, own2, recv2, taps_ref, 2, second)
+    for n in range(inner_len):
+        both = jnp.concatenate(
+            [gated[pl.ds(n, used, stride=inner_len), :], lags[pl.ds(n, used, stride=inner_len), :]],
+            1,
+        ).astype(jnp.bfloat16)
+        wave = jnp.dot(ahead[...], both, preferred_element_type=jnp.float32)
+        for i in range(2):
+            at = pl.ds(i * inner_len + n, padded_rows, stride=two)
+            part = wave[i * padded_rows : (i + 1) * padded_rows]
+            waves[at, :] = part[:, :width]
+            filter_waves[at, :] = part[:, width:]
+    if padded_rows > rows:
+        sums[rows * two :, :] = jnp.zeros(((padded_rows - rows) * two, width), jnp.float32)
+
+    def one(k, _):
+        at = pl.ds(pl.multiple_of(k * two, two), two)
+        both = jnp.concatenate([waves[at, :], filter_waves[at, :]], 1).astype(jnp.bfloat16)
+        freq = jnp.dot(middle[k], both, preferred_element_type=jnp.float32)
+        data_real, filter_real = freq[:inner_len, :width], freq[:inner_len, width:]
+        data_imag, filter_imag = freq[inner_len:, :width], freq[inner_len:, width:]
+        spectrum = jnp.concatenate(
+            [
+                data_real * filter_real - data_imag * filter_imag,
+                data_real * filter_imag + data_imag * filter_real,
+            ],
+            0,
+        ).astype(jnp.bfloat16)
+        sums[at, :] = jnp.dot(middle_back[k], spectrum, preferred_element_type=jnp.float32)
+        return 0
+
+    lax.fori_loop(0, rows, one, 0, unroll=11 if rows % 11 == 0 else 1)
+    for n in range(0, inner_len, 2):
+        pieces = [
+            jnp.concatenate(
+                [
+                    sums[pl.ds(n + i, padded_rows, stride=two), :],
+                    sums[pl.ds(inner_len + n + i, padded_rows, stride=two), :],
+                ],
+                0,
+            )
+            for i in range(2)
+        ]
+        wave = jnp.dot(
+            back[...],
+            jnp.concatenate(pieces, 1).astype(jnp.bfloat16),
+            preferred_element_type=jnp.float32,
+        )
+        for i in range(2):
+            at = pl.ds(n + i, used, stride=inner_len)
+            mixed_ref[at, :] = wave[:, i * width : (i + 1) * width] + skip_ref[...] * gated[at, :]
+
+
+def mix(where, own1, recv1, own2, recv2, taps, skip, tables, filters):
+    length, width = own1.shape
+    rows, two = tables[1].shape[:2]
+    padded_rows = tables[0].shape[0] // 2
+    vmem = pl.BlockSpec(memory_space=pltpu.VMEM)
+    return pl.pallas_call(
+        mix_kernel,
+        out_shape=jax.ShapeDtypeStruct((length, width), jnp.float32),
+        in_specs=[pl.BlockSpec(memory_space=pltpu.SMEM)] + [vmem] * 18,
+        out_specs=vmem,
+        scratch_shapes=[
+            pltpu.VMEM((length + 8, width), jnp.float32),
+            pltpu.VMEM((length, width), jnp.float32),
+            pltpu.VMEM((length, width), jnp.float32),
+            pltpu.VMEM((padded_rows * two, width), jnp.float32),
+            pltpu.VMEM((padded_rows * two, width), jnp.float32),
+            pltpu.VMEM((padded_rows * two, width), jnp.float32),
+        ],
+        compiler_params=pltpu.CompilerParams(vmem_limit_bytes=40 * 2**20),
+        cost_estimate=pl.CostEstimate(
+            flops=2 * 8 * length * inner_len * width, bytes_accessed=6 * 2**20, transcendentals=0
+        ),
+        name="mix",
+    )(where, own1, recv1, own2, recv2, taps, skip, *tables, *filters)
+
+
+def gate_kernel(where_ref, own0, recv0, mixed_ref, taps_ref, *refs):
+    outs, padded, product = refs[:8], refs[8], refs[9]
+    place = where_ref[0]
+    block = own0.shape[0] // 8
+
+    def store(at, value):
+        product[at, :] = (mixed_ref[at, :] * value).astype(jnp.bfloat16)
+
+    smooth_into(padded, own0, recv0, taps_ref, 0, store)
+    for i in range(8):
+        start = pl.multiple_of(jnp.bitwise_xor(place, i) * block, block)
+        outs[i][...] = product[pl.ds(start, block), :]
+
+
+def gate(where, own0, recv0, mixed, taps):
+    length, width = own0.shape
+    vmem = pl.BlockSpec(memory_space=pltpu.VMEM)
+    return pl.pallas_call(
+        gate_kernel,
+        out_shape=(jax.ShapeDtypeStruct((length // 8, width), jnp.bfloat16),) * 8,
+        in_specs=[pl.BlockSpec(memory_space=pltpu.SMEM)] + [vmem] * 4,
+        out_specs=(vmem,) * 8,
+        scratch_shapes=[
+            pltpu.VMEM((length + 8, width), jnp.float32),
+            pltpu.VMEM((length, width), jnp.bfloat16),
+        ],
+        compiler_params=pltpu.CompilerParams(vmem_limit_bytes=16 * 2**20),
+        cost_estimate=pl.CostEstimate(
+            flops=8 * length * width, bytes_accessed=12 * length * width, transcendentals=0
+        ),
+        name="gate",
+    )(where, own0, recv0, mixed, taps)
+
+
+def emit_kernel(where_ref, *refs, added):
+    parts, weight_ref = refs[:8], refs[8]
+    extra = refs[9 : 9 + added]
+    out_ref, joined = refs[9 + added :]
+    place = where_ref[0]
+    width = parts[0].shape[1]
+
+    @pl.when(pl.program_id(0) == 0)
+    def _():
+        for i in range(8):
+            start = pl.multiple_of(jnp.bitwise_xor(place, i) * width, width)
+            joined[:, pl.ds(start, width)] = parts[i][...]
+
+    total = jnp.dot(joined[...], weight_ref[...], preferred_element_type=jnp.float32)
+    for term in extra:
+        total = total + term[...].astype(jnp.float32)
+    out_ref[...] = total.astype(out_ref.dtype)
+
+
+def emit(where, parts, weight, extra, out_dtype):
+    rows, width = parts[0].shape
+    columns = weight.shape[1] // 4
+    tile = columns // 4
+    whole = pl.BlockSpec((rows, width), lambda i, at: (0, 0))
+    tiled = pl.BlockSpec((rows, tile), lambda i, at: (0, i))
+    return pl.pallas_call(
+        functools.partial(emit_kernel, added=len(extra)),
+        out_shape=jax.ShapeDtypeStruct((rows, columns), out_dtype),
+        grid_spec=pltpu.PrefetchScalarGridSpec(
+            num_scalar_prefetch=1,
+            grid=(4,),
+            in_specs=[whole] * 8
+            + [pl.BlockSpec((weight.shape[0], tile), lambda i, at: (0, 4 * at[1] + i))]
+            + [tiled] * len(extra),
+            out_specs=tiled,
+            scratch_shapes=[pltpu.VMEM((rows, 8 * width), jnp.bfloat16)],
+        ),
+        compiler_params=pltpu.CompilerParams(vmem_limit_bytes=16 * 2**20),
+        cost_estimate=pl.CostEstimate(
+            flops=2 * rows * weight.shape[0] * columns,
+            bytes_accessed=2 * weight.shape[0] * columns,
+            transcendentals=0,
+        ),
+        name="emit",
+    )(where, *parts, weight, *extra)
+
+
+def swap(value, axis, count, turn):
+    return lax.ppermute(value, axis, [(i, i ^ turn) for i in range(count)])
+
+
+def fast_body(tokens, in_weight, short_taps, skip_gain, long_filter, out_weight):
+    seq, chans = lax.axis_size("seq"), lax.axis_size("chan")
+    place, chan = lax.axis_index("seq"), lax.axis_index("chan")
+    depth, side = place // 2, place % 2
+    rows, width = tokens.shape
+    length = rows * seq
+    part = width // seq
+    half = width // 2
+    where = jnp.stack([place, chan]).astype(jnp.int32)
+
+    ours = lax.dynamic_slice_in_dim(tokens, side * half, half, 1)
+    theirs = lax.dynamic_slice_in_dim(tokens, (1 - side) * half, half, 1)
+    pair = jnp.concatenate([ours, swap(theirs, "seq", seq, 1)], 0)
+    far = swap(pair, "seq", seq, 4)
+    line = [pair, swap(pair, "seq", seq, 2), far, swap(far, "seq", seq, 2)]
+    across = [swap(value, "chan", chans, 2) for value in line]
+    groups = []
+    for i in range(4):
+        groups += [
+            line[i],
+            swap(line[i], "chan", chans, 1),
+            across[i],
+            swap(across[i], "chan", chans, 1),
+        ]
+
+    filters = []
+    for turn in range(seq):
+        piece = lax.dynamic_slice_in_dim(long_filter, (place ^ turn) * part, part, 1)
+        filters.append(piece if turn == 0 else swap(piece, "seq", seq, turn))
+
+    def branch(index):
+        parts = []
+        for turn in range(4):
+            piece = lax.dynamic_slice_in_dim(
+                in_weight[:, index, :], (depth ^ turn) * 2 * part, 2 * part, 1
+            )
+            parts.append(piece if turn == 0 else swap(piece, "seq", seq, 2 * turn))
+        own, send = project(where, groups, parts, length)
+        return own, swap(send, "seq", seq, 1)
+
+    taps = lax.dynamic_slice_in_dim(short_taps, place * part, part, 2)
+    skip = lax.dynamic_slice_in_dim(skip_gain, place * part, part, 0)[None]
+    own1, recv1 = branch(1)
+    own2, recv2 = branch(2)
+    own0, recv0 = branch(0)
+    mixed = mix(where, own1, recv1, own2, recv2, taps, skip, wave_tables(length), filters)
+    pieces = gate(where, own0, recv0, mixed, taps)
+    joined = [
+        piece if turn == 0 else swap(piece, "seq", seq, turn) for turn, piece in enumerate(pieces)
+    ]
+
+    def share(turn, extra, dtype):
+        return emit(jnp.stack([place, chan ^ turn]).astype(jnp.int32), joined, out_weight, extra, dtype)
+
+    from_core = swap(share(3, [], jnp.bfloat16), "chan", chans, 1)
+    near = swap(share(1, [], jnp.bfloat16), "chan", chans, 1)
+    from_chip = swap(share(2, [from_core], jnp.bfloat16), "chan", chans, 2)
+    own = share(0, [near], jnp.float32)
+    return (own + from_chip.astype(jnp.float32)).astype(jnp.bfloat16)
+
+
 def solution(mesh):
     in_specs = (
         P("seq", "chan"),
@@ -139,4 +505,6 @@
         P("chan", None),
     )
     out_specs = P("seq", "chan")
-    return jax.shard_map(body, mesh=mesh, in_specs=in_specs, out_specs=out_specs, check_vma=False)
+    seq, chans = mesh.shape["seq"], mesh.shape["chan"]
+    chosen = fast_body if seq == 8 and chans == 4 else body
+    return jax.shard_map(chosen, mesh=mesh, in_specs=in_specs, out_specs=out_specs, check_vma=False)

time: 745 us -> 263 us (0.35)
  waiting for transfers between devices: 561 us -> 110 us
  matrix products: 84.7 us -> 0 us
  starting transfers between devices: 11.9 us -> 61 us
  Pallas kernels: 0 us -> 48.9 us
  blocking collectives: 18.1 us -> 0 us
  between operations: 13.8 us -> 0.27 us
  other arithmetic: 9.52 us -> 1.27 us
    all_gather x2 -> x0, waiting for transfers between devices: 490 us -> none  [the longest x1 482 us: body(): lax.all_gather(flat_weight, 'seq', axis=0, tiled=True)]
    ppermute x0 -> x45, waiting for transfers between devices: none -> 110 us  [swap(): return lax.ppermute(value, axis, [(i, i ^ turn) for i in range(count)])]
    dot_general x14 -> x0, matrix products: 84.7 us -> none  [the longest x1 13.1 us: body(): jnp.dot(whole, lax.all_gather(flat_weight, 'seq', axis=0, tiled=True), pr...]
    ppermute x0 -> x45, starting transfers between devices: none -> 61 us  [swap(): return lax.ppermute(value, axis, [(i, i ^ turn) for i in range(count)])]
    pallas_call x0 -> x9, Pallas kernels: none -> 48.9 us  [the longest x3 22.2 us: project(): pl.pallas_call(project_kernel, out_shape=(jax.ShapeDtypeStruct((length, w...]
    all_to_all x2 -> x0, waiting for transfers between devices: 40.2 us -> none  [the longest x1 40.2 us: body(): lax.all_to_all(outgoing, 'seq', split_axis=1, concat_axis=2, tiled=True)]
    reduce_scatter x1 -> x0, waiting for transfers between devices: 30.6 us -> none  [body(): lax.psum_scatter(lax.dot_general(out_weight, returned, (((0,), (0,)), (()...]
    unnamed x21 -> x56, local copies, waits for them, and re-layouts: 12 us -> 30.8 us
  transfers between devices with their start and end apart: 5 -> 45, of which waited for: 4 -> 17; matrix products, arithmetic and copies ran while one was open for 5% -> 4% of each run, Pallas kernels for 0% -> 17%
where the time goes in v1:
time: 263 us; the launch traced here: 262 us
  waiting for transfers between devices  110 us (42%)
  starting transfers between devices  61 us (23%)
  Pallas kernels  48.9 us (19%)
  local copies, waits for them, and re-layouts  40.8 us (16%)
    ppermute x45, waiting for transfers between devices, swap(): return lax.ppermute(value, axis, [(i, i ^ turn) for i in range(count)])  110 us
    ppermute x45, starting transfers between devices, swap(): return lax.ppermute(value, axis, [(i, i ^ turn) for i in range(count)])  61 us
    unnamed x56, local copies, waits for them, and re-layouts  30.8 us
    pallas_call x3, Pallas kernels, project(): pl.pallas_call(project_kernel, out_shape=(jax.ShapeDtypeStruct((length, w...  22.2 us
    pallas_call x1, Pallas kernels, mix(): pl.pallas_call(mix_kernel, out_shape=jax.ShapeDtypeStruct((length, width)...  16.1 us
    pallas_call x4, Pallas kernels, emit(): pl.pallas_call(functools.partial(emit_kernel, added=len(extra)), out_shap...  9.63 us
  transfers between devices with their start and end apart: 45, of which 17 were waited for; matrix products, arithmetic and copies ran while one was open for 4% of the time, Pallas kernels for 17%

profile of v1, /device:TPU:0, one launch (start us, length us, event | category | flops | bytes accessed | tf_op | source)
XLA Modules:
  0.0 261.8 jit_solution(6635350263075234155)
XLA Ops:
  1.1 3.0 %collective-permute-start = (bf16[256,512]{1,0:T(8,128)(2,1)S(1)}, bf16[256,512]{1,0:T(8,128)(2,1)S(1)}, u32[]{:S(2)}, u32[]{:S(2)}) collective-permute-start(bf16[256,512]{1,0:T(8,128)(2,1)S(1)} %get-tuple-element.57), channel_id=1, source_target_pairs={{0,4},{4,0},{8,12},{12,8},{16,20},{20,16},{24,28},{28,24},{1,5},{5... | collective-permute-start | bytes 786440 | tf_op jit(solution)/shard_map/ppermute | solution.py:434
  4.1 6.3 %collective-permute-done = bf16[256,512]{1,0:T(8,128)(2,1)S(1)} collective-permute-done((bf16[256,512]{1,0:T(8,128)(2,1)S(1)}, bf16[256,512]{1,0:T(8,128)(2,1)S(1)}, u32[]{:S(2)}, u32[]{:S(2)}) %collective-permute-start) | collective-permute-done | bytes 262176 | tf_op jit(solution)/shard_map/ppermute | solution.py:434
  10.4 2.9 %collective-permute-start.8 = (bf16[512,512]{1,0:T(8,128)(2,1)S(1)}, bf16[512,512]{1,0:T(8,128)(2,1)S(1)}, u32[]{:S(2)}, u32[]{:S(2)}) collective-permute-start(bf16[512,512]{1,0:T(8,128)(2,1)S(1)} %pad_maximum_fusion.refs_0_), channel_id=1, source_target_pairs={{0,16},{4,20},{8,24},{12,28},{16,0},{20,4},{24,8},{28,12},{1,17},{... | collective-permute-start | bytes 1572872 | tf_op jit(solution)/shard_map/ppermute | solution.py:434
  13.3 3.5 %fusion = (bf16[512,1,1024]{2,0,1:T(8,128)(2,1)}, bf16[512,1,1024]{2,0,1:T(8,128)(2,1)}, bf16[512,1,1024]{2,0,1:T(8,128)(2,1)S(1)}) fusion(bf16[512,3,1024]{2,0,1:T(8,128)(2,1)} %param.11), kind=kLoop, calls=%fused_computation.30 | loop fusion | bytes 6291456 | tf_op jit(solution)/shard_map/slice | solution.py:471
  20.9 10.4 %collective-permute-done.20.refs_17_ = bf16[512,256]{1,0:T(8,128)(2,1)S(1)} collective-permute-done((bf16[512,256]{1,0:T(8,128)(2,1)S(1)}, bf16[512,256]{1,0:T(8,128)(2,1)S(1)}, u32[]{:S(2)}, u32[]{:S(2)}) %collective-permute-start.20) | collective-permute-done | bytes 262176 | tf_op jit(solution)/shard_map/ppermute | solution.py:434
  33.4 20.4 %collective-permute-done.21.refs_18_ = bf16[512,256]{1,0:T(8,128)(2,1)S(1)} collective-permute-done((bf16[512,256]{1,0:T(8,128)(2,1)S(1)}, bf16[512,256]{1,0:T(8,128)(2,1)S(1)}, u32[]{:S(2)}, u32[]{:S(2)}) %collective-permute-start.21) | collective-permute-done | bytes 262176 | tf_op jit(solution)/shard_map/ppermute | solution.py:434
  61.2 13.3 %collective-permute-done.24.refs_17_ = bf16[512,256]{1,0:T(8,128)(2,1)S(1)} collective-permute-done((bf16[512,256]{1,0:T(8,128)(2,1)S(1)}, bf16[512,256]{1,0:T(8,128)(2,1)S(1)}, u32[]{:S(2)}, u32[]{:S(2)}) %collective-permute-start.24) | collective-permute-done | bytes 262176 | tf_op jit(solution)/shard_map/ppermute | solution.py:434
  78.6 11.5 %collective-permute-done.10.refs_10_ = bf16[512,512]{1,0:T(8,128)(2,1)} collective-permute-done((bf16[512,512]{1,0:T(8,128)(2,1)S(1)}, bf16[512,512]{1,0:T(8,128)(2,1)}, u32[]{:S(2)}, u32[]{:S(2)}) %collective-permute-start.10) | collective-permute-done | bytes 524320 | tf_op jit(solution)/shard_map/ppermute | solution.py:434
  91.5 8.6 %collective-permute-done.14.refs_14_ = bf16[512,512]{1,0:T(8,128)(2,1)} collective-permute-done((bf16[512,512]{1,0:T(8,128)(2,1)S(1)}, bf16[512,512]{1,0:T(8,128)(2,1)}, u32[]{:S(2)}, u32[]{:S(2)}) %collective-permute-start.14) | collective-permute-done | bytes 524320 | tf_op jit(solution)/shard_map/ppermute | solution.py:434
  101.5 2.8 %collective-permute-start.26 = (bf16[512,256]{1,0:T(8,128)(2,1)}, bf16[512,256]{1,0:T(8,128)(2,1)S(1)}, u32[]{:S(2)}, u32[]{:S(2)}) collective-permute-start(bf16[512,256]{1,0:T(8,128)(2,1)} %get-tuple-element.36), channel_id=1, source_target_pairs={{0,24},{4,28},{8,16},{12,20},{16,8},{20,12},{24,0},{28,4},{1,25},{... | collective-permute-start | bytes 786440 | tf_op jit(solution)/shard_map/ppermute | solution.py:434
  106.0 2.8 %collective-permute-start.18 = (bf16[512,256]{1,0:T(8,128)(2,1)S(1)}, bf16[512,256]{1,0:T(8,128)(2,1)S(1)}, u32[]{:S(2)}, u32[]{:S(2)}) collective-permute-start(bf16[512,256]{1,0:T(8,128)(2,1)S(1)} %get-tuple-element.44), channel_id=1, source_target_pairs={{0,24},{4,28},{8,16},{12,20},{16,8},{20,12},{24,0},{28,4},{1,25},{... | collective-permute-start | bytes 786440 | tf_op jit(solution)/shard_map/ppermute | solution.py:434
  113.7 7.4 %project.4 = (f32[2048,128]{1,0:T(8,128)S(1)}, bf16[2048,128]{1,0:T(8,128)(2,1)}) custom-call(s32[2]{0:T(128)S(1)} %pad_add_fusion.where_ref, bf16[512,512]{1,0:T(8,128)(2,1)S(1)} %pad_maximum_fusion.refs_0_, bf16[512,512]{1,0:T(8,128)(2,1)S(1)} %collective-permute-done.1.refs_1_, bf16[512,512]{1,0:T(8,128)(2,1)S(1)} %collective-permute-done.2.refs_2_, ...), custom_call_target="tpu_custom_call" | custom-call | flops 2147483648 | bytes 8388608 | tf_op jit(solution)/shard_map/project/pallas_call | solution.py:205
  124.4 7.3 %project.5 = (f32[2048,128]{1,0:T(8,128)S(1)}, bf16[2048,128]{1,0:T(8,128)(2,1)}) custom-call(s32[2]{0:T(128)S(1)} %pad_add_fusion.where_ref, bf16[512,512]{1,0:T(8,128)(2,1)S(1)} %pad_maximum_fusion.refs_0_, bf16[512,512]{1,0:T(8,128)(2,1)S(1)} %collective-permute-done.1.refs_1_, bf16[512,512]{1,0:T(8,128)(2,1)S(1)} %collective-permute-done.2.refs_2_, ...), custom_call_target="tpu_custom_call" | custom-call | flops 2147483648 | bytes 8388608 | tf_op jit(solution)/shard_map/project/pallas_call | solution.py:205
  133.3 11.7 %collective-permute-done.17.refs_18_ = bf16[512,256]{1,0:T(8,128)(2,1)S(1)} collective-permute-done((bf16[512,256]{1,0:T(8,128)(2,1)S(1)}, bf16[512,256]{1,0:T(8,128)(2,1)S(1)}, u32[]{:S(2)}, u32[]{:S(2)}) %collective-permute-start.17) | collective-permute-done | bytes 262176 | tf_op jit(solution)/shard_map/ppermute | solution.py:434
  145.0 7.5 %project.3 = (f32[2048,128]{1,0:T(8,128)S(1)}, bf16[2048,128]{1,0:T(8,128)(2,1)}) custom-call(s32[2]{0:T(128)S(1)} %pad_add_fusion.where_ref, bf16[512,512]{1,0:T(8,128)(2,1)S(1)} %pad_maximum_fusion.refs_0_, bf16[512,512]{1,0:T(8,128)(2,1)S(1)} %collective-permute-done.1.refs_1_, bf16[512,512]{1,0:T(8,128)(2,1)S(1)} %collective-permute-done.2.refs_2_, ...), custom_call_target="tpu_custom_call" | custom-call | flops 2147483648 | bytes 8388608 | tf_op jit(solution)/shard_map/project/pallas_call | solution.py:205
  156.7 6.1 %collective-permute-start.29 = (bf16[256,128]{1,0:T(8,128)(2,1)S(1)}, bf16[256,128]{1,0:T(8,128)(2,1)S(1)}, u32[]{:S(2)}, u32[]{:S(2)}) collective-permute-start(bf16[256,128]{1,0:T(8,128)(2,1)S(1)} %get-tuple-element.52), channel_id=1, source_target_pairs={{0,8},{4,12},{8,0},{12,4},{16,24},{20,28},{24,16},{28,20},{1,9},{5... | collective-permute-start | bytes 196616 | tf_op jit(solution)/shard_map/ppermute | solution.py:434
  162.9 6.1 %collective-permute-done.28.refs_1_ = bf16[256,128]{1,0:T(8,128)(2,1)S(1)} collective-permute-done((bf16[256,128]{1,0:T(8,128)(2,1)S(1)}, bf16[256,128]{1,0:T(8,128)(2,1)S(1)}, u32[]{:S(2)}, u32[]{:S(2)}) %collective-permute-start.28) | collective-permute-done | bytes 65568 | tf_op jit(solution)/shard_map/ppermute | solution.py:434
  169.0 7.1 %collective-permute-start.30 = (bf16[256,128]{1,0:T(8,128)(2,1)S(1)}, bf16[256,128]{1,0:T(8,128)(2,1)S(1)}, u32[]{:S(2)}, u32[]{:S(2)}) collective-permute-start(bf16[256,128]{1,0:T(8,128)(2,1)S(1)} %get-tuple-element.51), channel_id=1, source_target_pairs={{0,12},{4,8},{8,4},{12,0},{16,28},{20,24},{24,20},{28,16},{1,13},{... | collective-permute-start | bytes 196616 | tf_op jit(solution)/shard_map/ppermute | solution.py:434
  176.1 2.2 collective-permute-done.30.refs_3_
  188.0 4.1 %collective-permute-done.34.refs_7_ = bf16[256,128]{1,0:T(8,128)(2,1)S(1)} collective-permute-done((bf16[256,128]{1,0:T(8,128)(2,1)S(1)}, bf16[256,128]{1,0:T(8,128)(2,1)S(1)}, u32[]{:S(2)}, u32[]{:S(2)}) %collective-permute-start.34) | collective-permute-done | bytes 65568 | tf_op jit(solution)/shard_map/ppermute | solution.py:434
  197.0 16.1 %mix.1.mixed_ref = f32[2048,128]{1,0:T(8,128)S(1)} custom-call(s32[2]{0:T(128)S(1)} %pad_add_fusion.where_ref, f32[2048,128]{1,0:T(8,128)S(1)} %copy-done.15, bf16[2048,128]{1,0:T(8,128)(2,1)} %collective-permute-done.23.recv1, f32[2048,128]{1,0:T(8,128)S(1)} %copy-done.17, bf16[2048,128]{1,0:T(8,128)(2,1)} %collective-permute-done.27.recv2, ...), custom_call_target="tpu_custom_call" | custom-call | flops 268435456 | bytes 6291456 | tf_op jit(solution)/shard_map/mix/pallas_call | solution.py:331
  221.8 3.5 %collective-permute-start.41 = (bf16[256,128]{1,0:T(8,128)(2,1)S(1)}, bf16[256,128]{1,0:T(8,128)(2,1)S(1)}, u32[]{:S(2)}, u32[]{:S(2)}) collective-permute-start(bf16[256,128]{1,0:T(8,128)(2,1)S(1)} %get-tuple-element.32), channel_id=1, source_target_pairs={{0,28},{4,24},{8,20},{12,16},{16,12},{20,8},{24,4},{28,0},{1,29},{... | collective-permute-start | bytes 196616 | tf_op jit(solution)/shard_map/ppermute | solution.py:434
  226.2 2.5 collective-permute-done.41.refs_7_
  228.8 3.4 %copy-done.1 = bf16[1024,4096]{1,0:T(8,128)(2,1)S(1)} copy-done((bf16[1024,4096]{1,0:T(8,128)(2,1)S(1)}, bf16[1024,4096]{1,0:T(8,128)(2,1)}, u32[]{:S(2)}) %copy-start.1) | copy-done | bytes 8388632
  232.1 2.4 emit.6
  234.7 3.4 %copy-done.2 = bf16[1024,4096]{1,0:T(8,128)(2,1)S(1)} copy-done((bf16[1024,4096]{1,0:T(8,128)(2,1)S(1)}, bf16[1024,4096]{1,0:T(8,128)(2,1)}, u32[]{:S(2)}) %copy-start.2) | copy-done | bytes 8388632
  238.1 2.4 emit.4
  241.1 3.4 %copy-done.3 = bf16[1024,4096]{1,0:T(8,128)(2,1)S(1)} copy-done((bf16[1024,4096]{1,0:T(8,128)(2,1)S(1)}, bf16[1024,4096]{1,0:T(8,128)(2,1)}, u32[]{:S(2)}) %copy-start.3) | copy-done | bytes 8388632
  244.4 2.5 emit.7
  248.5 3.4 %copy-done.4 = bf16[1024,4096]{1,0:T(8,128)(2,1)S(1)} copy-done((bf16[1024,4096]{1,0:T(8,128)(2,1)S(1)}, bf16[1024,4096]{1,0:T(8,128)(2,1)}, u32[]{:S(2)}) %copy-start.4) | copy-done | bytes 8388632
  251.9 2.5 emit.5
  254.3 6.5 %collective-permute-done.44 = bf16[256,1024]{1,0:T(8,128)(2,1)S(1)} collective-permute-done((bf16[256,1024]{1,0:T(8,128)(2,1)S(1)}, bf16[256,1024]{1,0:T(8,128)(2,1)S(1)}, u32[]{:S(2)}, u32[]{:S(2)}) %collective-permute-start.44) | collective-permute-done | bytes 524320 | tf_op jit(solution)/shard_map/ppermute | solution.py:434
  (137 shorter events, 64.5 us)
Async XLA Ops:
  1.1 9.3 %collective-permute-start = (bf16[256,512]{1,0:T(8,128)(2,1)S(1)}, bf16[256,512]{1,0:T(8,128)(2,1)S(1)}, u32[]{:S(2)}, u32[]{:S(2)}) collective-permute-start(bf16[256,512]{1,0:T(8,128)(2,1)S(1)} %get-tuple-element.57), channel_id=1, source_target_pairs={{0,4},{4,0},{8,12},{12,8},{16,20},{20,16},{24,28},{28,24},{1,5},{5... | collective-permute-start | bytes 786440 | tf_op jit(solution)/shard_map/ppermute | solution.py:434
  10.4 44.1 %collective-permute-start.8 = (bf16[512,512]{1,0:T(8,128)(2,1)S(1)}, bf16[512,512]{1,0:T(8,128)(2,1)S(1)}, u32[]{:S(2)}, u32[]{:S(2)}) collective-permute-start(bf16[512,512]{1,0:T(8,128)(2,1)S(1)} %pad_maximum_fusion.refs_0_), channel_id=1, source_target_pairs={{0,16},{4,20},{8,24},{12,28},{16,0},{20,4},{24,8},{28,12},{1,17},{... | collective-permute-start | bytes 1572872 | tf_op jit(solution)/shard_map/ppermute | solution.py:434
  17.0 14.3 %collective-permute-start.20 = (bf16[512,256]{1,0:T(8,128)(2,1)S(1)}, bf16[512,256]{1,0:T(8,128)(2,1)S(1)}, u32[]{:S(2)}, u32[]{:S(2)}) collective-permute-start(bf16[512,256]{1,0:T(8,128)(2,1)S(1)} %get-tuple-element.42), channel_id=1, source_target_pairs={{0,8},{4,12},{8,0},{12,4},{16,24},{20,28},{24,16},{28,20},{1,9},{5... | collective-permute-start | bytes 786440 | tf_op jit(solution)/shard_map/ppermute | solution.py:434
  18.6 35.2 %collective-permute-start.21 = (bf16[512,256]{1,0:T(8,128)(2,1)S(1)}, bf16[512,256]{1,0:T(8,128)(2,1)S(1)}, u32[]{:S(2)}, u32[]{:S(2)}) collective-permute-start(bf16[512,256]{1,0:T(8,128)(2,1)S(1)} %get-tuple-element.41), channel_id=1, source_target_pairs={{0,16},{4,20},{8,24},{12,28},{16,0},{20,4},{24,8},{28,12},{1,17},{... | collective-permute-start | bytes 786440 | tf_op jit(solution)/shard_map/ppermute | solution.py:434
  19.0 40.6 %collective-permute-start.2 = (bf16[512,512]{1,0:T(8,128)(2,1)S(1)}, bf16[512,512]{1,0:T(8,128)(2,1)S(1)}, u32[]{:S(2)}, u32[]{:S(2)}) collective-permute-start(bf16[512,512]{1,0:T(8,128)(2,1)S(1)} %pad_maximum_fusion.refs_0_), channel_id=1, source_target_pairs={{0,2},{1,3},{2,0},{3,1},{4,6},{5,7},{6,4},{7,5},{8,10},{9,11},{10,... | collective-permute-start | bytes 1572872 | tf_op jit(solution)/shard_map/ppermute | solution.py:434
  20.5 39.1 %collective-permute-start.4 = (bf16[512,512]{1,0:T(8,128)(2,1)S(1)}, bf16[512,512]{1,0:T(8,128)(2,1)S(1)}, u32[]{:S(2)}, u32[]{:S(2)}) collective-permute-start(bf16[512,512]{1,0:T(8,128)(2,1)S(1)} %pad_maximum_fusion.refs_0_), channel_id=1, source_target_pairs={{0,8},{4,12},{8,0},{12,4},{16,24},{20,28},{24,16},{28,20},{1,9},{5... | collective-permute-start | bytes 1572872 | tf_op jit(solution)/shard_map/ppermute | solution.py:434
  32.0 24.7 %collective-permute-start.22 = (bf16[512,256]{1,0:T(8,128)(2,1)S(1)}, bf16[512,256]{1,0:T(8,128)(2,1)S(1)}, u32[]{:S(2)}, u32[]{:S(2)}) collective-permute-start(bf16[512,256]{1,0:T(8,128)(2,1)S(1)} %get-tuple-element.40), channel_id=1, source_target_pairs={{0,24},{4,28},{8,16},{12,20},{16,8},{20,12},{24,0},{28,4},{1,25},{... | collective-permute-start | bytes 786440 | tf_op jit(solution)/shard_map/ppermute | solution.py:434
  54.5 22.2 %collective-permute-start.1 = (bf16[512,512]{1,0:T(8,128)(2,1)S(1)}, bf16[512,512]{1,0:T(8,128)(2,1)S(1)}, u32[]{:S(2)}, u32[]{:S(2)}) collective-permute-start(bf16[512,512]{1,0:T(8,128)(2,1)S(1)} %pad_maximum_fusion.refs_0_), channel_id=1, source_target_pairs={{0,1},{1,0},{2,3},{3,2},{4,5},{5,4},{6,7},{7,6},{8,9},{9,8},{10,11... | collective-permute-start | bytes 1572872 | tf_op jit(solution)/shard_map/ppermute | solution.py:434
  54.5 22.2 %collective-permute-start.12 = (bf16[512,512]{1,0:T(8,128)(2,1)S(1)}, bf16[512,512]{1,0:T(8,128)(2,1)S(1)}, u32[]{:S(2)}, u32[]{:S(2)}) collective-permute-start(bf16[512,512]{1,0:T(8,128)(2,1)S(1)} %collective-permute-done.8.refs_8_), channel_id=1, source_target_pairs={{0,8},{4,12},{8,0},{12,4},{16,24},{20,28},{24,16},{28,20},{1,9},{5... | collective-permute-start | bytes 1572872 | tf_op jit(solution)/shard_map/ppermute | solution.py:434
  57.4 17.1 %collective-permute-start.24 = (bf16[512,256]{1,0:T(8,128)(2,1)S(1)}, bf16[512,256]{1,0:T(8,128)(2,1)S(1)}, u32[]{:S(2)}, u32[]{:S(2)}) collective-permute-start(bf16[512,256]{1,0:T(8,128)(2,1)S(1)} %get-tuple-element.38), channel_id=1, source_target_pairs={{0,8},{4,12},{8,0},{12,4},{16,24},{20,28},{24,16},{28,20},{1,9},{5... | collective-permute-start | bytes 786440 | tf_op jit(solution)/shard_map/ppermute | solution.py:434
  59.6 17.7 %collective-permute-start.3 = (bf16[512,512]{1,0:T(8,128)(2,1)S(1)}, bf16[512,512]{1,0:T(8,128)(2,1)S(1)}, u32[]{:S(2)}, u32[]{:S(2)}) collective-permute-start(bf16[512,512]{1,0:T(8,128)(2,1)S(1)} %collective-permute-done.2.refs_2_), channel_id=1, source_target_pairs={{0,1},{1,0},{2,3},{3,2},{4,5},{5,4},{6,7},{7,6},{8,9},{9,8},{10,11... | collective-permute-start | bytes 1572872 | tf_op jit(solution)/shard_map/ppermute | solution.py:434
  59.6 18.7 %collective-permute-start.6 = (bf16[512,512]{1,0:T(8,128)(2,1)S(1)}, bf16[512,512]{1,0:T(8,128)(2,1)}, u32[]{:S(2)}, u32[]{:S(2)}) collective-permute-start(bf16[512,512]{1,0:T(8,128)(2,1)S(1)} %collective-permute-done.4.refs_4_), channel_id=1, source_target_pairs={{0,2},{1,3},{2,0},{3,1},{4,6},{5,7},{6,4},{7,5},{8,10},{9,11},{10,... | collective-permute-start | bytes 1572872 | tf_op jit(solution)/shard_map/ppermute | solution.py:434
  75.2 14.9 %collective-permute-start.10 = (bf16[512,512]{1,0:T(8,128)(2,1)S(1)}, bf16[512,512]{1,0:T(8,128)(2,1)}, u32[]{:S(2)}, u32[]{:S(2)}) collective-permute-start(bf16[512,512]{1,0:T(8,128)(2,1)S(1)} %collective-permute-done.8.refs_8_), channel_id=1, source_target_pairs={{0,2},{1,3},{2,0},{3,1},{4,6},{5,7},{6,4},{7,5},{8,10},{9,11},{10,... | collective-permute-start | bytes 1572872 | tf_op jit(solution)/shard_map/ppermute | solution.py:434
  76.8 13.4 %collective-permute-start.5 = (bf16[512,512]{1,0:T(8,128)(2,1)S(1)}, bf16[512,512]{1,0:T(8,128)(2,1)S(1)}, u32[]{:S(2)}, u32[]{:S(2)}) collective-permute-start(bf16[512,512]{1,0:T(8,128)(2,1)S(1)} %collective-permute-done.4.refs_4_), channel_id=1, source_target_pairs={{0,1},{1,0},{2,3},{3,2},{4,5},{5,4},{6,7},{7,6},{8,9},{9,8},{10,11... | collective-permute-start | bytes 1572872 | tf_op jit(solution)/shard_map/ppermute | solution.py:434
  76.8 23.4 %collective-permute-start.14 = (bf16[512,512]{1,0:T(8,128)(2,1)S(1)}, bf16[512,512]{1,0:T(8,128)(2,1)}, u32[]{:S(2)}, u32[]{:S(2)}) collective-permute-start(bf16[512,512]{1,0:T(8,128)(2,1)S(1)} %collective-permute-done.12.refs_12_), channel_id=1, source_target_pairs={{0,2},{1,3},{2,0},{3,1},{4,6},{5,7},{6,4},{7,5},{8,10},{9,11},{10,... | collective-permute-start | bytes 1572872 | tf_op jit(solution)/shard_map/ppermute | solution.py:434
  78.1 23.3 %collective-permute-start.9 = (bf16[512,512]{1,0:T(8,128)(2,1)S(1)}, bf16[512,512]{1,0:T(8,128)(2,1)}, u32[]{:S(2)}, u32[]{:S(2)}) collective-permute-start(bf16[512,512]{1,0:T(8,128)(2,1)S(1)} %collective-permute-done.8.refs_8_), channel_id=1, source_target_pairs={{0,1},{1,0},{2,3},{3,2},{4,5},{5,4},{6,7},{7,6},{8,9},{9,8},{10,11... | collective-permute-start | bytes 1572872 | tf_op jit(solution)/shard_map/ppermute | solution.py:434
  78.3 23.2 %collective-permute-start.7 = (bf16[512,512]{1,0:T(8,128)(2,1)}, bf16[512,512]{1,0:T(8,128)(2,1)}, u32[]{:S(2)}, u32[]{:S(2)}) collective-permute-start(bf16[512,512]{1,0:T(8,128)(2,1)} %collective-permute-done.6.refs_6_), channel_id=1, source_target_pairs={{0,1},{1,0},{2,3},{3,2},{4,5},{5,4},{6,7},{7,6},{8,9},{9,8},{10,11... | collective-permute-start | bytes 1572872 | tf_op jit(solution)/shard_map/ppermute | solution.py:434
  90.2 14.2 %collective-permute-start.11 = (bf16[512,512]{1,0:T(8,128)(2,1)}, bf16[512,512]{1,0:T(8,128)(2,1)}, u32[]{:S(2)}, u32[]{:S(2)}) collective-permute-start(bf16[512,512]{1,0:T(8,128)(2,1)} %collective-permute-done.10.refs_10_), channel_id=1, source_target_pairs={{0,1},{1,0},{2,3},{3,2},{4,5},{5,4},{6,7},{7,6},{8,9},{9,8},{10,11... | collective-permute-start | bytes 1572872 | tf_op jit(solution)/shard_map/ppermute | solution.py:434
  91.0 14.1 %collective-permute-start.13 = (bf16[512,512]{1,0:T(8,128)(2,1)S(1)}, bf16[512,512]{1,0:T(8,128)(2,1)}, u32[]{:S(2)}, u32[]{:S(2)}) collective-permute-start(bf16[512,512]{1,0:T(8,128)(2,1)S(1)} %collective-permute-done.12.refs_12_), channel_id=1, source_target_pairs={{0,1},{1,0},{2,3},{3,2},{4,5},{5,4},{6,7},{7,6},{8,9},{9,8},{10,11... | collective-permute-start | bytes 1572872 | tf_op jit(solution)/shard_map/ppermute | solution.py:434
  101.4 21.5 %collective-permute-start.25 = (bf16[512,256]{1,0:T(8,128)(2,1)}, bf16[512,256]{1,0:T(8,128)(2,1)S(1)}, u32[]{:S(2)}, u32[]{:S(2)}) collective-permute-start(bf16[512,256]{1,0:T(8,128)(2,1)} %get-tuple-element.37), channel_id=1, source_target_pairs={{0,16},{4,20},{8,24},{12,28},{16,0},{20,4},{24,8},{28,12},{1,17},{... | collective-permute-start | bytes 786440 | tf_op jit(solution)/shard_map/ppermute | solution.py:434
  101.5 22.9 %collective-permute-start.26 = (bf16[512,256]{1,0:T(8,128)(2,1)}, bf16[512,256]{1,0:T(8,128)(2,1)S(1)}, u32[]{:S(2)}, u32[]{:S(2)}) collective-permute-start(bf16[512,256]{1,0:T(8,128)(2,1)} %get-tuple-element.36), channel_id=1, source_target_pairs={{0,24},{4,28},{8,16},{12,20},{16,8},{20,12},{24,0},{28,4},{1,25},{... | collective-permute-start | bytes 786440 | tf_op jit(solution)/shard_map/ppermute | solution.py:434
  104.4 28.9 %collective-permute-start.16 = (bf16[512,256]{1,0:T(8,128)(2,1)S(1)}, bf16[512,256]{1,0:T(8,128)(2,1)S(1)}, u32[]{:S(2)}, u32[]{:S(2)}) collective-permute-start(bf16[512,256]{1,0:T(8,128)(2,1)S(1)} %get-tuple-element.46), channel_id=1, source_target_pairs={{0,8},{4,12},{8,0},{12,4},{16,24},{20,28},{24,16},{28,20},{1,9},{5... | collective-permute-start | bytes 786440 | tf_op jit(solution)/shard_map/ppermute | solution.py:434
  105.0 40.0 %collective-permute-start.17 = (bf16[512,256]{1,0:T(8,128)(2,1)S(1)}, bf16[512,256]{1,0:T(8,128)(2,1)S(1)}, u32[]{:S(2)}, u32[]{:S(2)}) collective-permute-start(bf16[512,256]{1,0:T(8,128)(2,1)S(1)} %get-tuple-element.45), channel_id=1, source_target_pairs={{0,16},{4,20},{8,24},{12,28},{16,0},{20,4},{24,8},{28,12},{1,17},{... | collective-permute-start | bytes 786440 | tf_op jit(solution)/shard_map/ppermute | solution.py:434
  106.0 39.0 %collective-permute-start.18 = (bf16[512,256]{1,0:T(8,128)(2,1)S(1)}, bf16[512,256]{1,0:T(8,128)(2,1)S(1)}, u32[]{:S(2)}, u32[]{:S(2)}) collective-permute-start(bf16[512,256]{1,0:T(8,128)(2,1)S(1)} %get-tuple-element.44), channel_id=1, source_target_pairs={{0,24},{4,28},{8,16},{12,20},{16,8},{20,12},{24,0},{28,4},{1,25},{... | collective-permute-start | bytes 786440 | tf_op jit(solution)/shard_map/ppermute | solution.py:434
  122.9 69.2 %collective-permute-start.23 = (bf16[2048,128]{1,0:T(8,128)(2,1)}, bf16[2048,128]{1,0:T(8,128)(2,1)}, u32[]{:S(2)}, u32[]{:S(2)}) collective-permute-start(bf16[2048,128]{1,0:T(8,128)(2,1)} %get-tuple-element.22), channel_id=1, source_target_pairs={{0,4},{4,0},{8,12},{12,8},{16,20},{20,16},{24,28},{28,24},{1,5},{5... | collective-permute-start | bytes 1572872 | tf_op jit(solution)/shard_map/ppermute | solution.py:434
  132.8 59.3 %collective-permute-start.27 = (bf16[2048,128]{1,0:T(8,128)(2,1)}, bf16[2048,128]{1,0:T(8,128)(2,1)}, u32[]{:S(2)}, u32[]{:S(2)}) collective-permute-start(bf16[2048,128]{1,0:T(8,128)(2,1)} %get-tuple-element.24), channel_id=1, source_target_pairs={{0,4},{4,0},{8,12},{12,8},{16,20},{20,16},{24,28},{28,24},{1,5},{5... | collective-permute-start | bytes 1572872 | tf_op jit(solution)/shard_map/ppermute | solution.py:434
  153.5 59.6 %collective-permute-start.19 = (bf16[2048,128]{1,0:T(8,128)(2,1)}, bf16[2048,128]{1,0:T(8,128)(2,1)S(1)}, u32[]{:S(2)}, u32[]{:S(2)}) collective-permute-start(bf16[2048,128]{1,0:T(8,128)(2,1)} %get-tuple-element.20), channel_id=1, source_target_pairs={{0,4},{4,0},{8,12},{12,8},{16,20},{20,16},{24,28},{28,24},{1,5},{5... | collective-permute-start | bytes 1572872 | tf_op jit(solution)/shard_map/ppermute | solution.py:434
  156.1 12.9 %collective-permute-start.28 = (bf16[256,128]{1,0:T(8,128)(2,1)S(1)}, bf16[256,128]{1,0:T(8,128)(2,1)S(1)}, u32[]{:S(2)}, u32[]{:S(2)}) collective-permute-start(bf16[256,128]{1,0:T(8,128)(2,1)S(1)} %get-tuple-element.53), channel_id=1, source_target_pairs={{0,4},{4,0},{8,12},{12,8},{16,20},{20,16},{24,28},{28,24},{1,5},{5... | collective-permute-start | bytes 196616 | tf_op jit(solution)/shard_map/ppermute | solution.py:434
  156.7 19.4 %collective-permute-start.29 = (bf16[256,128]{1,0:T(8,128)(2,1)S(1)}, bf16[256,128]{1,0:T(8,128)(2,1)S(1)}, u32[]{:S(2)}, u32[]{:S(2)}) collective-permute-start(bf16[256,128]{1,0:T(8,128)(2,1)S(1)} %get-tuple-element.52), channel_id=1, source_target_pairs={{0,8},{4,12},{8,0},{12,4},{16,24},{20,28},{24,16},{28,20},{1,9},{5... | collective-permute-start | bytes 196616 | tf_op jit(solution)/shard_map/ppermute | solution.py:434
  169.0 9.3 %collective-permute-start.30 = (bf16[256,128]{1,0:T(8,128)(2,1)S(1)}, bf16[256,128]{1,0:T(8,128)(2,1)S(1)}, u32[]{:S(2)}, u32[]{:S(2)}) collective-permute-start(bf16[256,128]{1,0:T(8,128)(2,1)S(1)} %get-tuple-element.51), channel_id=1, source_target_pairs={{0,12},{4,8},{8,4},{12,0},{16,28},{20,24},{24,20},{28,16},{1,13},{... | collective-permute-start | bytes 196616 | tf_op jit(solution)/shard_map/ppermute | solution.py:434
  215.4 9.9 %collective-permute-start.37 = (bf16[256,128]{1,0:T(8,128)(2,1)S(1)}, bf16[256,128]{1,0:T(8,128)(2,1)S(1)}, u32[]{:S(2)}, u32[]{:S(2)}) collective-permute-start(bf16[256,128]{1,0:T(8,128)(2,1)S(1)} %get-tuple-element.28), channel_id=1, source_target_pairs={{0,12},{4,8},{8,4},{12,0},{16,28},{20,24},{24,20},{28,16},{1,13},{... | collective-permute-start | bytes 196616 | tf_op jit(solution)/shard_map/ppermute | solution.py:434
  246.9 13.9 %collective-permute-start.44 = (bf16[256,1024]{1,0:T(8,128)(2,1)S(1)}, bf16[256,1024]{1,0:T(8,128)(2,1)S(1)}, u32[]{:S(2)}, u32[]{:S(2)}) collective-permute-start(bf16[256,1024]{1,0:T(8,128)(2,1)S(1)} %emit.7), channel_id=1, source_target_pairs={{0,2},{1,3},{2,0},{3,1},{4,6},{5,7},{6,4},{7,5},{8,10},{9,11},{10,... | collective-permute-start | bytes 1572872 | tf_op jit(solution)/shard_map/ppermute | solution.py:434
  (41 other events, 430.7 us)

commit v2 on v1

--- a/solution.py
+++ b/solution.py
@@ -164,69 +164,148 @@
     )
 
 
-def project_kernel(where_ref, *refs):
-    groups, parts = refs[:16], refs[16:20]
-    own_ref, send_ref, held, weights, sems = refs[20:]
+def cut_kernel(where_ref, *refs, index, counts, after):
+    place = where_ref[0]
+    depth, side = place // 2, place % 2
+    tokens, weight, filters = [
+        refs[sum(counts[:i]) : sum(counts[: i + 1])] for i in range(3)
+    ]
+    outs, sems = list(refs[sum(counts) + after : -1]), refs[-1]
+    copies = []
+
+    def copy(source, target):
+        copies.append(pltpu.make_async_copy(source, target, sems.at[len(copies)]))
+
+    for source in tokens:
+        half = outs[0].shape[1]
+        for which in (1 - side, side):
+            columns = pl.ds(pl.multiple_of(which * half, half), half)
+            copy(source.at[:, columns], outs.pop(0))
+    rows, width = weight[0].shape[1], outs[0].shape[1]
+    for turn in (2, 1, 3, 0):
+        start = pl.multiple_of(jnp.bitwise_xor(depth, turn) * width, width)
+        columns = pl.ds(start, width)
+        copy(weight[0].at[index, :, columns], outs[turn].at[pl.ds(0, rows), :])
+        for source in filters:
+            copy(source.at[:, columns], outs[turn].at[pl.ds(rows, source.shape[0]), :])
+    for one in copies:
+        one.start()
+    for one in copies:
+        one.wait()
+
+
+def cut(where, tokens, weight, index, filters, after):
+    rows = weight.shape[1] + sum(value.shape[0] for value in filters)
+    shapes = []
+    for value in tokens:
+        shapes += [jax.ShapeDtypeStruct((value.shape[0], value.shape[1] // 2), value.dtype)] * 2
+    shapes += [jax.ShapeDtypeStruct((rows, weight.shape[2] // 4), weight.dtype)] * 4
+    counts = (len(tokens), 1, len(filters))
+    return pl.pallas_call(
+        functools.partial(cut_kernel, index=index, counts=counts, after=len(after)),
+        out_shape=tuple(shapes),
+        in_specs=[pl.BlockSpec(memory_space=pltpu.SMEM)]
+        + [pl.BlockSpec(memory_space=pltpu.HBM)] * sum(counts)
+        + [pl.BlockSpec(memory_space=pl.ANY)] * len(after),
+        out_specs=(pl.BlockSpec(memory_space=pltpu.VMEM),) * len(shapes),
+        scratch_shapes=[pltpu.SemaphoreType.DMA((10,))],
+        compiler_params=pltpu.CompilerParams(vmem_limit_bytes=8 * 2**20),
+        name="cut",
+    )(where, *tokens, weight, *filters, *after)
+
+
+def join_kernel(*refs, count):
+    out_ref = refs[-1]
+    start = 0
+    for source in refs[:count]:
+        out_ref[start : start + source.shape[0], :] = source[...]
+        start += source.shape[0]
+
+
+def join(values, after):
+    rows = sum(value.shape[0] for value in values)
+    vmem = pl.BlockSpec(memory_space=pltpu.VMEM)
+    return pl.pallas_call(
+        functools.partial(join_kernel, count=len(values)),
+        out_shape=jax.ShapeDtypeStruct((rows, values[0].shape[1]), values[0].dtype),
+        in_specs=[vmem] * len(values) + [pl.BlockSpec(memory_space=pl.ANY)] * len(after),
+        out_specs=vmem,
+        compiler_params=pltpu.CompilerParams(vmem_limit_bytes=8 * 2**20),
+        name="join",
+    )(*values, *after)
+
+
+def project_kernel(where_ref, *refs, filter_rows, after):
+    line, across, cores, parts = refs[:4], refs[4:8], refs[8:10], refs[10:14]
+    if filter_rows:
+        own_ref, send_ref, lags_ref, weights = refs[14 + after :]
+    else:
+        own_ref, send_ref, weights = refs[14 + after :]
     place, chan = where_ref[0], where_ref[1]
     depth, side = place // 2, place % 2
-    weight_copies = [
-        pltpu.make_async_copy(parts[i], weights.at[i], sems.at[i]) for i in range(4)
-    ]
-    token_copies = [
-        pltpu.make_async_copy(groups[i], held.at[i], sems.at[4 + i]) for i in range(16)
-    ]
-    for copy in weight_copies + token_copies:
-        copy.start()
-    for copy in weight_copies:
-        copy.wait()
-    block = own_ref.shape[0] // 8
-    half = own_ref.shape[1]
+    rows = line[0].shape[1]
+    for i in range(4):
+        slot = jnp.bitwise_xor(depth, jnp.bitwise_xor(chan, i))
+        start = pl.multiple_of(slot * rows, rows)
+        weights[pl.ds(start, rows), :] = parts[i][0:rows, :]
+    length, half = own_ref.shape
+    block = length // 8
     for step in range(4):
-        total = None
-        for turn in range(4):
-            token_copies[4 * step + turn].wait()
-            slot = jnp.bitwise_xor(depth, jnp.bitwise_xor(chan, turn))
-            term = jnp.dot(
-                held[4 * step + turn], weights[slot], preferred_element_type=jnp.float32
-            )
-            total = term if total is None else total + term
-        low, high = total[:, :half], total[:, half:]
-        own = jnp.where(side == 0, low, high)
-        send = jnp.where(side == 0, high, low).astype(jnp.bfloat16)
+        low = 4 * block * (step % 2)
+        both = cores[step // 2]
+        joined = jnp.concatenate(
+            [
+                line[step][...],
+                both[low : low + 2 * block, :],
+                across[step][...],
+                both[low + 2 * block : low + 4 * block, :],
+            ],
+            1,
+        )
+        total = jnp.dot(joined, weights[...], preferred_element_type=jnp.float32)
+        left, right = total[:, :half], total[:, half:]
+        own = jnp.where(side == 0, left, right)
+        send = jnp.where(side == 0, right, left).astype(jnp.bfloat16)
         for pair in range(2):
             start = pl.multiple_of(jnp.bitwise_xor(place, 2 * step + pair) * block, block)
             own_ref[pl.ds(start, block), :] = own[pair * block : (pair + 1) * block]
             send_ref[pl.ds(start, block), :] = send[pair * block : (pair + 1) * block]
-
-
-def project(where, groups, parts, length):
-    width = parts[0].shape[1] // 2
-    depth = parts[0].shape[0]
+    if filter_rows:
+        for i in range(4):
+            piece = parts[i][rows:, :].astype(jnp.float32)
+            left, right = piece[:, :half], piece[:, half:]
+            at = slice(i * filter_rows, (i + 1) * filter_rows)
+            lags_ref[at, :] = jnp.where(side == 0, left, right).astype(jnp.bfloat16)
+            at = slice(length + i * filter_rows, length + (i + 1) * filter_rows)
+            send_ref[at, :] = jnp.where(side == 0, right, left).astype(jnp.bfloat16)
+
+
+def project(where, line, across, cores, parts, length, after):
+    depth, width = line[0].shape[1], parts[0].shape[1]
+    filter_rows = parts[0].shape[0] - depth
+    vmem = pl.BlockSpec(memory_space=pltpu.VMEM)
+    shapes = [
+        jax.ShapeDtypeStruct((length, width // 2), jnp.float32),
+        jax.ShapeDtypeStruct((length + 4 * filter_rows, width // 2), jnp.bfloat16),
+    ]
+    if filter_rows:
+        shapes.append(jax.ShapeDtypeStruct((4 * filter_rows, width // 2), jnp.bfloat16))
     return pl.pallas_call(
-        project_kernel,
-        out_shape=(
-            jax.ShapeDtypeStruct((length, width), jnp.float32),
-            jax.ShapeDtypeStruct((length, width), jnp.bfloat16),
-        ),
+        functools.partial(project_kernel, filter_rows=filter_rows, after=len(after)),
+        out_shape=tuple(shapes),
         in_specs=[pl.BlockSpec(memory_space=pltpu.SMEM)]
-        + [pl.BlockSpec(memory_space=pl.ANY)] * 20,
-        out_specs=(
-            pl.BlockSpec(memory_space=pltpu.VMEM),
-            pl.BlockSpec(memory_space=pltpu.VMEM),
-        ),
-        scratch_shapes=[
-            pltpu.VMEM((16,) + groups[0].shape, jnp.bfloat16),
-            pltpu.VMEM((4,) + parts[0].shape, jnp.bfloat16),
-            pltpu.SemaphoreType.DMA((20,)),
-        ],
+        + [vmem] * 14
+        + [pl.BlockSpec(memory_space=pl.ANY)] * len(after),
+        out_specs=(vmem,) * len(shapes),
+        scratch_shapes=[pltpu.VMEM((4 * depth, width), jnp.bfloat16)],
         compiler_params=pltpu.CompilerParams(vmem_limit_bytes=24 * 2**20),
         cost_estimate=pl.CostEstimate(
-            flops=2 * length * 4 * depth * 2 * width,
+            flops=2 * length * 4 * depth * width,
             bytes_accessed=2 * length * 4 * depth,
             transcendentals=0,
         ),
         name="project",
-    )(where, *groups, *parts)
+    )(where, *line, *across, *cores, *parts, *after)
 
 
 def smooth_into(padded, own_ref, recv_ref, taps_ref, branch, store):
@@ -251,17 +330,19 @@
 def mix_kernel(
     where_ref, own1, recv1, own2, recv2, taps_ref, skip_ref, ahead, middle, middle_back, back, *refs
 ):
-    filters, mixed_ref = refs[:8], refs[8]
-    padded, gated, lags, waves, filter_waves, sums = refs[9:]
+    lags_here, lags_there, mixed_ref = refs[:3]
+    padded, gated, lags, waves, filter_waves, sums = refs[3:]
     place = where_ref[0]
     length, width = own1.shape
     block = length // 8
     rows, two = middle.shape[0], middle.shape[1]
     padded_rows = ahead.shape[0] // 2
     used = ahead.shape[1]
-    for i in range(8):
-        start = pl.multiple_of(jnp.bitwise_xor(place, i) * block, block)
-        lags[pl.ds(start, block), :] = filters[i][...].astype(jnp.float32)
+    for i in range(4):
+        at = slice(i * block, (i + 1) * block)
+        for side, source in enumerate((lags_here, lags_there)):
+            start = pl.multiple_of(jnp.bitwise_xor(place, 2 * i + side) * block, block)
+            lags[pl.ds(start, block), :] = source[at, :].astype(jnp.float32)
 
     def first(at, value):
         gated[at, :] = value
@@ -323,7 +404,7 @@
             mixed_ref[at, :] = wave[:, i * width : (i + 1) * width] + skip_ref[...] * gated[at, :]
 
 
-def mix(where, own1, recv1, own2, recv2, taps, skip, tables, filters):
+def mix(where, own1, recv1, own2, recv2, taps, skip, tables, lags_here, lags_there):
     length, width = own1.shape
     rows, two = tables[1].shape[:2]
     padded_rows = tables[0].shape[0] // 2
@@ -331,7 +412,7 @@
     return pl.pallas_call(
         mix_kernel,
         out_shape=jax.ShapeDtypeStruct((length, width), jnp.float32),
-        in_specs=[pl.BlockSpec(memory_space=pltpu.SMEM)] + [vmem] * 18,
+        in_specs=[pl.BlockSpec(memory_space=pltpu.SMEM)] + [vmem] * 12,
         out_specs=vmem,
         scratch_shapes=[
             pltpu.VMEM((length + 8, width), jnp.float32),
@@ -346,7 +427,7 @@
             flops=2 * 8 * length * inner_len * width, bytes_accessed=6 * 2**20, transcendentals=0
         ),
         name="mix",
-    )(where, own1, recv1, own2, recv2, taps, skip, *tables, *filters)
+    )(where, own1, recv1, own2, recv2, taps, skip, *tables, lags_here, lags_there)
 
 
 def gate_kernel(where_ref, own0, recv0, mixed_ref, taps_ref, *refs):
@@ -383,43 +464,50 @@
     )(where, own0, recv0, mixed, taps)
 
 
-def emit_kernel(where_ref, *refs, added):
-    parts, weight_ref = refs[:8], refs[8]
-    extra = refs[9 : 9 + added]
-    out_ref, joined = refs[9 + added :]
-    place = where_ref[0]
+def emit_kernel(where_ref, weight, *refs, added):
+    parts, extra = refs[:8], refs[8 : 8 + added]
+    out_ref, joined, tiles, sems = refs[8 + added :]
+    place, column = where_ref[0], where_ref[1]
     width = parts[0].shape[1]
-
-    @pl.when(pl.program_id(0) == 0)
-    def _():
-        for i in range(8):
-            start = pl.multiple_of(jnp.bitwise_xor(place, i) * width, width)
-            joined[:, pl.ds(start, width)] = parts[i][...]
-
-    total = jnp.dot(joined[...], weight_ref[...], preferred_element_type=jnp.float32)
-    for term in extra:
-        total = total + term[...].astype(jnp.float32)
-    out_ref[...] = total.astype(out_ref.dtype)
+    count, _, tile = tiles.shape
+    copies = []
+    for i in range(count):
+        start = pl.multiple_of((column * count + i) * tile, tile)
+        copies.append(
+            pltpu.make_async_copy(weight.at[:, pl.ds(start, tile)], tiles.at[i], sems.at[i])
+        )
+        copies[i].start()
+    for i in range(8):
+        start = pl.multiple_of(jnp.bitwise_xor(place, i) * width, width)
+        joined[:, pl.ds(start, width)] = parts[i][...]
+    for i in range(count):
+        copies[i].wait()
+        total = jnp.dot(joined[...], tiles[i], preferred_element_type=jnp.float32)
+        at = slice(i * tile, (i + 1) * tile)
+        for term in extra:
+            total = total + term[:, at].astype(jnp.float32)
+        out_ref[:, at] = total.astype(out_ref.dtype)
 
 
 def emit(where, parts, weight, extra, out_dtype):
     rows, width = parts[0].shape
     columns = weight.shape[1] // 4
-    tile = columns // 4
-    whole = pl.BlockSpec((rows, width), lambda i, at: (0, 0))
-    tiled = pl.BlockSpec((rows, tile), lambda i, at: (0, i))
+    count = 4
+    vmem = pl.BlockSpec(memory_space=pltpu.VMEM)
     return pl.pallas_call(
         functools.partial(emit_kernel, added=len(extra)),
         out_shape=jax.ShapeDtypeStruct((rows, columns), out_dtype),
-        grid_spec=pltpu.PrefetchScalarGridSpec(
-            num_scalar_prefetch=1,
-            grid=(4,),
-            in_specs=[whole] * 8
-            + [pl.BlockSpec((weight.shape[0], tile), lambda i, at: (0, 4 * at[1] + i))]
-            + [tiled] * len(extra),
-            out_specs=tiled,
-            scratch_shapes=[pltpu.VMEM((rows, 8 * width), jnp.bfloat16)],
-        ),
+        in_specs=[
+            pl.BlockSpec(memory_space=pltpu.SMEM),
+            pl.BlockSpec(memory_space=pltpu.HBM),
+        ]
+        + [vmem] * (8 + len(extra)),
+        out_specs=vmem,
+        scratch_shapes=[
+            pltpu.VMEM((rows, 8 * width), jnp.bfloat16),
+            pltpu.VMEM((count, weight.shape[0], columns // count), jnp.bfloat16),
+            pltpu.SemaphoreType.DMA((count,)),
+        ],
         compiler_params=pltpu.CompilerParams(vmem_limit_bytes=16 * 2**20),
         cost_estimate=pl.CostEstimate(
             flops=2 * rows * weight.shape[0] * columns,
@@ -427,7 +515,7 @@
             transcendentals=0,
         ),
         name="emit",
-    )(where, *parts, weight, *extra)
+    )(where, weight, *parts, *extra)
 
 
 def swap(value, axis, count, turn):
@@ -437,49 +525,62 @@
 def fast_body(tokens, in_weight, short_taps, skip_gain, long_filter, out_weight):
     seq, chans = lax.axis_size("seq"), lax.axis_size("chan")
     place, chan = lax.axis_index("seq"), lax.axis_index("chan")
-    depth, side = place // 2, place % 2
     rows, width = tokens.shape
     length = rows * seq
     part = width // seq
-    half = width // 2
     where = jnp.stack([place, chan]).astype(jnp.int32)
 
-    ours = lax.dynamic_slice_in_dim(tokens, side * half, half, 1)
-    theirs = lax.dynamic_slice_in_dim(tokens, (1 - side) * half, half, 1)
-    pair = jnp.concatenate([ours, swap(theirs, "seq", seq, 1)], 0)
-    far = swap(pair, "seq", seq, 4)
-    line = [pair, swap(pair, "seq", seq, 2), far, swap(far, "seq", seq, 2)]
-    across = [swap(value, "chan", chans, 2) for value in line]
-    groups = []
-    for i in range(4):
-        groups += [
-            line[i],
-            swap(line[i], "chan", chans, 1),
-            across[i],
-            swap(across[i], "chan", chans, 1),
-        ]
-
-    filters = []
-    for turn in range(seq):
-        piece = lax.dynamic_slice_in_dim(long_filter, (place ^ turn) * part, part, 1)
-        filters.append(piece if turn == 0 else swap(piece, "seq", seq, turn))
-
-    def branch(index):
-        parts = []
-        for turn in range(4):
-            piece = lax.dynamic_slice_in_dim(
-                in_weight[:, index, :], (depth ^ turn) * 2 * part, 2 * part, 1
-            )
-            parts.append(piece if turn == 0 else swap(piece, "seq", seq, 2 * turn))
-        own, send = project(where, groups, parts, length)
-        return own, swap(send, "seq", seq, 1)
+    weight = jnp.transpose(in_weight, (1, 0, 2))
+
+    def far_part(parts, turn):
+        return swap(parts[turn], "seq", seq, 2 * turn)
+
+    theirs, ours, *cut1 = cut(where, [tokens], weight, 1, [long_filter], [])
+    w1_2, w1_1 = far_part(cut1, 2), far_part(cut1, 1)
+    far_ours = swap(ours, "seq", seq, 4)
+    beside = swap(theirs, "seq", seq, 1)
+    pair = join([ours, beside], [])
+    far_beside = swap(beside, "seq", seq, 4)
+    near = swap(pair, "seq", seq, 2)
+    pair_across = swap(pair, "chan", chans, 2)
+    far = join([far_ours, far_beside], [w1_2, w1_1])
+    cut2 = cut(where, [], weight, 2, [], [far])
+    w1_3 = far_part(cut1, 3)
+    far_near = swap(far, "seq", seq, 2)
+    w2_2 = far_part(cut2, 2)
+    far_across = swap(far, "chan", chans, 2)
+    near_across = swap(near, "chan", chans, 2)
+    core_a = swap(join([pair, pair_across, near, near_across], [w1_3]), "chan", chans, 1)
+    far_near_across = swap(far_near, "chan", chans, 2)
+    cut0 = cut(where, [], weight, 0, [], [far_near])
+    w2_1 = far_part(cut2, 1)
+    w2_3 = far_part(cut2, 3)
+    core_b = swap(
+        join([far, far_across, far_near, far_near_across], [w2_2, w2_1]), "chan", chans, 1
+    )
+    w0_2, w0_1, w0_3 = far_part(cut0, 2), far_part(cut0, 1), far_part(cut0, 3)
+    line, across = [pair, near, far, far_near], [
+        pair_across,
+        near_across,
+        far_across,
+        far_near_across,
+    ]
+    cores = [core_a, core_b]
+    parts1 = [cut1[0], w1_1, w1_2, w1_3]
+    parts2 = [cut2[0], w2_1, w2_2, w2_3]
+    parts0 = [cut0[0], w0_1, w0_2, w0_3]
 
     taps = lax.dynamic_slice_in_dim(short_taps, place * part, part, 2)
     skip = lax.dynamic_slice_in_dim(skip_gain, place * part, part, 0)[None]
-    own1, recv1 = branch(1)
-    own2, recv2 = branch(2)
-    own0, recv0 = branch(0)
-    mixed = mix(where, own1, recv1, own2, recv2, taps, skip, wave_tables(length), filters)
+    own1, send1, lags_here = project(where, line, across, cores, parts1, length, [])
+    recv1 = swap(send1, "seq", seq, 1)
+    own2, send2 = project(where, line, across, cores, parts2, length, [w0_2, w0_1])
+    recv2 = swap(send2, "seq", seq, 1)
+    own0, send0 = project(where, line, across, cores, parts0, length, [])
+    recv0 = swap(send0, "seq", seq, 1)
+    mixed = mix(
+        where, own1, recv1, own2, recv2, taps, skip, wave_tables(length), lags_here, recv1[length:]
+    )
     pieces = gate(where, own0, recv0, mixed, taps)
     joined = [
         piece if turn == 0 else swap(piece, "seq", seq, turn) for turn, piece in enumerate(pieces)

time: 263 us -> 222 us (0.84)
  local copies, waits for them, and re-layouts: 40.8 us -> 22.7 us
  starting transfers between devices: 61 us -> 49.1 us
  Pallas kernels: 48.9 us -> 42.3 us
  waiting for transfers between devices: 110 us -> 106 us
    ppermute x45 -> x33, starting transfers between devices: 61 us -> 49.1 us  [swap(): return lax.ppermute(value, axis, [(i, i ^ turn) for i in range(count)])]
    unnamed x56 -> x42, local copies, waits for them, and re-layouts: 30.8 us -> 21.9 us
    pallas_call x3 -> x10, Pallas kernels: 22.2 us -> 14.7 us  [the longest x3 11.7 us: project(): pl.pallas_call(functools.partial(project_kernel, filter_rows=filter_rows,...]
    dynamic_slice x5 -> x0, local copies, waits for them, and re-layouts: 5.75 us -> none  [the longest x3 3.57 us: branch(): lax.dynamic_slice_in_dim(in_weight[:, index, :], (depth ^ turn) * 2 * par...]
    ppermute x45 -> x33, waiting for transfers between devices: 110 us -> 106 us  [swap(): return lax.ppermute(value, axis, [(i, i ^ turn) for i in range(count)])]
    slice x1, local copies, waits for them, and re-layouts: 3.52 us -> 0.02 us  [fast_body(): recv1[length:]]
  transfers between devices with their start and end apart: 45 -> 33, of which waited for: 17 -> 15; matrix products, arithmetic and copies ran while one was open for 4% -> 0% of each run, Pallas kernels for 17% -> 17%
where the time goes in v2:
time: 222 us; the launch traced here: 221 us
  waiting for transfers between devices  106 us (48%)
  starting transfers between devices  49.1 us (22%)
  Pallas kernels  42.3 us (19%)
  local copies, waits for them, and re-layouts  22.7 us (10%)
    ppermute x33, waiting for transfers between devices, swap(): return lax.ppermute(value, axis, [(i, i ^ turn) for i in range(count)])  106 us
    ppermute x33, starting transfers between devices, swap(): return lax.ppermute(value, axis, [(i, i ^ turn) for i in range(count)])  49.1 us
    unnamed x42, local copies, waits for them, and re-layouts  21.9 us
    pallas_call x1, Pallas kernels, mix(): pl.pallas_call(mix_kernel, out_shape=jax.ShapeDtypeStruct((length, width)...  15.3 us
    pallas_call x3, Pallas kernels, project(): pl.pallas_call(functools.partial(project_kernel, filter_rows=filter_rows,...  11.7 us
    pallas_call x4, Pallas kernels, emit(): pl.pallas_call(functools.partial(emit_kernel, added=len(extra)), out_shap...  10.9 us
  transfers between devices with their start and end apart: 33, of which 15 were waited for; matrix products, arithmetic and copies ran while one was open for 0% of the time, Pallas kernels for 17%

profile of v2, /device:TPU:0, one launch (start us, length us, event | category | flops | bytes accessed | tf_op | source)
XLA Modules:
  0.0 221.2 jit_solution(8145914587065277309)
XLA Ops:
  5.0 3.0 %collective-permute-start = (bf16[256,512]{1,0:T(8,128)(2,1)S(1)}, bf16[256,512]{1,0:T(8,128)(2,1)S(1)}, u32[]{:S(2)}, u32[]{:S(2)}) collective-permute-start(bf16[256,512]{1,0:T(8,128)(2,1)S(1)} %get-tuple-element.35), channel_id=1, source_target_pairs={{0,4},{4,0},{8,12},{12,8},{16,20},{20,16},{24,28},{28,24},{1,5},{5... | collective-permute-start | bytes 786440 | tf_op jit(solution)/shard_map/ppermute | solution.py:522
  8.0 2.6 %collective-permute-start.4 = (bf16[768,256]{1,0:T(8,128)(2,1)S(1)}, bf16[768,256]{1,0:T(8,128)(2,1)S(1)}, u32[]{:S(2)}, u32[]{:S(2)}) collective-permute-start(bf16[768,256]{1,0:T(8,128)(2,1)S(1)} %get-tuple-element.36), channel_id=1, source_target_pairs={{0,16},{4,20},{8,24},{12,28},{16,0},{20,4},{24,8},{28,12},{1,17},{... | collective-permute-start | bytes 1179656 | tf_op jit(solution)/shard_map/ppermute | solution.py:522
  14.3 2.8 %collective-permute-start.3 = (bf16[256,512]{1,0:T(8,128)(2,1)S(1)}, bf16[256,512]{1,0:T(8,128)(2,1)S(1)}, u32[]{:S(2)}, u32[]{:S(2)}) collective-permute-start(bf16[256,512]{1,0:T(8,128)(2,1)S(1)} %collective-permute-done.refs_1_), channel_id=1, source_target_pairs={{0,16},{4,20},{8,24},{12,28},{16,0},{20,4},{24,8},{28,12},{1,17},{... | collective-permute-start | bytes 786440 | tf_op jit(solution)/shard_map/ppermute | solution.py:522
  18.8 27.2 %collective-permute-done.2.refs_0_ = bf16[256,512]{1,0:T(8,128)(2,1)S(1)} collective-permute-done((bf16[256,512]{1,0:T(8,128)(2,1)S(1)}, bf16[256,512]{1,0:T(8,128)(2,1)S(1)}, u32[]{:S(2)}, u32[]{:S(2)}) %collective-permute-start.2) | collective-permute-done | bytes 262176 | tf_op jit(solution)/shard_map/ppermute | solution.py:522
  46.1 4.5 %collective-permute-done.3.refs_1_ = bf16[256,512]{1,0:T(8,128)(2,1)S(1)} collective-permute-done((bf16[256,512]{1,0:T(8,128)(2,1)S(1)}, bf16[256,512]{1,0:T(8,128)(2,1)S(1)}, u32[]{:S(2)}, u32[]{:S(2)}) %collective-permute-start.3) | collective-permute-done | bytes 262176 | tf_op jit(solution)/shard_map/ppermute | solution.py:522
  52.7 2.9 %collective-permute-start.11 = (bf16[768,256]{1,0:T(8,128)(2,1)S(1)}, bf16[768,256]{1,0:T(8,128)(2,1)S(1)}, u32[]{:S(2)}, u32[]{:S(2)}) collective-permute-start(bf16[768,256]{1,0:T(8,128)(2,1)S(1)} %get-tuple-element.38), channel_id=1, source_target_pairs={{0,24},{4,28},{8,16},{12,20},{16,8},{20,12},{24,0},{28,4},{1,25},{... | collective-permute-start | bytes 1179656 | tf_op jit(solution)/shard_map/ppermute | solution.py:522
  57.6 5.9 %collective-permute-done.6.refs_2_.refs_1_.refs_3_ = bf16[512,512]{1,0:T(8,128)(2,1)S(1)} collective-permute-done((bf16[512,512]{1,0:T(8,128)(2,1)S(1)}, bf16[512,512]{1,0:T(8,128)(2,1)S(1)}, u32[]{:S(2)}, u32[]{:S(2)}) %collective-permute-start.6) | collective-permute-done | bytes 524320 | tf_op jit(solution)/shard_map/ppermute | solution.py:522
  65.8 8.7 %collective-permute-done.11.refs_4_.refs_13_ = bf16[768,256]{1,0:T(8,128)(2,1)S(1)} collective-permute-done((bf16[768,256]{1,0:T(8,128)(2,1)S(1)}, bf16[768,256]{1,0:T(8,128)(2,1)S(1)}, u32[]{:S(2)}, u32[]{:S(2)}) %collective-permute-start.11) | collective-permute-done | bytes 393248 | tf_op jit(solution)/shard_map/ppermute | solution.py:522
  76.7 2.5 %collective-permute-start.14 = (bf16[512,256]{1,0:T(8,128)(2,1)S(1)}, bf16[512,256]{1,0:T(8,128)(2,1)S(1)}, u32[]{:S(2)}, u32[]{:S(2)}) collective-permute-start(bf16[512,256]{1,0:T(8,128)(2,1)S(1)} %get-tuple-element.40), channel_id=1, source_target_pairs={{0,8},{4,12},{8,0},{12,4},{16,24},{20,28},{24,16},{28,20},{1,9},{5... | collective-permute-start | bytes 786440 | tf_op jit(solution)/shard_map/ppermute | solution.py:522
  79.5 9.4 %collective-permute-done.13.refs_4_.refs_12_ = bf16[512,256]{1,0:T(8,128)(2,1)S(1)} collective-permute-done((bf16[512,256]{1,0:T(8,128)(2,1)S(1)}, bf16[512,256]{1,0:T(8,128)(2,1)S(1)}, u32[]{:S(2)}, u32[]{:S(2)}) %collective-permute-start.13) | collective-permute-done | bytes 262176 | tf_op jit(solution)/shard_map/ppermute | solution.py:522
  88.9 9.5 %collective-permute-done.10.refs_3_.refs_7_ = bf16[512,512]{1,0:T(8,128)(2,1)S(1)} collective-permute-done((bf16[512,512]{1,0:T(8,128)(2,1)S(1)}, bf16[512,512]{1,0:T(8,128)(2,1)S(1)}, u32[]{:S(2)}, u32[]{:S(2)}) %collective-permute-start.10) | collective-permute-done | bytes 524320 | tf_op jit(solution)/shard_map/ppermute | solution.py:522
  98.7 3.2 %collective-permute-start.21 = (bf16[512,256]{1,0:T(8,128)(2,1)S(1)}, bf16[512,256]{1,0:T(8,128)(2,1)S(1)}, u32[]{:S(2)}, u32[]{:S(2)}) collective-permute-start(bf16[512,256]{1,0:T(8,128)(2,1)S(1)} %get-tuple-element.51), channel_id=1, source_target_pairs={{0,24},{4,28},{8,16},{12,20},{16,8},{20,12},{24,0},{28,4},{1,25},{... | collective-permute-start | bytes 786440 | tf_op jit(solution)/shard_map/ppermute | solution.py:522
  104.2 3.2 %collective-permute-start.18 = (bf16[512,256]{1,0:T(8,128)(2,1)S(1)}, bf16[512,256]{1,0:T(8,128)(2,1)S(1)}, u32[]{:S(2)}, u32[]{:S(2)}) collective-permute-start(bf16[512,256]{1,0:T(8,128)(2,1)S(1)} %get-tuple-element.44), channel_id=1, source_target_pairs={{0,24},{4,28},{8,16},{12,20},{16,8},{20,12},{24,0},{28,4},{1,25},{... | collective-permute-start | bytes 786440 | tf_op jit(solution)/shard_map/ppermute | solution.py:522
  107.3 4.0 %project.4 = (f32[2048,128]{1,0:T(8,128)S(1)}, bf16[3072,128]{1,0:T(8,128)(2,1)}, bf16[1024,128]{1,0:T(8,128)(2,1)S(1)}) custom-call(s32[2]{0:T(128)S(1)} %pad_add_fusion.where_ref, bf16[512,512]{1,0:T(8,128)(2,1)S(1)} %join.4.refs_0_, bf16[512,512]{1,0:T(8,128)(2,1)S(1)} %collective-permute-done.1.refs_2_.refs_1_, ...), custom_call_target="tpu_custom_call" | custom-call | flops 2147483648 | bytes 8388608 | tf_op jit(solution)/shard_map/project/pallas_call | solution.py:293
  111.9 3.2 %collective-permute-done.16.refs_11_.refs_15_ = bf16[512,256]{1,0:T(8,128)(2,1)S(1)} collective-permute-done((bf16[512,256]{1,0:T(8,128)(2,1)S(1)}, bf16[512,256]{1,0:T(8,128)(2,1)S(1)}, u32[]{:S(2)}, u32[]{:S(2)}) %collective-permute-start.16) | collective-permute-done | bytes 262176 | tf_op jit(solution)/shard_map/ppermute | solution.py:522
  115.1 16.6 %collective-permute-done.17.refs_12_.refs_14_ = bf16[512,256]{1,0:T(8,128)(2,1)S(1)} collective-permute-done((bf16[512,256]{1,0:T(8,128)(2,1)S(1)}, bf16[512,256]{1,0:T(8,128)(2,1)S(1)}, u32[]{:S(2)}, u32[]{:S(2)}) %collective-permute-start.17) | collective-permute-done | bytes 262176 | tf_op jit(solution)/shard_map/ppermute | solution.py:522
  131.7 3.9 %project.5 = (f32[2048,128]{1,0:T(8,128)S(1)}, bf16[2048,128]{1,0:T(8,128)(2,1)}) custom-call(s32[2]{0:T(128)S(1)} %pad_add_fusion.where_ref, bf16[512,512]{1,0:T(8,128)(2,1)S(1)} %join.4.refs_0_, bf16[512,512]{1,0:T(8,128)(2,1)S(1)} %collective-permute-done.1.refs_2_.refs_1_, bf16[512,512]{1,0:T(8,128)(2,1)S(1)} %join.5.refs_1_.refs_0_.refs_2_, ...), custom_call_target="tpu_custom_call" | custom-call | flops 2147483648 | bytes 8388608 | tf_op jit(solution)/shard_map/project/pallas_call | solution.py:293
  136.2 3.8 %project.3 = (f32[2048,128]{1,0:T(8,128)S(1)}, bf16[2048,128]{1,0:T(8,128)(2,1)}) custom-call(s32[2]{0:T(128)S(1)} %pad_add_fusion.where_ref, bf16[512,512]{1,0:T(8,128)(2,1)S(1)} %join.4.refs_0_, bf16[512,512]{1,0:T(8,128)(2,1)S(1)} %collective-permute-done.1.refs_2_.refs_1_, bf16[512,512]{1,0:T(8,128)(2,1)S(1)} %join.5.refs_1_.refs_0_.refs_2_, ...), custom_call_target="tpu_custom_call" | custom-call | flops 2147483648 | bytes 8388608 | tf_op jit(solution)/shard_map/project/pallas_call | solution.py:293
  143.3 7.4 %collective-permute-done.22.recv2 = bf16[2048,128]{1,0:T(8,128)(2,1)S(1)} collective-permute-done((bf16[2048,128]{1,0:T(8,128)(2,1)}, bf16[2048,128]{1,0:T(8,128)(2,1)S(1)}, u32[]{:S(2)}, u32[]{:S(2)}) %collective-permute-start.22) | collective-permute-done | bytes 524320 | tf_op jit(solution)/shard_map/ppermute | solution.py:522
  154.1 15.3 %mix.1.mixed_ref = f32[2048,128]{1,0:T(8,128)S(1)} custom-call(s32[2]{0:T(128)S(1)} %pad_add_fusion.where_ref, f32[2048,128]{1,0:T(8,128)S(1)} %copy-done.12, bf16[3072,128]{1,0:T(8,128)(2,1)S(1)} %collective-permute-done.20.recv1, f32[2048,128]{1,0:T(8,128)S(1)} %copy-done.14, bf16[2048,128]{1,0:T(8,128)(2,1)S(1)} %collective-permute-done.22.recv2, ...), custom_call_target="tpu_custom_call" | custom-call | flops 268435456 | bytes 6291456 | tf_op jit(solution)/shard_map/mix/pallas_call | solution.py:412
  171.6 2.9 %collective-permute-start.25 = (bf16[256,128]{1,0:T(8,128)(2,1)S(1)}, bf16[256,128]{1,0:T(8,128)(2,1)S(1)}, u32[]{:S(2)}, u32[]{:S(2)}) collective-permute-start(bf16[256,128]{1,0:T(8,128)(2,1)S(1)} %get-tuple-element.58), channel_id=1, source_target_pairs={{0,12},{4,8},{8,4},{12,0},{16,28},{20,24},{24,20},{28,16},{1,13},{... | collective-permute-start | bytes 196616 | tf_op jit(solution)/shard_map/ppermute | solution.py:522
  177.4 2.9 %collective-permute-start.28 = (bf16[256,128]{1,0:T(8,128)(2,1)S(1)}, bf16[256,128]{1,0:T(8,128)(2,1)S(1)}, u32[]{:S(2)}, u32[]{:S(2)}) collective-permute-start(bf16[256,128]{1,0:T(8,128)(2,1)S(1)} %get-tuple-element.61), channel_id=1, source_target_pairs={{0,24},{4,28},{8,16},{12,20},{16,8},{20,12},{24,0},{28,4},{1,25},{... | collective-permute-start | bytes 196616 | tf_op jit(solution)/shard_map/ppermute | solution.py:522
  183.5 3.8 %collective-permute-done.29.refs_7_ = bf16[256,128]{1,0:T(8,128)(2,1)S(1)} collective-permute-done((bf16[256,128]{1,0:T(8,128)(2,1)S(1)}, bf16[256,128]{1,0:T(8,128)(2,1)S(1)}, u32[]{:S(2)}, u32[]{:S(2)}) %collective-permute-start.29) | collective-permute-done | bytes 65568 | tf_op jit(solution)/shard_map/ppermute | solution.py:522
  187.3 3.4 %copy-done.1 = bf16[1024,4096]{1,0:T(8,128)(2,1)S(1)} copy-done((bf16[1024,4096]{1,0:T(8,128)(2,1)S(1)}, bf16[1024,4096]{1,0:T(8,128)(2,1)}, u32[]{:S(2)}) %copy-start.1) | copy-done | bytes 8388632
  190.6 2.7 %emit.6 = bf16[256,1024]{1,0:T(8,128)(2,1)S(1)} custom-call(s32[2]{0:T(128)S(1)} %pad_add_fusion.3.where_ref, bf16[1024,4096]{1,0:T(8,128)(2,1)S(1)} %copy-done.1, bf16[256,128]{1,0:T(8,128)(2,1)S(1)} %get-tuple-element.55.refs_0_, bf16[256,128]{1,0:T(8,128)(2,1)S(1)} %collective-permute-done.23.refs_1_, ...), custom_call_target="tpu_custom_call" | custom-call | flops 536870912 | bytes 2097152 | tf_op jit(solution)/shard_map/emit/pallas_call | solution.py:497
  193.6 3.4 %copy-done.2 = bf16[1024,4096]{1,0:T(8,128)(2,1)S(1)} copy-done((bf16[1024,4096]{1,0:T(8,128)(2,1)S(1)}, bf16[1024,4096]{1,0:T(8,128)(2,1)}, u32[]{:S(2)}) %copy-start.2) | copy-done | bytes 8388632
  197.0 2.7 %emit.4 = bf16[256,1024]{1,0:T(8,128)(2,1)S(1)} custom-call(s32[2]{0:T(128)S(1)} %pad_add_fusion.1.where_ref, bf16[1024,4096]{1,0:T(8,128)(2,1)S(1)} %copy-done.2, bf16[256,128]{1,0:T(8,128)(2,1)S(1)} %get-tuple-element.55.refs_0_, bf16[256,128]{1,0:T(8,128)(2,1)S(1)} %collective-permute-done.23.refs_1_, ...), custom_call_target="tpu_custom_call" | custom-call | flops 536870912 | bytes 2097152 | tf_op jit(solution)/shard_map/emit/pallas_call | solution.py:497
  200.3 3.4 %copy-done.3 = bf16[1024,4096]{1,0:T(8,128)(2,1)S(1)} copy-done((bf16[1024,4096]{1,0:T(8,128)(2,1)S(1)}, bf16[1024,4096]{1,0:T(8,128)(2,1)}, u32[]{:S(2)}) %copy-start.3) | copy-done | bytes 8388632
  203.6 2.7 %emit.7 = bf16[256,1024]{1,0:T(8,128)(2,1)S(1)} custom-call(s32[2]{0:T(128)S(1)} %pad_add_fusion.2.where_ref, bf16[1024,4096]{1,0:T(8,128)(2,1)S(1)} %copy-done.3, bf16[256,128]{1,0:T(8,128)(2,1)S(1)} %get-tuple-element.55.refs_0_, bf16[256,128]{1,0:T(8,128)(2,1)S(1)} %collective-permute-done.23.refs_1_, ...), custom_call_target="tpu_custom_call" | custom-call | flops 536870912 | bytes 2097152 | tf_op jit(solution)/shard_map/emit/pallas_call | solution.py:497
  207.9 3.4 %copy-done.4 = bf16[1024,4096]{1,0:T(8,128)(2,1)S(1)} copy-done((bf16[1024,4096]{1,0:T(8,128)(2,1)S(1)}, bf16[1024,4096]{1,0:T(8,128)(2,1)}, u32[]{:S(2)}) %copy-start.4) | copy-done | bytes 8388632
  211.3 2.7 %emit.5 = f32[256,1024]{1,0:T(8,128)S(1)} custom-call(s32[2]{0:T(128)S(1)} %pad_add_fusion.where_ref, bf16[1024,4096]{1,0:T(8,128)(2,1)S(1)} %copy-done.4, bf16[256,128]{1,0:T(8,128)(2,1)S(1)} %get-tuple-element.55.refs_0_, bf16[256,128]{1,0:T(8,128)(2,1)S(1)} %collective-permute-done.23.refs_1_, bf16[256,128]{1,0:T(8,128)(2,1)S(1)} %collective-permute-done.24.refs_2_, ...), custom_call_target="tpu_custom_call" | custom-call | flops 536870912 | bytes 2097152 | tf_op jit(solution)/shard_map/emit/pallas_call | solution.py:497
  214.1 6.2 %collective-permute-done.32 = bf16[256,1024]{1,0:T(8,128)(2,1)S(1)} collective-permute-done((bf16[256,1024]{1,0:T(8,128)(2,1)S(1)}, bf16[256,1024]{1,0:T(8,128)(2,1)S(1)}, u32[]{:S(2)}, u32[]{:S(2)}) %collective-permute-start.32) | collective-permute-done | bytes 524320 | tf_op jit(solution)/shard_map/ppermute | solution.py:522
  (100 shorter events, 41.2 us)
Async XLA Ops:
  5.0 9.3 %collective-permute-start = (bf16[256,512]{1,0:T(8,128)(2,1)S(1)}, bf16[256,512]{1,0:T(8,128)(2,1)S(1)}, u32[]{:S(2)}, u32[]{:S(2)}) collective-permute-start(bf16[256,512]{1,0:T(8,128)(2,1)S(1)} %get-tuple-element.35), channel_id=1, source_target_pairs={{0,4},{4,0},{8,12},{12,8},{16,20},{20,16},{24,28},{28,24},{1,5},{5... | collective-permute-start | bytes 786440 | tf_op jit(solution)/shard_map/ppermute | solution.py:522
  8.0 38.1 %collective-permute-start.4 = (bf16[768,256]{1,0:T(8,128)(2,1)S(1)}, bf16[768,256]{1,0:T(8,128)(2,1)S(1)}, u32[]{:S(2)}, u32[]{:S(2)}) collective-permute-start(bf16[768,256]{1,0:T(8,128)(2,1)S(1)} %get-tuple-element.36), channel_id=1, source_target_pairs={{0,16},{4,20},{8,24},{12,28},{16,0},{20,4},{24,8},{28,12},{1,17},{... | collective-permute-start | bytes 1179656 | tf_op jit(solution)/shard_map/ppermute | solution.py:522
  10.6 35.5 %collective-permute-start.5 = (bf16[768,256]{1,0:T(8,128)(2,1)S(1)}, bf16[768,256]{1,0:T(8,128)(2,1)S(1)}, u32[]{:S(2)}, u32[]{:S(2)}) collective-permute-start(bf16[768,256]{1,0:T(8,128)(2,1)S(1)} %get-tuple-element.37), channel_id=1, source_target_pairs={{0,8},{4,12},{8,0},{12,4},{16,24},{20,28},{24,16},{28,20},{1,9},{5... | collective-permute-start | bytes 1179656 | tf_op jit(solution)/shard_map/ppermute | solution.py:522
  12.2 33.9 %collective-permute-start.2 = (bf16[256,512]{1,0:T(8,128)(2,1)S(1)}, bf16[256,512]{1,0:T(8,128)(2,1)S(1)}, u32[]{:S(2)}, u32[]{:S(2)}) collective-permute-start(bf16[256,512]{1,0:T(8,128)(2,1)S(1)} %get-tuple-element.34.refs_0_), channel_id=1, source_target_pairs={{0,16},{4,20},{8,24},{12,28},{16,0},{20,4},{24,8},{28,12},{1,17},{... | collective-permute-start | bytes 786440 | tf_op jit(solution)/shard_map/ppermute | solution.py:522
  14.3 36.2 %collective-permute-start.3 = (bf16[256,512]{1,0:T(8,128)(2,1)S(1)}, bf16[256,512]{1,0:T(8,128)(2,1)S(1)}, u32[]{:S(2)}, u32[]{:S(2)}) collective-permute-start(bf16[256,512]{1,0:T(8,128)(2,1)S(1)} %collective-permute-done.refs_1_), channel_id=1, source_target_pairs={{0,16},{4,20},{8,24},{12,28},{16,0},{20,4},{24,8},{28,12},{1,17},{... | collective-permute-start | bytes 786440 | tf_op jit(solution)/shard_map/ppermute | solution.py:522
  17.2 38.4 %collective-permute-start.1 = (bf16[512,512]{1,0:T(8,128)(2,1)S(1)}, bf16[512,512]{1,0:T(8,128)(2,1)S(1)}, u32[]{:S(2)}, u32[]{:S(2)}) collective-permute-start(bf16[512,512]{1,0:T(8,128)(2,1)S(1)} %join.4.refs_0_), channel_id=1, source_target_pairs={{0,8},{4,12},{8,0},{12,4},{16,24},{20,28},{24,16},{28,20},{1,9},{5... | collective-permute-start | bytes 1572872 | tf_op jit(solution)/shard_map/ppermute | solution.py:522
  50.5 12.9 %collective-permute-start.6 = (bf16[512,512]{1,0:T(8,128)(2,1)S(1)}, bf16[512,512]{1,0:T(8,128)(2,1)S(1)}, u32[]{:S(2)}, u32[]{:S(2)}) collective-permute-start(bf16[512,512]{1,0:T(8,128)(2,1)S(1)} %join.5.refs_1_.refs_0_.refs_2_), channel_id=1, source_target_pairs={{0,8},{4,12},{8,0},{12,4},{16,24},{20,28},{24,16},{28,20},{1,9},{5... | collective-permute-start | bytes 1572872 | tf_op jit(solution)/shard_map/ppermute | solution.py:522
  51.2 25.6 %collective-permute-start.7 = (bf16[512,512]{1,0:T(8,128)(2,1)S(1)}, bf16[512,512]{1,0:T(8,128)(2,1)S(1)}, u32[]{:S(2)}, u32[]{:S(2)}) collective-permute-start(bf16[512,512]{1,0:T(8,128)(2,1)S(1)} %join.4.refs_0_), channel_id=1, source_target_pairs={{0,2},{1,3},{2,0},{3,1},{4,6},{5,7},{6,4},{7,5},{8,10},{9,11},{10,... | collective-permute-start | bytes 1572872 | tf_op jit(solution)/shard_map/ppermute | solution.py:522
  52.7 21.8 %collective-permute-start.11 = (bf16[768,256]{1,0:T(8,128)(2,1)S(1)}, bf16[768,256]{1,0:T(8,128)(2,1)S(1)}, u32[]{:S(2)}, u32[]{:S(2)}) collective-permute-start(bf16[768,256]{1,0:T(8,128)(2,1)S(1)} %get-tuple-element.38), channel_id=1, source_target_pairs={{0,24},{4,28},{8,16},{12,20},{16,8},{20,12},{24,0},{28,4},{1,25},{... | collective-permute-start | bytes 1179656 | tf_op jit(solution)/shard_map/ppermute | solution.py:522
  55.6 23.6 %collective-permute-start.8 = (bf16[512,512]{1,0:T(8,128)(2,1)S(1)}, bf16[512,512]{1,0:T(8,128)(2,1)S(1)}, u32[]{:S(2)}, u32[]{:S(2)}) collective-permute-start(bf16[512,512]{1,0:T(8,128)(2,1)S(1)} %collective-permute-done.1.refs_2_.refs_1_), channel_id=1, source_target_pairs={{0,2},{1,3},{2,0},{3,1},{4,6},{5,7},{6,4},{7,5},{8,10},{9,11},{10,... | collective-permute-start | bytes 1572872 | tf_op jit(solution)/shard_map/ppermute | solution.py:522
  56.1 32.8 %collective-permute-start.9 = (bf16[512,512]{1,0:T(8,128)(2,1)S(1)}, bf16[512,512]{1,0:T(8,128)(2,1)S(1)}, u32[]{:S(2)}, u32[]{:S(2)}) collective-permute-start(bf16[512,512]{1,0:T(8,128)(2,1)S(1)} %join.5.refs_1_.refs_0_.refs_2_), channel_id=1, source_target_pairs={{0,2},{1,3},{2,0},{3,1},{4,6},{5,7},{6,4},{7,5},{8,10},{9,11},{10,... | collective-permute-start | bytes 1572872 | tf_op jit(solution)/shard_map/ppermute | solution.py:522
  63.5 35.0 %collective-permute-start.10 = (bf16[512,512]{1,0:T(8,128)(2,1)S(1)}, bf16[512,512]{1,0:T(8,128)(2,1)S(1)}, u32[]{:S(2)}, u32[]{:S(2)}) collective-permute-start(bf16[512,512]{1,0:T(8,128)(2,1)S(1)} %collective-permute-done.6.refs_2_.refs_1_.refs_3_), channel_id=1, source_target_pairs={{0,2},{1,3},{2,0},{3,1},{4,6},{5,7},{6,4},{7,5},{8,10},{9,11},{10,... | collective-permute-start | bytes 1572872 | tf_op jit(solution)/shard_map/ppermute | solution.py:522
  74.5 14.3 %collective-permute-start.13 = (bf16[512,256]{1,0:T(8,128)(2,1)S(1)}, bf16[512,256]{1,0:T(8,128)(2,1)S(1)}, u32[]{:S(2)}, u32[]{:S(2)}) collective-permute-start(bf16[512,256]{1,0:T(8,128)(2,1)S(1)} %get-tuple-element.39), channel_id=1, source_target_pairs={{0,16},{4,20},{8,24},{12,28},{16,0},{20,4},{24,8},{28,12},{1,17},{... | collective-permute-start | bytes 786440 | tf_op jit(solution)/shard_map/ppermute | solution.py:522
  76.7 12.2 %collective-permute-start.14 = (bf16[512,256]{1,0:T(8,128)(2,1)S(1)}, bf16[512,256]{1,0:T(8,128)(2,1)S(1)}, u32[]{:S(2)}, u32[]{:S(2)}) collective-permute-start(bf16[512,256]{1,0:T(8,128)(2,1)S(1)} %get-tuple-element.40), channel_id=1, source_target_pairs={{0,8},{4,12},{8,0},{12,4},{16,24},{20,28},{24,16},{28,20},{1,9},{5... | collective-permute-start | bytes 786440 | tf_op jit(solution)/shard_map/ppermute | solution.py:522
  79.4 24.8 %collective-permute-start.12 = (bf16[2048,512]{1,0:T(8,128)(2,1)S(1)}, bf16[2048,512]{1,0:T(8,128)(2,1)S(1)}, u32[]{:S(2)}, u32[]{:S(2)}) collective-permute-start(bf16[2048,512]{1,0:T(8,128)(2,1)S(1)} %join.6), channel_id=1, source_target_pairs={{0,1},{1,0},{2,3},{3,2},{4,5},{5,4},{6,7},{7,6},{8,9},{9,8},{10,11... | collective-permute-start | bytes 6291464 | tf_op jit(solution)/shard_map/ppermute | solution.py:522
  98.6 8.8 %collective-permute-start.15 = (bf16[2048,512]{1,0:T(8,128)(2,1)S(1)}, bf16[2048,512]{1,0:T(8,128)(2,1)S(1)}, u32[]{:S(2)}, u32[]{:S(2)}) collective-permute-start(bf16[2048,512]{1,0:T(8,128)(2,1)S(1)} %join.7), channel_id=1, source_target_pairs={{0,1},{1,0},{2,3},{3,2},{4,5},{5,4},{6,7},{7,6},{8,9},{9,8},{10,11... | collective-permute-start | bytes 6291464 | tf_op jit(solution)/shard_map/ppermute | solution.py:522
  98.7 13.2 %collective-permute-start.21 = (bf16[512,256]{1,0:T(8,128)(2,1)S(1)}, bf16[512,256]{1,0:T(8,128)(2,1)S(1)}, u32[]{:S(2)}, u32[]{:S(2)}) collective-permute-start(bf16[512,256]{1,0:T(8,128)(2,1)S(1)} %get-tuple-element.51), channel_id=1, source_target_pairs={{0,24},{4,28},{8,16},{12,20},{16,8},{20,12},{24,0},{28,4},{1,25},{... | collective-permute-start | bytes 786440 | tf_op jit(solution)/shard_map/ppermute | solution.py:522
  102.9 12.2 %collective-permute-start.16 = (bf16[512,256]{1,0:T(8,128)(2,1)S(1)}, bf16[512,256]{1,0:T(8,128)(2,1)S(1)}, u32[]{:S(2)}, u32[]{:S(2)}) collective-permute-start(bf16[512,256]{1,0:T(8,128)(2,1)S(1)} %get-tuple-element.42), channel_id=1, source_target_pairs={{0,8},{4,12},{8,0},{12,4},{16,24},{20,28},{24,16},{28,20},{1,9},{5... | collective-permute-start | bytes 786440 | tf_op jit(solution)/shard_map/ppermute | solution.py:522
  103.7 28.0 %collective-permute-start.17 = (bf16[512,256]{1,0:T(8,128)(2,1)S(1)}, bf16[512,256]{1,0:T(8,128)(2,1)S(1)}, u32[]{:S(2)}, u32[]{:S(2)}) collective-permute-start(bf16[512,256]{1,0:T(8,128)(2,1)S(1)} %get-tuple-element.43), channel_id=1, source_target_pairs={{0,16},{4,20},{8,24},{12,28},{16,0},{20,4},{24,8},{28,12},{1,17},{... | collective-permute-start | bytes 786440 | tf_op jit(solution)/shard_map/ppermute | solution.py:522
  104.2 32.0 %collective-permute-start.18 = (bf16[512,256]{1,0:T(8,128)(2,1)S(1)}, bf16[512,256]{1,0:T(8,128)(2,1)S(1)}, u32[]{:S(2)}, u32[]{:S(2)}) collective-permute-start(bf16[512,256]{1,0:T(8,128)(2,1)S(1)} %get-tuple-element.44), channel_id=1, source_target_pairs={{0,24},{4,28},{8,16},{12,20},{16,8},{20,12},{24,0},{28,4},{1,25},{... | collective-permute-start | bytes 786440 | tf_op jit(solution)/shard_map/ppermute | solution.py:522
  111.4 31.9 %collective-permute-start.20 = (bf16[3072,128]{1,0:T(8,128)(2,1)}, bf16[3072,128]{1,0:T(8,128)(2,1)S(1)}, u32[]{:S(2)}, u32[]{:S(2)}) collective-permute-start(bf16[3072,128]{1,0:T(8,128)(2,1)} %get-tuple-element.49), channel_id=1, source_target_pairs={{0,4},{4,0},{8,12},{12,8},{16,20},{20,16},{24,28},{28,24},{1,5},{5... | collective-permute-start | bytes 2359304 | tf_op jit(solution)/shard_map/ppermute | solution.py:522
  135.6 15.1 %collective-permute-start.22 = (bf16[2048,128]{1,0:T(8,128)(2,1)}, bf16[2048,128]{1,0:T(8,128)(2,1)S(1)}, u32[]{:S(2)}, u32[]{:S(2)}) collective-permute-start(bf16[2048,128]{1,0:T(8,128)(2,1)} %get-tuple-element.53), channel_id=1, source_target_pairs={{0,4},{4,0},{8,12},{12,8},{16,20},{20,16},{24,28},{28,24},{1,5},{5... | collective-permute-start | bytes 1572872 | tf_op jit(solution)/shard_map/ppermute | solution.py:522
  141.0 28.4 %collective-permute-start.19 = (bf16[2048,128]{1,0:T(8,128)(2,1)}, bf16[2048,128]{1,0:T(8,128)(2,1)}, u32[]{:S(2)}, u32[]{:S(2)}) collective-permute-start(bf16[2048,128]{1,0:T(8,128)(2,1)} %get-tuple-element.46), channel_id=1, source_target_pairs={{0,4},{4,0},{8,12},{12,8},{16,20},{20,16},{24,28},{28,24},{1,5},{5... | collective-permute-start | bytes 1572872 | tf_op jit(solution)/shard_map/ppermute | solution.py:522
  170.9 6.5 %collective-permute-start.23 = (bf16[256,128]{1,0:T(8,128)(2,1)S(1)}, bf16[256,128]{1,0:T(8,128)(2,1)S(1)}, u32[]{:S(2)}, u32[]{:S(2)}) collective-permute-start(bf16[256,128]{1,0:T(8,128)(2,1)S(1)} %get-tuple-element.56), channel_id=1, source_target_pairs={{0,4},{4,0},{8,12},{12,8},{16,20},{20,16},{24,28},{28,24},{1,5},{5... | collective-permute-start | bytes 196616 | tf_op jit(solution)/shard_map/ppermute | solution.py:522
  171.6 8.7 %collective-permute-start.24 = (bf16[256,128]{1,0:T(8,128)(2,1)S(1)}, bf16[256,128]{1,0:T(8,128)(2,1)S(1)}, u32[]{:S(2)}, u32[]{:S(2)}) collective-permute-start(bf16[256,128]{1,0:T(8,128)(2,1)S(1)} %get-tuple-element.57), channel_id=1, source_target_pairs={{0,8},{4,12},{8,0},{12,4},{16,24},{20,28},{24,16},{28,20},{1,9},{5... | collective-permute-start | bytes 196616 | tf_op jit(solution)/shard_map/ppermute | solution.py:522
  171.6 10.6 %collective-permute-start.25 = (bf16[256,128]{1,0:T(8,128)(2,1)S(1)}, bf16[256,128]{1,0:T(8,128)(2,1)S(1)}, u32[]{:S(2)}, u32[]{:S(2)}) collective-permute-start(bf16[256,128]{1,0:T(8,128)(2,1)S(1)} %get-tuple-element.58), channel_id=1, source_target_pairs={{0,12},{4,8},{8,4},{12,0},{16,28},{20,24},{24,20},{28,16},{1,13},{... | collective-permute-start | bytes 196616 | tf_op jit(solution)/shard_map/ppermute | solution.py:522
  174.5 7.7 %collective-permute-start.26 = (bf16[256,128]{1,0:T(8,128)(2,1)S(1)}, bf16[256,128]{1,0:T(8,128)(2,1)S(1)}, u32[]{:S(2)}, u32[]{:S(2)}) collective-permute-start(bf16[256,128]{1,0:T(8,128)(2,1)S(1)} %get-tuple-element.59), channel_id=1, source_target_pairs={{0,16},{4,20},{8,24},{12,28},{16,0},{20,4},{24,8},{28,12},{1,17},{... | collective-permute-start | bytes 196616 | tf_op jit(solution)/shard_map/ppermute | solution.py:522
  175.9 6.4 %collective-permute-start.27 = (bf16[256,128]{1,0:T(8,128)(2,1)S(1)}, bf16[256,128]{1,0:T(8,128)(2,1)S(1)}, u32[]{:S(2)}, u32[]{:S(2)}) collective-permute-start(bf16[256,128]{1,0:T(8,128)(2,1)S(1)} %get-tuple-element.60), channel_id=1, source_target_pairs={{0,20},{4,16},{8,28},{12,24},{16,4},{20,0},{24,12},{28,8},{1,21},{... | collective-permute-start | bytes 196616 | tf_op jit(solution)/shard_map/ppermute | solution.py:522
  180.3 7.0 %collective-permute-start.29 = (bf16[256,128]{1,0:T(8,128)(2,1)S(1)}, bf16[256,128]{1,0:T(8,128)(2,1)S(1)}, u32[]{:S(2)}, u32[]{:S(2)}) collective-permute-start(bf16[256,128]{1,0:T(8,128)(2,1)S(1)} %get-tuple-element.62), channel_id=1, source_target_pairs={{0,28},{4,24},{8,20},{12,16},{16,12},{20,8},{24,4},{28,0},{1,29},{... | collective-permute-start | bytes 196616 | tf_op jit(solution)/shard_map/ppermute | solution.py:522
  193.4 6.9 %collective-permute-start.31 = (bf16[256,1024]{1,0:T(8,128)(2,1)S(1)}, bf16[256,1024]{1,0:T(8,128)(2,1)S(1)}, u32[]{:S(2)}, u32[]{:S(2)}) collective-permute-start(bf16[256,1024]{1,0:T(8,128)(2,1)S(1)} %emit.6), channel_id=1, source_target_pairs={{0,1},{1,0},{2,3},{3,2},{4,5},{5,4},{6,7},{7,6},{8,9},{9,8},{10,11... | collective-permute-start | bytes 1572872 | tf_op jit(solution)/shard_map/ppermute | solution.py:522
  199.7 8.3 %collective-permute-start.30 = (bf16[256,1024]{1,0:T(8,128)(2,1)S(1)}, bf16[256,1024]{1,0:T(8,128)(2,1)S(1)}, u32[]{:S(2)}, u32[]{:S(2)}) collective-permute-start(bf16[256,1024]{1,0:T(8,128)(2,1)S(1)} %emit.4), channel_id=1, source_target_pairs={{0,1},{1,0},{2,3},{3,2},{4,5},{5,4},{6,7},{7,6},{8,9},{9,8},{10,11... | collective-permute-start | bytes 1572872 | tf_op jit(solution)/shard_map/ppermute | solution.py:522
  206.4 13.9 %collective-permute-start.32 = (bf16[256,1024]{1,0:T(8,128)(2,1)S(1)}, bf16[256,1024]{1,0:T(8,128)(2,1)S(1)}, u32[]{:S(2)}, u32[]{:S(2)}) collective-permute-start(bf16[256,1024]{1,0:T(8,128)(2,1)S(1)} %emit.7), channel_id=1, source_target_pairs={{0,2},{1,3},{2,0},{3,1},{4,6},{5,7},{6,4},{7,5},{8,10},{9,11},{10,... | collective-permute-start | bytes 1572872 | tf_op jit(solution)/shard_map/ppermute | solution.py:522
  (22 other events, 358.5 us)

commit v3 on v2

--- a/solution.py
+++ b/solution.py
@@ -194,7 +194,7 @@
         one.wait()
 
 
-def cut(where, tokens, weight, index, filters, after):
+def cut(where, tokens, weight, index, filters, after, limit):
     rows = weight.shape[1] + sum(value.shape[0] for value in filters)
     shapes = []
     for value in tokens:
@@ -209,7 +209,7 @@
         + [pl.BlockSpec(memory_space=pl.ANY)] * len(after),
         out_specs=(pl.BlockSpec(memory_space=pltpu.VMEM),) * len(shapes),
         scratch_shapes=[pltpu.SemaphoreType.DMA((10,))],
-        compiler_params=pltpu.CompilerParams(vmem_limit_bytes=8 * 2**20),
+        compiler_params=pltpu.CompilerParams(vmem_limit_bytes=limit),
         name="cut",
     )(where, *tokens, weight, *filters, *after)
 
@@ -298,7 +298,7 @@
         + [pl.BlockSpec(memory_space=pl.ANY)] * len(after),
         out_specs=(vmem,) * len(shapes),
         scratch_shapes=[pltpu.VMEM((4 * depth, width), jnp.bfloat16)],
-        compiler_params=pltpu.CompilerParams(vmem_limit_bytes=24 * 2**20),
+        compiler_params=pltpu.CompilerParams(vmem_limit_bytes=12 * 2**20),
         cost_estimate=pl.CostEstimate(
             flops=2 * length * 4 * depth * width,
             bytes_accessed=2 * length * 4 * depth,
@@ -328,10 +328,22 @@
 
 
 def mix_kernel(
-    where_ref, own1, recv1, own2, recv2, taps_ref, skip_ref, ahead, middle, middle_back, back, *refs
+    where_ref,
+    own1,
+    recv1,
+    own2,
+    recv2,
+    taps_ref,
+    skip_ref,
+    ahead,
+    middle,
+    middle_back,
+    back,
+    *refs,
+    after,
 ):
-    lags_here, lags_there, mixed_ref = refs[:3]
-    padded, gated, lags, waves, filter_waves, sums = refs[3:]
+    lags_here, lags_there = refs[:2]
+    mixed_ref, padded, gated, lags, waves, filter_waves, sums = refs[2 + after :]
     place = where_ref[0]
     length, width = own1.shape
     block = length // 8
@@ -404,15 +416,17 @@
             mixed_ref[at, :] = wave[:, i * width : (i + 1) * width] + skip_ref[...] * gated[at, :]
 
 
-def mix(where, own1, recv1, own2, recv2, taps, skip, tables, lags_here, lags_there):
+def mix(where, own1, recv1, own2, recv2, taps, skip, tables, lags_here, lags_there, after):
     length, width = own1.shape
     rows, two = tables[1].shape[:2]
     padded_rows = tables[0].shape[0] // 2
     vmem = pl.BlockSpec(memory_space=pltpu.VMEM)
     return pl.pallas_call(
-        mix_kernel,
+        functools.partial(mix_kernel, after=len(after)),
         out_shape=jax.ShapeDtypeStruct((length, width), jnp.float32),
-        in_specs=[pl.BlockSpec(memory_space=pltpu.SMEM)] + [vmem] * 12,
+        in_specs=[pl.BlockSpec(memory_space=pltpu.SMEM)]
+        + [vmem] * 12
+        + [pl.BlockSpec(memory_space=pl.ANY)] * len(after),
         out_specs=vmem,
         scratch_shapes=[
             pltpu.VMEM((length + 8, width), jnp.float32),
@@ -422,12 +436,12 @@
             pltpu.VMEM((padded_rows * two, width), jnp.float32),
             pltpu.VMEM((padded_rows * two, width), jnp.float32),
         ],
-        compiler_params=pltpu.CompilerParams(vmem_limit_bytes=40 * 2**20),
+        compiler_params=pltpu.CompilerParams(vmem_limit_bytes=20 * 2**20),
         cost_estimate=pl.CostEstimate(
             flops=2 * 8 * length * inner_len * width, bytes_accessed=6 * 2**20, transcendentals=0
         ),
         name="mix",
-    )(where, own1, recv1, own2, recv2, taps, skip, *tables, lags_here, lags_there)
+    )(where, own1, recv1, own2, recv2, taps, skip, *tables, lags_here, lags_there, *after)
 
 
 def gate_kernel(where_ref, own0, recv0, mixed_ref, taps_ref, *refs):
@@ -456,7 +470,7 @@
             pltpu.VMEM((length + 8, width), jnp.float32),
             pltpu.VMEM((length, width), jnp.bfloat16),
         ],
-        compiler_params=pltpu.CompilerParams(vmem_limit_bytes=16 * 2**20),
+        compiler_params=pltpu.CompilerParams(vmem_limit_bytes=8 * 2**20),
         cost_estimate=pl.CostEstimate(
             flops=8 * length * width, bytes_accessed=12 * length * width, transcendentals=0
         ),
@@ -464,54 +478,65 @@
     )(where, own0, recv0, mixed, taps)
 
 
-def emit_kernel(where_ref, weight, *refs, added):
+def emit_kernel(where_ref, weight, *refs, turns, added):
     parts, extra = refs[:8], refs[8 : 8 + added]
-    out_ref, joined, tiles, sems = refs[8 + added :]
-    place, column = where_ref[0], where_ref[1]
+    outs = refs[8 + added : 8 + added + len(turns)]
+    joined, tiles, sems = refs[8 + added + len(turns) :]
+    place, chan = where_ref[0], where_ref[1]
     width = parts[0].shape[1]
-    count, _, tile = tiles.shape
+    columns = outs[0].shape[1]
+    count, depth, _ = tiles.shape
     copies = []
-    for i in range(count):
-        start = pl.multiple_of((column * count + i) * tile, tile)
-        copies.append(
-            pltpu.make_async_copy(weight.at[:, pl.ds(start, tile)], tiles.at[i], sems.at[i])
-        )
-        copies[i].start()
+    for i, turn in enumerate(turns):
+        start = pl.multiple_of(jnp.bitwise_xor(chan, turn) * columns, columns)
+        for step in range(count // len(turns)):
+            slot = i * (count // len(turns)) + step
+            source = weight.at[pl.ds(step * depth, depth), pl.ds(start, columns)]
+            copies.append(pltpu.make_async_copy(source, tiles.at[slot], sems.at[slot]))
+            copies[slot].start()
     for i in range(8):
         start = pl.multiple_of(jnp.bitwise_xor(place, i) * width, width)
         joined[:, pl.ds(start, width)] = parts[i][...]
-    for i in range(count):
-        copies[i].wait()
-        total = jnp.dot(joined[...], tiles[i], preferred_element_type=jnp.float32)
-        at = slice(i * tile, (i + 1) * tile)
-        for term in extra:
-            total = total + term[:, at].astype(jnp.float32)
-        out_ref[:, at] = total.astype(out_ref.dtype)
-
-
-def emit(where, parts, weight, extra, out_dtype):
+    for i in range(len(turns)):
+        total = None
+        for step in range(count // len(turns)):
+            slot = i * (count // len(turns)) + step
+            copies[slot].wait()
+            term = jnp.dot(
+                joined[:, step * depth : (step + 1) * depth],
+                tiles[slot],
+                preferred_element_type=jnp.float32,
+            )
+            total = term if total is None else total + term
+        if added:
+            total = total + extra[i][...].astype(jnp.float32)
+        outs[i][...] = total.astype(outs[i].dtype)
+
+
+def emit(where, parts, weight, turns, extra, out_dtype):
     rows, width = parts[0].shape
     columns = weight.shape[1] // 4
-    count = 4
+    steps = 4
     vmem = pl.BlockSpec(memory_space=pltpu.VMEM)
+    shape = jax.ShapeDtypeStruct((rows, columns), out_dtype)
     return pl.pallas_call(
-        functools.partial(emit_kernel, added=len(extra)),
-        out_shape=jax.ShapeDtypeStruct((rows, columns), out_dtype),
+        functools.partial(emit_kernel, turns=turns, added=len(extra)),
+        out_shape=(shape,) * len(turns),
         in_specs=[
             pl.BlockSpec(memory_space=pltpu.SMEM),
-            pl.BlockSpec(memory_space=pltpu.HBM),
+            pl.BlockSpec(memory_space=pl.ANY),
         ]
         + [vmem] * (8 + len(extra)),
-        out_specs=vmem,
+        out_specs=(vmem,) * len(turns),
         scratch_shapes=[
             pltpu.VMEM((rows, 8 * width), jnp.bfloat16),
-            pltpu.VMEM((count, weight.shape[0], columns // count), jnp.bfloat16),
-            pltpu.SemaphoreType.DMA((count,)),
+            pltpu.VMEM((steps * len(turns), weight.shape[0] // steps, columns), jnp.bfloat16),
+            pltpu.SemaphoreType.DMA((steps * len(turns),)),
         ],
-        compiler_params=pltpu.CompilerParams(vmem_limit_bytes=16 * 2**20),
+        compiler_params=pltpu.CompilerParams(vmem_limit_bytes=57 * 2**20),
         cost_estimate=pl.CostEstimate(
-            flops=2 * rows * weight.shape[0] * columns,
-            bytes_accessed=2 * weight.shape[0] * columns,
+            flops=2 * rows * weight.shape[0] * columns * len(turns),
+            bytes_accessed=2 * weight.shape[0] * columns * len(turns),
             transcendentals=0,
         ),
         name="emit",
@@ -535,7 +560,7 @@
     def far_part(parts, turn):
         return swap(parts[turn], "seq", seq, 2 * turn)
 
-    theirs, ours, *cut1 = cut(where, [tokens], weight, 1, [long_filter], [])
+    theirs, ours, *cut1 = cut(where, [tokens], weight, 1, [long_filter], [], 56 * 2**20)
     w1_2, w1_1 = far_part(cut1, 2), far_part(cut1, 1)
     far_ours = swap(ours, "seq", seq, 4)
     beside = swap(theirs, "seq", seq, 1)
@@ -544,7 +569,7 @@
     near = swap(pair, "seq", seq, 2)
     pair_across = swap(pair, "chan", chans, 2)
     far = join([far_ours, far_beside], [w1_2, w1_1])
-    cut2 = cut(where, [], weight, 2, [], [far])
+    cut2 = cut(where, [], weight, 2, [], [near], 8 * 2**20)
     w1_3 = far_part(cut1, 3)
     far_near = swap(far, "seq", seq, 2)
     w2_2 = far_part(cut2, 2)
@@ -552,7 +577,7 @@
     near_across = swap(near, "chan", chans, 2)
     core_a = swap(join([pair, pair_across, near, near_across], [w1_3]), "chan", chans, 1)
     far_near_across = swap(far_near, "chan", chans, 2)
-    cut0 = cut(where, [], weight, 0, [], [far_near])
+    cut0 = cut(where, [], weight, 0, [], [far_near], 8 * 2**20)
     w2_1 = far_part(cut2, 1)
     w2_3 = far_part(cut2, 3)
     core_b = swap(
@@ -574,25 +599,24 @@
     skip = lax.dynamic_slice_in_dim(skip_gain, place * part, part, 0)[None]
     own1, send1, lags_here = project(where, line, across, cores, parts1, length, [])
     recv1 = swap(send1, "seq", seq, 1)
-    own2, send2 = project(where, line, across, cores, parts2, length, [w0_2, w0_1])
+    own2, send2 = project(where, line, across, cores, parts2, length, [])
     recv2 = swap(send2, "seq", seq, 1)
     own0, send0 = project(where, line, across, cores, parts0, length, [])
     recv0 = swap(send0, "seq", seq, 1)
     mixed = mix(
-        where, own1, recv1, own2, recv2, taps, skip, wave_tables(length), lags_here, recv1[length:]
+        where, own1, recv1, own2, recv2, taps, skip, wave_tables(length), lags_here, recv1[length:], [send0]
     )
     pieces = gate(where, own0, recv0, mixed, taps)
     joined = [
         piece if turn == 0 else swap(piece, "seq", seq, turn) for turn, piece in enumerate(pieces)
     ]
 
-    def share(turn, extra, dtype):
-        return emit(jnp.stack([place, chan ^ turn]).astype(jnp.int32), joined, out_weight, extra, dtype)
-
-    from_core = swap(share(3, [], jnp.bfloat16), "chan", chans, 1)
-    near = swap(share(1, [], jnp.bfloat16), "chan", chans, 1)
-    from_chip = swap(share(2, [from_core], jnp.bfloat16), "chan", chans, 2)
-    own = share(0, [near], jnp.float32)
+    across_out, beside_out = emit(where, joined, out_weight, (3, 1), [], jnp.bfloat16)
+    from_core = swap(across_out, "chan", chans, 1)
+    near_sum = swap(beside_out, "chan", chans, 1)
+    (chip_out,) = emit(where, joined, out_weight, (2,), [from_core], jnp.bfloat16)
+    from_chip = swap(chip_out, "chan", chans, 2)
+    (own,) = emit(where, joined, out_weight, (0,), [near_sum], jnp.float32)
     return (own + from_chip.astype(jnp.float32)).astype(jnp.bfloat16)
 
 

time: 222 us -> 209 us (0.941)
  local copies, waits for them, and re-layouts: 22.7 us -> 9.95 us
  waiting for transfers between devices: 106 us -> 98.9 us
  Pallas kernels: 42.3 us -> 47.8 us
    unnamed x42 -> x56, local copies, waits for them, and re-layouts: 21.9 us -> 9.17 us
    ppermute x33, waiting for transfers between devices: 106 us -> 98.9 us  [swap(): return lax.ppermute(value, axis, [(i, i ^ turn) for i in range(count)])]
    pallas_call x3, Pallas kernels: 2.68 us -> 5.46 us  [cut(): pl.pallas_call(functools.partial(cut_kernel, index=index, counts=counts,...]
    pallas_call x5 -> x4, Pallas kernels: 26.2 us -> 28.8 us  [the longest x1 15.3 us: mix(): pl.pallas_call(functools.partial(mix_kernel, after=len(after)), out_shape...]
  transfers between devices with their start and end apart: 33 -> 33, of which waited for: 15 -> 14; matrix products, arithmetic and copies ran while one was open for 0% -> 0% of each run, Pallas kernels for 17% -> 18%
where the time goes in v3:
time: 209 us
  waiting for transfers between devices  98.9 us (47%)
  starting transfers between devices  49 us (23%)
  Pallas kernels  47.8 us (23%)
  local copies, waits for them, and re-layouts  9.95 us (5%)
  other arithmetic  2.84 us (1%)
    ppermute x33, waiting for transfers between devices, swap(): return lax.ppermute(value, axis, [(i, i ^ turn) for i in range(count)])  98.9 us
    ppermute x33, starting transfers between devices, swap(): return lax.ppermute(value, axis, [(i, i ^ turn) for i in range(count)])  49 us
    pallas_call x1, Pallas kernels, mix(): pl.pallas_call(functools.partial(mix_kernel, after=len(after)), out_shape...  15.3 us
    pallas_call x3, Pallas kernels, emit(): pl.pallas_call(functools.partial(emit_kernel, turns=turns, added=len(extr...  13.6 us
    pallas_call x3, Pallas kernels, project(): pl.pallas_call(functools.partial(project_kernel, filter_rows=filter_rows,...  11.7 us
    unnamed x56, local copies, waits for them, and re-layouts  9.17 us
    pallas_call x3, Pallas kernels, cut(): pl.pallas_call(functools.partial(cut_kernel, index=index, counts=counts,...  5.46 us
  transfers between devices with their start and end apart: 33, of which 14 were waited for; matrix products, arithmetic and copies ran while one was open for 0% of the time, Pallas kernels for 18%

profile of v3, /device:TPU:0, one launch (start us, length us, event | category | flops | bytes accessed | tf_op | source)
XLA Modules:
  0.0 208.7 jit_solution(1999971427884865530)
XLA Ops:
  0.7 3.9 %cut.3 = (bf16[256,512]{1,0:T(8,128)(2,1)}, bf16[256,512]{1,0:T(8,128)(2,1)}, bf16[768,256]{1,0:T(8,128)(2,1)}, bf16[768,256]{1,0:T(8,128)(2,1)}, bf16[768,256]{1,0:T(8,128)(2,1)}, /*index=5*/bf16[768,256]{1,0:T(8,128)(2,1)}) custom-call(s32[2]{0:T(128)} %pad_add_fusion.where_ref, bf16[256,1024]{1,0:T(8,128)(2,1)} %refs_0_.1, bf16[3,512,1024]{2,1,0:T(8,128)(2,1)} %bitcast.5, ...), custom_call_target="tpu_custom_call" | custom-call | tf_op jit(solution)/shard_map/cut/pallas_call | solution.py:204
  4.6 3.0 %collective-permute-start = (bf16[256,512]{1,0:T(8,128)(2,1)}, bf16[256,512]{1,0:T(8,128)(2,1)S(1)}, u32[]{:S(2)}, u32[]{:S(2)}) collective-permute-start(bf16[256,512]{1,0:T(8,128)(2,1)} %get-tuple-element.37), channel_id=1, source_target_pairs={{0,4},{4,0},{8,12},{12,8},{16,20},{20,16},{24,28},{28,24},{1,5},{5... | collective-permute-start | bytes 786440 | tf_op jit(solution)/shard_map/ppermute | solution.py:547
  7.6 2.6 %collective-permute-start.4 = (bf16[768,256]{1,0:T(8,128)(2,1)}, bf16[768,256]{1,0:T(8,128)(2,1)S(1)}, u32[]{:S(2)}, u32[]{:S(2)}) collective-permute-start(bf16[768,256]{1,0:T(8,128)(2,1)} %get-tuple-element.38), channel_id=1, source_target_pairs={{0,16},{4,20},{8,24},{12,28},{16,0},{20,4},{24,8},{28,12},{1,17},{... | collective-permute-start | bytes 1179656 | tf_op jit(solution)/shard_map/ppermute | solution.py:547
  12.1 2.0 collective-permute-done.refs_1_
  14.1 2.8 %collective-permute-start.3 = (bf16[256,512]{1,0:T(8,128)(2,1)S(1)}, bf16[256,512]{1,0:T(8,128)(2,1)S(1)}, u32[]{:S(2)}, u32[]{:S(2)}) collective-permute-start(bf16[256,512]{1,0:T(8,128)(2,1)S(1)} %collective-permute-done.refs_1_), channel_id=1, source_target_pairs={{0,16},{4,20},{8,24},{12,28},{16,0},{20,4},{24,8},{28,12},{1,17},{... | collective-permute-start | bytes 786440 | tf_op jit(solution)/shard_map/ppermute | solution.py:547
  19.6 26.3 %collective-permute-done.2.refs_0_ = bf16[256,512]{1,0:T(8,128)(2,1)S(1)} collective-permute-done((bf16[256,512]{1,0:T(8,128)(2,1)}, bf16[256,512]{1,0:T(8,128)(2,1)S(1)}, u32[]{:S(2)}, u32[]{:S(2)}) %collective-permute-start.2) | collective-permute-done | bytes 262176 | tf_op jit(solution)/shard_map/ppermute | solution.py:547
  45.8 4.5 %collective-permute-done.3.refs_1_ = bf16[256,512]{1,0:T(8,128)(2,1)S(1)} collective-permute-done((bf16[256,512]{1,0:T(8,128)(2,1)S(1)}, bf16[256,512]{1,0:T(8,128)(2,1)S(1)}, u32[]{:S(2)}, u32[]{:S(2)}) %collective-permute-start.3) | collective-permute-done | bytes 262176 | tf_op jit(solution)/shard_map/ppermute | solution.py:547
  52.5 2.9 %collective-permute-start.11 = (bf16[768,256]{1,0:T(8,128)(2,1)S(1)}, bf16[768,256]{1,0:T(8,128)(2,1)S(1)}, u32[]{:S(2)}, u32[]{:S(2)}) collective-permute-start(bf16[768,256]{1,0:T(8,128)(2,1)S(1)} %copy-done.27), channel_id=1, source_target_pairs={{0,24},{4,28},{8,16},{12,20},{16,8},{20,12},{24,0},{28,4},{1,25},{... | collective-permute-start | bytes 1179656 | tf_op jit(solution)/shard_map/ppermute | solution.py:547
  57.4 5.9 %collective-permute-done.6.refs_2_.refs_1_.refs_3_ = bf16[512,512]{1,0:T(8,128)(2,1)S(1)} collective-permute-done((bf16[512,512]{1,0:T(8,128)(2,1)S(1)}, bf16[512,512]{1,0:T(8,128)(2,1)S(1)}, u32[]{:S(2)}, u32[]{:S(2)}) %collective-permute-start.6) | collective-permute-done | bytes 524320 | tf_op jit(solution)/shard_map/ppermute | solution.py:547
  65.6 8.7 %collective-permute-done.11.refs_4_.refs_13_ = bf16[768,256]{1,0:T(8,128)(2,1)S(1)} collective-permute-done((bf16[768,256]{1,0:T(8,128)(2,1)S(1)}, bf16[768,256]{1,0:T(8,128)(2,1)S(1)}, u32[]{:S(2)}, u32[]{:S(2)}) %collective-permute-start.11) | collective-permute-done | bytes 393248 | tf_op jit(solution)/shard_map/ppermute | solution.py:547
  74.3 2.2 %collective-permute-start.13 = (bf16[512,256]{1,0:T(8,128)(2,1)S(1)}, bf16[512,256]{1,0:T(8,128)(2,1)S(1)}, u32[]{:S(2)}, u32[]{:S(2)}) collective-permute-start(bf16[512,256]{1,0:T(8,128)(2,1)S(1)} %get-tuple-element.41), channel_id=1, source_target_pairs={{0,16},{4,20},{8,24},{12,28},{16,0},{20,4},{24,8},{28,12},{1,17},{... | collective-permute-start | bytes 786440 | tf_op jit(solution)/shard_map/ppermute | solution.py:547
  76.5 2.5 %collective-permute-start.14 = (bf16[512,256]{1,0:T(8,128)(2,1)S(1)}, bf16[512,256]{1,0:T(8,128)(2,1)S(1)}, u32[]{:S(2)}, u32[]{:S(2)}) collective-permute-start(bf16[512,256]{1,0:T(8,128)(2,1)S(1)} %get-tuple-element.42), channel_id=1, source_target_pairs={{0,8},{4,12},{8,0},{12,4},{16,24},{20,28},{24,16},{28,20},{1,9},{5... | collective-permute-start | bytes 786440 | tf_op jit(solution)/shard_map/ppermute | solution.py:547
  79.2 9.0 %collective-permute-done.9.refs_1_.refs_6_ = bf16[512,512]{1,0:T(8,128)(2,1)S(1)} collective-permute-done((bf16[512,512]{1,0:T(8,128)(2,1)S(1)}, bf16[512,512]{1,0:T(8,128)(2,1)S(1)}, u32[]{:S(2)}, u32[]{:S(2)}) %collective-permute-start.9) | collective-permute-done | bytes 524320 | tf_op jit(solution)/shard_map/ppermute | solution.py:547
  88.3 10.0 %collective-permute-done.10.refs_3_.refs_7_ = bf16[512,512]{1,0:T(8,128)(2,1)S(1)} collective-permute-done((bf16[512,512]{1,0:T(8,128)(2,1)S(1)}, bf16[512,512]{1,0:T(8,128)(2,1)S(1)}, u32[]{:S(2)}, u32[]{:S(2)}) %collective-permute-start.10) | collective-permute-done | bytes 524320 | tf_op jit(solution)/shard_map/ppermute | solution.py:547
  98.5 3.2 %collective-permute-start.21 = (bf16[512,256]{1,0:T(8,128)(2,1)S(1)}, bf16[512,256]{1,0:T(8,128)(2,1)S(1)}, u32[]{:S(2)}, u32[]{:S(2)}) collective-permute-start(bf16[512,256]{1,0:T(8,128)(2,1)S(1)} %get-tuple-element.53), channel_id=1, source_target_pairs={{0,24},{4,28},{8,16},{12,20},{16,8},{20,12},{24,0},{28,4},{1,25},{... | collective-permute-start | bytes 786440 | tf_op jit(solution)/shard_map/ppermute | solution.py:547
  103.8 3.2 %collective-permute-start.18 = (bf16[512,256]{1,0:T(8,128)(2,1)S(1)}, bf16[512,256]{1,0:T(8,128)(2,1)S(1)}, u32[]{:S(2)}, u32[]{:S(2)}) collective-permute-start(bf16[512,256]{1,0:T(8,128)(2,1)S(1)} %get-tuple-element.46), channel_id=1, source_target_pairs={{0,24},{4,28},{8,16},{12,20},{16,8},{20,12},{24,0},{28,4},{1,25},{... | collective-permute-start | bytes 786440 | tf_op jit(solution)/shard_map/ppermute | solution.py:547
  107.0 4.0 %project.4 = (f32[2048,128]{1,0:T(8,128)S(1)}, bf16[3072,128]{1,0:T(8,128)(2,1)}, bf16[1024,128]{1,0:T(8,128)(2,1)S(1)}) custom-call(s32[2]{0:T(128)S(1)} %copy-done.15, bf16[512,512]{1,0:T(8,128)(2,1)S(1)} %join.4.refs_0_, bf16[512,512]{1,0:T(8,128)(2,1)S(1)} %collective-permute-done.1.refs_2_.refs_1_, bf16[512,512]{1,0:T(8,128)(2,1)S(1)} %join.5.refs_0_.refs_2_, ...), custom_call_target="tpu_custom_call" | custom-call | flops 2147483648 | bytes 8388608 | tf_op jit(solution)/shard_map/project/pallas_call | solution.py:293
  111.5 3.8 %project.5 = (f32[2048,128]{1,0:T(8,128)S(1)}, bf16[2048,128]{1,0:T(8,128)(2,1)}) custom-call(s32[2]{0:T(128)S(1)} %copy-done.15, bf16[512,512]{1,0:T(8,128)(2,1)S(1)} %join.4.refs_0_, bf16[512,512]{1,0:T(8,128)(2,1)S(1)} %collective-permute-done.1.refs_2_.refs_1_, bf16[512,512]{1,0:T(8,128)(2,1)S(1)} %join.5.refs_0_.refs_2_, ...), custom_call_target="tpu_custom_call" | custom-call | flops 2147483648 | bytes 8388608 | tf_op jit(solution)/shard_map/project/pallas_call | solution.py:293
  117.9 13.7 %collective-permute-done.17.refs_12_ = bf16[512,256]{1,0:T(8,128)(2,1)S(1)} collective-permute-done((bf16[512,256]{1,0:T(8,128)(2,1)S(1)}, bf16[512,256]{1,0:T(8,128)(2,1)S(1)}, u32[]{:S(2)}, u32[]{:S(2)}) %collective-permute-start.17) | collective-permute-done | bytes 262176 | tf_op jit(solution)/shard_map/ppermute | solution.py:547
  131.6 3.8 %project.3 = (f32[2048,128]{1,0:T(8,128)S(1)}, bf16[2048,128]{1,0:T(8,128)(2,1)}) custom-call(s32[2]{0:T(128)S(1)} %copy-done.15, bf16[512,512]{1,0:T(8,128)(2,1)S(1)} %join.4.refs_0_, bf16[512,512]{1,0:T(8,128)(2,1)S(1)} %collective-permute-done.1.refs_2_.refs_1_, bf16[512,512]{1,0:T(8,128)(2,1)S(1)} %join.5.refs_0_.refs_2_, ...), custom_call_target="tpu_custom_call" | custom-call | flops 2147483648 | bytes 8388608 | tf_op jit(solution)/shard_map/project/pallas_call | solution.py:293
  137.7 5.2 %collective-permute-done.22.recv2 = bf16[2048,128]{1,0:T(8,128)(2,1)S(1)} collective-permute-done((bf16[2048,128]{1,0:T(8,128)(2,1)}, bf16[2048,128]{1,0:T(8,128)(2,1)S(1)}, u32[]{:S(2)}, u32[]{:S(2)}) %collective-permute-start.22) | collective-permute-done | bytes 524320 | tf_op jit(solution)/shard_map/ppermute | solution.py:547
  146.3 15.3 %mix.1.mixed_ref = f32[2048,128]{1,0:T(8,128)S(1)} custom-call(s32[2]{0:T(128)S(1)} %copy-done.15, f32[2048,128]{1,0:T(8,128)S(1)} %copy-done.5, bf16[3072,128]{1,0:T(8,128)(2,1)S(1)} %collective-permute-done.20.recv1, f32[2048,128]{1,0:T(8,128)S(1)} %copy-done.7, bf16[2048,128]{1,0:T(8,128)(2,1)S(1)} %collective-permute-done.22.recv2, ...), custom_call_target="tpu_custom_call" | custom-call | flops 268435456 | bytes 6291456 | tf_op jit(solution)/shard_map/mix/pallas_call | solution.py:424
  164.3 1.7 collective-permute-start.24
  167.2 1.9 collective-permute-start.26
  170.1 2.3 %collective-permute-start.28 = (bf16[256,128]{1,0:T(8,128)(2,1)S(1)}, bf16[256,128]{1,0:T(8,128)(2,1)S(1)}, u32[]{:S(2)}, u32[]{:S(2)}) collective-permute-start(bf16[256,128]{1,0:T(8,128)(2,1)S(1)} %get-tuple-element.63), channel_id=1, source_target_pairs={{0,24},{4,28},{8,16},{12,20},{16,8},{20,12},{24,0},{28,4},{1,25},{... | collective-permute-start | bytes 196616 | tf_op jit(solution)/shard_map/ppermute | solution.py:547
  172.5 2.4 %collective-permute-start.29 = (bf16[256,128]{1,0:T(8,128)(2,1)S(1)}, bf16[256,128]{1,0:T(8,128)(2,1)S(1)}, u32[]{:S(2)}, u32[]{:S(2)}) collective-permute-start(bf16[256,128]{1,0:T(8,128)(2,1)S(1)} %get-tuple-element.64), channel_id=1, source_target_pairs={{0,28},{4,24},{8,20},{12,16},{16,12},{20,8},{24,4},{28,0},{1,29},{... | collective-permute-start | bytes 196616 | tf_op jit(solution)/shard_map/ppermute | solution.py:547
  174.9 2.3 %collective-permute-done.26.refs_4_ = bf16[256,128]{1,0:T(8,128)(2,1)S(1)} collective-permute-done((bf16[256,128]{1,0:T(8,128)(2,1)S(1)}, bf16[256,128]{1,0:T(8,128)(2,1)S(1)}, u32[]{:S(2)}, u32[]{:S(2)}) %collective-permute-start.26) | collective-permute-done | bytes 65568 | tf_op jit(solution)/shard_map/ppermute | solution.py:547
  180.2 4.8 %emit.3 = (bf16[256,1024]{1,0:T(8,128)(2,1)}, bf16[256,1024]{1,0:T(8,128)(2,1)}) custom-call(s32[2]{0:T(128)} %pad_add_fusion.where_ref, bf16[1024,4096]{1,0:T(8,128)(2,1)} %weight.5, bf16[256,128]{1,0:T(8,128)(2,1)} %copy-done.10, bf16[256,128]{1,0:T(8,128)(2,1)} %copy-done.18, bf16[256,128]{1,0:T(8,128)(2,1)} %copy-done.19, bf16[256,128]{1,0:T(8,128)(2,1)} %copy-done.20, ...), custom_call_target="tpu_custom_call" | custom-call | flops 1073741824 | bytes 4194304 | tf_op jit(solution)/shard_map/emit/pallas_call | solution.py:522
  188.0 4.3 %emit.5 = bf16[256,1024]{1,0:T(8,128)(2,1)} custom-call(s32[2]{0:T(128)} %pad_add_fusion.where_ref, bf16[1024,4096]{1,0:T(8,128)(2,1)} %weight.5, bf16[256,128]{1,0:T(8,128)(2,1)} %copy-done.10, bf16[256,128]{1,0:T(8,128)(2,1)} %copy-done.18, bf16[256,128]{1,0:T(8,128)(2,1)} %copy-done.19, bf16[256,128]{1,0:T(8,128)(2,1)} %copy-done.20, ...), custom_call_target="tpu_custom_call" | custom-call | flops 536870912 | bytes 2097152 | tf_op jit(solution)/shard_map/emit/pallas_call | solution.py:522
  194.6 4.5 %emit.4 = f32[256,1024]{1,0:T(8,128)} custom-call(s32[2]{0:T(128)} %pad_add_fusion.where_ref, bf16[1024,4096]{1,0:T(8,128)(2,1)} %weight.5, bf16[256,128]{1,0:T(8,128)(2,1)} %copy-done.10, bf16[256,128]{1,0:T(8,128)(2,1)} %copy-done.18, bf16[256,128]{1,0:T(8,128)(2,1)} %copy-done.19, bf16[256,128]{1,0:T(8,128)(2,1)} %copy-done.20, ...), custom_call_target="tpu_custom_call" | custom-call | flops 536870912 | bytes 2097152 | tf_op jit(solution)/shard_map/emit/pallas_call | solution.py:522
  199.1 7.4 %collective-permute-done.32 = bf16[256,1024]{1,0:T(8,128)(2,1)S(1)} collective-permute-done((bf16[256,1024]{1,0:T(8,128)(2,1)}, bf16[256,1024]{1,0:T(8,128)(2,1)S(1)}, u32[]{:S(2)}, u32[]{:S(2)}) %collective-permute-start.32) | collective-permute-done | bytes 524320 | tf_op jit(solution)/shard_map/ppermute | solution.py:547
  206.5 2.2 %add_convert_fusion = bf16[256,1024]{1,0:T(8,128)(2,1)} fusion(f32[256,1024]{1,0:T(8,128)} %emit.4, bf16[256,1024]{1,0:T(8,128)(2,1)S(1)} %collective-permute-done.32), kind=kLoop, calls=%fused_computation | loop fusion | flops 786432 | bytes 2097152 | tf_op jit(solution)/shard_map/convert_element_type | solution.py:620
  (110 shorter events, 36.1 us)
Async XLA Ops:
  4.6 9.5 %collective-permute-start = (bf16[256,512]{1,0:T(8,128)(2,1)}, bf16[256,512]{1,0:T(8,128)(2,1)S(1)}, u32[]{:S(2)}, u32[]{:S(2)}) collective-permute-start(bf16[256,512]{1,0:T(8,128)(2,1)} %get-tuple-element.37), channel_id=1, source_target_pairs={{0,4},{4,0},{8,12},{12,8},{16,20},{20,16},{24,28},{28,24},{1,5},{5... | collective-permute-start | bytes 786440 | tf_op jit(solution)/shard_map/ppermute | solution.py:547
  7.6 38.3 %collective-permute-start.4 = (bf16[768,256]{1,0:T(8,128)(2,1)}, bf16[768,256]{1,0:T(8,128)(2,1)S(1)}, u32[]{:S(2)}, u32[]{:S(2)}) collective-permute-start(bf16[768,256]{1,0:T(8,128)(2,1)} %get-tuple-element.38), channel_id=1, source_target_pairs={{0,16},{4,20},{8,24},{12,28},{16,0},{20,4},{24,8},{28,12},{1,17},{... | collective-permute-start | bytes 1179656 | tf_op jit(solution)/shard_map/ppermute | solution.py:547
  10.2 35.7 %collective-permute-start.5 = (bf16[768,256]{1,0:T(8,128)(2,1)}, bf16[768,256]{1,0:T(8,128)(2,1)S(1)}, u32[]{:S(2)}, u32[]{:S(2)}) collective-permute-start(bf16[768,256]{1,0:T(8,128)(2,1)} %get-tuple-element.39), channel_id=1, source_target_pairs={{0,8},{4,12},{8,0},{12,4},{16,24},{20,28},{24,16},{28,20},{1,9},{5... | collective-permute-start | bytes 1179656 | tf_op jit(solution)/shard_map/ppermute | solution.py:547
  11.7 34.1 %collective-permute-start.2 = (bf16[256,512]{1,0:T(8,128)(2,1)}, bf16[256,512]{1,0:T(8,128)(2,1)S(1)}, u32[]{:S(2)}, u32[]{:S(2)}) collective-permute-start(bf16[256,512]{1,0:T(8,128)(2,1)} %get-tuple-element.36.refs_0_), channel_id=1, source_target_pairs={{0,16},{4,20},{8,24},{12,28},{16,0},{20,4},{24,8},{28,12},{1,17},{... | collective-permute-start | bytes 786440 | tf_op jit(solution)/shard_map/ppermute | solution.py:547
  14.1 36.2 %collective-permute-start.3 = (bf16[256,512]{1,0:T(8,128)(2,1)S(1)}, bf16[256,512]{1,0:T(8,128)(2,1)S(1)}, u32[]{:S(2)}, u32[]{:S(2)}) collective-permute-start(bf16[256,512]{1,0:T(8,128)(2,1)S(1)} %collective-permute-done.refs_1_), channel_id=1, source_target_pairs={{0,16},{4,20},{8,24},{12,28},{16,0},{20,4},{24,8},{28,12},{1,17},{... | collective-permute-start | bytes 786440 | tf_op jit(solution)/shard_map/ppermute | solution.py:547
  17.9 37.5 %collective-permute-start.1 = (bf16[512,512]{1,0:T(8,128)(2,1)S(1)}, bf16[512,512]{1,0:T(8,128)(2,1)S(1)}, u32[]{:S(2)}, u32[]{:S(2)}) collective-permute-start(bf16[512,512]{1,0:T(8,128)(2,1)S(1)} %join.4.refs_0_), channel_id=1, source_target_pairs={{0,8},{4,12},{8,0},{12,4},{16,24},{20,28},{24,16},{28,20},{1,9},{5... | collective-permute-start | bytes 1572872 | tf_op jit(solution)/shard_map/ppermute | solution.py:547
  50.3 12.9 %collective-permute-start.6 = (bf16[512,512]{1,0:T(8,128)(2,1)S(1)}, bf16[512,512]{1,0:T(8,128)(2,1)S(1)}, u32[]{:S(2)}, u32[]{:S(2)}) collective-permute-start(bf16[512,512]{1,0:T(8,128)(2,1)S(1)} %join.5.refs_0_.refs_2_), channel_id=1, source_target_pairs={{0,8},{4,12},{8,0},{12,4},{16,24},{20,28},{24,16},{28,20},{1,9},{5... | collective-permute-start | bytes 1572872 | tf_op jit(solution)/shard_map/ppermute | solution.py:547
  51.0 25.6 %collective-permute-start.7 = (bf16[512,512]{1,0:T(8,128)(2,1)S(1)}, bf16[512,512]{1,0:T(8,128)(2,1)S(1)}, u32[]{:S(2)}, u32[]{:S(2)}) collective-permute-start(bf16[512,512]{1,0:T(8,128)(2,1)S(1)} %join.4.refs_0_), channel_id=1, source_target_pairs={{0,2},{1,3},{2,0},{3,1},{4,6},{5,7},{6,4},{7,5},{8,10},{9,11},{10,... | collective-permute-start | bytes 1572872 | tf_op jit(solution)/shard_map/ppermute | solution.py:547
  52.5 21.8 %collective-permute-start.11 = (bf16[768,256]{1,0:T(8,128)(2,1)S(1)}, bf16[768,256]{1,0:T(8,128)(2,1)S(1)}, u32[]{:S(2)}, u32[]{:S(2)}) collective-permute-start(bf16[768,256]{1,0:T(8,128)(2,1)S(1)} %copy-done.27), channel_id=1, source_target_pairs={{0,24},{4,28},{8,16},{12,20},{16,8},{20,12},{24,0},{28,4},{1,25},{... | collective-permute-start | bytes 1179656 | tf_op jit(solution)/shard_map/ppermute | solution.py:547
  55.4 23.6 %collective-permute-start.8 = (bf16[512,512]{1,0:T(8,128)(2,1)S(1)}, bf16[512,512]{1,0:T(8,128)(2,1)S(1)}, u32[]{:S(2)}, u32[]{:S(2)}) collective-permute-start(bf16[512,512]{1,0:T(8,128)(2,1)S(1)} %collective-permute-done.1.refs_2_.refs_1_), channel_id=1, source_target_pairs={{0,2},{1,3},{2,0},{3,1},{4,6},{5,7},{6,4},{7,5},{8,10},{9,11},{10,... | collective-permute-start | bytes 1572872 | tf_op jit(solution)/shard_map/ppermute | solution.py:547
  55.9 32.4 %collective-permute-start.9 = (bf16[512,512]{1,0:T(8,128)(2,1)S(1)}, bf16[512,512]{1,0:T(8,128)(2,1)S(1)}, u32[]{:S(2)}, u32[]{:S(2)}) collective-permute-start(bf16[512,512]{1,0:T(8,128)(2,1)S(1)} %join.5.refs_0_.refs_2_), channel_id=1, source_target_pairs={{0,2},{1,3},{2,0},{3,1},{4,6},{5,7},{6,4},{7,5},{8,10},{9,11},{10,... | collective-permute-start | bytes 1572872 | tf_op jit(solution)/shard_map/ppermute | solution.py:547
  63.3 35.0 %collective-permute-start.10 = (bf16[512,512]{1,0:T(8,128)(2,1)S(1)}, bf16[512,512]{1,0:T(8,128)(2,1)S(1)}, u32[]{:S(2)}, u32[]{:S(2)}) collective-permute-start(bf16[512,512]{1,0:T(8,128)(2,1)S(1)} %collective-permute-done.6.refs_2_.refs_1_.refs_3_), channel_id=1, source_target_pairs={{0,2},{1,3},{2,0},{3,1},{4,6},{5,7},{6,4},{7,5},{8,10},{9,11},{10,... | collective-permute-start | bytes 1572872 | tf_op jit(solution)/shard_map/ppermute | solution.py:547
  74.3 14.0 %collective-permute-start.13 = (bf16[512,256]{1,0:T(8,128)(2,1)S(1)}, bf16[512,256]{1,0:T(8,128)(2,1)S(1)}, u32[]{:S(2)}, u32[]{:S(2)}) collective-permute-start(bf16[512,256]{1,0:T(8,128)(2,1)S(1)} %get-tuple-element.41), channel_id=1, source_target_pairs={{0,16},{4,20},{8,24},{12,28},{16,0},{20,4},{24,8},{28,12},{1,17},{... | collective-permute-start | bytes 786440 | tf_op jit(solution)/shard_map/ppermute | solution.py:547
  76.5 11.7 %collective-permute-start.14 = (bf16[512,256]{1,0:T(8,128)(2,1)S(1)}, bf16[512,256]{1,0:T(8,128)(2,1)S(1)}, u32[]{:S(2)}, u32[]{:S(2)}) collective-permute-start(bf16[512,256]{1,0:T(8,128)(2,1)S(1)} %get-tuple-element.42), channel_id=1, source_target_pairs={{0,8},{4,12},{8,0},{12,4},{16,24},{20,28},{24,16},{28,20},{1,9},{5... | collective-permute-start | bytes 786440 | tf_op jit(solution)/shard_map/ppermute | solution.py:547
  79.2 24.6 %collective-permute-start.12 = (bf16[2048,512]{1,0:T(8,128)(2,1)S(1)}, bf16[2048,512]{1,0:T(8,128)(2,1)S(1)}, u32[]{:S(2)}, u32[]{:S(2)}) collective-permute-start(bf16[2048,512]{1,0:T(8,128)(2,1)S(1)} %join.6), channel_id=1, source_target_pairs={{0,1},{1,0},{2,3},{3,2},{4,5},{5,4},{6,7},{7,6},{8,9},{9,8},{10,11... | collective-permute-start | bytes 6291464 | tf_op jit(solution)/shard_map/ppermute | solution.py:547
  98.4 8.6 %collective-permute-start.15 = (bf16[2048,512]{1,0:T(8,128)(2,1)S(1)}, bf16[2048,512]{1,0:T(8,128)(2,1)S(1)}, u32[]{:S(2)}, u32[]{:S(2)}) collective-permute-start(bf16[2048,512]{1,0:T(8,128)(2,1)S(1)} %join.7), channel_id=1, source_target_pairs={{0,1},{1,0},{2,3},{3,2},{4,5},{5,4},{6,7},{7,6},{8,9},{9,8},{10,11... | collective-permute-start | bytes 6291464 | tf_op jit(solution)/shard_map/ppermute | solution.py:547
  98.5 13.1 %collective-permute-start.21 = (bf16[512,256]{1,0:T(8,128)(2,1)S(1)}, bf16[512,256]{1,0:T(8,128)(2,1)S(1)}, u32[]{:S(2)}, u32[]{:S(2)}) collective-permute-start(bf16[512,256]{1,0:T(8,128)(2,1)S(1)} %get-tuple-element.53), channel_id=1, source_target_pairs={{0,24},{4,28},{8,16},{12,20},{16,8},{20,12},{24,0},{28,4},{1,25},{... | collective-permute-start | bytes 786440 | tf_op jit(solution)/shard_map/ppermute | solution.py:547
  102.5 15.3 %collective-permute-start.16 = (bf16[512,256]{1,0:T(8,128)(2,1)S(1)}, bf16[512,256]{1,0:T(8,128)(2,1)S(1)}, u32[]{:S(2)}, u32[]{:S(2)}) collective-permute-start(bf16[512,256]{1,0:T(8,128)(2,1)S(1)} %get-tuple-element.44), channel_id=1, source_target_pairs={{0,8},{4,12},{8,0},{12,4},{16,24},{20,28},{24,16},{28,20},{1,9},{5... | collective-permute-start | bytes 786440 | tf_op jit(solution)/shard_map/ppermute | solution.py:547
  103.3 28.2 %collective-permute-start.17 = (bf16[512,256]{1,0:T(8,128)(2,1)S(1)}, bf16[512,256]{1,0:T(8,128)(2,1)S(1)}, u32[]{:S(2)}, u32[]{:S(2)}) collective-permute-start(bf16[512,256]{1,0:T(8,128)(2,1)S(1)} %get-tuple-element.45), channel_id=1, source_target_pairs={{0,16},{4,20},{8,24},{12,28},{16,0},{20,4},{24,8},{28,12},{1,17},{... | collective-permute-start | bytes 786440 | tf_op jit(solution)/shard_map/ppermute | solution.py:547
  103.8 27.7 %collective-permute-start.18 = (bf16[512,256]{1,0:T(8,128)(2,1)S(1)}, bf16[512,256]{1,0:T(8,128)(2,1)S(1)}, u32[]{:S(2)}, u32[]{:S(2)}) collective-permute-start(bf16[512,256]{1,0:T(8,128)(2,1)S(1)} %get-tuple-element.46), channel_id=1, source_target_pairs={{0,24},{4,28},{8,16},{12,20},{16,8},{20,12},{24,0},{28,4},{1,25},{... | collective-permute-start | bytes 786440 | tf_op jit(solution)/shard_map/ppermute | solution.py:547
  111.0 26.7 %collective-permute-start.20 = (bf16[3072,128]{1,0:T(8,128)(2,1)}, bf16[3072,128]{1,0:T(8,128)(2,1)S(1)}, u32[]{:S(2)}, u32[]{:S(2)}) collective-permute-start(bf16[3072,128]{1,0:T(8,128)(2,1)} %get-tuple-element.51), channel_id=1, source_target_pairs={{0,4},{4,0},{8,12},{12,8},{16,20},{20,16},{24,28},{28,24},{1,5},{5... | collective-permute-start | bytes 2359304 | tf_op jit(solution)/shard_map/ppermute | solution.py:547
  116.4 26.6 %collective-permute-start.22 = (bf16[2048,128]{1,0:T(8,128)(2,1)}, bf16[2048,128]{1,0:T(8,128)(2,1)S(1)}, u32[]{:S(2)}, u32[]{:S(2)}) collective-permute-start(bf16[2048,128]{1,0:T(8,128)(2,1)} %get-tuple-element.55), channel_id=1, source_target_pairs={{0,4},{4,0},{8,12},{12,8},{16,20},{20,16},{24,28},{28,24},{1,5},{5... | collective-permute-start | bytes 1572872 | tf_op jit(solution)/shard_map/ppermute | solution.py:547
  136.4 25.2 %collective-permute-start.19 = (bf16[2048,128]{1,0:T(8,128)(2,1)}, bf16[2048,128]{1,0:T(8,128)(2,1)}, u32[]{:S(2)}, u32[]{:S(2)}) collective-permute-start(bf16[2048,128]{1,0:T(8,128)(2,1)} %get-tuple-element.48.refs_2_), channel_id=1, source_target_pairs={{0,4},{4,0},{8,12},{12,8},{16,20},{20,16},{24,28},{28,24},{1,5},{5... | collective-permute-start | bytes 1572872 | tf_op jit(solution)/shard_map/ppermute | solution.py:547
  163.7 6.4 %collective-permute-start.23 = (bf16[256,128]{1,0:T(8,128)(2,1)S(1)}, bf16[256,128]{1,0:T(8,128)(2,1)S(1)}, u32[]{:S(2)}, u32[]{:S(2)}) collective-permute-start(bf16[256,128]{1,0:T(8,128)(2,1)S(1)} %get-tuple-element.58), channel_id=1, source_target_pairs={{0,4},{4,0},{8,12},{12,8},{16,20},{20,16},{24,28},{28,24},{1,5},{5... | collective-permute-start | bytes 196616 | tf_op jit(solution)/shard_map/ppermute | solution.py:547
  164.3 8.2 %collective-permute-start.24 = (bf16[256,128]{1,0:T(8,128)(2,1)S(1)}, bf16[256,128]{1,0:T(8,128)(2,1)S(1)}, u32[]{:S(2)}, u32[]{:S(2)}) collective-permute-start(bf16[256,128]{1,0:T(8,128)(2,1)S(1)} %get-tuple-element.59), channel_id=1, source_target_pairs={{0,8},{4,12},{8,0},{12,4},{16,24},{20,28},{24,16},{28,20},{1,9},{5... | collective-permute-start | bytes 196616 | tf_op jit(solution)/shard_map/ppermute | solution.py:547
  166.0 8.9 %collective-permute-start.25 = (bf16[256,128]{1,0:T(8,128)(2,1)S(1)}, bf16[256,128]{1,0:T(8,128)(2,1)S(1)}, u32[]{:S(2)}, u32[]{:S(2)}) collective-permute-start(bf16[256,128]{1,0:T(8,128)(2,1)S(1)} %get-tuple-element.60), channel_id=1, source_target_pairs={{0,12},{4,8},{8,4},{12,0},{16,28},{20,24},{24,20},{28,16},{1,13},{... | collective-permute-start | bytes 196616 | tf_op jit(solution)/shard_map/ppermute | solution.py:547
  167.2 10.0 %collective-permute-start.26 = (bf16[256,128]{1,0:T(8,128)(2,1)S(1)}, bf16[256,128]{1,0:T(8,128)(2,1)S(1)}, u32[]{:S(2)}, u32[]{:S(2)}) collective-permute-start(bf16[256,128]{1,0:T(8,128)(2,1)S(1)} %get-tuple-element.61), channel_id=1, source_target_pairs={{0,16},{4,20},{8,24},{12,28},{16,0},{20,4},{24,8},{28,12},{1,17},{... | collective-permute-start | bytes 196616 | tf_op jit(solution)/shard_map/ppermute | solution.py:547
  169.2 9.6 %collective-permute-start.27 = (bf16[256,128]{1,0:T(8,128)(2,1)S(1)}, bf16[256,128]{1,0:T(8,128)(2,1)S(1)}, u32[]{:S(2)}, u32[]{:S(2)}) collective-permute-start(bf16[256,128]{1,0:T(8,128)(2,1)S(1)} %get-tuple-element.62), channel_id=1, source_target_pairs={{0,20},{4,16},{8,28},{12,24},{16,4},{20,0},{24,12},{28,8},{1,21},{... | collective-permute-start | bytes 196616 | tf_op jit(solution)/shard_map/ppermute | solution.py:547
  170.1 8.6 %collective-permute-start.28 = (bf16[256,128]{1,0:T(8,128)(2,1)S(1)}, bf16[256,128]{1,0:T(8,128)(2,1)S(1)}, u32[]{:S(2)}, u32[]{:S(2)}) collective-permute-start(bf16[256,128]{1,0:T(8,128)(2,1)S(1)} %get-tuple-element.63), channel_id=1, source_target_pairs={{0,24},{4,28},{8,16},{12,20},{16,8},{20,12},{24,0},{28,4},{1,25},{... | collective-permute-start | bytes 196616 | tf_op jit(solution)/shard_map/ppermute | solution.py:547
  172.5 7.1 %collective-permute-start.29 = (bf16[256,128]{1,0:T(8,128)(2,1)S(1)}, bf16[256,128]{1,0:T(8,128)(2,1)S(1)}, u32[]{:S(2)}, u32[]{:S(2)}) collective-permute-start(bf16[256,128]{1,0:T(8,128)(2,1)S(1)} %get-tuple-element.64), channel_id=1, source_target_pairs={{0,28},{4,24},{8,20},{12,16},{16,12},{20,8},{24,4},{28,0},{1,29},{... | collective-permute-start | bytes 196616 | tf_op jit(solution)/shard_map/ppermute | solution.py:547
  185.1 8.8 %collective-permute-start.30 = (bf16[256,1024]{1,0:T(8,128)(2,1)}, bf16[256,1024]{1,0:T(8,128)(2,1)S(1)}, u32[]{:S(2)}, u32[]{:S(2)}) collective-permute-start(bf16[256,1024]{1,0:T(8,128)(2,1)} %get-tuple-element.65), channel_id=1, source_target_pairs={{0,1},{1,0},{2,3},{3,2},{4,5},{5,4},{6,7},{7,6},{8,9},{9,8},{10,11... | collective-permute-start | bytes 1572872 | tf_op jit(solution)/shard_map/ppermute | solution.py:547
  192.2 14.2 %collective-permute-start.32 = (bf16[256,1024]{1,0:T(8,128)(2,1)}, bf16[256,1024]{1,0:T(8,128)(2,1)S(1)}, u32[]{:S(2)}, u32[]{:S(2)}) collective-permute-start(bf16[256,1024]{1,0:T(8,128)(2,1)} %emit.5), channel_id=1, source_target_pairs={{0,2},{1,3},{2,0},{3,1},{4,6},{5,7},{6,4},{7,5},{8,10},{9,11},{10,... | collective-permute-start | bytes 1572872 | tf_op jit(solution)/shard_map/ppermute | solution.py:547
  (29 other events, 411.4 us)

commit v4 on v3

v4 whole, which is shorter than its diff:
```python
import functools
import math

import jax
import jax.numpy as jnp
import numpy as np
from jax import lax
from jax.experimental import pallas as pl
from jax.experimental.pallas import tpu as pltpu
from jax.sharding import PartitionSpec as P

exact_prec = lax.Precision.HIGHEST
inner_len = 64


def dft_tables(half_len, blocks):
    full_len = 2 * half_len
    full_size = full_len * blocks
    half_index = jnp.arange(half_len, dtype=jnp.int32)
    full_index = jnp.arange(full_len, dtype=jnp.int32)
    block_index = jnp.arange(blocks, dtype=jnp.int32)
    outer_angle = (half_index[:, None] * full_index[None, :] % full_len).astype(jnp.float32) * (
        2.0 * math.pi / full_len
    )
    inner_angle = (block_index[:, None] * block_index[None, :] % blocks).astype(jnp.float32) * (
        2.0 * math.pi / blocks
    )
    twist_angle = (full_index[:, None] * block_index[None, :] % full_size).astype(jnp.float32) * (
        2.0 * math.pi / full_size
    )
    return (
        jnp.cos(outer_angle),
        jnp.sin(outer_angle),
        jnp.cos(inner_angle),
        jnp.sin(inner_angle),
        jnp.cos(twist_angle),
        jnp.sin(twist_angle),
    )


def forward_dft(signal, tables):
    outer_cos, outer_sin, inner_cos, inner_sin, twist_cos, twist_sin = tables
    real_section = jnp.einsum("cmn,mk->ckn", signal, outer_cos, precision=exact_prec)
    imag_section = -jnp.einsum("cmn,mk->ckn", signal, outer_sin, precision=exact_prec)
    real_twist = real_section * twist_cos + imag_section * twist_sin
    imag_twist = imag_section * twist_cos - real_section * twist_sin
    real_freq = jnp.einsum("ckn,nj->ckj", real_twist, inner_cos, precision=exact_prec) + jnp.einsum(
        "ckn,nj->ckj", imag_twist, inner_sin, precision=exact_prec
    )
    imag_freq = jnp.einsum("ckn,nj->ckj", imag_twist, inner_cos, precision=exact_prec) - jnp.einsum(
        "ckn,nj->ckj", real_twist, inner_sin, precision=exact_prec
    )
    return (real_freq, imag_freq)


def inverse_real(spectrum_real, spectrum_imag, tables):
    outer_cos, outer_sin, inner_cos, inner_sin, twist_cos, twist_sin = tables
    full_size = outer_cos.shape[1] * inner_cos.shape[0]
    back_real = jnp.einsum(
        "ckj,jn->ckn", spectrum_real, inner_cos, precision=exact_prec
    ) - jnp.einsum("ckj,jn->ckn", spectrum_imag, inner_sin, precision=exact_prec)
    back_imag = jnp.einsum(
        "ckj,jn->ckn", spectrum_imag, inner_cos, precision=exact_prec
    ) + jnp.einsum("ckj,jn->ckn", spectrum_real, inner_sin, precision=exact_prec)
    turn_real = back_real * twist_cos - back_imag * twist_sin
    turn_imag = back_imag * twist_cos + back_real * twist_sin
    summed_real = jnp.einsum(
        "ckn,mk->cmn", turn_real, outer_cos, precision=exact_prec
    ) - jnp.einsum("ckn,mk->cmn", turn_imag, outer_sin, precision=exact_prec)
    return summed_real / full_size


def causal_conv(signal, kernel, blocks):
    channels, length = signal.shape
    half_len = length // blocks
    tables = dft_tables(half_len, blocks)
    stacked = jnp.concatenate([signal, kernel], 0).reshape(2 * channels, half_len, blocks)
    real_freq, imag_freq = forward_dft(stacked, tables)
    data_real, filter_real = (real_freq[:channels], real_freq[channels:])
    data_imag, filter_imag = (imag_freq[:channels], imag_freq[channels:])
    spectrum_real = data_real * filter_real - data_imag * filter_imag
    spectrum_imag = data_real * filter_imag + data_imag * filter_real
    return inverse_real(spectrum_real, spectrum_imag, tables).reshape(channels, length)


def body(tokens, in_weight, short_taps, skip_gain, long_filter, out_weight):
    row_count, chan_width = tokens.shape
    blocks = lax.axis_size("seq")
    part_width = chan_width // blocks
    flat_weight = in_weight.reshape(in_weight.shape[0], 3 * chan_width)
    whole = lax.all_gather(tokens, "chan", axis=1, tiled=True)
    projected = jnp.dot(
        whole,
        lax.all_gather(flat_weight, "seq", axis=0, tiled=True),
        preferred_element_type=jnp.float32,
    )
    projected = projected.astype(jnp.bfloat16).reshape(row_count, 3, chan_width)
    outgoing = jnp.transpose(projected, (1, 2, 0))
    filter_rows = jnp.transpose(long_filter)[None]
    channel_major, filter_major = (
        lax.all_to_all(outgoing, "seq", split_axis=1, concat_axis=2, tiled=True),
        lax.all_to_all(filter_rows, "seq", split_axis=1, concat_axis=2, tiled=True),
    )
    offset = lax.axis_index("seq") * part_width
    local_taps = lax.dynamic_slice_in_dim(short_taps, offset, part_width, 2)
    local_skip = lax.dynamic_slice_in_dim(skip_gain, offset, part_width, 0)
    values = channel_major.astype(jnp.float32)
    tap_count = short_taps.shape[1]
    length = values.shape[2]
    padded = jnp.pad(values, ((0, 0), (0, 0), (tap_count - 1, 0)))
    smoothed = jnp.zeros_like(values)
    for tap_index in range(tap_count):
        lag_start = tap_count - 1 - tap_index
        smoothed = (
            smoothed
            + local_taps[:, tap_index, :, None] * padded[:, :, lag_start : lag_start + length]
        )
    gate_query = smoothed[0]
    gated = smoothed[1] * smoothed[2]
    mixed_seq = (
        causal_conv(gated, filter_major[0].astype(jnp.float32), blocks)
        + local_skip[:, None] * gated
    )
    product = (mixed_seq * gate_query).astype(jnp.bfloat16)
    returned = lax.all_to_all(product, "seq", split_axis=1, concat_axis=0, tiled=True)
    summed = lax.psum_scatter(
        lax.dot_general(
            out_weight, returned, (((0,), (0,)), ((), ())), preferred_element_type=jnp.float32
        ).astype(jnp.bfloat16),
        "chan",
        scatter_dimension=0,
        tiled=True,
    ).astype(jnp.float32)
    return jnp.transpose(summed).astype(jnp.bfloat16)


def wave_tables(length):
    span = 2 * length
    outer = span // inner_len
    used, rows = outer // 2, outer // 2 + 1
    padded_rows = -(-rows // 8) * 8
    m, k = np.arange(used), np.arange(rows)
    n, j = np.arange(inner_len), np.arange(inner_len)
    angle = (2.0 * math.pi / outer) * (np.outer(k, m) % outer)
    ahead = np.zeros((2, padded_rows, used))
    ahead[0, :rows], ahead[1, :rows] = np.cos(angle), -np.sin(angle)
    weight = np.where((k == 0) | (k == used), 1.0, 2.0) / span
    back = np.zeros((used, 2, padded_rows))
    back[:, 0, :rows] = (np.cos(angle) * weight[:, None]).T
    back[:, 1, :rows] = (-np.sin(angle) * weight[:, None]).T
    turn = n[None, None, :] * (k[:, None, None] + outer * j[None, :, None]) % span
    cos, sin = np.cos(turn * (2.0 * math.pi / span)), np.sin(turn * (2.0 * math.pi / span))
    middle = np.concatenate(
        [np.concatenate([cos, sin], 2), np.concatenate([-sin, cos], 2)], 1
    )
    return tuple(
        jnp.asarray(table, jnp.bfloat16)
        for table in (
            ahead.reshape(2 * padded_rows, used),
            middle,
            np.swapaxes(middle, 1, 2),
            back.reshape(used, 2 * padded_rows),
        )
    )


def halve_kernel(
    where_ref, tokens, filters, weight, theirs, ours, filter_theirs, *refs, turns, index
):
    pieces, sems = refs[:-1], refs[-1]
    depth, side = where_ref[0] // 2, where_ref[0] % 2
    half = ours.shape[1]
    part = half // 4
    copies = []

    def copy(source, block, width, target):
        columns = pl.ds(pl.multiple_of(block * width, width), width)
        copies.append(
            pltpu.make_async_copy(source.at[:, columns], target, sems.at[len(copies)])
        )

    copy(tokens, side, half, ours)
    copy(tokens, 1 - side, half, theirs)
    for i in range(4):
        copy(filters, 2 * i + 1 - side, part, filter_theirs.at[:, pl.ds(i * part, part)])
    for turn, piece in zip(turns, pieces, strict=True):
        copy(weight.at[index], jnp.bitwise_xor(depth, turn), piece.shape[1], piece)
    for one in copies:
        one.start()
    for one in copies:
        one.wait()


def halve(where, tokens, filters, weight, turns, index):
    shapes = []
    for value in (tokens, tokens, filters):
        shapes.append(jax.ShapeDtypeStruct((value.shape[0], value.shape[1] // 2), value.dtype))
    shapes += [jax.ShapeDtypeStruct((weight.shape[1], weight.shape[2] // 4), weight.dtype)] * len(
        turns
    )
    return pl.pallas_call(
        functools.partial(halve_kernel, turns=turns, index=index),
        out_shape=tuple(shapes),
        in_specs=[pl.BlockSpec(memory_space=pltpu.SMEM)]
        + [pl.BlockSpec(memory_space=pl.ANY)] * 3,
        out_specs=(pl.BlockSpec(memory_space=pltpu.VMEM),) * len(shapes),
        scratch_shapes=[pltpu.SemaphoreType.DMA((6 + len(turns),))],
        compiler_params=pltpu.CompilerParams(vmem_limit_bytes=61 * 2**20),
        name="halve",
    )(where, tokens, filters, weight)


def cut_kernel(where_ref, weight, filters, filter_beside, *refs, plan, after):
    place = where_ref[0]
    depth, side = place // 2, place % 2
    outs, sems = refs[after:-1], refs[-1]
    copies = []

    def copy(source, target):
        copies.append(pltpu.make_async_copy(source, target, sems.at[len(copies)]))

    def columns_of(block, width):
        return pl.ds(pl.multiple_of(block * width, width), width)

    rows, width = weight.shape[1], outs[0].shape[1]
    half = width // 2
    for out, (turn, names) in zip(outs, plan, strict=True):
        block = jnp.bitwise_xor(depth, turn)
        low = 0
        for name in names:
            if name == "f":
                at = pl.ds(low, filters.shape[0])
                here = columns_of(2 * block + side, half)
                copy(filters.at[:, here], out.at[at, pl.ds(0, half)])
                there = columns_of(block, half)
                copy(filter_beside.at[:, there], out.at[at, pl.ds(half, half)])
                low += filters.shape[0]
            else:
                source = weight.at[name, :, columns_of(block, width)]
                copy(source, out.at[pl.ds(low, rows), :])
                low += rows
    for one in copies:
        one.start()
    for one in copies:
        one.wait()


def cut(where, weight, filters, filter_beside, plan, after):
    count_of = {"f": filters.shape[0]}
    shapes = []
    for _, names in plan:
        rows = sum(count_of.get(name, weight.shape[1]) for name in names)
        shapes.append(jax.ShapeDtypeStruct((rows, weight.shape[2] // 4), weight.dtype))
    return pl.pallas_call(
        functools.partial(cut_kernel, plan=plan, after=len(after)),
        out_shape=tuple(shapes),
        in_specs=[pl.BlockSpec(memory_space=pltpu.SMEM)]
        + [pl.BlockSpec(memory_space=pl.ANY)] * (3 + len(after)),
        out_specs=(pl.BlockSpec(memory_space=pltpu.VMEM),) * len(shapes),
        scratch_shapes=[pltpu.SemaphoreType.DMA((24,))],
        compiler_params=pltpu.CompilerParams(vmem_limit_bytes=8 * 2**20),
        name="cut",
    )(where, weight, filters, filter_beside, *after)


def join_kernel(*refs, pieces, outs):
    for out_ref, group in zip(refs[len(refs) - outs :], pieces, strict=True):
        start = 0
        for at, low, count in group:
            out_ref[start : start + count, :] = refs[at][low : low + count, :]
            start += count


def join(values, pieces, after):
    shapes = []
    for group in pieces:
        rows = sum(count for _, _, count in group)
        shapes.append(jax.ShapeDtypeStruct((rows, values[0].shape[1]), values[0].dtype))
    vmem = pl.BlockSpec(memory_space=pltpu.VMEM)
    return pl.pallas_call(
        functools.partial(join_kernel, pieces=pieces, outs=len(pieces)),
        out_shape=tuple(shapes),
        in_specs=[vmem] * len(values) + [pl.BlockSpec(memory_space=pl.ANY)] * len(after),
        out_specs=(vmem,) * len(shapes),
        compiler_params=pltpu.CompilerParams(vmem_limit_bytes=8 * 2**20),
        name="join",
    )(*values, *after)


def project_kernel(where_ref, *refs, lows, after):
    line, across, cores, parts = refs[:4], refs[4:7], refs[7:9], refs[9:13]
    own_ref, send_ref, weights = refs[13 + after :]
    place, chan = where_ref[0], where_ref[1]
    depth, side = place // 2, place % 2
    rows = line[0].shape[1]
    for i in range(4):
        slot = jnp.bitwise_xor(depth, jnp.bitwise_xor(chan, i))
        start = pl.multiple_of(slot * rows, rows)
        weights[pl.ds(start, rows), :] = parts[i][lows[i] : lows[i] + rows, :]
    length, half = own_ref.shape
    block = length // 8
    for step in range(4):
        low = 4 * block * (step % 2)
        both = cores[step // 2]
        beside = across[(0, 1, 1, 2)[step]]
        at = 2 * block if step == 1 else 0
        joined = jnp.concatenate(
            [
                line[step][...],
                both[low : low + 2 * block, :],
                beside[at : at + 2 * block, :],
                both[low + 2 * block : low + 4 * block, :],
            ],
            1,
        )
        total = jnp.dot(joined, weights[...], preferred_element_type=jnp.float32)
        left, right = total[:, :half], total[:, half:]
        own = jnp.where(side == 0, left, right)
        send = jnp.where(side == 0, right, left).astype(jnp.bfloat16)
        for pair in range(2):
            start = pl.multiple_of(jnp.bitwise_xor(place, 2 * step + pair) * block, block)
            own_ref[pl.ds(start, block), :] = own[pair * block : (pair + 1) * block]
            send_ref[pl.ds(start, block), :] = send[pair * block : (pair + 1) * block]


def project(where, line, across, cores, parts, lows, length, after):
    depth, width = line[0].shape[1], parts[0].shape[1]
    vmem = pl.BlockSpec(memory_space=pltpu.VMEM)
    return pl.pallas_call(
        functools.partial(project_kernel, lows=lows, after=len(after)),
        out_shape=(
            jax.ShapeDtypeStruct((length, width // 2), jnp.float32),
            jax.ShapeDtypeStruct((length, width // 2), jnp.bfloat16),
        ),
        in_specs=[pl.BlockSpec(memory_space=pltpu.SMEM)]
        + [vmem] * 13
        + [pl.BlockSpec(memory_space=pl.ANY)] * len(after),
        out_specs=(vmem, vmem),
        scratch_shapes=[pltpu.VMEM((4 * depth, width), jnp.bfloat16)],
        compiler_params=pltpu.CompilerParams(vmem_limit_bytes=12 * 2**20),
        cost_estimate=pl.CostEstimate(
            flops=2 * length * 4 * depth * 2 * width,
            bytes_accessed=2 * length * 4 * depth,
            transcendentals=0,
        ),
        name="project",
    )(where, *line, *across, *cores, *parts, *after)


def smooth_into(padded, own_ref, recv_ref, taps, branch, store):
    length = own_ref.shape[0]
    tap_count = taps.shape[1]
    block = length // 8
    padded[0:8, :] = jnp.zeros((8, padded.shape[1]), jnp.float32)
    for i in range(8):
        rows = slice(i * block, (i + 1) * block)
        padded[8 + i * block : 8 + (i + 1) * block, :] = own_ref[rows, :] + recv_ref[
            rows, :
        ].astype(jnp.float32)
    for i in range(8):
        total = None
        for tap in range(tap_count):
            start = 8 + i * block - tap
            term = taps[branch, tap : tap + 1, :] * padded[start : start + block, :]
            total = term if total is None else total + term
        store(slice(i * block, (i + 1) * block), total)


def ahead_into(signal, table, waves):
    padded_rows, used = table.shape[0] // 2, table.shape[1]
    two = 2 * inner_len
    for n in range(0, inner_len, 2):
        both = jnp.concatenate(
            [signal[pl.ds(n + i, used, stride=inner_len), :] for i in range(2)], 1
        ).astype(jnp.bfloat16)
        wave = jnp.dot(table[...], both, preferred_element_type=jnp.float32)
        width = wave.shape[1] // 2
        for i in range(2):
            part = wave[:, i * width : (i + 1) * width]
            for half in range(2):
                at = pl.ds(half * inner_len + n + i, padded_rows, stride=two)
                waves[at, :] = part[half * padded_rows : (half + 1) * padded_rows]


def unroll_of(rows):
    return 11 if rows % 11 == 0 else 1


def spectrum_kernel(where_ref, ahead, middle, *refs, lows):
    filters, freq_ref, lags, waves = refs[:4], refs[4], refs[5], refs[6]
    place = where_ref[0]
    length, width = lags.shape
    block = length // 8
    rows, two = middle.shape[:2]
    for i in range(4):
        at = slice(lows[i], lows[i] + block)
        for pair in range(2):
            start = pl.multiple_of(jnp.bitwise_xor(place, 2 * i + pair) * block, block)
            piece = filters[i][at, pair * width : (pair + 1) * width]
            lags[pl.ds(start, block), :] = piece.astype(jnp.float32)
    ahead_into(lags, ahead, waves)

    def one(k, _):
        at = pl.ds(pl.multiple_of(k * two, two), two)
        wave = waves[at, :].astype(jnp.bfloat16)
        freq_ref[at, :] = jnp.dot(middle[k], wave, preferred_element_type=jnp.float32)
        return 0

    lax.fori_loop(0, rows, one, 0, unroll=unroll_of(rows))


def spectrum(where, tables, filters, lows, length):
    ahead, middle = tables[:2]
    rows, two = middle.shape[:2]
    width = filters[0].shape[1] // 2
    vmem = pl.BlockSpec(memory_space=pltpu.VMEM)
    return pl.pallas_call(
        functools.partial(spectrum_kernel, lows=lows),
        out_shape=jax.ShapeDtypeStruct((rows * two, width), jnp.float32),
        in_specs=[pl.BlockSpec(memory_space=pltpu.SMEM)] + [vmem] * 6,
        out_specs=vmem,
        scratch_shapes=[
            pltpu.VMEM((length, width), jnp.float32),
            pltpu.VMEM((ahead.shape[0] // 2 * two, width), jnp.float32),
        ],
        compiler_params=pltpu.CompilerParams(vmem_limit_bytes=8 * 2**20),
        cost_estimate=pl.CostEstimate(
            flops=2 * 2 * length * inner_len * width, bytes_accessed=2**20, transcendentals=0
        ),
        name="spectrum",
    )(where, ahead, middle, *filters)


def mix_kernel(
    where_ref,
    own1,
    recv1,
    own2,
    recv2,
    taps_ref,
    skip_ref,
    ahead,
    middle,
    middle_back,
    back,
    freq_ref,
    weight,
    *refs,
    after,
):
    mixed_ref, held_ref, padded, gated, waves, sums, sem = refs[after:]
    loading = pltpu.make_async_copy(weight, held_ref, sem)
    loading.start()
    place = where_ref[0]
    width = own1.shape[1]
    ours = pl.ds(pl.multiple_of(place * width, width), width)
    taps, skip = taps_ref[:, :, ours], skip_ref[:, ours]
    rows, two = middle.shape[0], middle.shape[1]
    padded_rows = ahead.shape[0] // 2
    used = ahead.shape[1]

    def first(at, value):
        gated[at, :] = value

    def second(at, value):
        gated[at, :] = gated[at, :] * value

    smooth_into(padded, own1, recv1, taps, 1, first)
    smooth_into(padded, own2, recv2, taps, 2, second)
    ahead_into(gated, ahead, waves)
    if padded_rows > rows:
        sums[rows * two :, :] = jnp.zeros(((padded_rows - rows) * two, width), jnp.float32)

    def one(k, _):
        at = pl.ds(pl.multiple_of(k * two, two), two)
        wave = waves[at, :].astype(jnp.bfloat16)
        data = jnp.dot(middle[k], wave, preferred_element_type=jnp.float32)
        filters = freq_ref[at, :]
        data_real, filter_real = data[:inner_len], filters[:inner_len]
        data_imag, filter_imag = data[inner_len:], filters[inner_len:]
        product = jnp.concatenate(
            [
                data_real * filter_real - data_imag * filter_imag,
                data_real * filter_imag + data_imag * filter_real,
            ],
            0,
        ).astype(jnp.bfloat16)
        sums[at, :] = jnp.dot(middle_back[k], product, preferred_element_type=jnp.float32)
        return 0

    lax.fori_loop(0, rows, one, 0, unroll=unroll_of(rows))
    for n in range(0, inner_len, 2):
        pieces = [
            jnp.concatenate(
                [
                    sums[pl.ds(n + i, padded_rows, stride=two), :],
                    sums[pl.ds(inner_len + n + i, padded_rows, stride=two), :],
                ],
                0,
            )
            for i in range(2)
        ]
        wave = jnp.dot(
            back[...],
            jnp.concatenate(pieces, 1).astype(jnp.bfloat16),
            preferred_element_type=jnp.float32,
        )
        for i in range(2):
            at = pl.ds(n + i, used, stride=inner_len)
            mixed_ref[at, :] = wave[:, i * width : (i + 1) * width] + skip * gated[at, :]
    loading.wait()


def mix(where, own1, recv1, own2, recv2, taps, skip, tables, freq, weight, after):
    length, width = own1.shape
    two = tables[1].shape[1]
    padded_rows = tables[0].shape[0] // 2
    vmem = pl.BlockSpec(memory_space=pltpu.VMEM)
    return pl.pallas_call(
        functools.partial(mix_kernel, after=len(after)),
        out_shape=(
            jax.ShapeDtypeStruct((length, width), jnp.float32),
            jax.ShapeDtypeStruct(weight.shape, weight.dtype),
        ),
        in_specs=[pl.BlockSpec(memory_space=pltpu.SMEM)]
        + [vmem] * 11
        + [pl.BlockSpec(memory_space=pl.ANY)] * (1 + len(after)),
        out_specs=(vmem, vmem),
        scratch_shapes=[
            pltpu.VMEM((length + 8, width), jnp.float32),
            pltpu.VMEM((length, width), jnp.float32),
            pltpu.VMEM((padded_rows * two, width), jnp.float32),
            pltpu.VMEM((padded_rows * two, width), jnp.float32),
            pltpu.SemaphoreType.DMA,
        ],
        compiler_params=pltpu.CompilerParams(vmem_limit_bytes=16 * 2**20),
        cost_estimate=pl.CostEstimate(
            flops=2 * 6 * length * inner_len * width, bytes_accessed=6 * 2**20, transcendentals=0
        ),
        name="mix",
    )(where, own1, recv1, own2, recv2, taps, skip, *tables, freq, weight, *after)


def gate_kernel(where_ref, own0, recv0, mixed_ref, taps_ref, *refs):
    outs, padded, product = refs[:8], refs[8], refs[9]
    place = where_ref[0]
    block, width = own0.shape[0] // 8, own0.shape[1]
    taps = taps_ref[:, :, pl.ds(pl.multiple_of(place * width, width), width)]

    def store(at, value):
        product[at, :] = (mixed_ref[at, :] * value).astype(jnp.bfloat16)

    smooth_into(padded, own0, recv0, taps, 0, store)
    for i in range(8):
        start = pl.multiple_of(jnp.bitwise_xor(place, i) * block, block)
        outs[i][...] = product[pl.ds(start, block), :]


def gate(where, own0, recv0, mixed, taps):
    length, width = own0.shape
    vmem = pl.BlockSpec(memory_space=pltpu.VMEM)
    return pl.pallas_call(
        gate_kernel,
        out_shape=(jax.ShapeDtypeStruct((length // 8, width), jnp.bfloat16),) * 8,
        in_specs=[pl.BlockSpec(memory_space=pltpu.SMEM)] + [vmem] * 4,
        out_specs=(vmem,) * 8,
        scratch_shapes=[
            pltpu.VMEM((length + 8, width), jnp.float32),
            pltpu.VMEM((length, width), jnp.bfloat16),
        ],
        compiler_params=pltpu.CompilerParams(vmem_limit_bytes=8 * 2**20),
        cost_estimate=pl.CostEstimate(
            flops=8 * length * width, bytes_accessed=12 * length * width, transcendentals=0
        ),
        name="gate",
    )(where, own0, recv0, mixed, taps)


def emit_kernel(where_ref, weight, *refs, turns, added):
    parts, extra = refs[:8], refs[8 : 8 + added]
    outs, joined = refs[8 + added : -1], refs[-1]
    place, chan = where_ref[0], where_ref[1]
    width = parts[0].shape[1]
    columns = outs[0].shape[1]
    tile = 256
    for i in range(8):
        start = pl.multiple_of(jnp.bitwise_xor(place, i) * width, width)
        joined[:, pl.ds(start, width)] = parts[i][...]
    for i, turn in enumerate(turns):
        for low in range(0, columns, tile):
            start = pl.multiple_of(jnp.bitwise_xor(chan, turn) * columns + low, tile)
            total = jnp.dot(
                joined[...], weight[:, pl.ds(start, tile)], preferred_element_type=jnp.float32
            )
            if added:
                total = total + extra[i][:, low : low + tile].astype(jnp.float32)
            outs[i][:, low : low + tile] = total.astype(outs[i].dtype)


def emit(where, parts, weight, turns, extra, out_dtype):
    rows, width = parts[0].shape
    columns = weight.shape[1] // 4
    vmem = pl.BlockSpec(memory_space=pltpu.VMEM)
    shape = jax.ShapeDtypeStruct((rows, columns), out_dtype)
    return pl.pallas_call(
        functools.partial(emit_kernel, turns=turns, added=len(extra)),
        out_shape=(shape,) * len(turns),
        in_specs=[pl.BlockSpec(memory_space=pltpu.SMEM)] + [vmem] * (9 + len(extra)),
        out_specs=(vmem,) * len(turns),
        scratch_shapes=[pltpu.VMEM((rows, 8 * width), jnp.bfloat16)],
        compiler_params=pltpu.CompilerParams(vmem_limit_bytes=8 * 2**20),
        cost_estimate=pl.CostEstimate(
            flops=2 * rows * weight.shape[0] * columns * len(turns),
            bytes_accessed=2 * weight.shape[0] * columns * len(turns),
            transcendentals=0,
        ),
        name="emit",
    )(where, weight, *parts, *extra)


def swap(value, axis, count, turn):
    return lax.ppermute(value, axis, [(i, i ^ turn) for i in range(count)])


def fast_body(tokens, in_weight, short_taps, skip_gain, long_filter, out_weight):
    seq, chans = lax.axis_size("seq"), lax.axis_size("chan")
    place, chan = lax.axis_index("seq"), lax.axis_index("chan")
    rows, width = tokens.shape
    length = rows * seq
    part = width // seq
    where = jnp.stack([place, chan]).astype(jnp.int32)

    weight = jnp.transpose(in_weight, (1, 0, 2))

    lags = tokens.shape[0]
    rows = in_weight.shape[0]

    theirs, ours, filter_theirs, cut1_1, cut1_2 = halve(
        where, tokens, long_filter, weight, (1, 2), 1
    )
    far_ours = swap(ours, "seq", seq, 4)
    beside = swap(theirs, "seq", seq, 1)
    w1_1 = swap(cut1_1, "seq", seq, 2)
    filter_beside = swap(filter_theirs, "seq", seq, 1)
    (pair,) = join([ours, beside], [[(0, 0, lags), (1, 0, lags)]], [far_ours, w1_1])
    far_beside = swap(beside, "seq", seq, 4)
    near = swap(pair, "seq", seq, 2)
    pair_across = swap(pair, "chan", chans, 2)
    w1_2 = swap(cut1_2, "seq", seq, 4)
    plan = [(0, (1, 2, "f", 0)), (3, (1, 2, "f")), (2, (2, "f")), (1, (2, "f"))]
    inputs = (where, weight, long_filter, filter_beside)
    w_0, cut12_3, cut2_2, cut2_1 = cut(*inputs, plan, [pair])
    whole = [(0, 0, lags), (1, 0, lags)]
    far, far_and_near = join(
        [far_ours, far_beside, near],
        [whole, whole + [(2, 0, 2 * lags)]],
        [pair_across, w1_2, cut12_3],
    )
    w12_3 = swap(cut12_3, "seq", seq, 6)
    w2_1 = swap(cut2_1, "seq", seq, 2)
    w2_2 = swap(cut2_2, "seq", seq, 4)
    far_near = swap(far, "seq", seq, 2)
    across = swap(far_and_near, "chan", chans, 2)
    every = [(0, 0, 2 * lags), (1, 0, 2 * lags)]
    (first,) = join(
        [pair, pair_across, near, across],
        [every + [(2, 0, 2 * lags), (3, 2 * lags, 2 * lags)]],
        [],
    )
    core_a = swap(first, "chan", chans, 1)
    far_near_across = swap(far_near, "chan", chans, 2)
    (second,) = join(
        [far, across, far_near, far_near_across],
        [every + [(2, 0, 2 * lags), (3, 0, 2 * lags)]],
        [w12_3, w2_1, w2_2],
    )
    core_b = swap(second, "chan", chans, 1)
    line, across = [pair, near, far, far_near], [pair_across, across, far_near_across]
    cores = [core_a, core_b]
    shared = (where, line, across, cores)
    parts1 = [w_0, w1_1, w1_2, w12_3]
    own1, send1 = project(*shared, parts1, (0, 0, 0, 0), length, [])
    recv1 = swap(send1, "seq", seq, 1)
    cut0_2, cut0_3, cut0_1 = cut(*inputs, [(2, (0,)), (3, (0,)), (1, (0,))], [w2_2])
    w0_2, w0_3 = swap(cut0_2, "seq", seq, 4), swap(cut0_3, "seq", seq, 6)
    w0_1 = swap(cut0_1, "seq", seq, 2)
    parts2 = [w_0, w2_1, w2_2, w12_3]
    tables = wave_tables(length)
    freq = spectrum(where, tables, parts2, (2 * rows, rows, rows, 2 * rows), length)
    own2, send2 = project(*shared, parts2, (rows, 0, 0, rows), length, [freq])
    recv2 = swap(send2, "seq", seq, 1)
    lows = (2 * rows + lags, 0, 0, 0)
    own0, send0 = project(*shared, [w_0, w0_1, w0_2, w0_3], lows, length, [])
    recv0 = swap(send0, "seq", seq, 1)
    mixed, held = mix(
        where,
        own1,
        recv1,
        own2,
        recv2,
        short_taps,
        skip_gain[None],
        tables,
        freq,
        out_weight,
        [send0],
    )
    pieces = gate(where, own0, recv0, mixed, short_taps)
    joined = [
        piece if turn == 0 else swap(piece, "seq", seq, turn) for turn, piece in enumerate(pieces)
    ]

    (across_out,) = emit(where, joined, held, (3,), [], jnp.bfloat16)
    from_core = swap(across_out, "chan", chans, 1)
    (beside_out,) = emit(where, joined, held, (1,), [], jnp.bfloat16)
    near_sum = swap(beside_out, "chan", chans, 1)
    (chip_out,) = emit(where, joined, held, (2,), [from_core], jnp.bfloat16)
    from_chip = swap(chip_out, "chan", chans, 2)
    (own,) = emit(where, joined, held, (0,), [near_sum], jnp.float32)
    return (own + from_chip.astype(jnp.float32)).astype(jnp.bfloat16)


def solution(mesh):
    in_specs = (
        P("seq", "chan"),
        P("seq", None, "chan"),
        P(None, None, "chan"),
        P("chan"),
        P("seq", "chan"),
        P("chan", None),
    )
    out_specs = P("seq", "chan")
    seq, chans = mesh.shape["seq"], mesh.shape["chan"]
    chosen = fast_body if seq == 8 and chans == 4 else body
    return jax.shard_map(chosen, mesh=mesh, in_specs=in_specs, out_specs=out_specs, check_vma=False)
```

time: 209 us -> 185 us (0.89)
  Pallas kernels: 47.8 us -> 33.5 us
  waiting for transfers between devices: 98.9 us -> 88.7 us
  starting transfers between devices: 49 us -> 57.8 us
  local copies, waits for them, and re-layouts: 9.95 us -> 2.91 us
    ppermute x33 -> x32, waiting for transfers between devices: 98.9 us -> 88.7 us  [swap(): return lax.ppermute(value, axis, [(i, i ^ turn) for i in range(count)])]
    ppermute x33 -> x32, starting transfers between devices: 49 us -> 57.8 us  [swap(): return lax.ppermute(value, axis, [(i, i ^ turn) for i in range(count)])]
    pallas_call x3 -> x4, Pallas kernels: 13.6 us -> 5.64 us  [emit(): pl.pallas_call(functools.partial(emit_kernel, turns=turns, added=len(extr...]
    pallas_call x1, Pallas kernels: 15.3 us -> 8.65 us  [mix(): pl.pallas_call(functools.partial(mix_kernel, after=len(after)), out_shape...]
    unnamed x56 -> x26, local copies, waits for them, and re-layouts: 9.17 us -> 2.91 us
    pallas_call x10 -> x11, Pallas kernels: 17.5 us -> 18.3 us  [the longest x3 9.06 us: project(): pl.pallas_call(functools.partial(project_kernel, lows=lows, after=len(aft...]
  transfers between devices with their start and end apart: 33 -> 32, of which waited for: 14 -> 16; matrix products, arithmetic and copies ran while one was open for 0% -> 0% of each run, Pallas kernels for 18% -> 15%
where the time goes in v4:
time: 185 us
  waiting for transfers between devices  88.7 us (48%)
  starting transfers between devices  57.8 us (31%)
  Pallas kernels  33.5 us (18%)
  local copies, waits for them, and re-layouts  2.91 us (2%)
    ppermute x32, waiting for transfers between devices, swap(): return lax.ppermute(value, axis, [(i, i ^ turn) for i in range(count)])  88.7 us
    ppermute x32, starting transfers between devices, swap(): return lax.ppermute(value, axis, [(i, i ^ turn) for i in range(count)])  57.8 us
    pallas_call x3, Pallas kernels, project(): pl.pallas_call(functools.partial(project_kernel, lows=lows, after=len(aft...  9.06 us
    pallas_call x1, Pallas kernels, mix(): pl.pallas_call(functools.partial(mix_kernel, after=len(after)), out_shape...  8.65 us
    pallas_call x4, Pallas kernels, emit(): pl.pallas_call(functools.partial(emit_kernel, turns=turns, added=len(extr...  5.64 us
  transfers between devices with their start and end apart: 32, of which 16 were waited for; matrix products, arithmetic and copies ran while one was open for 0% of the time, Pallas kernels for 15%

profile of v4, /device:TPU:0, one launch (start us, length us, event | category | flops | bytes accessed | tf_op | source)
XLA Modules:
  0.0 184.9 jit_solution(10075146322795679353)
XLA Ops:
  0.6 3.2 %halve.1 = (bf16[256,512]{1,0:T(8,128)(2,1)}, bf16[256,512]{1,0:T(8,128)(2,1)}, bf16[256,512]{1,0:T(8,128)(2,1)}, bf16[512,256]{1,0:T(8,128)(2,1)}, bf16[512,256]{1,0:T(8,128)(2,1)}) custom-call(s32[2]{0:T(128)} %pad_add_fusion.where_ref, bf16[256,1024]{1,0:T(8,128)(2,1)} %tokens.1, bf16[256,1024]{1,0:T(8,128)(2,1)} %filters.5, bf16[3,512,1024]{2,1,0:T(8,128)(2,1)} %bitcast.4), custom_call_target="tpu_custom_call" | custom-call | tf_op jit(solution)/shard_map/halve/pallas_call | solution.py:201
  3.8 3.0 %collective-permute-start = (bf16[256,512]{1,0:T(8,128)(2,1)}, bf16[256,512]{1,0:T(8,128)(2,1)S(1)}, u32[]{:S(2)}, u32[]{:S(2)}) collective-permute-start(bf16[256,512]{1,0:T(8,128)(2,1)} %get-tuple-element.36), channel_id=1, source_target_pairs={{0,4},{4,0},{8,12},{12,8},{16,20},{20,16},{24,28},{28,24},{1,5},{5... | collective-permute-start | bytes 786440 | tf_op jit(solution)/shard_map/ppermute | solution.py:622
  6.8 2.6 %collective-permute-start.1 = (bf16[256,512]{1,0:T(8,128)(2,1)}, bf16[256,512]{1,0:T(8,128)(2,1)S(1)}, u32[]{:S(2)}, u32[]{:S(2)}) collective-permute-start(bf16[256,512]{1,0:T(8,128)(2,1)} %get-tuple-element.35.refs_0_), channel_id=1, source_target_pairs={{0,16},{4,20},{8,24},{12,28},{16,0},{20,4},{24,8},{28,12},{1,17},{... | collective-permute-start | bytes 786440 | tf_op jit(solution)/shard_map/ppermute | solution.py:622
  9.4 1.6 collective-permute-start.2
  11.0 2.3 %collective-permute-done.refs_1_ = bf16[256,512]{1,0:T(8,128)(2,1)S(1)} collective-permute-done((bf16[256,512]{1,0:T(8,128)(2,1)}, bf16[256,512]{1,0:T(8,128)(2,1)S(1)}, u32[]{:S(2)}, u32[]{:S(2)}) %collective-permute-start) | collective-permute-done | bytes 262176 | tf_op jit(solution)/shard_map/ppermute | solution.py:622
  13.3 8.1 %collective-permute-done.1.refs_2_.refs_0_ = bf16[256,512]{1,0:T(8,128)(2,1)S(1)} collective-permute-done((bf16[256,512]{1,0:T(8,128)(2,1)}, bf16[256,512]{1,0:T(8,128)(2,1)S(1)}, u32[]{:S(2)}, u32[]{:S(2)}) %collective-permute-start.1) | collective-permute-done | bytes 262176 | tf_op jit(solution)/shard_map/ppermute | solution.py:622
  26.2 2.3 %collective-permute-start.6 = (bf16[512,256]{1,0:T(8,128)(2,1)}, bf16[512,256]{1,0:T(8,128)(2,1)S(1)}, u32[]{:S(2)}, u32[]{:S(2)}) collective-permute-start(bf16[512,256]{1,0:T(8,128)(2,1)} %get-tuple-element.38), channel_id=1, source_target_pairs={{0,16},{4,20},{8,24},{12,28},{16,0},{20,4},{24,8},{28,12},{1,17},{... | collective-permute-start | bytes 786440 | tf_op jit(solution)/shard_map/ppermute | solution.py:622
  29.1 3.5 %collective-permute-done.7.filter_beside = bf16[256,512]{1,0:T(8,128)(2,1)S(1)} collective-permute-done((bf16[256,512]{1,0:T(8,128)(2,1)}, bf16[256,512]{1,0:T(8,128)(2,1)S(1)}, u32[]{:S(2)}, u32[]{:S(2)}) %collective-permute-start.7) | collective-permute-done | bytes 262176 | tf_op jit(solution)/shard_map/ppermute | solution.py:622
  32.5 1.9 %copy-done = bf16[512,3,1024]{2,0,1:T(8,128)(2,1)S(1)} copy-done((bf16[512,3,1024]{2,0,1:T(8,128)(2,1)S(1)}, bf16[512,3,1024]{2,0,1:T(8,128)(2,1)}, u32[]{:S(2)}) %copy-start) | copy-done | bytes 3145752
  35.6 6.6 %collective-permute-done.6.refs_4_.refs_11_ = bf16[512,256]{1,0:T(8,128)(2,1)S(1)} collective-permute-done((bf16[512,256]{1,0:T(8,128)(2,1)}, bf16[512,256]{1,0:T(8,128)(2,1)S(1)}, u32[]{:S(2)}, u32[]{:S(2)}) %collective-permute-start.6) | collective-permute-done | bytes 262176 | tf_op jit(solution)/shard_map/ppermute | solution.py:622
  42.2 9.0 %collective-permute-done.4.refs_1_ = bf16[256,512]{1,0:T(8,128)(2,1)S(1)} collective-permute-done((bf16[256,512]{1,0:T(8,128)(2,1)S(1)}, bf16[256,512]{1,0:T(8,128)(2,1)S(1)}, u32[]{:S(2)}, u32[]{:S(2)}) %collective-permute-start.4) | collective-permute-done | bytes 262176 | tf_op jit(solution)/shard_map/ppermute | solution.py:622
  51.9 2.4 %collective-permute-start.12 = (bf16[1280,256]{1,0:T(8,128)(2,1)S(1)}, bf16[1280,256]{1,0:T(8,128)(2,1)S(1)}, u32[]{:S(2)}, u32[]{:S(2)}) collective-permute-start(bf16[1280,256]{1,0:T(8,128)(2,1)S(1)} %get-tuple-element.40.refs_5_), channel_id=1, source_target_pairs={{0,24},{4,28},{8,16},{12,20},{16,8},{20,12},{24,0},{28,4},{1,25},{... | collective-permute-start | bytes 1966088 | tf_op jit(solution)/shard_map/ppermute | solution.py:622
  54.4 9.9 %collective-permute-done.8.refs_2_.refs_3_ = bf16[512,512]{1,0:T(8,128)(2,1)S(1)} collective-permute-done((bf16[512,512]{1,0:T(8,128)(2,1)S(1)}, bf16[512,512]{1,0:T(8,128)(2,1)S(1)}, u32[]{:S(2)}, u32[]{:S(2)}) %collective-permute-start.8) | collective-permute-done | bytes 524320 | tf_op jit(solution)/shard_map/ppermute | solution.py:622
  65.8 2.5 %collective-permute-start.13 = (bf16[768,256]{1,0:T(8,128)(2,1)S(1)}, bf16[768,256]{1,0:T(8,128)(2,1)S(1)}, u32[]{:S(2)}, u32[]{:S(2)}) collective-permute-start(bf16[768,256]{1,0:T(8,128)(2,1)S(1)} %get-tuple-element.43), channel_id=1, source_target_pairs={{0,8},{4,12},{8,0},{12,4},{16,24},{20,28},{24,16},{28,20},{1,9},{5... | collective-permute-start | bytes 1179656 | tf_op jit(solution)/shard_map/ppermute | solution.py:622
  68.3 15.5 %collective-permute-start.14 = (bf16[768,256]{1,0:T(8,128)(2,1)S(1)}, bf16[768,256]{1,0:T(8,128)(2,1)S(1)}, u32[]{:S(2)}, u32[]{:S(2)}) collective-permute-start(bf16[768,256]{1,0:T(8,128)(2,1)S(1)} %get-tuple-element.44), channel_id=1, source_target_pairs={{0,16},{4,20},{8,24},{12,28},{16,0},{20,4},{24,8},{28,12},{1,17},{... | collective-permute-start | bytes 1179656 | tf_op jit(solution)/shard_map/ppermute | solution.py:622
  84.0 4.2 %collective-permute-done.13.refs_5_.refs_1_.refs_10_ = bf16[768,256]{1,0:T(8,128)(2,1)S(1)} collective-permute-done((bf16[768,256]{1,0:T(8,128)(2,1)S(1)}, bf16[768,256]{1,0:T(8,128)(2,1)S(1)}, u32[]{:S(2)}, u32[]{:S(2)}) %collective-permute-start.13) | collective-permute-done | bytes 393248 | tf_op jit(solution)/shard_map/ppermute | solution.py:622
  88.2 10.5 %collective-permute-done.14.refs_6_.refs_2_.refs_11_.refs_0_ = bf16[768,256]{1,0:T(8,128)(2,1)S(1)} collective-permute-done((bf16[768,256]{1,0:T(8,128)(2,1)S(1)}, bf16[768,256]{1,0:T(8,128)(2,1)S(1)}, u32[]{:S(2)}, u32[]{:S(2)}) %collective-permute-start.14) | collective-permute-done | bytes 393248 | tf_op jit(solution)/shard_map/ppermute | solution.py:622
  100.0 3.2 %collective-permute-start.19 = (bf16[512,256]{1,0:T(8,128)(2,1)S(1)}, bf16[512,256]{1,0:T(8,128)(2,1)S(1)}, u32[]{:S(2)}, u32[]{:S(2)}) collective-permute-start(bf16[512,256]{1,0:T(8,128)(2,1)S(1)} %get-tuple-element.51), channel_id=1, source_target_pairs={{0,16},{4,20},{8,24},{12,28},{16,0},{20,4},{24,8},{28,12},{1,17},{... | collective-permute-start | bytes 786440 | tf_op jit(solution)/shard_map/ppermute | solution.py:622
  104.3 3.6 %spectrum.1.refs_13_.freq_ref = f32[4224,128]{1,0:T(8,128)S(1)} custom-call(s32[2]{0:T(128)S(1)} %copy-done.8, bf16[80,32]{1,0:T(8,128)(2,1)S(1)} %copy-done.7, bf16[33,128,128]{2,1,0:T(8,128)(2,1)S(1)} %copy-done.3, bf16[1792,256]{1,0:T(8,128)(2,1)S(1)} %get-tuple-element.45.refs_9_.refs_0_, ...), custom_call_target="tpu_custom_call" | custom-call | flops 67108864 | bytes 1048576 | tf_op jit(solution)/shard_map/spectrum/pallas_call | solution.py:417
  107.9 3.0 %project.3 = (f32[2048,128]{1,0:T(8,128)S(1)}, bf16[2048,128]{1,0:T(8,128)(2,1)S(1)}) custom-call(s32[2]{0:T(128)S(1)} %copy-done.8, bf16[512,512]{1,0:T(8,128)(2,1)S(1)} %join.4.refs_0_, bf16[512,512]{1,0:T(8,128)(2,1)S(1)} %collective-permute-done.3.refs_2_.refs_1_, bf16[512,512]{1,0:T(8,128)(2,1)S(1)} %get-tuple-element.41.refs_0_.refs_2_, ...), custom_call_target="tpu_custom_call" | custom-call | flops 4294967296 | bytes 8388608 | tf_op jit(solution)/shard_map/project/pallas_call | solution.py:329
  112.5 3.0 %project.4 = (f32[2048,128]{1,0:T(8,128)S(1)}, bf16[2048,128]{1,0:T(8,128)(2,1)S(1)}) custom-call(s32[2]{0:T(128)S(1)} %copy-done.8, bf16[512,512]{1,0:T(8,128)(2,1)S(1)} %join.4.refs_0_, bf16[512,512]{1,0:T(8,128)(2,1)S(1)} %collective-permute-done.3.refs_2_.refs_1_, bf16[512,512]{1,0:T(8,128)(2,1)S(1)} %get-tuple-element.41.refs_0_.refs_2_, ...), custom_call_target="tpu_custom_call" | custom-call | flops 4294967296 | bytes 8388608 | tf_op jit(solution)/shard_map/project/pallas_call | solution.py:329
  116.2 5.3 %collective-permute-done.19.refs_11_ = bf16[512,256]{1,0:T(8,128)(2,1)S(1)} collective-permute-done((bf16[512,256]{1,0:T(8,128)(2,1)S(1)}, bf16[512,256]{1,0:T(8,128)(2,1)S(1)}, u32[]{:S(2)}, u32[]{:S(2)}) %collective-permute-start.19) | collective-permute-done | bytes 262176 | tf_op jit(solution)/shard_map/ppermute | solution.py:622
  121.5 3.0 %project.5 = (f32[2048,128]{1,0:T(8,128)S(1)}, bf16[2048,128]{1,0:T(8,128)(2,1)S(1)}) custom-call(s32[2]{0:T(128)S(1)} %copy-done.8, bf16[512,512]{1,0:T(8,128)(2,1)S(1)} %join.4.refs_0_, bf16[512,512]{1,0:T(8,128)(2,1)S(1)} %collective-permute-done.3.refs_2_.refs_1_, bf16[512,512]{1,0:T(8,128)(2,1)S(1)} %get-tuple-element.41.refs_0_.refs_2_, ...), custom_call_target="tpu_custom_call" | custom-call | flops 4294967296 | bytes 8388608 | tf_op jit(solution)/shard_map/project/pallas_call | solution.py:329
  126.1 11.0 %collective-permute-done.17.recv2 = bf16[2048,128]{1,0:T(8,128)(2,1)S(1)} collective-permute-done((bf16[2048,128]{1,0:T(8,128)(2,1)S(1)}, bf16[2048,128]{1,0:T(8,128)(2,1)S(1)}, u32[]{:S(2)}, u32[]{:S(2)}) %collective-permute-start.17) | collective-permute-done | bytes 524320 | tf_op jit(solution)/shard_map/ppermute | solution.py:622
  137.2 8.6 %mix.1 = (f32[2048,128]{1,0:T(8,128)S(1)}, bf16[1024,4096]{1,0:T(8,128)(2,1)S(1)}) custom-call(s32[2]{0:T(128)S(1)} %copy-done.8, f32[2048,128]{1,0:T(8,128)S(1)} %get-tuple-element.46.own1, bf16[2048,128]{1,0:T(8,128)(2,1)S(1)} %collective-permute-done.16.recv1, f32[2048,128]{1,0:T(8,128)S(1)} %get-tuple-element.48.own2, ...), custom_call_target="tpu_custom_call" | custom-call | flops 201326592 | bytes 6291456 | tf_op jit(solution)/shard_map/mix/pallas_call | solution.py:519
  149.5 2.0 %collective-permute-start.24 = (bf16[256,128]{1,0:T(8,128)(2,1)S(1)}, bf16[256,128]{1,0:T(8,128)(2,1)S(1)}, u32[]{:S(2)}, u32[]{:S(2)}) collective-permute-start(bf16[256,128]{1,0:T(8,128)(2,1)S(1)} %get-tuple-element.60), channel_id=1, source_target_pairs={{0,12},{4,8},{8,4},{12,0},{16,28},{20,24},{24,20},{28,16},{1,13},{... | collective-permute-start | bytes 196616 | tf_op jit(solution)/shard_map/ppermute | solution.py:622
  152.7 2.6 %collective-permute-start.26 = (bf16[256,128]{1,0:T(8,128)(2,1)S(1)}, bf16[256,128]{1,0:T(8,128)(2,1)S(1)}, u32[]{:S(2)}, u32[]{:S(2)}) collective-permute-start(bf16[256,128]{1,0:T(8,128)(2,1)S(1)} %get-tuple-element.62), channel_id=1, source_target_pairs={{0,20},{4,16},{8,28},{12,24},{16,4},{20,0},{24,12},{28,8},{1,21},{... | collective-permute-start | bytes 196616 | tf_op jit(solution)/shard_map/ppermute | solution.py:622
  155.4 2.6 %collective-permute-start.27 = (bf16[256,128]{1,0:T(8,128)(2,1)S(1)}, bf16[256,128]{1,0:T(8,128)(2,1)S(1)}, u32[]{:S(2)}, u32[]{:S(2)}) collective-permute-start(bf16[256,128]{1,0:T(8,128)(2,1)S(1)} %get-tuple-element.63), channel_id=1, source_target_pairs={{0,24},{4,28},{8,16},{12,20},{16,8},{20,12},{24,0},{28,4},{1,25},{... | collective-permute-start | bytes 196616 | tf_op jit(solution)/shard_map/ppermute | solution.py:622
  159.5 3.9 %collective-permute-done.26.refs_5_ = bf16[256,128]{1,0:T(8,128)(2,1)S(1)} collective-permute-done((bf16[256,128]{1,0:T(8,128)(2,1)S(1)}, bf16[256,128]{1,0:T(8,128)(2,1)S(1)}, u32[]{:S(2)}, u32[]{:S(2)}) %collective-permute-start.26) | collective-permute-done | bytes 65568 | tf_op jit(solution)/shard_map/ppermute | solution.py:622
  163.4 1.7 collective-permute-done.28.refs_7_
  170.0 1.6 collective-permute-start.31
  173.0 10.9 %collective-permute-done.31 = bf16[256,1024]{1,0:T(8,128)(2,1)S(1)} collective-permute-done((bf16[256,1024]{1,0:T(8,128)(2,1)S(1)}, bf16[256,1024]{1,0:T(8,128)(2,1)S(1)}, u32[]{:S(2)}, u32[]{:S(2)}) %collective-permute-start.31) | collective-permute-done | bytes 524320 | tf_op jit(solution)/shard_map/ppermute | solution.py:622
  (78 shorter events, 29.3 us)
Async XLA Ops:
  3.8 9.5 %collective-permute-start = (bf16[256,512]{1,0:T(8,128)(2,1)}, bf16[256,512]{1,0:T(8,128)(2,1)S(1)}, u32[]{:S(2)}, u32[]{:S(2)}) collective-permute-start(bf16[256,512]{1,0:T(8,128)(2,1)} %get-tuple-element.36), channel_id=1, source_target_pairs={{0,4},{4,0},{8,12},{12,8},{16,20},{20,16},{24,28},{28,24},{1,5},{5... | collective-permute-start | bytes 786440 | tf_op jit(solution)/shard_map/ppermute | solution.py:622
  6.8 14.6 %collective-permute-start.1 = (bf16[256,512]{1,0:T(8,128)(2,1)}, bf16[256,512]{1,0:T(8,128)(2,1)S(1)}, u32[]{:S(2)}, u32[]{:S(2)}) collective-permute-start(bf16[256,512]{1,0:T(8,128)(2,1)} %get-tuple-element.35.refs_0_), channel_id=1, source_target_pairs={{0,16},{4,20},{8,24},{12,28},{16,0},{20,4},{24,8},{28,12},{1,17},{... | collective-permute-start | bytes 786440 | tf_op jit(solution)/shard_map/ppermute | solution.py:622
  9.4 12.2 %collective-permute-start.2 = (bf16[512,256]{1,0:T(8,128)(2,1)}, bf16[512,256]{1,0:T(8,128)(2,1)S(1)}, u32[]{:S(2)}, u32[]{:S(2)}) collective-permute-start(bf16[512,256]{1,0:T(8,128)(2,1)} %get-tuple-element.37), channel_id=1, source_target_pairs={{0,8},{4,12},{8,0},{12,4},{16,24},{20,28},{24,16},{28,20},{1,9},{5... | collective-permute-start | bytes 786440 | tf_op jit(solution)/shard_map/ppermute | solution.py:622
  22.6 28.6 %collective-permute-start.3 = (bf16[512,512]{1,0:T(8,128)(2,1)S(1)}, bf16[512,512]{1,0:T(8,128)(2,1)S(1)}, u32[]{:S(2)}, u32[]{:S(2)}) collective-permute-start(bf16[512,512]{1,0:T(8,128)(2,1)S(1)} %join.4.refs_0_), channel_id=1, source_target_pairs={{0,8},{4,12},{8,0},{12,4},{16,24},{20,28},{24,16},{28,20},{1,9},{5... | collective-permute-start | bytes 1572872 | tf_op jit(solution)/shard_map/ppermute | solution.py:622
  24.1 27.1 %collective-permute-start.5 = (bf16[512,512]{1,0:T(8,128)(2,1)S(1)}, bf16[512,512]{1,0:T(8,128)(2,1)S(1)}, u32[]{:S(2)}, u32[]{:S(2)}) collective-permute-start(bf16[512,512]{1,0:T(8,128)(2,1)S(1)} %join.4.refs_0_), channel_id=1, source_target_pairs={{0,2},{1,3},{2,0},{3,1},{4,6},{5,7},{6,4},{7,5},{8,10},{9,11},{10,... | collective-permute-start | bytes 1572872 | tf_op jit(solution)/shard_map/ppermute | solution.py:622
  25.6 6.9 %collective-permute-start.7 = (bf16[256,512]{1,0:T(8,128)(2,1)}, bf16[256,512]{1,0:T(8,128)(2,1)S(1)}, u32[]{:S(2)}, u32[]{:S(2)}) collective-permute-start(bf16[256,512]{1,0:T(8,128)(2,1)} %get-tuple-element.39), channel_id=1, source_target_pairs={{0,4},{4,0},{8,12},{12,8},{16,20},{20,16},{24,28},{28,24},{1,5},{5... | collective-permute-start | bytes 786440 | tf_op jit(solution)/shard_map/ppermute | solution.py:622
  26.2 16.1 %collective-permute-start.6 = (bf16[512,256]{1,0:T(8,128)(2,1)}, bf16[512,256]{1,0:T(8,128)(2,1)S(1)}, u32[]{:S(2)}, u32[]{:S(2)}) collective-permute-start(bf16[512,256]{1,0:T(8,128)(2,1)} %get-tuple-element.38), channel_id=1, source_target_pairs={{0,16},{4,20},{8,24},{12,28},{16,0},{20,4},{24,8},{28,12},{1,17},{... | collective-permute-start | bytes 786440 | tf_op jit(solution)/shard_map/ppermute | solution.py:622
  28.5 22.8 %collective-permute-start.4 = (bf16[256,512]{1,0:T(8,128)(2,1)S(1)}, bf16[256,512]{1,0:T(8,128)(2,1)S(1)}, u32[]{:S(2)}, u32[]{:S(2)}) collective-permute-start(bf16[256,512]{1,0:T(8,128)(2,1)S(1)} %collective-permute-done.refs_1_), channel_id=1, source_target_pairs={{0,16},{4,20},{8,24},{12,28},{16,0},{20,4},{24,8},{28,12},{1,17},{... | collective-permute-start | bytes 786440 | tf_op jit(solution)/shard_map/ppermute | solution.py:622
  51.3 32.4 %collective-permute-start.9 = (bf16[1024,512]{1,0:T(8,128)(2,1)S(1)}, bf16[1024,512]{1,0:T(8,128)(2,1)S(1)}, u32[]{:S(2)}, u32[]{:S(2)}) collective-permute-start(bf16[1024,512]{1,0:T(8,128)(2,1)S(1)} %get-tuple-element.42), channel_id=1, source_target_pairs={{0,2},{1,3},{2,0},{3,1},{4,6},{5,7},{6,4},{7,5},{8,10},{9,11},{10,... | collective-permute-start | bytes 3145736 | tf_op jit(solution)/shard_map/ppermute | solution.py:622
  51.9 12.4 %collective-permute-start.8 = (bf16[512,512]{1,0:T(8,128)(2,1)S(1)}, bf16[512,512]{1,0:T(8,128)(2,1)S(1)}, u32[]{:S(2)}, u32[]{:S(2)}) collective-permute-start(bf16[512,512]{1,0:T(8,128)(2,1)S(1)} %get-tuple-element.41.refs_0_.refs_2_), channel_id=1, source_target_pairs={{0,8},{4,12},{8,0},{12,4},{16,24},{20,28},{24,16},{28,20},{1,9},{5... | collective-permute-start | bytes 1572872 | tf_op jit(solution)/shard_map/ppermute | solution.py:622
  51.9 46.8 %collective-permute-start.12 = (bf16[1280,256]{1,0:T(8,128)(2,1)S(1)}, bf16[1280,256]{1,0:T(8,128)(2,1)S(1)}, u32[]{:S(2)}, u32[]{:S(2)}) collective-permute-start(bf16[1280,256]{1,0:T(8,128)(2,1)S(1)} %get-tuple-element.40.refs_5_), channel_id=1, source_target_pairs={{0,24},{4,28},{8,16},{12,20},{16,8},{20,12},{24,0},{28,4},{1,25},{... | collective-permute-start | bytes 1966088 | tf_op jit(solution)/shard_map/ppermute | solution.py:622
  64.3 34.4 %collective-permute-start.10 = (bf16[512,512]{1,0:T(8,128)(2,1)S(1)}, bf16[512,512]{1,0:T(8,128)(2,1)S(1)}, u32[]{:S(2)}, u32[]{:S(2)}) collective-permute-start(bf16[512,512]{1,0:T(8,128)(2,1)S(1)} %collective-permute-done.8.refs_2_.refs_3_), channel_id=1, source_target_pairs={{0,2},{1,3},{2,0},{3,1},{4,6},{5,7},{6,4},{7,5},{8,10},{9,11},{10,... | collective-permute-start | bytes 1572872 | tf_op jit(solution)/shard_map/ppermute | solution.py:622
  65.8 22.4 %collective-permute-start.13 = (bf16[768,256]{1,0:T(8,128)(2,1)S(1)}, bf16[768,256]{1,0:T(8,128)(2,1)S(1)}, u32[]{:S(2)}, u32[]{:S(2)}) collective-permute-start(bf16[768,256]{1,0:T(8,128)(2,1)S(1)} %get-tuple-element.43), channel_id=1, source_target_pairs={{0,8},{4,12},{8,0},{12,4},{16,24},{20,28},{24,16},{28,20},{1,9},{5... | collective-permute-start | bytes 1179656 | tf_op jit(solution)/shard_map/ppermute | solution.py:622
  68.3 30.4 %collective-permute-start.14 = (bf16[768,256]{1,0:T(8,128)(2,1)S(1)}, bf16[768,256]{1,0:T(8,128)(2,1)S(1)}, u32[]{:S(2)}, u32[]{:S(2)}) collective-permute-start(bf16[768,256]{1,0:T(8,128)(2,1)S(1)} %get-tuple-element.44), channel_id=1, source_target_pairs={{0,16},{4,20},{8,24},{12,28},{16,0},{20,4},{24,8},{28,12},{1,17},{... | collective-permute-start | bytes 1179656 | tf_op jit(solution)/shard_map/ppermute | solution.py:622
  83.9 24.0 %collective-permute-start.11 = (bf16[2048,512]{1,0:T(8,128)(2,1)S(1)}, bf16[2048,512]{1,0:T(8,128)(2,1)S(1)}, u32[]{:S(2)}, u32[]{:S(2)}) collective-permute-start(bf16[2048,512]{1,0:T(8,128)(2,1)S(1)} %join.6), channel_id=1, source_target_pairs={{0,1},{1,0},{2,3},{3,2},{4,5},{5,4},{6,7},{7,6},{8,9},{9,8},{10,11... | collective-permute-start | bytes 6291464 | tf_op jit(solution)/shard_map/ppermute | solution.py:622
  98.9 9.0 %collective-permute-start.15 = (bf16[2048,512]{1,0:T(8,128)(2,1)S(1)}, bf16[2048,512]{1,0:T(8,128)(2,1)S(1)}, u32[]{:S(2)}, u32[]{:S(2)}) collective-permute-start(bf16[2048,512]{1,0:T(8,128)(2,1)S(1)} %join.7), channel_id=1, source_target_pairs={{0,1},{1,0},{2,3},{3,2},{4,5},{5,4},{6,7},{7,6},{8,9},{9,8},{10,11... | collective-permute-start | bytes 6291464 | tf_op jit(solution)/shard_map/ppermute | solution.py:622
  99.9 16.3 %collective-permute-start.18 = (bf16[512,256]{1,0:T(8,128)(2,1)S(1)}, bf16[512,256]{1,0:T(8,128)(2,1)S(1)}, u32[]{:S(2)}, u32[]{:S(2)}) collective-permute-start(bf16[512,256]{1,0:T(8,128)(2,1)S(1)} %get-tuple-element.50), channel_id=1, source_target_pairs={{0,8},{4,12},{8,0},{12,4},{16,24},{20,28},{24,16},{28,20},{1,9},{5... | collective-permute-start | bytes 786440 | tf_op jit(solution)/shard_map/ppermute | solution.py:622
  100.0 21.6 %collective-permute-start.19 = (bf16[512,256]{1,0:T(8,128)(2,1)S(1)}, bf16[512,256]{1,0:T(8,128)(2,1)S(1)}, u32[]{:S(2)}, u32[]{:S(2)}) collective-permute-start(bf16[512,256]{1,0:T(8,128)(2,1)S(1)} %get-tuple-element.51), channel_id=1, source_target_pairs={{0,16},{4,20},{8,24},{12,28},{16,0},{20,4},{24,8},{28,12},{1,17},{... | collective-permute-start | bytes 786440 | tf_op jit(solution)/shard_map/ppermute | solution.py:622
  103.1 18.4 %collective-permute-start.20 = (bf16[512,256]{1,0:T(8,128)(2,1)S(1)}, bf16[512,256]{1,0:T(8,128)(2,1)S(1)}, u32[]{:S(2)}, u32[]{:S(2)}) collective-permute-start(bf16[512,256]{1,0:T(8,128)(2,1)S(1)} %get-tuple-element.52), channel_id=1, source_target_pairs={{0,24},{4,28},{8,16},{12,20},{16,8},{20,12},{24,0},{28,4},{1,25},{... | collective-permute-start | bytes 786440 | tf_op jit(solution)/shard_map/ppermute | solution.py:622
  111.0 15.1 %collective-permute-start.16 = (bf16[2048,128]{1,0:T(8,128)(2,1)S(1)}, bf16[2048,128]{1,0:T(8,128)(2,1)S(1)}, u32[]{:S(2)}, u32[]{:S(2)}) collective-permute-start(bf16[2048,128]{1,0:T(8,128)(2,1)S(1)} %get-tuple-element.47), channel_id=1, source_target_pairs={{0,4},{4,0},{8,12},{12,8},{16,20},{20,16},{24,28},{28,24},{1,5},{5... | collective-permute-start | bytes 1572872 | tf_op jit(solution)/shard_map/ppermute | solution.py:622
  115.6 21.5 %collective-permute-start.17 = (bf16[2048,128]{1,0:T(8,128)(2,1)S(1)}, bf16[2048,128]{1,0:T(8,128)(2,1)S(1)}, u32[]{:S(2)}, u32[]{:S(2)}) collective-permute-start(bf16[2048,128]{1,0:T(8,128)(2,1)S(1)} %get-tuple-element.49), channel_id=1, source_target_pairs={{0,4},{4,0},{8,12},{12,8},{16,20},{20,16},{24,28},{28,24},{1,5},{5... | collective-permute-start | bytes 1572872 | tf_op jit(solution)/shard_map/ppermute | solution.py:622
  124.5 22.4 %collective-permute-start.21 = (bf16[2048,128]{1,0:T(8,128)(2,1)S(1)}, bf16[2048,128]{1,0:T(8,128)(2,1)S(1)}, u32[]{:S(2)}, u32[]{:S(2)}) collective-permute-start(bf16[2048,128]{1,0:T(8,128)(2,1)S(1)} %get-tuple-element.53.refs_0_), channel_id=1, source_target_pairs={{0,4},{4,0},{8,12},{12,8},{16,20},{20,16},{24,28},{28,24},{1,5},{5... | collective-permute-start | bytes 1572872 | tf_op jit(solution)/shard_map/ppermute | solution.py:622
  147.9 7.4 %collective-permute-start.22 = (bf16[256,128]{1,0:T(8,128)(2,1)S(1)}, bf16[256,128]{1,0:T(8,128)(2,1)S(1)}, u32[]{:S(2)}, u32[]{:S(2)}) collective-permute-start(bf16[256,128]{1,0:T(8,128)(2,1)S(1)} %get-tuple-element.58), channel_id=1, source_target_pairs={{0,4},{4,0},{8,12},{12,8},{16,20},{20,16},{24,28},{28,24},{1,5},{5... | collective-permute-start | bytes 196616 | tf_op jit(solution)/shard_map/ppermute | solution.py:622
  149.5 8.5 %collective-permute-start.23 = (bf16[256,128]{1,0:T(8,128)(2,1)S(1)}, bf16[256,128]{1,0:T(8,128)(2,1)S(1)}, u32[]{:S(2)}, u32[]{:S(2)}) collective-permute-start(bf16[256,128]{1,0:T(8,128)(2,1)S(1)} %get-tuple-element.59), channel_id=1, source_target_pairs={{0,8},{4,12},{8,0},{12,4},{16,24},{20,28},{24,16},{28,20},{1,9},{5... | collective-permute-start | bytes 196616 | tf_op jit(solution)/shard_map/ppermute | solution.py:622
  149.5 9.7 %collective-permute-start.24 = (bf16[256,128]{1,0:T(8,128)(2,1)S(1)}, bf16[256,128]{1,0:T(8,128)(2,1)S(1)}, u32[]{:S(2)}, u32[]{:S(2)}) collective-permute-start(bf16[256,128]{1,0:T(8,128)(2,1)S(1)} %get-tuple-element.60), channel_id=1, source_target_pairs={{0,12},{4,8},{8,4},{12,0},{16,28},{20,24},{24,20},{28,16},{1,13},{... | collective-permute-start | bytes 196616 | tf_op jit(solution)/shard_map/ppermute | solution.py:622
  151.5 8.0 %collective-permute-start.25 = (bf16[256,128]{1,0:T(8,128)(2,1)S(1)}, bf16[256,128]{1,0:T(8,128)(2,1)S(1)}, u32[]{:S(2)}, u32[]{:S(2)}) collective-permute-start(bf16[256,128]{1,0:T(8,128)(2,1)S(1)} %get-tuple-element.61), channel_id=1, source_target_pairs={{0,16},{4,20},{8,24},{12,28},{16,0},{20,4},{24,8},{28,12},{1,17},{... | collective-permute-start | bytes 196616 | tf_op jit(solution)/shard_map/ppermute | solution.py:622
  152.7 10.7 %collective-permute-start.26 = (bf16[256,128]{1,0:T(8,128)(2,1)S(1)}, bf16[256,128]{1,0:T(8,128)(2,1)S(1)}, u32[]{:S(2)}, u32[]{:S(2)}) collective-permute-start(bf16[256,128]{1,0:T(8,128)(2,1)S(1)} %get-tuple-element.62), channel_id=1, source_target_pairs={{0,20},{4,16},{8,28},{12,24},{16,4},{20,0},{24,12},{28,8},{1,21},{... | collective-permute-start | bytes 196616 | tf_op jit(solution)/shard_map/ppermute | solution.py:622
  155.4 8.1 %collective-permute-start.27 = (bf16[256,128]{1,0:T(8,128)(2,1)S(1)}, bf16[256,128]{1,0:T(8,128)(2,1)S(1)}, u32[]{:S(2)}, u32[]{:S(2)}) collective-permute-start(bf16[256,128]{1,0:T(8,128)(2,1)S(1)} %get-tuple-element.63), channel_id=1, source_target_pairs={{0,24},{4,28},{8,16},{12,20},{16,8},{20,12},{24,0},{28,4},{1,25},{... | collective-permute-start | bytes 196616 | tf_op jit(solution)/shard_map/ppermute | solution.py:622
  158.0 7.1 %collective-permute-start.28 = (bf16[256,128]{1,0:T(8,128)(2,1)S(1)}, bf16[256,128]{1,0:T(8,128)(2,1)S(1)}, u32[]{:S(2)}, u32[]{:S(2)}) collective-permute-start(bf16[256,128]{1,0:T(8,128)(2,1)S(1)} %get-tuple-element.64), channel_id=1, source_target_pairs={{0,28},{4,24},{8,20},{12,16},{16,12},{20,8},{24,4},{28,0},{1,29},{... | collective-permute-start | bytes 196616 | tf_op jit(solution)/shard_map/ppermute | solution.py:622
  166.5 2.1 %collective-permute-start.30 = (bf16[256,1024]{1,0:T(8,128)(2,1)S(1)}, bf16[256,1024]{1,0:T(8,128)(2,1)S(1)}, u32[]{:S(2)}, u32[]{:S(2)}) collective-permute-start(bf16[256,1024]{1,0:T(8,128)(2,1)S(1)} %emit.6), channel_id=1, source_target_pairs={{0,1},{1,0},{2,3},{3,2},{4,5},{5,4},{6,7},{7,6},{8,9},{9,8},{10,11... | collective-permute-start | bytes 1572872 | tf_op jit(solution)/shard_map/ppermute | solution.py:622
  168.0 3.6 %collective-permute-start.29 = (bf16[256,1024]{1,0:T(8,128)(2,1)S(1)}, bf16[256,1024]{1,0:T(8,128)(2,1)S(1)}, u32[]{:S(2)}, u32[]{:S(2)}) collective-permute-start(bf16[256,1024]{1,0:T(8,128)(2,1)S(1)} %emit.4), channel_id=1, source_target_pairs={{0,1},{1,0},{2,3},{3,2},{4,5},{5,4},{6,7},{7,6},{8,9},{9,8},{10,11... | collective-permute-start | bytes 1572872 | tf_op jit(solution)/shard_map/ppermute | solution.py:622
  170.0 14.0 %collective-permute-start.31 = (bf16[256,1024]{1,0:T(8,128)(2,1)S(1)}, bf16[256,1024]{1,0:T(8,128)(2,1)S(1)}, u32[]{:S(2)}, u32[]{:S(2)}) collective-permute-start(bf16[256,1024]{1,0:T(8,128)(2,1)S(1)} %emit.7), channel_id=1, source_target_pairs={{0,2},{1,3},{2,0},{3,1},{4,6},{5,7},{6,4},{7,5},{8,10},{9,11},{10,... | collective-permute-start | bytes 1572872 | tf_op jit(solution)/shard_map/ppermute | solution.py:622
  (13 other events, 221.9 us)

commit v5 on v4

--- a/solution.py
+++ b/solution.py
@@ -164,12 +164,10 @@
     )
 
 
-def halve_kernel(
-    where_ref, tokens, filters, weight, theirs, ours, filter_theirs, *refs, turns, index
-):
+def halve_kernel(where_ref, tokens, filters, weight, ours, theirs, *refs, turns, names):
     pieces, sems = refs[:-1], refs[-1]
     depth, side = where_ref[0] // 2, where_ref[0] % 2
-    half = ours.shape[1]
+    rows, half = ours.shape
     part = half // 4
     copies = []
 
@@ -180,31 +178,38 @@
         )
 
     copy(tokens, side, half, ours)
-    copy(tokens, 1 - side, half, theirs)
+    copy(tokens, 1 - side, half, theirs.at[pl.ds(0, rows), :])
     for i in range(4):
-        copy(filters, 2 * i + 1 - side, part, filter_theirs.at[:, pl.ds(i * part, part)])
+        target = theirs.at[pl.ds(rows, filters.shape[0]), pl.ds(i * part, part)]
+        copy(filters, 2 * i + 1 - side, part, target)
+    depth_rows = weight.shape[1]
     for turn, piece in zip(turns, pieces, strict=True):
-        copy(weight.at[index], jnp.bitwise_xor(depth, turn), piece.shape[1], piece)
+        for i, name in enumerate(names):
+            target = piece.at[pl.ds(i * depth_rows, depth_rows), :]
+            copy(weight.at[name], jnp.bitwise_xor(depth, turn), piece.shape[1], target)
     for one in copies:
         one.start()
     for one in copies:
         one.wait()
 
 
-def halve(where, tokens, filters, weight, turns, index):
-    shapes = []
-    for value in (tokens, tokens, filters):
-        shapes.append(jax.ShapeDtypeStruct((value.shape[0], value.shape[1] // 2), value.dtype))
-    shapes += [jax.ShapeDtypeStruct((weight.shape[1], weight.shape[2] // 4), weight.dtype)] * len(
-        turns
-    )
+def halve(where, tokens, filters, weight, turns, names):
+    rows, half = tokens.shape[0], tokens.shape[1] // 2
+    piece = jax.ShapeDtypeStruct(
+        (len(names) * weight.shape[1], weight.shape[2] // 4), weight.dtype
+    )
+    vmem = pl.BlockSpec(memory_space=pltpu.VMEM)
     return pl.pallas_call(
-        functools.partial(halve_kernel, turns=turns, index=index),
-        out_shape=tuple(shapes),
+        functools.partial(halve_kernel, turns=turns, names=names),
+        out_shape=(
+            jax.ShapeDtypeStruct((rows, half), tokens.dtype),
+            jax.ShapeDtypeStruct((rows + filters.shape[0], half), tokens.dtype),
+        )
+        + (piece,) * len(turns),
         in_specs=[pl.BlockSpec(memory_space=pltpu.SMEM)]
         + [pl.BlockSpec(memory_space=pl.ANY)] * 3,
-        out_specs=(pl.BlockSpec(memory_space=pltpu.VMEM),) * len(shapes),
-        scratch_shapes=[pltpu.SemaphoreType.DMA((6 + len(turns),))],
+        out_specs=(vmem,) * (2 + len(turns)),
+        scratch_shapes=[pltpu.SemaphoreType.DMA((6 + len(turns) * len(names),))],
         compiler_params=pltpu.CompilerParams(vmem_limit_bytes=61 * 2**20),
         name="halve",
     )(where, tokens, filters, weight)
@@ -233,7 +238,8 @@
                 here = columns_of(2 * block + side, half)
                 copy(filters.at[:, here], out.at[at, pl.ds(0, half)])
                 there = columns_of(block, half)
-                copy(filter_beside.at[:, there], out.at[at, pl.ds(half, half)])
+                below = pl.ds(filter_beside.shape[0] - filters.shape[0], filters.shape[0])
+                copy(filter_beside.at[below, there], out.at[at, pl.ds(half, half)])
                 low += filters.shape[0]
             else:
                 source = weight.at[name, :, columns_of(block, width)]
@@ -635,62 +641,56 @@
     lags = tokens.shape[0]
     rows = in_weight.shape[0]
 
-    theirs, ours, filter_theirs, cut1_1, cut1_2 = halve(
-        where, tokens, long_filter, weight, (1, 2), 1
-    )
-    far_ours = swap(ours, "seq", seq, 4)
+    ours, theirs, cut_2, cut_1 = halve(where, tokens, long_filter, weight, (2, 1), (1, 2))
     beside = swap(theirs, "seq", seq, 1)
-    w1_1 = swap(cut1_1, "seq", seq, 2)
-    filter_beside = swap(filter_theirs, "seq", seq, 1)
-    (pair,) = join([ours, beside], [[(0, 0, lags), (1, 0, lags)]], [far_ours, w1_1])
-    far_beside = swap(beside, "seq", seq, 4)
+    w_2, w_1 = swap(cut_2, "seq", seq, 4), swap(cut_1, "seq", seq, 2)
+    whole = [(0, 0, lags), (1, 0, lags)]
+    (pair,) = join([ours, beside], [whole], [])
+    far = swap(pair, "seq", seq, 4)
     near = swap(pair, "seq", seq, 2)
     pair_across = swap(pair, "chan", chans, 2)
-    w1_2 = swap(cut1_2, "seq", seq, 4)
-    plan = [(0, (1, 2, "f", 0)), (3, (1, 2, "f")), (2, (2, "f")), (1, (2, "f"))]
-    inputs = (where, weight, long_filter, filter_beside)
-    w_0, cut12_3, cut2_2, cut2_1 = cut(*inputs, plan, [pair])
-    whole = [(0, 0, lags), (1, 0, lags)]
-    far, far_and_near = join(
-        [far_ours, far_beside, near],
-        [whole, whole + [(2, 0, 2 * lags)]],
-        [pair_across, w1_2, cut12_3],
-    )
-    w12_3 = swap(cut12_3, "seq", seq, 6)
-    w2_1 = swap(cut2_1, "seq", seq, 2)
-    w2_2 = swap(cut2_2, "seq", seq, 4)
+    inputs = (where, weight, long_filter, beside)
+    plan = [(0, (1, 2, 0, "f")), (3, (1, 2, "f"))]
+    plan += [(2, (0, "f")), (3, (0,)), (1, (0, "f"))]
+    w_0, cut_3, cut0_2, cut0_3, cut0_1 = cut(*inputs, plan, [pair])
+    (far_and_near,) = join(
+        [far, near],
+        [[(0, 0, 2 * lags), (1, 0, 2 * lags)]],
+        [pair_across, cut_3, w_2, w_1],
+    )
+    w_3 = swap(cut_3, "seq", seq, 6)
     far_near = swap(far, "seq", seq, 2)
     across = swap(far_and_near, "chan", chans, 2)
     every = [(0, 0, 2 * lags), (1, 0, 2 * lags)]
     (first,) = join(
         [pair, pair_across, near, across],
         [every + [(2, 0, 2 * lags), (3, 2 * lags, 2 * lags)]],
-        [],
+        [w_3],
     )
     core_a = swap(first, "chan", chans, 1)
     far_near_across = swap(far_near, "chan", chans, 2)
     (second,) = join(
         [far, across, far_near, far_near_across],
         [every + [(2, 0, 2 * lags), (3, 0, 2 * lags)]],
-        [w12_3, w2_1, w2_2],
+        [],
     )
     core_b = swap(second, "chan", chans, 1)
     line, across = [pair, near, far, far_near], [pair_across, across, far_near_across]
     cores = [core_a, core_b]
     shared = (where, line, across, cores)
-    parts1 = [w_0, w1_1, w1_2, w12_3]
-    own1, send1 = project(*shared, parts1, (0, 0, 0, 0), length, [])
+    parts = [w_0, w_1, w_2, w_3]
+    own1, send1 = project(*shared, parts, (0,) * 4, length, [])
     recv1 = swap(send1, "seq", seq, 1)
-    cut0_2, cut0_3, cut0_1 = cut(*inputs, [(2, (0,)), (3, (0,)), (1, (0,))], [w2_2])
     w0_2, w0_3 = swap(cut0_2, "seq", seq, 4), swap(cut0_3, "seq", seq, 6)
     w0_1 = swap(cut0_1, "seq", seq, 2)
-    parts2 = [w_0, w2_1, w2_2, w12_3]
     tables = wave_tables(length)
-    freq = spectrum(where, tables, parts2, (2 * rows, rows, rows, 2 * rows), length)
-    own2, send2 = project(*shared, parts2, (rows, 0, 0, rows), length, [freq])
+    parts0 = [w_0, w0_1, w0_2, w0_3]
+    freq = spectrum(
+        where, tables, [w_0, w0_1, w0_2, w_3], (3 * rows, rows, rows, 2 * rows), length
+    )
+    own2, send2 = project(*shared, parts, (rows,) * 4, length, [])
     recv2 = swap(send2, "seq", seq, 1)
-    lows = (2 * rows + lags, 0, 0, 0)
-    own0, send0 = project(*shared, [w_0, w0_1, w0_2, w0_3], lows, length, [])
+    own0, send0 = project(*shared, parts0, (2 * rows, 0, 0, 0), length, [])
     recv0 = swap(send0, "seq", seq, 1)
     mixed, held = mix(
         where,

time: 185 us -> 179 us (0.968)
  starting transfers between devices: 57.8 us -> 45 us
  waiting for transfers between devices: 88.7 us -> 96.2 us
    ppermute x32 -> x28, starting transfers between devices: 57.8 us -> 45 us  [swap(): return lax.ppermute(value, axis, [(i, i ^ turn) for i in range(count)])]
    ppermute x32 -> x28, waiting for transfers between devices: 88.7 us -> 96.2 us  [swap(): return lax.ppermute(value, axis, [(i, i ^ turn) for i in range(count)])]
  transfers between devices with their start and end apart: 32 -> 28, of which waited for: 16 -> 13; matrix products, arithmetic and copies ran while one was open for 0% -> 0% of each run, Pallas kernels for 15% -> 15%
where the time goes in v5:
time: 179 us
  waiting for transfers between devices  96.2 us (54%)
  starting transfers between devices  45 us (25%)
  Pallas kernels  33 us (18%)
  local copies, waits for them, and re-layouts  2.9 us (2%)
    ppermute x28, waiting for transfers between devices, swap(): return lax.ppermute(value, axis, [(i, i ^ turn) for i in range(count)])  96.2 us
    ppermute x28, starting transfers between devices, swap(): return lax.ppermute(value, axis, [(i, i ^ turn) for i in range(count)])  45 us
    pallas_call x3, Pallas kernels, project(): pl.pallas_call(functools.partial(project_kernel, lows=lows, after=len(aft...  9.06 us
    pallas_call x1, Pallas kernels, mix(): pl.pallas_call(functools.partial(mix_kernel, after=len(after)), out_shape...  8.65 us
    pallas_call x4, Pallas kernels, emit(): pl.pallas_call(functools.partial(emit_kernel, turns=turns, added=len(extr...  5.62 us
    pallas_call x1, Pallas kernels, halve(): pl.pallas_call(functools.partial(halve_kernel, turns=turns, names=names),...  3.59 us
  transfers between devices with their start and end apart: 28, of which 13 were waited for; matrix products, arithmetic and copies ran while one was open for 0% of the time, Pallas kernels for 15%

profile of v5, /device:TPU:0, one launch (start us, length us, event | category | flops | bytes accessed | tf_op | source)
XLA Modules:
  0.0 179.1 jit_solution(18162738627212775854)
XLA Ops:
  0.6 3.6 %halve.1 = (bf16[256,512]{1,0:T(8,128)(2,1)}, bf16[512,512]{1,0:T(8,128)(2,1)}, bf16[1024,256]{1,0:T(8,128)(2,1)}, bf16[1024,256]{1,0:T(8,128)(2,1)}) custom-call(s32[2]{0:T(128)} %pad_add_fusion.where_ref, bf16[256,1024]{1,0:T(8,128)(2,1)} %tokens.1, bf16[256,1024]{1,0:T(8,128)(2,1)} %filters.3, bf16[3,512,1024]{2,1,0:T(8,128)(2,1)} %bitcast.4), custom_call_target="tpu_custom_call" | custom-call | tf_op jit(solution)/shard_map/halve/pallas_call | solution.py:202
  4.2 3.0 %collective-permute-start = (bf16[512,512]{1,0:T(8,128)(2,1)}, bf16[512,512]{1,0:T(8,128)(2,1)S(1)}, u32[]{:S(2)}, u32[]{:S(2)}) collective-permute-start(bf16[512,512]{1,0:T(8,128)(2,1)} %get-tuple-element.31), channel_id=1, source_target_pairs={{0,4},{4,0},{8,12},{12,8},{16,20},{20,16},{24,28},{28,24},{1,5},{5... | collective-permute-start | bytes 1572872 | tf_op jit(solution)/shard_map/ppermute | solution.py:628
  7.2 2.6 %collective-permute-start.5 = (bf16[1024,256]{1,0:T(8,128)(2,1)}, bf16[1024,256]{1,0:T(8,128)(2,1)S(1)}, u32[]{:S(2)}, u32[]{:S(2)}) collective-permute-start(bf16[1024,256]{1,0:T(8,128)(2,1)} %get-tuple-element.33), channel_id=1, source_target_pairs={{0,16},{4,20},{8,24},{12,28},{16,0},{20,4},{24,8},{28,12},{1,17},{... | collective-permute-start | bytes 1572872 | tf_op jit(solution)/shard_map/ppermute | solution.py:628
  9.8 1.6 collective-permute-start.6
  11.4 8.0 %collective-permute-done.refs_1_.filter_beside = bf16[512,512]{1,0:T(8,128)(2,1)S(1)} collective-permute-done((bf16[512,512]{1,0:T(8,128)(2,1)}, bf16[512,512]{1,0:T(8,128)(2,1)S(1)}, u32[]{:S(2)}, u32[]{:S(2)}) %collective-permute-start) | collective-permute-done | bytes 524320 | tf_op jit(solution)/shard_map/ppermute | solution.py:628
  20.3 1.9 %collective-permute-start.1 = (bf16[512,512]{1,0:T(8,128)(2,1)S(1)}, bf16[512,512]{1,0:T(8,128)(2,1)S(1)}, u32[]{:S(2)}, u32[]{:S(2)}) collective-permute-start(bf16[512,512]{1,0:T(8,128)(2,1)S(1)} %join.4.refs_0_), channel_id=1, source_target_pairs={{0,8},{4,12},{8,0},{12,4},{16,24},{20,28},{24,16},{28,20},{1,9},{5... | collective-permute-start | bytes 1572872 | tf_op jit(solution)/shard_map/ppermute | solution.py:628
  22.2 2.6 %collective-permute-start.2 = (bf16[512,512]{1,0:T(8,128)(2,1)S(1)}, bf16[512,512]{1,0:T(8,128)(2,1)S(1)}, u32[]{:S(2)}, u32[]{:S(2)}) collective-permute-start(bf16[512,512]{1,0:T(8,128)(2,1)S(1)} %join.4.refs_0_), channel_id=1, source_target_pairs={{0,16},{4,20},{8,24},{12,28},{16,0},{20,4},{24,8},{28,12},{1,17},{... | collective-permute-start | bytes 1572872 | tf_op jit(solution)/shard_map/ppermute | solution.py:628
  24.8 1.5 collective-permute-start.4
  26.4 1.9 %copy-done = bf16[512,3,1024]{2,0,1:T(8,128)(2,1)S(1)} copy-done((bf16[512,3,1024]{2,0,1:T(8,128)(2,1)S(1)}, bf16[512,3,1024]{2,0,1:T(8,128)(2,1)}, u32[]{:S(2)}) %copy-start) | copy-done | bytes 3145752
  29.5 4.8 %collective-permute-done.5.refs_4_.refs_11_ = bf16[1024,256]{1,0:T(8,128)(2,1)S(1)} collective-permute-done((bf16[1024,256]{1,0:T(8,128)(2,1)}, bf16[1024,256]{1,0:T(8,128)(2,1)S(1)}, u32[]{:S(2)}, u32[]{:S(2)}) %collective-permute-start.5) | collective-permute-done | bytes 524320 | tf_op jit(solution)/shard_map/ppermute | solution.py:628
  34.2 11.5 %collective-permute-done.6.refs_5_.refs_10_ = bf16[1024,256]{1,0:T(8,128)(2,1)S(1)} collective-permute-done((bf16[1024,256]{1,0:T(8,128)(2,1)}, bf16[1024,256]{1,0:T(8,128)(2,1)S(1)}, u32[]{:S(2)}, u32[]{:S(2)}) %collective-permute-start.6) | collective-permute-done | bytes 524320 | tf_op jit(solution)/shard_map/ppermute | solution.py:628
  45.7 10.0 %collective-permute-done.1.refs_1_.refs_2_ = bf16[512,512]{1,0:T(8,128)(2,1)S(1)} collective-permute-done((bf16[512,512]{1,0:T(8,128)(2,1)S(1)}, bf16[512,512]{1,0:T(8,128)(2,1)S(1)}, u32[]{:S(2)}, u32[]{:S(2)}) %collective-permute-start.1) | collective-permute-done | bytes 524320 | tf_op jit(solution)/shard_map/ppermute | solution.py:628
  55.8 1.6 collective-permute-start.7
  58.7 2.5 %collective-permute-start.9 = (bf16[1280,256]{1,0:T(8,128)(2,1)S(1)}, bf16[1280,256]{1,0:T(8,128)(2,1)S(1)}, u32[]{:S(2)}, u32[]{:S(2)}) collective-permute-start(bf16[1280,256]{1,0:T(8,128)(2,1)S(1)} %get-tuple-element.32.refs_3_), channel_id=1, source_target_pairs={{0,24},{4,28},{8,16},{12,20},{16,8},{20,12},{24,0},{28,4},{1,25},{... | collective-permute-start | bytes 1966088 | tf_op jit(solution)/shard_map/ppermute | solution.py:628
  61.2 9.9 %collective-permute-done.3.refs_2_.refs_3_ = bf16[512,512]{1,0:T(8,128)(2,1)S(1)} collective-permute-done((bf16[512,512]{1,0:T(8,128)(2,1)S(1)}, bf16[512,512]{1,0:T(8,128)(2,1)S(1)}, u32[]{:S(2)}, u32[]{:S(2)}) %collective-permute-start.3) | collective-permute-done | bytes 524320 | tf_op jit(solution)/shard_map/ppermute | solution.py:628
  71.6 14.0 %collective-permute-done.9.refs_4_.refs_12_.refs_3_ = bf16[1280,256]{1,0:T(8,128)(2,1)S(1)} collective-permute-done((bf16[1280,256]{1,0:T(8,128)(2,1)S(1)}, bf16[1280,256]{1,0:T(8,128)(2,1)S(1)}, u32[]{:S(2)}, u32[]{:S(2)}) %collective-permute-start.9) | collective-permute-done | bytes 655392 | tf_op jit(solution)/shard_map/ppermute | solution.py:628
  85.8 5.3 %collective-permute-done.8.refs_3_.refs_6_ = bf16[512,512]{1,0:T(8,128)(2,1)S(1)} collective-permute-done((bf16[512,512]{1,0:T(8,128)(2,1)S(1)}, bf16[512,512]{1,0:T(8,128)(2,1)S(1)}, u32[]{:S(2)}, u32[]{:S(2)}) %collective-permute-start.8) | collective-permute-done | bytes 524320 | tf_op jit(solution)/shard_map/ppermute | solution.py:628
  92.5 4.8 %collective-permute-start.15 = (bf16[768,256]{1,0:T(8,128)(2,1)S(1)}, bf16[768,256]{1,0:T(8,128)(2,1)S(1)}, u32[]{:S(2)}, u32[]{:S(2)}) collective-permute-start(bf16[768,256]{1,0:T(8,128)(2,1)S(1)} %get-tuple-element.41), channel_id=1, source_target_pairs={{0,16},{4,20},{8,24},{12,28},{16,0},{20,4},{24,8},{28,12},{1,17},{... | collective-permute-start | bytes 1179656 | tf_op jit(solution)/shard_map/ppermute | solution.py:628
  97.3 3.0 %project.3 = (f32[2048,128]{1,0:T(8,128)S(1)}, bf16[2048,128]{1,0:T(8,128)(2,1)S(1)}) custom-call(s32[2]{0:T(128)S(1)} %copy-done.7, bf16[512,512]{1,0:T(8,128)(2,1)S(1)} %join.4.refs_0_, bf16[512,512]{1,0:T(8,128)(2,1)S(1)} %collective-permute-done.1.refs_1_.refs_2_, bf16[512,512]{1,0:T(8,128)(2,1)S(1)} %collective-permute-done.2.refs_0_.refs_2_, ...), custom_call_target="tpu_custom_call" | custom-call | flops 4294967296 | bytes 8388608 | tf_op jit(solution)/shard_map/project/pallas_call | solution.py:335
  100.3 1.6 collective-permute-start.12
  101.9 3.0 %project.4 = (f32[2048,128]{1,0:T(8,128)S(1)}, bf16[2048,128]{1,0:T(8,128)(2,1)S(1)}) custom-call(s32[2]{0:T(128)S(1)} %copy-done.7, bf16[512,512]{1,0:T(8,128)(2,1)S(1)} %join.4.refs_0_, bf16[512,512]{1,0:T(8,128)(2,1)S(1)} %collective-permute-done.1.refs_1_.refs_2_, bf16[512,512]{1,0:T(8,128)(2,1)S(1)} %collective-permute-done.2.refs_0_.refs_2_, ...), custom_call_target="tpu_custom_call" | custom-call | flops 4294967296 | bytes 8388608 | tf_op jit(solution)/shard_map/project/pallas_call | solution.py:335
  105.5 15.0 %collective-permute-done.16.refs_12_ = bf16[512,256]{1,0:T(8,128)(2,1)S(1)} collective-permute-done((bf16[512,256]{1,0:T(8,128)(2,1)S(1)}, bf16[512,256]{1,0:T(8,128)(2,1)S(1)}, u32[]{:S(2)}, u32[]{:S(2)}) %collective-permute-start.16) | collective-permute-done | bytes 262176 | tf_op jit(solution)/shard_map/ppermute | solution.py:628
  121.2 3.0 %project.5 = (f32[2048,128]{1,0:T(8,128)S(1)}, bf16[2048,128]{1,0:T(8,128)(2,1)S(1)}) custom-call(s32[2]{0:T(128)S(1)} %copy-done.7, bf16[512,512]{1,0:T(8,128)(2,1)S(1)} %join.4.refs_0_, bf16[512,512]{1,0:T(8,128)(2,1)S(1)} %collective-permute-done.1.refs_1_.refs_2_, bf16[512,512]{1,0:T(8,128)(2,1)S(1)} %collective-permute-done.2.refs_0_.refs_2_, ...), custom_call_target="tpu_custom_call" | custom-call | flops 4294967296 | bytes 8388608 | tf_op jit(solution)/shard_map/project/pallas_call | solution.py:335
  124.3 1.6 collective-permute-start.17
  125.9 3.6 %spectrum.1.freq_ref = f32[4224,128]{1,0:T(8,128)S(1)} custom-call(s32[2]{0:T(128)S(1)} %copy-done.7, bf16[80,32]{1,0:T(8,128)(2,1)S(1)} %copy-done.6, bf16[33,128,128]{2,1,0:T(8,128)(2,1)S(1)} %copy-done.1, bf16[1792,256]{1,0:T(8,128)(2,1)S(1)} %get-tuple-element.35.refs_9_.refs_0_, bf16[768,256]{1,0:T(8,128)(2,1)S(1)} %collective-permute-done.14.refs_1_.refs_10_, ...), custom_call_target="tpu_custom_call" | custom-call | flops 67108864 | bytes 1048576 | tf_op jit(solution)/shard_map/spectrum/pallas_call | solution.py:423
  129.5 8.6 %mix.1 = (f32[2048,128]{1,0:T(8,128)S(1)}, bf16[1024,4096]{1,0:T(8,128)(2,1)S(1)}) custom-call(s32[2]{0:T(128)S(1)} %copy-done.7, f32[2048,128]{1,0:T(8,128)S(1)} %get-tuple-element.36.own1, bf16[2048,128]{1,0:T(8,128)(2,1)S(1)} %collective-permute-done.12.recv1, f32[2048,128]{1,0:T(8,128)S(1)} %get-tuple-element.38.own2, ...), custom_call_target="tpu_custom_call" | custom-call | flops 201326592 | bytes 6291456 | tf_op jit(solution)/shard_map/mix/pallas_call | solution.py:525
  139.9 6.3 %collective-permute-start.19 = (bf16[256,128]{1,0:T(8,128)(2,1)S(1)}, bf16[256,128]{1,0:T(8,128)(2,1)S(1)}, u32[]{:S(2)}, u32[]{:S(2)}) collective-permute-start(bf16[256,128]{1,0:T(8,128)(2,1)S(1)} %get-tuple-element.49), channel_id=1, source_target_pairs={{0,8},{4,12},{8,0},{12,4},{16,24},{20,28},{24,16},{28,20},{1,9},{5... | collective-permute-start | bytes 196616 | tf_op jit(solution)/shard_map/ppermute | solution.py:628
  146.5 2.9 %collective-permute-start.21 = (bf16[256,128]{1,0:T(8,128)(2,1)S(1)}, bf16[256,128]{1,0:T(8,128)(2,1)S(1)}, u32[]{:S(2)}, u32[]{:S(2)}) collective-permute-start(bf16[256,128]{1,0:T(8,128)(2,1)S(1)} %get-tuple-element.51), channel_id=1, source_target_pairs={{0,16},{4,20},{8,24},{12,28},{16,0},{20,4},{24,8},{28,12},{1,17},{... | collective-permute-start | bytes 196616 | tf_op jit(solution)/shard_map/ppermute | solution.py:628
  150.0 2.2 %collective-permute-start.23 = (bf16[256,128]{1,0:T(8,128)(2,1)S(1)}, bf16[256,128]{1,0:T(8,128)(2,1)S(1)}, u32[]{:S(2)}, u32[]{:S(2)}) collective-permute-start(bf16[256,128]{1,0:T(8,128)(2,1)S(1)} %get-tuple-element.53), channel_id=1, source_target_pairs={{0,24},{4,28},{8,16},{12,20},{16,8},{20,12},{24,0},{28,4},{1,25},{... | collective-permute-start | bytes 196616 | tf_op jit(solution)/shard_map/ppermute | solution.py:628
  152.2 1.9 %collective-permute-start.24 = (bf16[256,128]{1,0:T(8,128)(2,1)S(1)}, bf16[256,128]{1,0:T(8,128)(2,1)S(1)}, u32[]{:S(2)}, u32[]{:S(2)}) collective-permute-start(bf16[256,128]{1,0:T(8,128)(2,1)S(1)} %get-tuple-element.54), channel_id=1, source_target_pairs={{0,28},{4,24},{8,20},{12,16},{16,12},{20,8},{24,4},{28,0},{1,29},{... | collective-permute-start | bytes 196616 | tf_op jit(solution)/shard_map/ppermute | solution.py:628
  154.1 2.6 %collective-permute-done.21.refs_4_ = bf16[256,128]{1,0:T(8,128)(2,1)S(1)} collective-permute-done((bf16[256,128]{1,0:T(8,128)(2,1)S(1)}, bf16[256,128]{1,0:T(8,128)(2,1)S(1)}, u32[]{:S(2)}, u32[]{:S(2)}) %collective-permute-start.21) | collective-permute-done | bytes 65568 | tf_op jit(solution)/shard_map/ppermute | solution.py:628
  166.2 12.0 %collective-permute-done.27 = bf16[256,1024]{1,0:T(8,128)(2,1)S(1)} collective-permute-done((bf16[256,1024]{1,0:T(8,128)(2,1)S(1)}, bf16[256,1024]{1,0:T(8,128)(2,1)S(1)}, u32[]{:S(2)}, u32[]{:S(2)}) %collective-permute-start.27) | collective-permute-done | bytes 524320 | tf_op jit(solution)/shard_map/ppermute | solution.py:628
  (67 shorter events, 20.6 us)
Async XLA Ops:
  0.6 25.7 %copy-start.2 = (bf16[256,1024]{1,0:T(8,128)(2,1)S(1)}, bf16[256,1024]{1,0:T(8,128)(2,1)}, u32[]{:S(2)}) copy-start(bf16[256,1024]{1,0:T(8,128)(2,1)} %filters.3) | copy-start | bytes 1572868
  0.6 25.7 %copy-start.7 = (s32[2]{0:T(128)S(1)}, s32[2]{0:T(128)}, u32[]{:S(2)}) copy-start(s32[2]{0:T(128)} %pad_add_fusion.where_ref) | copy-start | bytes 28
  4.2 15.1 %collective-permute-start = (bf16[512,512]{1,0:T(8,128)(2,1)}, bf16[512,512]{1,0:T(8,128)(2,1)S(1)}, u32[]{:S(2)}, u32[]{:S(2)}) collective-permute-start(bf16[512,512]{1,0:T(8,128)(2,1)} %get-tuple-element.31), channel_id=1, source_target_pairs={{0,4},{4,0},{8,12},{12,8},{16,20},{20,16},{24,28},{28,24},{1,5},{5... | collective-permute-start | bytes 1572872 | tf_op jit(solution)/shard_map/ppermute | solution.py:628
  7.2 27.0 %collective-permute-start.5 = (bf16[1024,256]{1,0:T(8,128)(2,1)}, bf16[1024,256]{1,0:T(8,128)(2,1)S(1)}, u32[]{:S(2)}, u32[]{:S(2)}) collective-permute-start(bf16[1024,256]{1,0:T(8,128)(2,1)} %get-tuple-element.33), channel_id=1, source_target_pairs={{0,16},{4,20},{8,24},{12,28},{16,0},{20,4},{24,8},{28,12},{1,17},{... | collective-permute-start | bytes 1572872 | tf_op jit(solution)/shard_map/ppermute | solution.py:628
  9.8 35.9 %collective-permute-start.6 = (bf16[1024,256]{1,0:T(8,128)(2,1)}, bf16[1024,256]{1,0:T(8,128)(2,1)S(1)}, u32[]{:S(2)}, u32[]{:S(2)}) collective-permute-start(bf16[1024,256]{1,0:T(8,128)(2,1)} %get-tuple-element.34), channel_id=1, source_target_pairs={{0,8},{4,12},{8,0},{12,4},{16,24},{20,28},{24,16},{28,20},{1,9},{5... | collective-permute-start | bytes 1572872 | tf_op jit(solution)/shard_map/ppermute | solution.py:628
  20.3 35.4 %collective-permute-start.1 = (bf16[512,512]{1,0:T(8,128)(2,1)S(1)}, bf16[512,512]{1,0:T(8,128)(2,1)S(1)}, u32[]{:S(2)}, u32[]{:S(2)}) collective-permute-start(bf16[512,512]{1,0:T(8,128)(2,1)S(1)} %join.4.refs_0_), channel_id=1, source_target_pairs={{0,8},{4,12},{8,0},{12,4},{16,24},{20,28},{24,16},{28,20},{1,9},{5... | collective-permute-start | bytes 1572872 | tf_op jit(solution)/shard_map/ppermute | solution.py:628
  22.2 33.5 %collective-permute-start.2 = (bf16[512,512]{1,0:T(8,128)(2,1)S(1)}, bf16[512,512]{1,0:T(8,128)(2,1)S(1)}, u32[]{:S(2)}, u32[]{:S(2)}) collective-permute-start(bf16[512,512]{1,0:T(8,128)(2,1)S(1)} %join.4.refs_0_), channel_id=1, source_target_pairs={{0,16},{4,20},{8,24},{12,28},{16,0},{20,4},{24,8},{28,12},{1,17},{... | collective-permute-start | bytes 1572872 | tf_op jit(solution)/shard_map/ppermute | solution.py:628
  24.8 30.9 %collective-permute-start.4 = (bf16[512,512]{1,0:T(8,128)(2,1)S(1)}, bf16[512,512]{1,0:T(8,128)(2,1)S(1)}, u32[]{:S(2)}, u32[]{:S(2)}) collective-permute-start(bf16[512,512]{1,0:T(8,128)(2,1)S(1)} %join.4.refs_0_), channel_id=1, source_target_pairs={{0,2},{1,3},{2,0},{3,1},{4,6},{5,7},{6,4},{7,5},{8,10},{9,11},{10,... | collective-permute-start | bytes 1572872 | tf_op jit(solution)/shard_map/ppermute | solution.py:628
  55.8 29.8 %collective-permute-start.7 = (bf16[1024,512]{1,0:T(8,128)(2,1)S(1)}, bf16[1024,512]{1,0:T(8,128)(2,1)S(1)}, u32[]{:S(2)}, u32[]{:S(2)}) collective-permute-start(bf16[1024,512]{1,0:T(8,128)(2,1)S(1)} %join.5), channel_id=1, source_target_pairs={{0,2},{1,3},{2,0},{3,1},{4,6},{5,7},{6,4},{7,5},{8,10},{9,11},{10,... | collective-permute-start | bytes 3145736 | tf_op jit(solution)/shard_map/ppermute | solution.py:628
  57.4 13.7 %collective-permute-start.3 = (bf16[512,512]{1,0:T(8,128)(2,1)S(1)}, bf16[512,512]{1,0:T(8,128)(2,1)S(1)}, u32[]{:S(2)}, u32[]{:S(2)}) collective-permute-start(bf16[512,512]{1,0:T(8,128)(2,1)S(1)} %collective-permute-done.2.refs_0_.refs_2_), channel_id=1, source_target_pairs={{0,8},{4,12},{8,0},{12,4},{16,24},{20,28},{24,16},{28,20},{1,9},{5... | collective-permute-start | bytes 1572872 | tf_op jit(solution)/shard_map/ppermute | solution.py:628
  58.7 26.9 %collective-permute-start.9 = (bf16[1280,256]{1,0:T(8,128)(2,1)S(1)}, bf16[1280,256]{1,0:T(8,128)(2,1)S(1)}, u32[]{:S(2)}, u32[]{:S(2)}) collective-permute-start(bf16[1280,256]{1,0:T(8,128)(2,1)S(1)} %get-tuple-element.32.refs_3_), channel_id=1, source_target_pairs={{0,24},{4,28},{8,16},{12,20},{16,8},{20,12},{24,0},{28,4},{1,25},{... | collective-permute-start | bytes 1966088 | tf_op jit(solution)/shard_map/ppermute | solution.py:628
  71.1 20.0 %collective-permute-start.8 = (bf16[512,512]{1,0:T(8,128)(2,1)S(1)}, bf16[512,512]{1,0:T(8,128)(2,1)S(1)}, u32[]{:S(2)}, u32[]{:S(2)}) collective-permute-start(bf16[512,512]{1,0:T(8,128)(2,1)S(1)} %collective-permute-done.3.refs_2_.refs_3_), channel_id=1, source_target_pairs={{0,2},{1,3},{2,0},{3,1},{4,6},{5,7},{6,4},{7,5},{8,10},{9,11},{10,... | collective-permute-start | bytes 1572872 | tf_op jit(solution)/shard_map/ppermute | solution.py:628
  85.7 11.5 %collective-permute-start.10 = (bf16[2048,512]{1,0:T(8,128)(2,1)S(1)}, bf16[2048,512]{1,0:T(8,128)(2,1)S(1)}, u32[]{:S(2)}, u32[]{:S(2)}) collective-permute-start(bf16[2048,512]{1,0:T(8,128)(2,1)S(1)} %join.6), channel_id=1, source_target_pairs={{0,1},{1,0},{2,3},{3,2},{4,5},{5,4},{6,7},{7,6},{8,9},{9,8},{10,11... | collective-permute-start | bytes 6291464 | tf_op jit(solution)/shard_map/ppermute | solution.py:628
  91.2 6.0 %collective-permute-start.11 = (bf16[2048,512]{1,0:T(8,128)(2,1)S(1)}, bf16[2048,512]{1,0:T(8,128)(2,1)S(1)}, u32[]{:S(2)}, u32[]{:S(2)}) collective-permute-start(bf16[2048,512]{1,0:T(8,128)(2,1)S(1)} %join.7), channel_id=1, source_target_pairs={{0,1},{1,0},{2,3},{3,2},{4,5},{5,4},{6,7},{7,6},{8,9},{9,8},{10,11... | collective-permute-start | bytes 6291464 | tf_op jit(solution)/shard_map/ppermute | solution.py:628
  91.3 29.2 %collective-permute-start.14 = (bf16[768,256]{1,0:T(8,128)(2,1)S(1)}, bf16[768,256]{1,0:T(8,128)(2,1)S(1)}, u32[]{:S(2)}, u32[]{:S(2)}) collective-permute-start(bf16[768,256]{1,0:T(8,128)(2,1)S(1)} %get-tuple-element.40), channel_id=1, source_target_pairs={{0,8},{4,12},{8,0},{12,4},{16,24},{20,28},{24,16},{28,20},{1,9},{5... | collective-permute-start | bytes 1179656 | tf_op jit(solution)/shard_map/ppermute | solution.py:628
  92.5 28.8 %collective-permute-start.15 = (bf16[768,256]{1,0:T(8,128)(2,1)S(1)}, bf16[768,256]{1,0:T(8,128)(2,1)S(1)}, u32[]{:S(2)}, u32[]{:S(2)}) collective-permute-start(bf16[768,256]{1,0:T(8,128)(2,1)S(1)} %get-tuple-element.41), channel_id=1, source_target_pairs={{0,16},{4,20},{8,24},{12,28},{16,0},{20,4},{24,8},{28,12},{1,17},{... | collective-permute-start | bytes 1179656 | tf_op jit(solution)/shard_map/ppermute | solution.py:628
  97.3 23.3 %collective-permute-start.16 = (bf16[512,256]{1,0:T(8,128)(2,1)S(1)}, bf16[512,256]{1,0:T(8,128)(2,1)S(1)}, u32[]{:S(2)}, u32[]{:S(2)}) collective-permute-start(bf16[512,256]{1,0:T(8,128)(2,1)S(1)} %get-tuple-element.42), channel_id=1, source_target_pairs={{0,24},{4,28},{8,16},{12,20},{16,8},{20,12},{24,0},{28,4},{1,25},{... | collective-permute-start | bytes 786440 | tf_op jit(solution)/shard_map/ppermute | solution.py:628
  100.3 29.2 %collective-permute-start.12 = (bf16[2048,128]{1,0:T(8,128)(2,1)S(1)}, bf16[2048,128]{1,0:T(8,128)(2,1)S(1)}, u32[]{:S(2)}, u32[]{:S(2)}) collective-permute-start(bf16[2048,128]{1,0:T(8,128)(2,1)S(1)} %get-tuple-element.37), channel_id=1, source_target_pairs={{0,4},{4,0},{8,12},{12,8},{16,20},{20,16},{24,28},{28,24},{1,5},{5... | collective-permute-start | bytes 1572872 | tf_op jit(solution)/shard_map/ppermute | solution.py:628
  104.9 24.6 %slice-start = ((s8[8388608]{0:T(1024)(128)(4,1)}), s8[4194304]{0:T(1024)(128)(4,1)S(1)}, s32[]{:S(2)}) async-start(s8[8388608]{0:T(1024)(128)(4,1)} %bitcast.6), calls=%async_computation | async-start | bytes 8388608
  104.9 24.6 %slice-start.1 = ((s8[8388608]{0:T(1024)(128)(4,1)}), s8[4194304]{0:T(1024)(128)(4,1)S(1)}, s32[]{:S(2)}) async-start(s8[8388608]{0:T(1024)(128)(4,1)} %bitcast.6), calls=%async_computation.1 | async-start | bytes 8388608
  104.9 24.5 %collective-permute-start.13 = (bf16[2048,128]{1,0:T(8,128)(2,1)S(1)}, bf16[2048,128]{1,0:T(8,128)(2,1)S(1)}, u32[]{:S(2)}, u32[]{:S(2)}) collective-permute-start(bf16[2048,128]{1,0:T(8,128)(2,1)S(1)} %get-tuple-element.39), channel_id=1, source_target_pairs={{0,4},{4,0},{8,12},{12,8},{16,20},{20,16},{24,28},{28,24},{1,5},{5... | collective-permute-start | bytes 1572872 | tf_op jit(solution)/shard_map/ppermute | solution.py:628
  124.3 13.9 %collective-permute-start.17 = (bf16[2048,128]{1,0:T(8,128)(2,1)S(1)}, bf16[2048,128]{1,0:T(8,128)(2,1)S(1)}, u32[]{:S(2)}, u32[]{:S(2)}) collective-permute-start(bf16[2048,128]{1,0:T(8,128)(2,1)S(1)} %get-tuple-element.43.refs_0_), channel_id=1, source_target_pairs={{0,4},{4,0},{8,12},{12,8},{16,20},{20,16},{24,28},{28,24},{1,5},{5... | collective-permute-start | bytes 1572872 | tf_op jit(solution)/shard_map/ppermute | solution.py:628
  139.2 10.8 %collective-permute-start.18 = (bf16[256,128]{1,0:T(8,128)(2,1)S(1)}, bf16[256,128]{1,0:T(8,128)(2,1)S(1)}, u32[]{:S(2)}, u32[]{:S(2)}) collective-permute-start(bf16[256,128]{1,0:T(8,128)(2,1)S(1)} %get-tuple-element.48), channel_id=1, source_target_pairs={{0,4},{4,0},{8,12},{12,8},{16,20},{20,16},{24,28},{28,24},{1,5},{5... | collective-permute-start | bytes 196616 | tf_op jit(solution)/shard_map/ppermute | solution.py:628
  139.9 12.4 %collective-permute-start.19 = (bf16[256,128]{1,0:T(8,128)(2,1)S(1)}, bf16[256,128]{1,0:T(8,128)(2,1)S(1)}, u32[]{:S(2)}, u32[]{:S(2)}) collective-permute-start(bf16[256,128]{1,0:T(8,128)(2,1)S(1)} %get-tuple-element.49), channel_id=1, source_target_pairs={{0,8},{4,12},{8,0},{12,4},{16,24},{20,28},{24,16},{28,20},{1,9},{5... | collective-permute-start | bytes 196616 | tf_op jit(solution)/shard_map/ppermute | solution.py:628
  146.1 8.0 %collective-permute-start.20 = (bf16[256,128]{1,0:T(8,128)(2,1)S(1)}, bf16[256,128]{1,0:T(8,128)(2,1)S(1)}, u32[]{:S(2)}, u32[]{:S(2)}) collective-permute-start(bf16[256,128]{1,0:T(8,128)(2,1)S(1)} %get-tuple-element.50), channel_id=1, source_target_pairs={{0,12},{4,8},{8,4},{12,0},{16,28},{20,24},{24,20},{28,16},{1,13},{... | collective-permute-start | bytes 196616 | tf_op jit(solution)/shard_map/ppermute | solution.py:628
  146.5 10.3 %collective-permute-start.21 = (bf16[256,128]{1,0:T(8,128)(2,1)S(1)}, bf16[256,128]{1,0:T(8,128)(2,1)S(1)}, u32[]{:S(2)}, u32[]{:S(2)}) collective-permute-start(bf16[256,128]{1,0:T(8,128)(2,1)S(1)} %get-tuple-element.51), channel_id=1, source_target_pairs={{0,16},{4,20},{8,24},{12,28},{16,0},{20,4},{24,8},{28,12},{1,17},{... | collective-permute-start | bytes 196616 | tf_op jit(solution)/shard_map/ppermute | solution.py:628
  149.4 8.9 %collective-permute-start.22 = (bf16[256,128]{1,0:T(8,128)(2,1)S(1)}, bf16[256,128]{1,0:T(8,128)(2,1)S(1)}, u32[]{:S(2)}, u32[]{:S(2)}) collective-permute-start(bf16[256,128]{1,0:T(8,128)(2,1)S(1)} %get-tuple-element.52), channel_id=1, source_target_pairs={{0,20},{4,16},{8,28},{12,24},{16,4},{20,0},{24,12},{28,8},{1,21},{... | collective-permute-start | bytes 196616 | tf_op jit(solution)/shard_map/ppermute | solution.py:628
  150.0 8.3 %collective-permute-start.23 = (bf16[256,128]{1,0:T(8,128)(2,1)S(1)}, bf16[256,128]{1,0:T(8,128)(2,1)S(1)}, u32[]{:S(2)}, u32[]{:S(2)}) collective-permute-start(bf16[256,128]{1,0:T(8,128)(2,1)S(1)} %get-tuple-element.53), channel_id=1, source_target_pairs={{0,24},{4,28},{8,16},{12,20},{16,8},{20,12},{24,0},{28,4},{1,25},{... | collective-permute-start | bytes 196616 | tf_op jit(solution)/shard_map/ppermute | solution.py:628
  152.2 7.1 %collective-permute-start.24 = (bf16[256,128]{1,0:T(8,128)(2,1)S(1)}, bf16[256,128]{1,0:T(8,128)(2,1)S(1)}, u32[]{:S(2)}, u32[]{:S(2)}) collective-permute-start(bf16[256,128]{1,0:T(8,128)(2,1)S(1)} %get-tuple-element.54), channel_id=1, source_target_pairs={{0,28},{4,24},{8,20},{12,16},{16,12},{20,8},{24,4},{28,0},{1,29},{... | collective-permute-start | bytes 196616 | tf_op jit(solution)/shard_map/ppermute | solution.py:628
  160.7 2.1 %collective-permute-start.26 = (bf16[256,1024]{1,0:T(8,128)(2,1)S(1)}, bf16[256,1024]{1,0:T(8,128)(2,1)S(1)}, u32[]{:S(2)}, u32[]{:S(2)}) collective-permute-start(bf16[256,1024]{1,0:T(8,128)(2,1)S(1)} %emit.6), channel_id=1, source_target_pairs={{0,1},{1,0},{2,3},{3,2},{4,5},{5,4},{6,7},{7,6},{8,9},{9,8},{10,11... | collective-permute-start | bytes 1572872 | tf_op jit(solution)/shard_map/ppermute | solution.py:628
  162.2 2.6 %collective-permute-start.25 = (bf16[256,1024]{1,0:T(8,128)(2,1)S(1)}, bf16[256,1024]{1,0:T(8,128)(2,1)S(1)}, u32[]{:S(2)}, u32[]{:S(2)}) collective-permute-start(bf16[256,1024]{1,0:T(8,128)(2,1)S(1)} %emit.4), channel_id=1, source_target_pairs={{0,1},{1,0},{2,3},{3,2},{4,5},{5,4},{6,7},{7,6},{8,9},{9,8},{10,11... | collective-permute-start | bytes 1572872 | tf_op jit(solution)/shard_map/ppermute | solution.py:628
  164.2 14.0 %collective-permute-start.27 = (bf16[256,1024]{1,0:T(8,128)(2,1)S(1)}, bf16[256,1024]{1,0:T(8,128)(2,1)S(1)}, u32[]{:S(2)}, u32[]{:S(2)}) collective-permute-start(bf16[256,1024]{1,0:T(8,128)(2,1)S(1)} %emit.7), channel_id=1, source_target_pairs={{0,2},{1,3},{2,0},{3,1},{4,6},{5,7},{6,4},{7,5},{8,10},{9,11},{10,... | collective-permute-start | bytes 1572872 | tf_op jit(solution)/shard_map/ppermute | solution.py:628
  (8 other events, 65.7 us)

commit v6 on v5

--- a/solution.py
+++ b/solution.py
@@ -164,7 +164,7 @@
     )
 
 
-def halve_kernel(where_ref, tokens, filters, weight, ours, theirs, *refs, turns, names):
+def halve_kernel(where_ref, tokens, filters, weight, ours, theirs, *refs, plan):
     pieces, sems = refs[:-1], refs[-1]
     depth, side = where_ref[0] // 2, where_ref[0] % 2
     rows, half = ours.shape
@@ -183,7 +183,7 @@
         target = theirs.at[pl.ds(rows, filters.shape[0]), pl.ds(i * part, part)]
         copy(filters, 2 * i + 1 - side, part, target)
     depth_rows = weight.shape[1]
-    for turn, piece in zip(turns, pieces, strict=True):
+    for piece, (turn, names) in zip(pieces, plan, strict=True):
         for i, name in enumerate(names):
             target = piece.at[pl.ds(i * depth_rows, depth_rows), :]
             copy(weight.at[name], jnp.bitwise_xor(depth, turn), piece.shape[1], target)
@@ -193,23 +193,26 @@
         one.wait()
 
 
-def halve(where, tokens, filters, weight, turns, names):
+def halve(where, tokens, filters, weight, plan):
     rows, half = tokens.shape[0], tokens.shape[1] // 2
-    piece = jax.ShapeDtypeStruct(
-        (len(names) * weight.shape[1], weight.shape[2] // 4), weight.dtype
+    pieces = tuple(
+        jax.ShapeDtypeStruct((len(names) * weight.shape[1], weight.shape[2] // 4), weight.dtype)
+        for _, names in plan
     )
     vmem = pl.BlockSpec(memory_space=pltpu.VMEM)
     return pl.pallas_call(
-        functools.partial(halve_kernel, turns=turns, names=names),
+        functools.partial(halve_kernel, plan=plan),
         out_shape=(
             jax.ShapeDtypeStruct((rows, half), tokens.dtype),
             jax.ShapeDtypeStruct((rows + filters.shape[0], half), tokens.dtype),
         )
-        + (piece,) * len(turns),
+        + pieces,
         in_specs=[pl.BlockSpec(memory_space=pltpu.SMEM)]
         + [pl.BlockSpec(memory_space=pl.ANY)] * 3,
-        out_specs=(vmem,) * (2 + len(turns)),
-        scratch_shapes=[pltpu.SemaphoreType.DMA((6 + len(turns) * len(names),))],
+        out_specs=(vmem,) * (2 + len(plan)),
+        scratch_shapes=[
+            pltpu.SemaphoreType.DMA((6 + sum(len(names) for _, names in plan),))
+        ],
         compiler_params=pltpu.CompilerParams(vmem_limit_bytes=61 * 2**20),
         name="halve",
     )(where, tokens, filters, weight)
@@ -393,7 +396,8 @@
 
 
 def spectrum_kernel(where_ref, ahead, middle, *refs, lows):
-    filters, freq_ref, lags, waves = refs[:4], refs[4], refs[5], refs[6]
+    filters = refs[:4]
+    freq_ref, lags, waves = refs[len(refs) - 3 :]
     place = where_ref[0]
     length, width = lags.shape
     block = length // 8
@@ -415,7 +419,7 @@
     lax.fori_loop(0, rows, one, 0, unroll=unroll_of(rows))
 
 
-def spectrum(where, tables, filters, lows, length):
+def spectrum(where, tables, filters, lows, length, after):
     ahead, middle = tables[:2]
     rows, two = middle.shape[:2]
     width = filters[0].shape[1] // 2
@@ -423,7 +427,9 @@
     return pl.pallas_call(
         functools.partial(spectrum_kernel, lows=lows),
         out_shape=jax.ShapeDtypeStruct((rows * two, width), jnp.float32),
-        in_specs=[pl.BlockSpec(memory_space=pltpu.SMEM)] + [vmem] * 6,
+        in_specs=[pl.BlockSpec(memory_space=pltpu.SMEM)]
+        + [vmem] * 6
+        + [pl.BlockSpec(memory_space=pl.ANY)] * len(after),
         out_specs=vmem,
         scratch_shapes=[
             pltpu.VMEM((length, width), jnp.float32),
@@ -434,7 +440,7 @@
             flops=2 * 2 * length * inner_len * width, bytes_accessed=2**20, transcendentals=0
         ),
         name="spectrum",
-    )(where, ahead, middle, *filters)
+    )(where, ahead, middle, *filters, *after)
 
 
 def mix_kernel(
@@ -582,16 +588,16 @@
     )(where, own0, recv0, mixed, taps)
 
 
-def emit_kernel(where_ref, weight, *refs, turns, added):
+def emit_kernel(where_ref, weight, *refs, order, turns, added):
     parts, extra = refs[:8], refs[8 : 8 + added]
     outs, joined = refs[8 + added : -1], refs[-1]
     place, chan = where_ref[0], where_ref[1]
     width = parts[0].shape[1]
     columns = outs[0].shape[1]
     tile = 256
-    for i in range(8):
-        start = pl.multiple_of(jnp.bitwise_xor(place, i) * width, width)
-        joined[:, pl.ds(start, width)] = parts[i][...]
+    for part, source in zip(parts, order, strict=True):
+        start = pl.multiple_of(jnp.bitwise_xor(place, source) * width, width)
+        joined[:, pl.ds(start, width)] = part[...]
     for i, turn in enumerate(turns):
         for low in range(0, columns, tile):
             start = pl.multiple_of(jnp.bitwise_xor(chan, turn) * columns + low, tile)
@@ -603,13 +609,13 @@
             outs[i][:, low : low + tile] = total.astype(outs[i].dtype)
 
 
-def emit(where, parts, weight, turns, extra, out_dtype):
+def emit(where, parts, order, weight, turns, extra, out_dtype):
     rows, width = parts[0].shape
     columns = weight.shape[1] // 4
     vmem = pl.BlockSpec(memory_space=pltpu.VMEM)
     shape = jax.ShapeDtypeStruct((rows, columns), out_dtype)
     return pl.pallas_call(
-        functools.partial(emit_kernel, turns=turns, added=len(extra)),
+        functools.partial(emit_kernel, order=order, turns=turns, added=len(extra)),
         out_shape=(shape,) * len(turns),
         in_specs=[pl.BlockSpec(memory_space=pltpu.SMEM)] + [vmem] * (9 + len(extra)),
         out_specs=(vmem,) * len(turns),
@@ -641,31 +647,34 @@
     lags = tokens.shape[0]
     rows = in_weight.shape[0]
 
-    ours, theirs, cut_2, cut_1 = halve(where, tokens, long_filter, weight, (2, 1), (1, 2))
+    ours, theirs, cut1_2, cut_1 = halve(
+        where, tokens, long_filter, weight, [(2, (1,)), (1, (1, 2))]
+    )
     beside = swap(theirs, "seq", seq, 1)
-    w_2, w_1 = swap(cut_2, "seq", seq, 4), swap(cut_1, "seq", seq, 2)
+    w1_2, w_1 = swap(cut1_2, "seq", seq, 4), swap(cut_1, "seq", seq, 2)
     whole = [(0, 0, lags), (1, 0, lags)]
-    (pair,) = join([ours, beside], [whole], [])
+    (pair,) = join([ours, beside], [whole], [w1_2])
     far = swap(pair, "seq", seq, 4)
     near = swap(pair, "seq", seq, 2)
     pair_across = swap(pair, "chan", chans, 2)
     inputs = (where, weight, long_filter, beside)
     plan = [(0, (1, 2, 0, "f")), (3, (1, 2, "f"))]
-    plan += [(2, (0, "f")), (3, (0,)), (1, (0, "f"))]
-    w_0, cut_3, cut0_2, cut0_3, cut0_1 = cut(*inputs, plan, [pair])
+    plan += [(2, (0, "f")), (3, (0,)), (1, (0, "f")), (2, (2,))]
+    w_0, cut_3, cut0_2, cut0_3, cut0_1, cut2_2 = cut(*inputs, plan, [pair])
     (far_and_near,) = join(
         [far, near],
         [[(0, 0, 2 * lags), (1, 0, 2 * lags)]],
-        [pair_across, cut_3, w_2, w_1],
+        [pair_across, cut_3, w_1],
     )
     w_3 = swap(cut_3, "seq", seq, 6)
+    w2_2 = swap(cut2_2, "seq", seq, 4)
     far_near = swap(far, "seq", seq, 2)
     across = swap(far_and_near, "chan", chans, 2)
     every = [(0, 0, 2 * lags), (1, 0, 2 * lags)]
     (first,) = join(
         [pair, pair_across, near, across],
         [every + [(2, 0, 2 * lags), (3, 2 * lags, 2 * lags)]],
-        [w_3],
+        [w_3, w2_2],
     )
     core_a = swap(first, "chan", chans, 1)
     far_near_across = swap(far_near, "chan", chans, 2)
@@ -678,18 +687,17 @@
     line, across = [pair, near, far, far_near], [pair_across, across, far_near_across]
     cores = [core_a, core_b]
     shared = (where, line, across, cores)
-    parts = [w_0, w_1, w_2, w_3]
-    own1, send1 = project(*shared, parts, (0,) * 4, length, [])
+    own1, send1 = project(*shared, [w_0, w_1, w1_2, w_3], (0,) * 4, length, [])
     recv1 = swap(send1, "seq", seq, 1)
     w0_2, w0_3 = swap(cut0_2, "seq", seq, 4), swap(cut0_3, "seq", seq, 6)
     w0_1 = swap(cut0_1, "seq", seq, 2)
     tables = wave_tables(length)
+    own2, send2 = project(*shared, [w_0, w_1, w2_2, w_3], (rows, rows, 0, rows), length, [])
+    recv2 = swap(send2, "seq", seq, 1)
+    freq = spectrum(
+        where, tables, [w_0, w0_1, w0_2, w_3], (3 * rows, rows, rows, 2 * rows), length, [send2]
+    )
     parts0 = [w_0, w0_1, w0_2, w0_3]
-    freq = spectrum(
-        where, tables, [w_0, w0_1, w0_2, w_3], (3 * rows, rows, rows, 2 * rows), length
-    )
-    own2, send2 = project(*shared, parts, (rows,) * 4, length, [])
-    recv2 = swap(send2, "seq", seq, 1)
     own0, send0 = project(*shared, parts0, (2 * rows, 0, 0, 0), length, [])
     recv0 = swap(send0, "seq", seq, 1)
     mixed, held = mix(
@@ -706,17 +714,16 @@
         [send0],
     )
     pieces = gate(where, own0, recv0, mixed, short_taps)
-    joined = [
-        piece if turn == 0 else swap(piece, "seq", seq, turn) for turn, piece in enumerate(pieces)
-    ]
-
-    (across_out,) = emit(where, joined, held, (3,), [], jnp.bfloat16)
+    order = (6, 7, 4, 5, 2, 3, 1, 0)
+    joined = [swap(pieces[turn], "seq", seq, turn) if turn else pieces[0] for turn in order]
+
+    (across_out,) = emit(where, joined, order, held, (3,), [], jnp.bfloat16)
     from_core = swap(across_out, "chan", chans, 1)
-    (beside_out,) = emit(where, joined, held, (1,), [], jnp.bfloat16)
+    (beside_out,) = emit(where, joined, order, held, (1,), [], jnp.bfloat16)
     near_sum = swap(beside_out, "chan", chans, 1)
-    (chip_out,) = emit(where, joined, held, (2,), [from_core], jnp.bfloat16)
+    (chip_out,) = emit(where, joined, order, held, (2,), [from_core], jnp.bfloat16)
     from_chip = swap(chip_out, "chan", chans, 2)
-    (own,) = emit(where, joined, held, (0,), [near_sum], jnp.float32)
+    (own,) = emit(where, joined, order, held, (0,), [near_sum], jnp.float32)
     return (own + from_chip.astype(jnp.float32)).astype(jnp.bfloat16)
 
 

time: 179 us -> 177 us (0.989)
  starting transfers between devices: 45 us -> 40.8 us
  waiting for transfers between devices: 96.2 us -> 98.3 us
    ppermute x28 -> x29, starting transfers between devices: 45 us -> 40.8 us  [swap(): return lax.ppermute(value, axis, [(i, i ^ turn) for i in range(count)])]
    ppermute x28 -> x29, waiting for transfers between devices: 96.2 us -> 98.3 us  [swap(): return lax.ppermute(value, axis, [(i, i ^ turn) for i in range(count)])]
  transfers between devices with their start and end apart: 28 -> 29, of which waited for: 13 -> 14; matrix products, arithmetic and copies ran while one was open for 0% -> 0% of each run, Pallas kernels for 15% -> 15%
where the time goes in v6:
time: 177 us
  waiting for transfers between devices  98.3 us (56%)
  starting transfers between devices  40.8 us (23%)
  Pallas kernels  32.9 us (19%)
  local copies, waits for them, and re-layouts  2.9 us (2%)
    ppermute x29, waiting for transfers between devices, swap(): return lax.ppermute(value, axis, [(i, i ^ turn) for i in range(count)])  98.3 us
    ppermute x29, starting transfers between devices, swap(): return lax.ppermute(value, axis, [(i, i ^ turn) for i in range(count)])  40.8 us
    pallas_call x3, Pallas kernels, project(): pl.pallas_call(functools.partial(project_kernel, lows=lows, after=len(aft...  9.06 us
    pallas_call x1, Pallas kernels, mix(): pl.pallas_call(functools.partial(mix_kernel, after=len(after)), out_shape...  8.65 us
    pallas_call x4, Pallas kernels, emit(): pl.pallas_call(functools.partial(emit_kernel, order=order, turns=turns, a...  5.62 us
    pallas_call x1, Pallas kernels, spectrum(): pl.pallas_call(functools.partial(spectrum_kernel, lows=lows), out_shape=j...  3.57 us
  transfers between devices with their start and end apart: 29, of which 14 were waited for; matrix products, arithmetic and copies ran while one was open for 0% of the time, Pallas kernels for 15%

profile of v6, /device:TPU:0, one launch (start us, length us, event | category | flops | bytes accessed | tf_op | source)
XLA Modules:
  0.0 176.8 jit_solution(10648876619049612431)
XLA Ops:
  0.7 3.4 %halve.1 = (bf16[256,512]{1,0:T(8,128)(2,1)}, bf16[512,512]{1,0:T(8,128)(2,1)}, bf16[512,256]{1,0:T(8,128)(2,1)}, bf16[1024,256]{1,0:T(8,128)(2,1)}) custom-call(s32[2]{0:T(128)} %pad_add_fusion.where_ref, bf16[256,1024]{1,0:T(8,128)(2,1)} %tokens.1, bf16[256,1024]{1,0:T(8,128)(2,1)} %filters.3, bf16[3,512,1024]{2,1,0:T(8,128)(2,1)} %bitcast.4), custom_call_target="tpu_custom_call" | custom-call | tf_op jit(solution)/shard_map/halve/pallas_call | solution.py:203
  4.1 3.0 %collective-permute-start = (bf16[512,512]{1,0:T(8,128)(2,1)}, bf16[512,512]{1,0:T(8,128)(2,1)S(1)}, u32[]{:S(2)}, u32[]{:S(2)}) collective-permute-start(bf16[512,512]{1,0:T(8,128)(2,1)} %get-tuple-element.32), channel_id=1, source_target_pairs={{0,4},{4,0},{8,12},{12,8},{16,20},{20,16},{24,28},{28,24},{1,5},{5... | collective-permute-start | bytes 1572872 | tf_op jit(solution)/shard_map/ppermute | solution.py:634
  7.1 2.6 %collective-permute-start.1 = (bf16[512,256]{1,0:T(8,128)(2,1)}, bf16[512,256]{1,0:T(8,128)(2,1)S(1)}, u32[]{:S(2)}, u32[]{:S(2)}) collective-permute-start(bf16[512,256]{1,0:T(8,128)(2,1)} %get-tuple-element.33), channel_id=1, source_target_pairs={{0,16},{4,20},{8,24},{12,28},{16,0},{20,4},{24,8},{28,12},{1,17},{... | collective-permute-start | bytes 786440 | tf_op jit(solution)/shard_map/ppermute | solution.py:634
  9.7 1.6 collective-permute-start.6
  11.2 10.4 %collective-permute-done.1.refs_2_.refs_11_ = bf16[512,256]{1,0:T(8,128)(2,1)S(1)} collective-permute-done((bf16[512,256]{1,0:T(8,128)(2,1)}, bf16[512,256]{1,0:T(8,128)(2,1)S(1)}, u32[]{:S(2)}, u32[]{:S(2)}) %collective-permute-start.1) | collective-permute-done | bytes 262176 | tf_op jit(solution)/shard_map/ppermute | solution.py:634
  22.7 1.6 collective-permute-start.5
  24.6 3.7 %collective-permute-start.2 = (bf16[512,512]{1,0:T(8,128)(2,1)S(1)}, bf16[512,512]{1,0:T(8,128)(2,1)S(1)}, u32[]{:S(2)}, u32[]{:S(2)}) collective-permute-start(bf16[512,512]{1,0:T(8,128)(2,1)S(1)} %join.4.refs_0_), channel_id=1, source_target_pairs={{0,8},{4,12},{8,0},{12,4},{16,24},{20,28},{24,16},{28,20},{1,9},{5... | collective-permute-start | bytes 1572872 | tf_op jit(solution)/shard_map/ppermute | solution.py:634
  28.3 1.9 %copy-done = bf16[512,3,1024]{2,0,1:T(8,128)(2,1)S(1)} copy-done((bf16[512,3,1024]{2,0,1:T(8,128)(2,1)S(1)}, bf16[512,3,1024]{2,0,1:T(8,128)(2,1)}, u32[]{:S(2)}) %copy-start) | copy-done | bytes 3145752
  31.5 4.0 %collective-permute-done.5.refs_2_.refs_1_.refs_4_ = bf16[512,512]{1,0:T(8,128)(2,1)S(1)} collective-permute-done((bf16[512,512]{1,0:T(8,128)(2,1)S(1)}, bf16[512,512]{1,0:T(8,128)(2,1)S(1)}, u32[]{:S(2)}, u32[]{:S(2)}) %collective-permute-start.5) | collective-permute-done | bytes 524320 | tf_op jit(solution)/shard_map/ppermute | solution.py:634
  35.4 13.5 %collective-permute-done.3.refs_0_.refs_2_ = bf16[512,512]{1,0:T(8,128)(2,1)S(1)} collective-permute-done((bf16[512,512]{1,0:T(8,128)(2,1)S(1)}, bf16[512,512]{1,0:T(8,128)(2,1)S(1)}, u32[]{:S(2)}, u32[]{:S(2)}) %collective-permute-start.3) | collective-permute-done | bytes 524320 | tf_op jit(solution)/shard_map/ppermute | solution.py:634
  50.0 1.6 collective-permute-start.7
  51.6 1.5 collective-permute-start.4
  54.4 11.0 %collective-permute-done.4.refs_2_.refs_3_ = bf16[512,512]{1,0:T(8,128)(2,1)S(1)} collective-permute-done((bf16[512,512]{1,0:T(8,128)(2,1)S(1)}, bf16[512,512]{1,0:T(8,128)(2,1)S(1)}, u32[]{:S(2)}, u32[]{:S(2)}) %collective-permute-start.4) | collective-permute-done | bytes 524320 | tf_op jit(solution)/shard_map/ppermute | solution.py:634
  66.0 2.4 %collective-permute-start.10 = (bf16[512,256]{1,0:T(8,128)(2,1)S(1)}, bf16[512,256]{1,0:T(8,128)(2,1)S(1)}, u32[]{:S(2)}, u32[]{:S(2)}) collective-permute-start(bf16[512,256]{1,0:T(8,128)(2,1)S(1)} %get-tuple-element.36), channel_id=1, source_target_pairs={{0,16},{4,20},{8,24},{12,28},{16,0},{20,4},{24,8},{28,12},{1,17},{... | collective-permute-start | bytes 786440 | tf_op jit(solution)/shard_map/ppermute | solution.py:634
  68.4 25.0 %collective-permute-done.10.refs_5_.refs_11_ = bf16[512,256]{1,0:T(8,128)(2,1)S(1)} collective-permute-done((bf16[512,256]{1,0:T(8,128)(2,1)S(1)}, bf16[512,256]{1,0:T(8,128)(2,1)S(1)}, u32[]{:S(2)}, u32[]{:S(2)}) %collective-permute-start.10) | collective-permute-done | bytes 262176 | tf_op jit(solution)/shard_map/ppermute | solution.py:634
  94.3 2.6 %collective-permute-start.17 = (bf16[512,256]{1,0:T(8,128)(2,1)S(1)}, bf16[512,256]{1,0:T(8,128)(2,1)S(1)}, u32[]{:S(2)}, u32[]{:S(2)}) collective-permute-start(bf16[512,256]{1,0:T(8,128)(2,1)S(1)} %get-tuple-element.44), channel_id=1, source_target_pairs={{0,24},{4,28},{8,16},{12,20},{16,8},{20,12},{24,0},{28,4},{1,25},{... | collective-permute-start | bytes 786440 | tf_op jit(solution)/shard_map/ppermute | solution.py:634
  96.9 1.7 collective-permute-start.16
  98.7 2.0 %collective-permute-done.12.refs_8_ = bf16[2048,512]{1,0:T(8,128)(2,1)S(1)} collective-permute-done((bf16[2048,512]{1,0:T(8,128)(2,1)S(1)}, bf16[2048,512]{1,0:T(8,128)(2,1)S(1)}, u32[]{:S(2)}, u32[]{:S(2)}) %collective-permute-start.12) | collective-permute-done | bytes 2097184 | tf_op jit(solution)/shard_map/ppermute | solution.py:634
  100.7 3.0 %project.3 = (f32[2048,128]{1,0:T(8,128)S(1)}, bf16[2048,128]{1,0:T(8,128)(2,1)S(1)}) custom-call(s32[2]{0:T(128)S(1)} %copy-done.7, bf16[512,512]{1,0:T(8,128)(2,1)S(1)} %join.4.refs_0_, bf16[512,512]{1,0:T(8,128)(2,1)S(1)} %collective-permute-done.2.refs_1_.refs_2_, bf16[512,512]{1,0:T(8,128)(2,1)S(1)} %collective-permute-done.3.refs_0_.refs_2_, ...), custom_call_target="tpu_custom_call" | custom-call | flops 4294967296 | bytes 8388608 | tf_op jit(solution)/shard_map/project/pallas_call | solution.py:338
  104.3 3.0 %project.4 = (f32[2048,128]{1,0:T(8,128)S(1)}, bf16[2048,128]{1,0:T(8,128)(2,1)S(1)}) custom-call(s32[2]{0:T(128)S(1)} %copy-done.7, bf16[512,512]{1,0:T(8,128)(2,1)S(1)} %join.4.refs_0_, bf16[512,512]{1,0:T(8,128)(2,1)S(1)} %collective-permute-done.2.refs_1_.refs_2_, bf16[512,512]{1,0:T(8,128)(2,1)S(1)} %collective-permute-done.3.refs_0_.refs_2_, ...), custom_call_target="tpu_custom_call" | custom-call | flops 4294967296 | bytes 8388608 | tf_op jit(solution)/shard_map/project/pallas_call | solution.py:338
  107.4 1.6 collective-permute-start.14
  109.0 9.4 %collective-permute-done.15.refs_1_.refs_10_ = bf16[768,256]{1,0:T(8,128)(2,1)S(1)} collective-permute-done((bf16[768,256]{1,0:T(8,128)(2,1)S(1)}, bf16[768,256]{1,0:T(8,128)(2,1)S(1)}, u32[]{:S(2)}, u32[]{:S(2)}) %collective-permute-start.15) | collective-permute-done | bytes 393248 | tf_op jit(solution)/shard_map/ppermute | solution.py:634
  118.4 6.0 %collective-permute-done.16.refs_2_.refs_11_ = bf16[768,256]{1,0:T(8,128)(2,1)S(1)} collective-permute-done((bf16[768,256]{1,0:T(8,128)(2,1)S(1)}, bf16[768,256]{1,0:T(8,128)(2,1)S(1)}, u32[]{:S(2)}, u32[]{:S(2)}) %collective-permute-start.16) | collective-permute-done | bytes 393248 | tf_op jit(solution)/shard_map/ppermute | solution.py:634
  124.3 3.0 %project.5 = (f32[2048,128]{1,0:T(8,128)S(1)}, bf16[2048,128]{1,0:T(8,128)(2,1)S(1)}) custom-call(s32[2]{0:T(128)S(1)} %copy-done.7, bf16[512,512]{1,0:T(8,128)(2,1)S(1)} %join.4.refs_0_, bf16[512,512]{1,0:T(8,128)(2,1)S(1)} %collective-permute-done.2.refs_1_.refs_2_, bf16[512,512]{1,0:T(8,128)(2,1)S(1)} %collective-permute-done.3.refs_0_.refs_2_, ...), custom_call_target="tpu_custom_call" | custom-call | flops 4294967296 | bytes 8388608 | tf_op jit(solution)/shard_map/project/pallas_call | solution.py:338
  128.0 3.6 %spectrum.1.freq_ref = f32[4224,128]{1,0:T(8,128)S(1)} custom-call(s32[2]{0:T(128)S(1)} %copy-done.7, bf16[80,32]{1,0:T(8,128)(2,1)S(1)} %copy-done.6, bf16[33,128,128]{2,1,0:T(8,128)(2,1)S(1)} %copy-done.1, bf16[1792,256]{1,0:T(8,128)(2,1)S(1)} %get-tuple-element.37.refs_9_.refs_0_, bf16[768,256]{1,0:T(8,128)(2,1)S(1)} %collective-permute-done.15.refs_1_.refs_10_, ...), custom_call_target="tpu_custom_call" | custom-call | flops 67108864 | bytes 1048576 | tf_op jit(solution)/shard_map/spectrum/pallas_call | solution.py:427
  131.7 8.7 %mix.1 = (f32[2048,128]{1,0:T(8,128)S(1)}, bf16[1024,4096]{1,0:T(8,128)(2,1)S(1)}) custom-call(s32[2]{0:T(128)S(1)} %copy-done.7, f32[2048,128]{1,0:T(8,128)S(1)} %get-tuple-element.38.own1, bf16[2048,128]{1,0:T(8,128)(2,1)S(1)} %collective-permute-done.13.recv1, f32[2048,128]{1,0:T(8,128)S(1)} %get-tuple-element.40.own2, ...), custom_call_target="tpu_custom_call" | custom-call | flops 201326592 | bytes 6291456 | tf_op jit(solution)/shard_map/mix/pallas_call | solution.py:531
  141.5 2.4 %collective-permute-start.19 = (bf16[256,128]{1,0:T(8,128)(2,1)S(1)}, bf16[256,128]{1,0:T(8,128)(2,1)S(1)}, u32[]{:S(2)}, u32[]{:S(2)}) collective-permute-start(bf16[256,128]{1,0:T(8,128)(2,1)S(1)} %get-tuple-element.49), channel_id=1, source_target_pairs={{0,24},{4,28},{8,16},{12,20},{16,8},{20,12},{24,0},{28,4},{1,25},{... | collective-permute-start | bytes 196616 | tf_op jit(solution)/shard_map/ppermute | solution.py:634
  143.9 2.2 %collective-permute-start.20 = (bf16[256,128]{1,0:T(8,128)(2,1)S(1)}, bf16[256,128]{1,0:T(8,128)(2,1)S(1)}, u32[]{:S(2)}, u32[]{:S(2)}) collective-permute-start(bf16[256,128]{1,0:T(8,128)(2,1)S(1)} %get-tuple-element.50), channel_id=1, source_target_pairs={{0,28},{4,24},{8,20},{12,16},{16,12},{20,8},{24,4},{28,0},{1,29},{... | collective-permute-start | bytes 196616 | tf_op jit(solution)/shard_map/ppermute | solution.py:634
  146.2 3.1 %collective-permute-start.22 = (bf16[256,128]{1,0:T(8,128)(2,1)S(1)}, bf16[256,128]{1,0:T(8,128)(2,1)S(1)}, u32[]{:S(2)}, u32[]{:S(2)}) collective-permute-start(bf16[256,128]{1,0:T(8,128)(2,1)S(1)} %get-tuple-element.52), channel_id=1, source_target_pairs={{0,20},{4,16},{8,28},{12,24},{16,4},{20,0},{24,12},{28,8},{1,21},{... | collective-permute-start | bytes 196616 | tf_op jit(solution)/shard_map/ppermute | solution.py:634
  149.2 2.8 %collective-permute-start.24 = (bf16[256,128]{1,0:T(8,128)(2,1)S(1)}, bf16[256,128]{1,0:T(8,128)(2,1)S(1)}, u32[]{:S(2)}, u32[]{:S(2)}) collective-permute-start(bf16[256,128]{1,0:T(8,128)(2,1)S(1)} %get-tuple-element.54), channel_id=1, source_target_pairs={{0,12},{4,8},{8,4},{12,0},{16,28},{20,24},{24,20},{28,16},{1,13},{... | collective-permute-start | bytes 196616 | tf_op jit(solution)/shard_map/ppermute | solution.py:634
  152.8 2.7 %collective-permute-done.22.refs_3_ = bf16[256,128]{1,0:T(8,128)(2,1)S(1)} collective-permute-done((bf16[256,128]{1,0:T(8,128)(2,1)S(1)}, bf16[256,128]{1,0:T(8,128)(2,1)S(1)}, u32[]{:S(2)}, u32[]{:S(2)}) %collective-permute-start.22) | collective-permute-done | bytes 65568 | tf_op jit(solution)/shard_map/ppermute | solution.py:634
  164.3 11.5 %collective-permute-done.28 = bf16[256,1024]{1,0:T(8,128)(2,1)S(1)} collective-permute-done((bf16[256,1024]{1,0:T(8,128)(2,1)S(1)}, bf16[256,1024]{1,0:T(8,128)(2,1)S(1)}, u32[]{:S(2)}, u32[]{:S(2)}) %collective-permute-start.28) | collective-permute-done | bytes 524320 | tf_op jit(solution)/shard_map/ppermute | solution.py:634
  (69 shorter events, 20.0 us)
Async XLA Ops:
  0.7 27.6 %copy-start.2 = (bf16[256,1024]{1,0:T(8,128)(2,1)S(1)}, bf16[256,1024]{1,0:T(8,128)(2,1)}, u32[]{:S(2)}) copy-start(bf16[256,1024]{1,0:T(8,128)(2,1)} %filters.3) | copy-start | bytes 1572868
  0.7 27.6 %copy-start.7 = (s32[2]{0:T(128)S(1)}, s32[2]{0:T(128)}, u32[]{:S(2)}) copy-start(s32[2]{0:T(128)} %pad_add_fusion.where_ref) | copy-start | bytes 28
  4.1 17.6 %collective-permute-start = (bf16[512,512]{1,0:T(8,128)(2,1)}, bf16[512,512]{1,0:T(8,128)(2,1)S(1)}, u32[]{:S(2)}, u32[]{:S(2)}) collective-permute-start(bf16[512,512]{1,0:T(8,128)(2,1)} %get-tuple-element.32), channel_id=1, source_target_pairs={{0,4},{4,0},{8,12},{12,8},{16,20},{20,16},{24,28},{28,24},{1,5},{5... | collective-permute-start | bytes 1572872 | tf_op jit(solution)/shard_map/ppermute | solution.py:634
  7.1 14.6 %collective-permute-start.1 = (bf16[512,256]{1,0:T(8,128)(2,1)}, bf16[512,256]{1,0:T(8,128)(2,1)S(1)}, u32[]{:S(2)}, u32[]{:S(2)}) collective-permute-start(bf16[512,256]{1,0:T(8,128)(2,1)} %get-tuple-element.33), channel_id=1, source_target_pairs={{0,16},{4,20},{8,24},{12,28},{16,0},{20,4},{24,8},{28,12},{1,17},{... | collective-permute-start | bytes 786440 | tf_op jit(solution)/shard_map/ppermute | solution.py:634
  9.7 21.8 %collective-permute-start.6 = (bf16[1024,256]{1,0:T(8,128)(2,1)}, bf16[1024,256]{1,0:T(8,128)(2,1)S(1)}, u32[]{:S(2)}, u32[]{:S(2)}) collective-permute-start(bf16[1024,256]{1,0:T(8,128)(2,1)} %get-tuple-element.35), channel_id=1, source_target_pairs={{0,8},{4,12},{8,0},{12,4},{16,24},{20,28},{24,16},{28,20},{1,9},{5... | collective-permute-start | bytes 1572872 | tf_op jit(solution)/shard_map/ppermute | solution.py:634
  22.7 12.8 %collective-permute-start.5 = (bf16[512,512]{1,0:T(8,128)(2,1)S(1)}, bf16[512,512]{1,0:T(8,128)(2,1)S(1)}, u32[]{:S(2)}, u32[]{:S(2)}) collective-permute-start(bf16[512,512]{1,0:T(8,128)(2,1)S(1)} %join.4.refs_0_), channel_id=1, source_target_pairs={{0,2},{1,3},{2,0},{3,1},{4,6},{5,7},{6,4},{7,5},{8,10},{9,11},{10,... | collective-permute-start | bytes 1572872 | tf_op jit(solution)/shard_map/ppermute | solution.py:634
  24.3 24.7 %collective-permute-start.3 = (bf16[512,512]{1,0:T(8,128)(2,1)S(1)}, bf16[512,512]{1,0:T(8,128)(2,1)S(1)}, u32[]{:S(2)}, u32[]{:S(2)}) collective-permute-start(bf16[512,512]{1,0:T(8,128)(2,1)S(1)} %join.4.refs_0_), channel_id=1, source_target_pairs={{0,16},{4,20},{8,24},{12,28},{16,0},{20,4},{24,8},{28,12},{1,17},{... | collective-permute-start | bytes 1572872 | tf_op jit(solution)/shard_map/ppermute | solution.py:634
  24.6 25.3 %collective-permute-start.2 = (bf16[512,512]{1,0:T(8,128)(2,1)S(1)}, bf16[512,512]{1,0:T(8,128)(2,1)S(1)}, u32[]{:S(2)}, u32[]{:S(2)}) collective-permute-start(bf16[512,512]{1,0:T(8,128)(2,1)S(1)} %join.4.refs_0_), channel_id=1, source_target_pairs={{0,8},{4,12},{8,0},{12,4},{16,24},{20,28},{24,16},{28,20},{1,9},{5... | collective-permute-start | bytes 1572872 | tf_op jit(solution)/shard_map/ppermute | solution.py:634
  50.0 43.3 %collective-permute-start.7 = (bf16[1024,512]{1,0:T(8,128)(2,1)S(1)}, bf16[1024,512]{1,0:T(8,128)(2,1)S(1)}, u32[]{:S(2)}, u32[]{:S(2)}) collective-permute-start(bf16[1024,512]{1,0:T(8,128)(2,1)S(1)} %join.5), channel_id=1, source_target_pairs={{0,2},{1,3},{2,0},{3,1},{4,6},{5,7},{6,4},{7,5},{8,10},{9,11},{10,... | collective-permute-start | bytes 3145736 | tf_op jit(solution)/shard_map/ppermute | solution.py:634
  51.6 13.9 %collective-permute-start.4 = (bf16[512,512]{1,0:T(8,128)(2,1)S(1)}, bf16[512,512]{1,0:T(8,128)(2,1)S(1)}, u32[]{:S(2)}, u32[]{:S(2)}) collective-permute-start(bf16[512,512]{1,0:T(8,128)(2,1)S(1)} %collective-permute-done.3.refs_0_.refs_2_), channel_id=1, source_target_pairs={{0,8},{4,12},{8,0},{12,4},{16,24},{20,28},{24,16},{28,20},{1,9},{5... | collective-permute-start | bytes 1572872 | tf_op jit(solution)/shard_map/ppermute | solution.py:634
  53.1 40.3 %collective-permute-start.9 = (bf16[1280,256]{1,0:T(8,128)(2,1)S(1)}, bf16[1280,256]{1,0:T(8,128)(2,1)S(1)}, u32[]{:S(2)}, u32[]{:S(2)}) collective-permute-start(bf16[1280,256]{1,0:T(8,128)(2,1)S(1)} %get-tuple-element.34.refs_3_), channel_id=1, source_target_pairs={{0,24},{4,28},{8,16},{12,20},{16,8},{20,12},{24,0},{28,4},{1,25},{... | collective-permute-start | bytes 1966088 | tf_op jit(solution)/shard_map/ppermute | solution.py:634
  65.5 28.1 %collective-permute-start.8 = (bf16[512,512]{1,0:T(8,128)(2,1)S(1)}, bf16[512,512]{1,0:T(8,128)(2,1)S(1)}, u32[]{:S(2)}, u32[]{:S(2)}) collective-permute-start(bf16[512,512]{1,0:T(8,128)(2,1)S(1)} %collective-permute-done.4.refs_2_.refs_3_), channel_id=1, source_target_pairs={{0,2},{1,3},{2,0},{3,1},{4,6},{5,7},{6,4},{7,5},{8,10},{9,11},{10,... | collective-permute-start | bytes 1572872 | tf_op jit(solution)/shard_map/ppermute | solution.py:634
  66.0 27.4 %collective-permute-start.10 = (bf16[512,256]{1,0:T(8,128)(2,1)S(1)}, bf16[512,256]{1,0:T(8,128)(2,1)S(1)}, u32[]{:S(2)}, u32[]{:S(2)}) collective-permute-start(bf16[512,256]{1,0:T(8,128)(2,1)S(1)} %get-tuple-element.36), channel_id=1, source_target_pairs={{0,16},{4,20},{8,24},{12,28},{16,0},{20,4},{24,8},{28,12},{1,17},{... | collective-permute-start | bytes 786440 | tf_op jit(solution)/shard_map/ppermute | solution.py:634
  93.5 5.2 %collective-permute-start.11 = (bf16[2048,512]{1,0:T(8,128)(2,1)S(1)}, bf16[2048,512]{1,0:T(8,128)(2,1)S(1)}, u32[]{:S(2)}, u32[]{:S(2)}) collective-permute-start(bf16[2048,512]{1,0:T(8,128)(2,1)S(1)} %join.6), channel_id=1, source_target_pairs={{0,1},{1,0},{2,3},{3,2},{4,5},{5,4},{6,7},{7,6},{8,9},{9,8},{10,11... | collective-permute-start | bytes 6291464 | tf_op jit(solution)/shard_map/ppermute | solution.py:634
  93.7 7.0 %collective-permute-start.12 = (bf16[2048,512]{1,0:T(8,128)(2,1)S(1)}, bf16[2048,512]{1,0:T(8,128)(2,1)S(1)}, u32[]{:S(2)}, u32[]{:S(2)}) collective-permute-start(bf16[2048,512]{1,0:T(8,128)(2,1)S(1)} %join.7), channel_id=1, source_target_pairs={{0,1},{1,0},{2,3},{3,2},{4,5},{5,4},{6,7},{7,6},{8,9},{9,8},{10,11... | collective-permute-start | bytes 6291464 | tf_op jit(solution)/shard_map/ppermute | solution.py:634
  94.3 14.7 %collective-permute-start.17 = (bf16[512,256]{1,0:T(8,128)(2,1)S(1)}, bf16[512,256]{1,0:T(8,128)(2,1)S(1)}, u32[]{:S(2)}, u32[]{:S(2)}) collective-permute-start(bf16[512,256]{1,0:T(8,128)(2,1)S(1)} %get-tuple-element.44), channel_id=1, source_target_pairs={{0,24},{4,28},{8,16},{12,20},{16,8},{20,12},{24,0},{28,4},{1,25},{... | collective-permute-start | bytes 786440 | tf_op jit(solution)/shard_map/ppermute | solution.py:634
  96.9 21.5 %collective-permute-start.15 = (bf16[768,256]{1,0:T(8,128)(2,1)S(1)}, bf16[768,256]{1,0:T(8,128)(2,1)S(1)}, u32[]{:S(2)}, u32[]{:S(2)}) collective-permute-start(bf16[768,256]{1,0:T(8,128)(2,1)S(1)} %get-tuple-element.42), channel_id=1, source_target_pairs={{0,8},{4,12},{8,0},{12,4},{16,24},{20,28},{24,16},{28,20},{1,9},{5... | collective-permute-start | bytes 1179656 | tf_op jit(solution)/shard_map/ppermute | solution.py:634
  96.9 27.4 %collective-permute-start.16 = (bf16[768,256]{1,0:T(8,128)(2,1)S(1)}, bf16[768,256]{1,0:T(8,128)(2,1)S(1)}, u32[]{:S(2)}, u32[]{:S(2)}) collective-permute-start(bf16[768,256]{1,0:T(8,128)(2,1)S(1)} %get-tuple-element.43), channel_id=1, source_target_pairs={{0,16},{4,20},{8,24},{12,28},{16,0},{20,4},{24,8},{28,12},{1,17},{... | collective-permute-start | bytes 1179656 | tf_op jit(solution)/shard_map/ppermute | solution.py:634
  103.7 27.9 %collective-permute-start.13 = (bf16[2048,128]{1,0:T(8,128)(2,1)S(1)}, bf16[2048,128]{1,0:T(8,128)(2,1)S(1)}, u32[]{:S(2)}, u32[]{:S(2)}) collective-permute-start(bf16[2048,128]{1,0:T(8,128)(2,1)S(1)} %get-tuple-element.39), channel_id=1, source_target_pairs={{0,4},{4,0},{8,12},{12,8},{16,20},{20,16},{24,28},{28,24},{1,5},{5... | collective-permute-start | bytes 1572872 | tf_op jit(solution)/shard_map/ppermute | solution.py:634
  107.4 24.3 %slice-start = ((s8[8388608]{0:T(1024)(128)(4,1)}), s8[4194304]{0:T(1024)(128)(4,1)S(1)}, s32[]{:S(2)}) async-start(s8[8388608]{0:T(1024)(128)(4,1)} %bitcast.6), calls=%async_computation | async-start | bytes 8388608
  107.4 24.2 %collective-permute-start.14 = (bf16[2048,128]{1,0:T(8,128)(2,1)S(1)}, bf16[2048,128]{1,0:T(8,128)(2,1)S(1)}, u32[]{:S(2)}, u32[]{:S(2)}) collective-permute-start(bf16[2048,128]{1,0:T(8,128)(2,1)S(1)} %get-tuple-element.41.refs_4_), channel_id=1, source_target_pairs={{0,4},{4,0},{8,12},{12,8},{16,20},{20,16},{24,28},{28,24},{1,5},{5... | collective-permute-start | bytes 1572872 | tf_op jit(solution)/shard_map/ppermute | solution.py:634
  127.4 13.1 %collective-permute-start.18 = (bf16[2048,128]{1,0:T(8,128)(2,1)S(1)}, bf16[2048,128]{1,0:T(8,128)(2,1)S(1)}, u32[]{:S(2)}, u32[]{:S(2)}) collective-permute-start(bf16[2048,128]{1,0:T(8,128)(2,1)S(1)} %get-tuple-element.45.refs_0_), channel_id=1, source_target_pairs={{0,4},{4,0},{8,12},{12,8},{16,20},{20,16},{24,28},{28,24},{1,5},{5... | collective-permute-start | bytes 1572872 | tf_op jit(solution)/shard_map/ppermute | solution.py:634
  141.5 7.7 %collective-permute-start.19 = (bf16[256,128]{1,0:T(8,128)(2,1)S(1)}, bf16[256,128]{1,0:T(8,128)(2,1)S(1)}, u32[]{:S(2)}, u32[]{:S(2)}) collective-permute-start(bf16[256,128]{1,0:T(8,128)(2,1)S(1)} %get-tuple-element.49), channel_id=1, source_target_pairs={{0,24},{4,28},{8,16},{12,20},{16,8},{20,12},{24,0},{28,4},{1,25},{... | collective-permute-start | bytes 196616 | tf_op jit(solution)/shard_map/ppermute | solution.py:634
  143.9 8.1 %collective-permute-start.20 = (bf16[256,128]{1,0:T(8,128)(2,1)S(1)}, bf16[256,128]{1,0:T(8,128)(2,1)S(1)}, u32[]{:S(2)}, u32[]{:S(2)}) collective-permute-start(bf16[256,128]{1,0:T(8,128)(2,1)S(1)} %get-tuple-element.50), channel_id=1, source_target_pairs={{0,28},{4,24},{8,20},{12,16},{16,12},{20,8},{24,4},{28,0},{1,29},{... | collective-permute-start | bytes 196616 | tf_op jit(solution)/shard_map/ppermute | solution.py:634
  146.2 6.6 %collective-permute-start.21 = (bf16[256,128]{1,0:T(8,128)(2,1)S(1)}, bf16[256,128]{1,0:T(8,128)(2,1)S(1)}, u32[]{:S(2)}, u32[]{:S(2)}) collective-permute-start(bf16[256,128]{1,0:T(8,128)(2,1)S(1)} %get-tuple-element.51), channel_id=1, source_target_pairs={{0,16},{4,20},{8,24},{12,28},{16,0},{20,4},{24,8},{28,12},{1,17},{... | collective-permute-start | bytes 196616 | tf_op jit(solution)/shard_map/ppermute | solution.py:634
  146.2 9.3 %collective-permute-start.22 = (bf16[256,128]{1,0:T(8,128)(2,1)S(1)}, bf16[256,128]{1,0:T(8,128)(2,1)S(1)}, u32[]{:S(2)}, u32[]{:S(2)}) collective-permute-start(bf16[256,128]{1,0:T(8,128)(2,1)S(1)} %get-tuple-element.52), channel_id=1, source_target_pairs={{0,20},{4,16},{8,28},{12,24},{16,4},{20,0},{24,12},{28,8},{1,21},{... | collective-permute-start | bytes 196616 | tf_op jit(solution)/shard_map/ppermute | solution.py:634
  149.2 6.2 %collective-permute-start.23 = (bf16[256,128]{1,0:T(8,128)(2,1)S(1)}, bf16[256,128]{1,0:T(8,128)(2,1)S(1)}, u32[]{:S(2)}, u32[]{:S(2)}) collective-permute-start(bf16[256,128]{1,0:T(8,128)(2,1)S(1)} %get-tuple-element.53), channel_id=1, source_target_pairs={{0,8},{4,12},{8,0},{12,4},{16,24},{20,28},{24,16},{28,20},{1,9},{5... | collective-permute-start | bytes 196616 | tf_op jit(solution)/shard_map/ppermute | solution.py:634
  149.2 7.2 %collective-permute-start.24 = (bf16[256,128]{1,0:T(8,128)(2,1)S(1)}, bf16[256,128]{1,0:T(8,128)(2,1)S(1)}, u32[]{:S(2)}, u32[]{:S(2)}) collective-permute-start(bf16[256,128]{1,0:T(8,128)(2,1)S(1)} %get-tuple-element.54), channel_id=1, source_target_pairs={{0,12},{4,8},{8,4},{12,0},{16,28},{20,24},{24,20},{28,16},{1,13},{... | collective-permute-start | bytes 196616 | tf_op jit(solution)/shard_map/ppermute | solution.py:634
  152.0 5.0 %collective-permute-start.25 = (bf16[256,128]{1,0:T(8,128)(2,1)S(1)}, bf16[256,128]{1,0:T(8,128)(2,1)S(1)}, u32[]{:S(2)}, u32[]{:S(2)}) collective-permute-start(bf16[256,128]{1,0:T(8,128)(2,1)S(1)} %get-tuple-element.55), channel_id=1, source_target_pairs={{0,4},{4,0},{8,12},{12,8},{16,20},{20,16},{24,28},{28,24},{1,5},{5... | collective-permute-start | bytes 196616 | tf_op jit(solution)/shard_map/ppermute | solution.py:634
  158.4 2.1 %collective-permute-start.27 = (bf16[256,1024]{1,0:T(8,128)(2,1)S(1)}, bf16[256,1024]{1,0:T(8,128)(2,1)S(1)}, u32[]{:S(2)}, u32[]{:S(2)}) collective-permute-start(bf16[256,1024]{1,0:T(8,128)(2,1)S(1)} %emit.6), channel_id=1, source_target_pairs={{0,1},{1,0},{2,3},{3,2},{4,5},{5,4},{6,7},{7,6},{8,9},{9,8},{10,11... | collective-permute-start | bytes 1572872 | tf_op jit(solution)/shard_map/ppermute | solution.py:634
  159.9 3.0 %collective-permute-start.26 = (bf16[256,1024]{1,0:T(8,128)(2,1)S(1)}, bf16[256,1024]{1,0:T(8,128)(2,1)S(1)}, u32[]{:S(2)}, u32[]{:S(2)}) collective-permute-start(bf16[256,1024]{1,0:T(8,128)(2,1)S(1)} %emit.4), channel_id=1, source_target_pairs={{0,1},{1,0},{2,3},{3,2},{4,5},{5,4},{6,7},{7,6},{8,9},{9,8},{10,11... | collective-permute-start | bytes 1572872 | tf_op jit(solution)/shard_map/ppermute | solution.py:634
  161.9 14.0 %collective-permute-start.28 = (bf16[256,1024]{1,0:T(8,128)(2,1)S(1)}, bf16[256,1024]{1,0:T(8,128)(2,1)S(1)}, u32[]{:S(2)}, u32[]{:S(2)}) collective-permute-start(bf16[256,1024]{1,0:T(8,128)(2,1)S(1)} %emit.7), channel_id=1, source_target_pairs={{0,2},{1,3},{2,0},{3,1},{4,6},{5,7},{6,4},{7,5},{8,10},{9,11},{10,... | collective-permute-start | bytes 1572872 | tf_op jit(solution)/shard_map/ppermute | solution.py:634
  (9 other events, 85.4 us)

commit v7 on v6

--- a/solution.py
+++ b/solution.py
@@ -164,9 +164,10 @@
     )
 
 
-def halve_kernel(where_ref, tokens, filters, weight, ours, theirs, *refs, plan):
+def halve_kernel(tokens, filters, weight, ours, theirs, *refs, plan):
     pieces, sems = refs[:-1], refs[-1]
-    depth, side = where_ref[0] // 2, where_ref[0] % 2
+    place = lax.axis_index("seq")
+    depth, side = place // 2, place % 2
     rows, half = ours.shape
     part = half // 4
     copies = []
@@ -193,7 +194,7 @@
         one.wait()
 
 
-def halve(where, tokens, filters, weight, plan):
+def halve(tokens, filters, weight, plan):
     rows, half = tokens.shape[0], tokens.shape[1] // 2
     pieces = tuple(
         jax.ShapeDtypeStruct((len(names) * weight.shape[1], weight.shape[2] // 4), weight.dtype)
@@ -207,19 +208,18 @@
             jax.ShapeDtypeStruct((rows + filters.shape[0], half), tokens.dtype),
         )
         + pieces,
-        in_specs=[pl.BlockSpec(memory_space=pltpu.SMEM)]
-        + [pl.BlockSpec(memory_space=pl.ANY)] * 3,
+        in_specs=[pl.BlockSpec(memory_space=pl.ANY)] * 3,
         out_specs=(vmem,) * (2 + len(plan)),
         scratch_shapes=[
             pltpu.SemaphoreType.DMA((6 + sum(len(names) for _, names in plan),))
         ],
-        compiler_params=pltpu.CompilerParams(vmem_limit_bytes=61 * 2**20),
+        compiler_params=pltpu.CompilerParams(vmem_limit_bytes=60 * 2**20),
         name="halve",
-    )(where, tokens, filters, weight)
-
-
-def cut_kernel(where_ref, weight, filters, filter_beside, *refs, plan, after):
-    place = where_ref[0]
+    )(tokens, filters, weight)
+
+
+def cut_kernel(weight, filters, filter_beside, *refs, plan, after):
+    place = lax.axis_index("seq")
     depth, side = place // 2, place % 2
     outs, sems = refs[after:-1], refs[-1]
     copies = []
@@ -254,7 +254,7 @@
         one.wait()
 
 
-def cut(where, weight, filters, filter_beside, plan, after):
+def cut(weight, filters, filter_beside, plan, after):
     count_of = {"f": filters.shape[0]}
     shapes = []
     for _, names in plan:
@@ -263,13 +263,12 @@
     return pl.pallas_call(
         functools.partial(cut_kernel, plan=plan, after=len(after)),
         out_shape=tuple(shapes),
-        in_specs=[pl.BlockSpec(memory_space=pltpu.SMEM)]
-        + [pl.BlockSpec(memory_space=pl.ANY)] * (3 + len(after)),
+        in_specs=[pl.BlockSpec(memory_space=pl.ANY)] * (3 + len(after)),
         out_specs=(pl.BlockSpec(memory_space=pltpu.VMEM),) * len(shapes),
         scratch_shapes=[pltpu.SemaphoreType.DMA((24,))],
         compiler_params=pltpu.CompilerParams(vmem_limit_bytes=8 * 2**20),
         name="cut",
-    )(where, weight, filters, filter_beside, *after)
+    )(weight, filters, filter_beside, *after)
 
 
 def join_kernel(*refs, pieces, outs):
@@ -296,10 +295,10 @@
     )(*values, *after)
 
 
-def project_kernel(where_ref, *refs, lows, after):
+def project_kernel(*refs, lows, after):
     line, across, cores, parts = refs[:4], refs[4:7], refs[7:9], refs[9:13]
     own_ref, send_ref, weights = refs[13 + after :]
-    place, chan = where_ref[0], where_ref[1]
+    place, chan = lax.axis_index("seq"), lax.axis_index("chan")
     depth, side = place // 2, place % 2
     rows = line[0].shape[1]
     for i in range(4):
@@ -332,7 +331,7 @@
             send_ref[pl.ds(start, block), :] = send[pair * block : (pair + 1) * block]
 
 
-def project(where, line, across, cores, parts, lows, length, after):
+def project(line, across, cores, parts, lows, length, after):
     depth, width = line[0].shape[1], parts[0].shape[1]
     vmem = pl.BlockSpec(memory_space=pltpu.VMEM)
     return pl.pallas_call(
@@ -341,8 +340,7 @@
             jax.ShapeDtypeStruct((length, width // 2), jnp.float32),
             jax.ShapeDtypeStruct((length, width // 2), jnp.bfloat16),
         ),
-        in_specs=[pl.BlockSpec(memory_space=pltpu.SMEM)]
-        + [vmem] * 13
+        in_specs=[vmem] * 13
         + [pl.BlockSpec(memory_space=pl.ANY)] * len(after),
         out_specs=(vmem, vmem),
         scratch_shapes=[pltpu.VMEM((4 * depth, width), jnp.bfloat16)],
@@ -353,7 +351,7 @@
             transcendentals=0,
         ),
         name="project",
-    )(where, *line, *across, *cores, *parts, *after)
+    )(*line, *across, *cores, *parts, *after)
 
 
 def smooth_into(padded, own_ref, recv_ref, taps, branch, store):
@@ -395,10 +393,10 @@
     return 11 if rows % 11 == 0 else 1
 
 
-def spectrum_kernel(where_ref, ahead, middle, *refs, lows):
+def spectrum_kernel(ahead, middle, *refs, lows):
     filters = refs[:4]
     freq_ref, lags, waves = refs[len(refs) - 3 :]
-    place = where_ref[0]
+    place = lax.axis_index("seq")
     length, width = lags.shape
     block = length // 8
     rows, two = middle.shape[:2]
@@ -419,7 +417,7 @@
     lax.fori_loop(0, rows, one, 0, unroll=unroll_of(rows))
 
 
-def spectrum(where, tables, filters, lows, length, after):
+def spectrum(tables, filters, lows, length, after):
     ahead, middle = tables[:2]
     rows, two = middle.shape[:2]
     width = filters[0].shape[1] // 2
@@ -427,8 +425,7 @@
     return pl.pallas_call(
         functools.partial(spectrum_kernel, lows=lows),
         out_shape=jax.ShapeDtypeStruct((rows * two, width), jnp.float32),
-        in_specs=[pl.BlockSpec(memory_space=pltpu.SMEM)]
-        + [vmem] * 6
+        in_specs=[vmem] * 6
         + [pl.BlockSpec(memory_space=pl.ANY)] * len(after),
         out_specs=vmem,
         scratch_shapes=[
@@ -440,11 +437,10 @@
             flops=2 * 2 * length * inner_len * width, bytes_accessed=2**20, transcendentals=0
         ),
         name="spectrum",
-    )(where, ahead, middle, *filters, *after)
+    )(ahead, middle, *filters, *after)
 
 
 def mix_kernel(
-    where_ref,
     own1,
     recv1,
     own2,
@@ -463,7 +459,7 @@
     mixed_ref, held_ref, padded, gated, waves, sums, sem = refs[after:]
     loading = pltpu.make_async_copy(weight, held_ref, sem)
     loading.start()
-    place = where_ref[0]
+    place = lax.axis_index("seq")
     width = own1.shape[1]
     ours = pl.ds(pl.multiple_of(place * width, width), width)
     taps, skip = taps_ref[:, :, ours], skip_ref[:, ours]
@@ -523,7 +519,7 @@
     loading.wait()
 
 
-def mix(where, own1, recv1, own2, recv2, taps, skip, tables, freq, weight, after):
+def mix(own1, recv1, own2, recv2, taps, skip, tables, freq, weight, after):
     length, width = own1.shape
     two = tables[1].shape[1]
     padded_rows = tables[0].shape[0] // 2
@@ -534,8 +530,7 @@
             jax.ShapeDtypeStruct((length, width), jnp.float32),
             jax.ShapeDtypeStruct(weight.shape, weight.dtype),
         ),
-        in_specs=[pl.BlockSpec(memory_space=pltpu.SMEM)]
-        + [vmem] * 11
+        in_specs=[vmem] * 11
         + [pl.BlockSpec(memory_space=pl.ANY)] * (1 + len(after)),
         out_specs=(vmem, vmem),
         scratch_shapes=[
@@ -550,12 +545,12 @@
             flops=2 * 6 * length * inner_len * width, bytes_accessed=6 * 2**20, transcendentals=0
         ),
         name="mix",
-    )(where, own1, recv1, own2, recv2, taps, skip, *tables, freq, weight, *after)
-
-
-def gate_kernel(where_ref, own0, recv0, mixed_ref, taps_ref, *refs):
+    )(own1, recv1, own2, recv2, taps, skip, *tables, freq, weight, *after)
+
+
+def gate_kernel(own0, recv0, mixed_ref, taps_ref, *refs):
     outs, padded, product = refs[:8], refs[8], refs[9]
-    place = where_ref[0]
+    place = lax.axis_index("seq")
     block, width = own0.shape[0] // 8, own0.shape[1]
     taps = taps_ref[:, :, pl.ds(pl.multiple_of(place * width, width), width)]
 
@@ -568,13 +563,13 @@
         outs[i][...] = product[pl.ds(start, block), :]
 
 
-def gate(where, own0, recv0, mixed, taps):
+def gate(own0, recv0, mixed, taps):
     length, width = own0.shape
     vmem = pl.BlockSpec(memory_space=pltpu.VMEM)
     return pl.pallas_call(
         gate_kernel,
         out_shape=(jax.ShapeDtypeStruct((length // 8, width), jnp.bfloat16),) * 8,
-        in_specs=[pl.BlockSpec(memory_space=pltpu.SMEM)] + [vmem] * 4,
+        in_specs=[vmem] * 4,
         out_specs=(vmem,) * 8,
         scratch_shapes=[
             pltpu.VMEM((length + 8, width), jnp.float32),
@@ -585,49 +580,53 @@
             flops=8 * length * width, bytes_accessed=12 * length * width, transcendentals=0
         ),
         name="gate",
-    )(where, own0, recv0, mixed, taps)
-
-
-def emit_kernel(where_ref, weight, *refs, order, turns, added):
-    parts, extra = refs[:8], refs[8 : 8 + added]
-    outs, joined = refs[8 + added : -1], refs[-1]
-    place, chan = where_ref[0], where_ref[1]
-    width = parts[0].shape[1]
-    columns = outs[0].shape[1]
+    )(own0, recv0, mixed, taps)
+
+
+def emit_kernel(weight, *refs, order, turn, added):
+    parts, extra = refs[: len(order)], refs[len(order) : len(order) + added]
+    out_ref = refs[len(order) + added]
+    place, chan = lax.axis_index("seq"), lax.axis_index("chan")
+    columns = out_ref.shape[1]
     tile = 256
-    for part, source in zip(parts, order, strict=True):
-        start = pl.multiple_of(jnp.bitwise_xor(place, source) * width, width)
-        joined[:, pl.ds(start, width)] = part[...]
-    for i, turn in enumerate(turns):
-        for low in range(0, columns, tile):
-            start = pl.multiple_of(jnp.bitwise_xor(chan, turn) * columns + low, tile)
-            total = jnp.dot(
-                joined[...], weight[:, pl.ds(start, tile)], preferred_element_type=jnp.float32
-            )
-            if added:
-                total = total + extra[i][:, low : low + tile].astype(jnp.float32)
-            outs[i][:, low : low + tile] = total.astype(outs[i].dtype)
-
-
-def emit(where, parts, order, weight, turns, extra, out_dtype):
-    rows, width = parts[0].shape
-    columns = weight.shape[1] // 4
+    if len(order) == 1:
+        joined = parts[0]
+    else:
+        joined = refs[-1]
+        width = parts[0].shape[1]
+        for part, source in zip(parts, order, strict=True):
+            start = pl.multiple_of(jnp.bitwise_xor(place, source) * width, width)
+            joined[:, pl.ds(start, width)] = part[...]
+    for low in range(0, columns, tile):
+        start = pl.multiple_of(jnp.bitwise_xor(chan, turn) * columns + low, tile)
+        total = jnp.dot(
+            joined[...], weight[:, pl.ds(start, tile)], preferred_element_type=jnp.float32
+        )
+        for term in extra:
+            total = total + term[:, low : low + tile].astype(jnp.float32)
+        out_ref[:, low : low + tile] = total.astype(out_ref.dtype)
+
+
+def emit(parts, order, weight, turn, extra, out_dtype):
+    rows = parts[0].shape[0]
+    depth, columns = weight.shape[0], weight.shape[1] // 4
     vmem = pl.BlockSpec(memory_space=pltpu.VMEM)
-    shape = jax.ShapeDtypeStruct((rows, columns), out_dtype)
+    shapes = [jax.ShapeDtypeStruct((rows, columns), out_dtype)]
+    if len(order) > 1:
+        shapes.append(jax.ShapeDtypeStruct((rows, depth), parts[0].dtype))
     return pl.pallas_call(
-        functools.partial(emit_kernel, order=order, turns=turns, added=len(extra)),
-        out_shape=(shape,) * len(turns),
-        in_specs=[pl.BlockSpec(memory_space=pltpu.SMEM)] + [vmem] * (9 + len(extra)),
-        out_specs=(vmem,) * len(turns),
-        scratch_shapes=[pltpu.VMEM((rows, 8 * width), jnp.bfloat16)],
+        functools.partial(emit_kernel, order=order, turn=turn, added=len(extra)),
+        out_shape=tuple(shapes),
+        in_specs=[vmem] * (1 + len(parts) + len(extra)),
+        out_specs=(vmem,) * len(shapes),
         compiler_params=pltpu.CompilerParams(vmem_limit_bytes=8 * 2**20),
         cost_estimate=pl.CostEstimate(
-            flops=2 * rows * weight.shape[0] * columns * len(turns),
-            bytes_accessed=2 * weight.shape[0] * columns * len(turns),
+            flops=2 * rows * depth * columns,
+            bytes_accessed=2 * depth * columns,
             transcendentals=0,
         ),
         name="emit",
-    )(where, weight, *parts, *extra)
+    )(weight, *parts, *extra)
 
 
 def swap(value, axis, count, turn):
@@ -636,11 +635,9 @@
 
 def fast_body(tokens, in_weight, short_taps, skip_gain, long_filter, out_weight):
     seq, chans = lax.axis_size("seq"), lax.axis_size("chan")
-    place, chan = lax.axis_index("seq"), lax.axis_index("chan")
     rows, width = tokens.shape
     length = rows * seq
     part = width // seq
-    where = jnp.stack([place, chan]).astype(jnp.int32)
 
     weight = jnp.transpose(in_weight, (1, 0, 2))
 
@@ -648,7 +645,7 @@
     rows = in_weight.shape[0]
 
     ours, theirs, cut1_2, cut_1 = halve(
-        where, tokens, long_filter, weight, [(2, (1,)), (1, (1, 2))]
+        tokens, long_filter, weight, [(2, (1,)), (1, (1, 2))]
     )
     beside = swap(theirs, "seq", seq, 1)
     w1_2, w_1 = swap(cut1_2, "seq", seq, 4), swap(cut_1, "seq", seq, 2)
@@ -657,7 +654,7 @@
     far = swap(pair, "seq", seq, 4)
     near = swap(pair, "seq", seq, 2)
     pair_across = swap(pair, "chan", chans, 2)
-    inputs = (where, weight, long_filter, beside)
+    inputs = (weight, long_filter, beside)
     plan = [(0, (1, 2, 0, "f")), (3, (1, 2, "f"))]
     plan += [(2, (0, "f")), (3, (0,)), (1, (0, "f")), (2, (2,))]
     w_0, cut_3, cut0_2, cut0_3, cut0_1, cut2_2 = cut(*inputs, plan, [pair])
@@ -686,7 +683,7 @@
     core_b = swap(second, "chan", chans, 1)
     line, across = [pair, near, far, far_near], [pair_across, across, far_near_across]
     cores = [core_a, core_b]
-    shared = (where, line, across, cores)
+    shared = (line, across, cores)
     own1, send1 = project(*shared, [w_0, w_1, w1_2, w_3], (0,) * 4, length, [])
     recv1 = swap(send1, "seq", seq, 1)
     w0_2, w0_3 = swap(cut0_2, "seq", seq, 4), swap(cut0_3, "seq", seq, 6)
@@ -695,13 +692,12 @@
     own2, send2 = project(*shared, [w_0, w_1, w2_2, w_3], (rows, rows, 0, rows), length, [])
     recv2 = swap(send2, "seq", seq, 1)
     freq = spectrum(
-        where, tables, [w_0, w0_1, w0_2, w_3], (3 * rows, rows, rows, 2 * rows), length, [send2]
+        tables, [w_0, w0_1, w0_2, w_3], (3 * rows, rows, rows, 2 * rows), length, [send2]
     )
     parts0 = [w_0, w0_1, w0_2, w0_3]
     own0, send0 = project(*shared, parts0, (2 * rows, 0, 0, 0), length, [])
     recv0 = swap(send0, "seq", seq, 1)
     mixed, held = mix(
-        where,
         own1,
         recv1,
         own2,
@@ -713,17 +709,17 @@
         out_weight,
         [send0],
     )
-    pieces = gate(where, own0, recv0, mixed, short_taps)
+    pieces = gate(own0, recv0, mixed, short_taps)
     order = (6, 7, 4, 5, 2, 3, 1, 0)
     joined = [swap(pieces[turn], "seq", seq, turn) if turn else pieces[0] for turn in order]
 
-    (across_out,) = emit(where, joined, order, held, (3,), [], jnp.bfloat16)
+    across_out, rows_here = emit(joined, order, held, 3, [], jnp.bfloat16)
     from_core = swap(across_out, "chan", chans, 1)
-    (beside_out,) = emit(where, joined, order, held, (1,), [], jnp.bfloat16)
+    (beside_out,) = emit([rows_here], (0,), held, 1, [], jnp.bfloat16)
     near_sum = swap(beside_out, "chan", chans, 1)
-    (chip_out,) = emit(where, joined, order, held, (2,), [from_core], jnp.bfloat16)
+    (chip_out,) = emit([rows_here], (0,), held, 2, [from_core], jnp.bfloat16)
     from_chip = swap(chip_out, "chan", chans, 2)
-    (own,) = emit(where, joined, order, held, (0,), [near_sum], jnp.float32)
+    (own,) = emit([rows_here], (0,), held, 0, [near_sum], jnp.float32)
     return (own + from_chip.astype(jnp.float32)).astype(jnp.bfloat16)
 
 

time: 177 us -> 172 us (0.972)
  Pallas kernels: 32.9 us -> 25.8 us
  waiting for transfers between devices: 98.3 us -> 104 us
  local copies, waits for them, and re-layouts: 2.9 us -> 1.01 us
    ppermute x29, waiting for transfers between devices: 98.3 us -> 104 us  [swap(): return lax.ppermute(value, axis, [(i, i ^ turn) for i in range(count)])]
    pallas_call x4, Pallas kernels: 5.62 us -> 3.13 us  [emit(): pl.pallas_call(functools.partial(emit_kernel, order=order, turn=turn, add...]
    unnamed x24 -> x22, local copies, waits for them, and re-layouts: 2.9 us -> 1.01 us
  transfers between devices with their start and end apart: 29 -> 29, of which waited for: 14 -> 18; matrix products, arithmetic and copies ran while one was open for 0% -> 0% of each run, Pallas kernels for 15% -> 13%
where the time goes in v7:
time: 172 us
  waiting for transfers between devices  104 us (60%)
  starting transfers between devices  40.7 us (24%)
  Pallas kernels  25.8 us (15%)
    ppermute x29, waiting for transfers between devices, swap(): return lax.ppermute(value, axis, [(i, i ^ turn) for i in range(count)])  104 us
    ppermute x29, starting transfers between devices, swap(): return lax.ppermute(value, axis, [(i, i ^ turn) for i in range(count)])  40.7 us
    pallas_call x1, Pallas kernels, mix(): pl.pallas_call(functools.partial(mix_kernel, after=len(after)), out_shape...  7.94 us
    pallas_call x3, Pallas kernels, project(): pl.pallas_call(functools.partial(project_kernel, lows=lows, after=len(aft...  7.46 us
  transfers between devices with their start and end apart: 29, of which 18 were waited for; matrix products, arithmetic and copies ran while one was open for 0% of the time, Pallas kernels for 13%

profile of v7, /device:TPU:0, one launch (start us, length us, event | category | flops | bytes accessed | tf_op | source)
XLA Modules:
  0.0 172.3 jit_solution(322433598691741473)
XLA Ops:
  0.0 2.7 %halve.1 = (bf16[256,512]{1,0:T(8,128)(2,1)}, bf16[512,512]{1,0:T(8,128)(2,1)}, bf16[512,256]{1,0:T(8,128)(2,1)}, bf16[1024,256]{1,0:T(8,128)(2,1)}) custom-call(bf16[256,1024]{1,0:T(8,128)(2,1)} %tokens.1, bf16[256,1024]{1,0:T(8,128)(2,1)} %filters.3, bf16[3,512,1024]{2,1,0:T(8,128)(2,1)} %bitcast.2), custom_call_target="tpu_custom_call" | custom-call | tf_op jit(solution)/shard_map/halve/pallas_call | solution.py:204
  2.8 3.0 %collective-permute-start = (bf16[512,512]{1,0:T(8,128)(2,1)}, bf16[512,512]{1,0:T(8,128)(2,1)S(1)}, u32[]{:S(2)}, u32[]{:S(2)}) collective-permute-start(bf16[512,512]{1,0:T(8,128)(2,1)} %get-tuple-element.34), channel_id=1, source_target_pairs={{0,4},{4,0},{8,12},{12,8},{16,20},{20,16},{24,28},{28,24},{1,5},{5... | collective-permute-start | bytes 1572872 | tf_op jit(solution)/shard_map/ppermute | solution.py:633
  5.8 2.6 %collective-permute-start.1 = (bf16[512,256]{1,0:T(8,128)(2,1)}, bf16[512,256]{1,0:T(8,128)(2,1)S(1)}, u32[]{:S(2)}, u32[]{:S(2)}) collective-permute-start(bf16[512,256]{1,0:T(8,128)(2,1)} %get-tuple-element.35), channel_id=1, source_target_pairs={{0,16},{4,20},{8,24},{12,28},{16,0},{20,4},{24,8},{28,12},{1,17},{... | collective-permute-start | bytes 786440 | tf_op jit(solution)/shard_map/ppermute | solution.py:633
  8.4 1.6 collective-permute-start.6
  9.9 10.4 %collective-permute-done.1.refs_2_.refs_11_ = bf16[512,256]{1,0:T(8,128)(2,1)S(1)} collective-permute-done((bf16[512,256]{1,0:T(8,128)(2,1)}, bf16[512,256]{1,0:T(8,128)(2,1)S(1)}, u32[]{:S(2)}, u32[]{:S(2)}) %collective-permute-start.1) | collective-permute-done | bytes 262176 | tf_op jit(solution)/shard_map/ppermute | solution.py:633
  21.4 1.6 collective-permute-start.5
  23.3 3.7 %collective-permute-start.2 = (bf16[512,512]{1,0:T(8,128)(2,1)S(1)}, bf16[512,512]{1,0:T(8,128)(2,1)S(1)}, u32[]{:S(2)}, u32[]{:S(2)}) collective-permute-start(bf16[512,512]{1,0:T(8,128)(2,1)S(1)} %join.4.refs_0_), channel_id=1, source_target_pairs={{0,8},{4,12},{8,0},{12,4},{16,24},{20,28},{24,16},{28,20},{1,9},{5... | collective-permute-start | bytes 1572872 | tf_op jit(solution)/shard_map/ppermute | solution.py:633
  29.0 5.2 %collective-permute-done.5.refs_2_.refs_1_.refs_4_ = bf16[512,512]{1,0:T(8,128)(2,1)S(1)} collective-permute-done((bf16[512,512]{1,0:T(8,128)(2,1)S(1)}, bf16[512,512]{1,0:T(8,128)(2,1)S(1)}, u32[]{:S(2)}, u32[]{:S(2)}) %collective-permute-start.5) | collective-permute-done | bytes 524320 | tf_op jit(solution)/shard_map/ppermute | solution.py:633
  34.1 13.5 %collective-permute-done.3.refs_0_.refs_2_ = bf16[512,512]{1,0:T(8,128)(2,1)S(1)} collective-permute-done((bf16[512,512]{1,0:T(8,128)(2,1)S(1)}, bf16[512,512]{1,0:T(8,128)(2,1)S(1)}, u32[]{:S(2)}, u32[]{:S(2)}) %collective-permute-start.3) | collective-permute-done | bytes 524320 | tf_op jit(solution)/shard_map/ppermute | solution.py:633
  48.7 1.6 collective-permute-start.7
  50.3 1.5 collective-permute-start.4
  53.1 11.0 %collective-permute-done.4.refs_2_.refs_3_ = bf16[512,512]{1,0:T(8,128)(2,1)S(1)} collective-permute-done((bf16[512,512]{1,0:T(8,128)(2,1)S(1)}, bf16[512,512]{1,0:T(8,128)(2,1)S(1)}, u32[]{:S(2)}, u32[]{:S(2)}) %collective-permute-start.4) | collective-permute-done | bytes 524320 | tf_op jit(solution)/shard_map/ppermute | solution.py:633
  64.7 2.4 %collective-permute-start.10 = (bf16[512,256]{1,0:T(8,128)(2,1)S(1)}, bf16[512,256]{1,0:T(8,128)(2,1)S(1)}, u32[]{:S(2)}, u32[]{:S(2)}) collective-permute-start(bf16[512,256]{1,0:T(8,128)(2,1)S(1)} %get-tuple-element.38), channel_id=1, source_target_pairs={{0,16},{4,20},{8,24},{12,28},{16,0},{20,4},{24,8},{28,12},{1,17},{... | collective-permute-start | bytes 786440 | tf_op jit(solution)/shard_map/ppermute | solution.py:633
  67.1 25.0 %collective-permute-done.10.refs_5_.refs_11_ = bf16[512,256]{1,0:T(8,128)(2,1)S(1)} collective-permute-done((bf16[512,256]{1,0:T(8,128)(2,1)S(1)}, bf16[512,256]{1,0:T(8,128)(2,1)S(1)}, u32[]{:S(2)}, u32[]{:S(2)}) %collective-permute-start.10) | collective-permute-done | bytes 262176 | tf_op jit(solution)/shard_map/ppermute | solution.py:633
  93.0 2.6 %collective-permute-start.17 = (bf16[512,256]{1,0:T(8,128)(2,1)S(1)}, bf16[512,256]{1,0:T(8,128)(2,1)S(1)}, u32[]{:S(2)}, u32[]{:S(2)}) collective-permute-start(bf16[512,256]{1,0:T(8,128)(2,1)S(1)} %get-tuple-element.46), channel_id=1, source_target_pairs={{0,24},{4,28},{8,16},{12,20},{16,8},{20,12},{24,0},{28,4},{1,25},{... | collective-permute-start | bytes 786440 | tf_op jit(solution)/shard_map/ppermute | solution.py:633
  95.6 1.7 %collective-permute-start.16 = (bf16[768,256]{1,0:T(8,128)(2,1)S(1)}, bf16[768,256]{1,0:T(8,128)(2,1)S(1)}, u32[]{:S(2)}, u32[]{:S(2)}) collective-permute-start(bf16[768,256]{1,0:T(8,128)(2,1)S(1)} %get-tuple-element.45), channel_id=1, source_target_pairs={{0,16},{4,20},{8,24},{12,28},{16,0},{20,4},{24,8},{28,12},{1,17},{... | collective-permute-start | bytes 1179656 | tf_op jit(solution)/shard_map/ppermute | solution.py:633
  97.4 2.0 %collective-permute-done.12.refs_8_ = bf16[2048,512]{1,0:T(8,128)(2,1)S(1)} collective-permute-done((bf16[2048,512]{1,0:T(8,128)(2,1)S(1)}, bf16[2048,512]{1,0:T(8,128)(2,1)S(1)}, u32[]{:S(2)}, u32[]{:S(2)}) %collective-permute-start.12) | collective-permute-done | bytes 2097184 | tf_op jit(solution)/shard_map/ppermute | solution.py:633
  99.4 2.5 %project.3 = (f32[2048,128]{1,0:T(8,128)S(1)}, bf16[2048,128]{1,0:T(8,128)(2,1)S(1)}) custom-call(bf16[512,512]{1,0:T(8,128)(2,1)S(1)} %join.4.refs_0_, bf16[512,512]{1,0:T(8,128)(2,1)S(1)} %collective-permute-done.2.refs_1_.refs_2_, bf16[512,512]{1,0:T(8,128)(2,1)S(1)} %collective-permute-done.3.refs_0_.refs_2_, ...), custom_call_target="tpu_custom_call" | custom-call | flops 4294967296 | bytes 8388608 | tf_op jit(solution)/shard_map/project/pallas_call | solution.py:337
  102.5 2.5 %project.4 = (f32[2048,128]{1,0:T(8,128)S(1)}, bf16[2048,128]{1,0:T(8,128)(2,1)S(1)}) custom-call(bf16[512,512]{1,0:T(8,128)(2,1)S(1)} %join.4.refs_0_, bf16[512,512]{1,0:T(8,128)(2,1)S(1)} %collective-permute-done.2.refs_1_.refs_2_, bf16[512,512]{1,0:T(8,128)(2,1)S(1)} %collective-permute-done.3.refs_0_.refs_2_, ...), custom_call_target="tpu_custom_call" | custom-call | flops 4294967296 | bytes 8388608 | tf_op jit(solution)/shard_map/project/pallas_call | solution.py:337
  105.1 1.6 collective-permute-start.14
  106.6 10.5 %collective-permute-done.15.refs_1_.refs_10_ = bf16[768,256]{1,0:T(8,128)(2,1)S(1)} collective-permute-done((bf16[768,256]{1,0:T(8,128)(2,1)S(1)}, bf16[768,256]{1,0:T(8,128)(2,1)S(1)}, u32[]{:S(2)}, u32[]{:S(2)}) %collective-permute-start.15) | collective-permute-done | bytes 393248 | tf_op jit(solution)/shard_map/ppermute | solution.py:633
  117.1 6.0 %collective-permute-done.16.refs_2_.refs_11_ = bf16[768,256]{1,0:T(8,128)(2,1)S(1)} collective-permute-done((bf16[768,256]{1,0:T(8,128)(2,1)S(1)}, bf16[768,256]{1,0:T(8,128)(2,1)S(1)}, u32[]{:S(2)}, u32[]{:S(2)}) %collective-permute-start.16) | collective-permute-done | bytes 393248 | tf_op jit(solution)/shard_map/ppermute | solution.py:633
  123.0 2.5 %project.5 = (f32[2048,128]{1,0:T(8,128)S(1)}, bf16[2048,128]{1,0:T(8,128)(2,1)S(1)}) custom-call(bf16[512,512]{1,0:T(8,128)(2,1)S(1)} %join.4.refs_0_, bf16[512,512]{1,0:T(8,128)(2,1)S(1)} %collective-permute-done.2.refs_1_.refs_2_, bf16[512,512]{1,0:T(8,128)(2,1)S(1)} %collective-permute-done.3.refs_0_.refs_2_, ...), custom_call_target="tpu_custom_call" | custom-call | flops 4294967296 | bytes 8388608 | tf_op jit(solution)/shard_map/project/pallas_call | solution.py:337
  126.2 3.0 %spectrum.1.freq_ref = f32[4224,128]{1,0:T(8,128)S(1)} custom-call(bf16[80,32]{1,0:T(8,128)(2,1)S(1)} %copy-done.6, bf16[33,128,128]{2,1,0:T(8,128)(2,1)S(1)} %copy-done.1, bf16[1792,256]{1,0:T(8,128)(2,1)S(1)} %get-tuple-element.39.refs_9_.refs_0_, bf16[768,256]{1,0:T(8,128)(2,1)S(1)} %collective-permute-done.15.refs_1_.refs_10_, ...), custom_call_target="tpu_custom_call" | custom-call | flops 67108864 | bytes 1048576 | tf_op jit(solution)/shard_map/spectrum/pallas_call | solution.py:425
  129.3 7.9 %mix.1 = (f32[2048,128]{1,0:T(8,128)S(1)}, bf16[1024,4096]{1,0:T(8,128)(2,1)S(1)}) custom-call(f32[2048,128]{1,0:T(8,128)S(1)} %get-tuple-element.40.own1, bf16[2048,128]{1,0:T(8,128)(2,1)S(1)} %collective-permute-done.13.recv1, f32[2048,128]{1,0:T(8,128)S(1)} %get-tuple-element.42.own2, bf16[2048,128]{1,0:T(8,128)(2,1)S(1)} %collective-permute-done.14.recv2, ...), custom_call_target="tpu_custom_call" | custom-call | flops 201326592 | bytes 6291456 | tf_op jit(solution)/shard_map/mix/pallas_call | solution.py:527
  137.2 1.5 collective-permute-done.18.recv0
  139.2 2.4 %collective-permute-start.19 = (bf16[256,128]{1,0:T(8,128)(2,1)S(1)}, bf16[256,128]{1,0:T(8,128)(2,1)S(1)}, u32[]{:S(2)}, u32[]{:S(2)}) collective-permute-start(bf16[256,128]{1,0:T(8,128)(2,1)S(1)} %get-tuple-element.51), channel_id=1, source_target_pairs={{0,24},{4,28},{8,16},{12,20},{16,8},{20,12},{24,0},{28,4},{1,25},{... | collective-permute-start | bytes 196616 | tf_op jit(solution)/shard_map/ppermute | solution.py:633
  141.6 1.5 collective-permute-start.20
  143.0 3.8 %collective-permute-start.22 = (bf16[256,128]{1,0:T(8,128)(2,1)S(1)}, bf16[256,128]{1,0:T(8,128)(2,1)S(1)}, u32[]{:S(2)}, u32[]{:S(2)}) collective-permute-start(bf16[256,128]{1,0:T(8,128)(2,1)S(1)} %get-tuple-element.54), channel_id=1, source_target_pairs={{0,20},{4,16},{8,28},{12,24},{16,4},{20,0},{24,12},{28,8},{1,21},{... | collective-permute-start | bytes 196616 | tf_op jit(solution)/shard_map/ppermute | solution.py:633
  146.9 2.0 %collective-permute-start.24 = (bf16[256,128]{1,0:T(8,128)(2,1)S(1)}, bf16[256,128]{1,0:T(8,128)(2,1)S(1)}, u32[]{:S(2)}, u32[]{:S(2)}) collective-permute-start(bf16[256,128]{1,0:T(8,128)(2,1)S(1)} %get-tuple-element.56), channel_id=1, source_target_pairs={{0,12},{4,8},{8,4},{12,0},{16,28},{20,24},{24,20},{28,16},{1,13},{... | collective-permute-start | bytes 196616 | tf_op jit(solution)/shard_map/ppermute | solution.py:633
  150.5 1.8 %collective-permute-done.22.refs_3_ = bf16[256,128]{1,0:T(8,128)(2,1)S(1)} collective-permute-done((bf16[256,128]{1,0:T(8,128)(2,1)S(1)}, bf16[256,128]{1,0:T(8,128)(2,1)S(1)}, u32[]{:S(2)}, u32[]{:S(2)}) %collective-permute-start.22) | collective-permute-done | bytes 65568 | tf_op jit(solution)/shard_map/ppermute | solution.py:633
  159.1 12.2 %collective-permute-done.28 = bf16[256,1024]{1,0:T(8,128)(2,1)S(1)} collective-permute-done((bf16[256,1024]{1,0:T(8,128)(2,1)S(1)}, bf16[256,1024]{1,0:T(8,128)(2,1)S(1)}, u32[]{:S(2)}, u32[]{:S(2)}) %collective-permute-start.28) | collective-permute-done | bytes 524320 | tf_op jit(solution)/shard_map/ppermute | solution.py:633
  (66 shorter events, 18.2 us)
Async XLA Ops:
  0.0 27.0 %copy-start = (bf16[512,3,1024]{2,0,1:T(8,128)(2,1)S(1)}, bf16[512,3,1024]{2,0,1:T(8,128)(2,1)}, u32[]{:S(2)}) copy-start(bf16[512,3,1024]{2,0,1:T(8,128)(2,1)} %param.11) | copy-start | bytes 9437188
  0.0 27.0 %copy-start.2 = (bf16[256,1024]{1,0:T(8,128)(2,1)S(1)}, bf16[256,1024]{1,0:T(8,128)(2,1)}, u32[]{:S(2)}) copy-start(bf16[256,1024]{1,0:T(8,128)(2,1)} %filters.3) | copy-start | bytes 1572868
  2.8 17.6 %collective-permute-start = (bf16[512,512]{1,0:T(8,128)(2,1)}, bf16[512,512]{1,0:T(8,128)(2,1)S(1)}, u32[]{:S(2)}, u32[]{:S(2)}) collective-permute-start(bf16[512,512]{1,0:T(8,128)(2,1)} %get-tuple-element.34), channel_id=1, source_target_pairs={{0,4},{4,0},{8,12},{12,8},{16,20},{20,16},{24,28},{28,24},{1,5},{5... | collective-permute-start | bytes 1572872 | tf_op jit(solution)/shard_map/ppermute | solution.py:633
  5.8 14.6 %collective-permute-start.1 = (bf16[512,256]{1,0:T(8,128)(2,1)}, bf16[512,256]{1,0:T(8,128)(2,1)S(1)}, u32[]{:S(2)}, u32[]{:S(2)}) collective-permute-start(bf16[512,256]{1,0:T(8,128)(2,1)} %get-tuple-element.35), channel_id=1, source_target_pairs={{0,16},{4,20},{8,24},{12,28},{16,0},{20,4},{24,8},{28,12},{1,17},{... | collective-permute-start | bytes 786440 | tf_op jit(solution)/shard_map/ppermute | solution.py:633
  8.4 20.6 %collective-permute-start.6 = (bf16[1024,256]{1,0:T(8,128)(2,1)}, bf16[1024,256]{1,0:T(8,128)(2,1)S(1)}, u32[]{:S(2)}, u32[]{:S(2)}) collective-permute-start(bf16[1024,256]{1,0:T(8,128)(2,1)} %get-tuple-element.37), channel_id=1, source_target_pairs={{0,8},{4,12},{8,0},{12,4},{16,24},{20,28},{24,16},{28,20},{1,9},{5... | collective-permute-start | bytes 1572872 | tf_op jit(solution)/shard_map/ppermute | solution.py:633
  21.4 12.8 %collective-permute-start.5 = (bf16[512,512]{1,0:T(8,128)(2,1)S(1)}, bf16[512,512]{1,0:T(8,128)(2,1)S(1)}, u32[]{:S(2)}, u32[]{:S(2)}) collective-permute-start(bf16[512,512]{1,0:T(8,128)(2,1)S(1)} %join.4.refs_0_), channel_id=1, source_target_pairs={{0,2},{1,3},{2,0},{3,1},{4,6},{5,7},{6,4},{7,5},{8,10},{9,11},{10,... | collective-permute-start | bytes 1572872 | tf_op jit(solution)/shard_map/ppermute | solution.py:633
  22.9 24.7 %collective-permute-start.3 = (bf16[512,512]{1,0:T(8,128)(2,1)S(1)}, bf16[512,512]{1,0:T(8,128)(2,1)S(1)}, u32[]{:S(2)}, u32[]{:S(2)}) collective-permute-start(bf16[512,512]{1,0:T(8,128)(2,1)S(1)} %join.4.refs_0_), channel_id=1, source_target_pairs={{0,16},{4,20},{8,24},{12,28},{16,0},{20,4},{24,8},{28,12},{1,17},{... | collective-permute-start | bytes 1572872 | tf_op jit(solution)/shard_map/ppermute | solution.py:633
  23.3 25.3 %collective-permute-start.2 = (bf16[512,512]{1,0:T(8,128)(2,1)S(1)}, bf16[512,512]{1,0:T(8,128)(2,1)S(1)}, u32[]{:S(2)}, u32[]{:S(2)}) collective-permute-start(bf16[512,512]{1,0:T(8,128)(2,1)S(1)} %join.4.refs_0_), channel_id=1, source_target_pairs={{0,8},{4,12},{8,0},{12,4},{16,24},{20,28},{24,16},{28,20},{1,9},{5... | collective-permute-start | bytes 1572872 | tf_op jit(solution)/shard_map/ppermute | solution.py:633
  48.7 43.3 %collective-permute-start.7 = (bf16[1024,512]{1,0:T(8,128)(2,1)S(1)}, bf16[1024,512]{1,0:T(8,128)(2,1)S(1)}, u32[]{:S(2)}, u32[]{:S(2)}) collective-permute-start(bf16[1024,512]{1,0:T(8,128)(2,1)S(1)} %join.5), channel_id=1, source_target_pairs={{0,2},{1,3},{2,0},{3,1},{4,6},{5,7},{6,4},{7,5},{8,10},{9,11},{10,... | collective-permute-start | bytes 3145736 | tf_op jit(solution)/shard_map/ppermute | solution.py:633
  50.3 13.9 %collective-permute-start.4 = (bf16[512,512]{1,0:T(8,128)(2,1)S(1)}, bf16[512,512]{1,0:T(8,128)(2,1)S(1)}, u32[]{:S(2)}, u32[]{:S(2)}) collective-permute-start(bf16[512,512]{1,0:T(8,128)(2,1)S(1)} %collective-permute-done.3.refs_0_.refs_2_), channel_id=1, source_target_pairs={{0,8},{4,12},{8,0},{12,4},{16,24},{20,28},{24,16},{28,20},{1,9},{5... | collective-permute-start | bytes 1572872 | tf_op jit(solution)/shard_map/ppermute | solution.py:633
  51.8 40.3 %collective-permute-start.9 = (bf16[1280,256]{1,0:T(8,128)(2,1)S(1)}, bf16[1280,256]{1,0:T(8,128)(2,1)S(1)}, u32[]{:S(2)}, u32[]{:S(2)}) collective-permute-start(bf16[1280,256]{1,0:T(8,128)(2,1)S(1)} %get-tuple-element.36.refs_3_), channel_id=1, source_target_pairs={{0,24},{4,28},{8,16},{12,20},{16,8},{20,12},{24,0},{28,4},{1,25},{... | collective-permute-start | bytes 1966088 | tf_op jit(solution)/shard_map/ppermute | solution.py:633
  64.2 28.1 %collective-permute-start.8 = (bf16[512,512]{1,0:T(8,128)(2,1)S(1)}, bf16[512,512]{1,0:T(8,128)(2,1)S(1)}, u32[]{:S(2)}, u32[]{:S(2)}) collective-permute-start(bf16[512,512]{1,0:T(8,128)(2,1)S(1)} %collective-permute-done.4.refs_2_.refs_3_), channel_id=1, source_target_pairs={{0,2},{1,3},{2,0},{3,1},{4,6},{5,7},{6,4},{7,5},{8,10},{9,11},{10,... | collective-permute-start | bytes 1572872 | tf_op jit(solution)/shard_map/ppermute | solution.py:633
  64.7 27.4 %collective-permute-start.10 = (bf16[512,256]{1,0:T(8,128)(2,1)S(1)}, bf16[512,256]{1,0:T(8,128)(2,1)S(1)}, u32[]{:S(2)}, u32[]{:S(2)}) collective-permute-start(bf16[512,256]{1,0:T(8,128)(2,1)S(1)} %get-tuple-element.38), channel_id=1, source_target_pairs={{0,16},{4,20},{8,24},{12,28},{16,0},{20,4},{24,8},{28,12},{1,17},{... | collective-permute-start | bytes 786440 | tf_op jit(solution)/shard_map/ppermute | solution.py:633
  92.2 5.2 %collective-permute-start.11 = (bf16[2048,512]{1,0:T(8,128)(2,1)S(1)}, bf16[2048,512]{1,0:T(8,128)(2,1)S(1)}, u32[]{:S(2)}, u32[]{:S(2)}) collective-permute-start(bf16[2048,512]{1,0:T(8,128)(2,1)S(1)} %join.6), channel_id=1, source_target_pairs={{0,1},{1,0},{2,3},{3,2},{4,5},{5,4},{6,7},{7,6},{8,9},{9,8},{10,11... | collective-permute-start | bytes 6291464 | tf_op jit(solution)/shard_map/ppermute | solution.py:633
  92.4 7.0 %collective-permute-start.12 = (bf16[2048,512]{1,0:T(8,128)(2,1)S(1)}, bf16[2048,512]{1,0:T(8,128)(2,1)S(1)}, u32[]{:S(2)}, u32[]{:S(2)}) collective-permute-start(bf16[2048,512]{1,0:T(8,128)(2,1)S(1)} %join.7), channel_id=1, source_target_pairs={{0,1},{1,0},{2,3},{3,2},{4,5},{5,4},{6,7},{7,6},{8,9},{9,8},{10,11... | collective-permute-start | bytes 6291464 | tf_op jit(solution)/shard_map/ppermute | solution.py:633
  93.0 13.6 %collective-permute-start.17 = (bf16[512,256]{1,0:T(8,128)(2,1)S(1)}, bf16[512,256]{1,0:T(8,128)(2,1)S(1)}, u32[]{:S(2)}, u32[]{:S(2)}) collective-permute-start(bf16[512,256]{1,0:T(8,128)(2,1)S(1)} %get-tuple-element.46), channel_id=1, source_target_pairs={{0,24},{4,28},{8,16},{12,20},{16,8},{20,12},{24,0},{28,4},{1,25},{... | collective-permute-start | bytes 786440 | tf_op jit(solution)/shard_map/ppermute | solution.py:633
  95.6 21.5 %collective-permute-start.15 = (bf16[768,256]{1,0:T(8,128)(2,1)S(1)}, bf16[768,256]{1,0:T(8,128)(2,1)S(1)}, u32[]{:S(2)}, u32[]{:S(2)}) collective-permute-start(bf16[768,256]{1,0:T(8,128)(2,1)S(1)} %get-tuple-element.44), channel_id=1, source_target_pairs={{0,8},{4,12},{8,0},{12,4},{16,24},{20,28},{24,16},{28,20},{1,9},{5... | collective-permute-start | bytes 1179656 | tf_op jit(solution)/shard_map/ppermute | solution.py:633
  95.6 27.4 %collective-permute-start.16 = (bf16[768,256]{1,0:T(8,128)(2,1)S(1)}, bf16[768,256]{1,0:T(8,128)(2,1)S(1)}, u32[]{:S(2)}, u32[]{:S(2)}) collective-permute-start(bf16[768,256]{1,0:T(8,128)(2,1)S(1)} %get-tuple-element.45), channel_id=1, source_target_pairs={{0,16},{4,20},{8,24},{12,28},{16,0},{20,4},{24,8},{28,12},{1,17},{... | collective-permute-start | bytes 1179656 | tf_op jit(solution)/shard_map/ppermute | solution.py:633
  101.9 27.3 %collective-permute-start.13 = (bf16[2048,128]{1,0:T(8,128)(2,1)S(1)}, bf16[2048,128]{1,0:T(8,128)(2,1)S(1)}, u32[]{:S(2)}, u32[]{:S(2)}) collective-permute-start(bf16[2048,128]{1,0:T(8,128)(2,1)S(1)} %get-tuple-element.41), channel_id=1, source_target_pairs={{0,4},{4,0},{8,12},{12,8},{16,20},{20,16},{24,28},{28,24},{1,5},{5... | collective-permute-start | bytes 1572872 | tf_op jit(solution)/shard_map/ppermute | solution.py:633
  105.0 24.2 %slice-start = ((s8[8388608]{0:T(1024)(128)(4,1)}), s8[4194304]{0:T(1024)(128)(4,1)S(1)}, s32[]{:S(2)}) async-start(s8[8388608]{0:T(1024)(128)(4,1)} %bitcast.4), calls=%async_computation | async-start | bytes 8388608
  105.1 24.2 %collective-permute-start.14 = (bf16[2048,128]{1,0:T(8,128)(2,1)S(1)}, bf16[2048,128]{1,0:T(8,128)(2,1)S(1)}, u32[]{:S(2)}, u32[]{:S(2)}) collective-permute-start(bf16[2048,128]{1,0:T(8,128)(2,1)S(1)} %get-tuple-element.43.refs_4_), channel_id=1, source_target_pairs={{0,4},{4,0},{8,12},{12,8},{16,20},{20,16},{24,28},{28,24},{1,5},{5... | collective-permute-start | bytes 1572872 | tf_op jit(solution)/shard_map/ppermute | solution.py:633
  125.6 13.1 %collective-permute-start.18 = (bf16[2048,128]{1,0:T(8,128)(2,1)S(1)}, bf16[2048,128]{1,0:T(8,128)(2,1)S(1)}, u32[]{:S(2)}, u32[]{:S(2)}) collective-permute-start(bf16[2048,128]{1,0:T(8,128)(2,1)S(1)} %get-tuple-element.47.refs_0_), channel_id=1, source_target_pairs={{0,4},{4,0},{8,12},{12,8},{16,20},{20,16},{24,28},{28,24},{1,5},{5... | collective-permute-start | bytes 1572872 | tf_op jit(solution)/shard_map/ppermute | solution.py:633
  139.2 7.7 %collective-permute-start.19 = (bf16[256,128]{1,0:T(8,128)(2,1)S(1)}, bf16[256,128]{1,0:T(8,128)(2,1)S(1)}, u32[]{:S(2)}, u32[]{:S(2)}) collective-permute-start(bf16[256,128]{1,0:T(8,128)(2,1)S(1)} %get-tuple-element.51), channel_id=1, source_target_pairs={{0,24},{4,28},{8,16},{12,20},{16,8},{20,12},{24,0},{28,4},{1,25},{... | collective-permute-start | bytes 196616 | tf_op jit(solution)/shard_map/ppermute | solution.py:633
  141.6 7.4 %collective-permute-start.20 = (bf16[256,128]{1,0:T(8,128)(2,1)S(1)}, bf16[256,128]{1,0:T(8,128)(2,1)S(1)}, u32[]{:S(2)}, u32[]{:S(2)}) collective-permute-start(bf16[256,128]{1,0:T(8,128)(2,1)S(1)} %get-tuple-element.52), channel_id=1, source_target_pairs={{0,28},{4,24},{8,20},{12,16},{16,12},{20,8},{24,4},{28,0},{1,29},{... | collective-permute-start | bytes 196616 | tf_op jit(solution)/shard_map/ppermute | solution.py:633
  143.0 7.4 %collective-permute-start.21 = (bf16[256,128]{1,0:T(8,128)(2,1)S(1)}, bf16[256,128]{1,0:T(8,128)(2,1)S(1)}, u32[]{:S(2)}, u32[]{:S(2)}) collective-permute-start(bf16[256,128]{1,0:T(8,128)(2,1)S(1)} %get-tuple-element.53), channel_id=1, source_target_pairs={{0,16},{4,20},{8,24},{12,28},{16,0},{20,4},{24,8},{28,12},{1,17},{... | collective-permute-start | bytes 196616 | tf_op jit(solution)/shard_map/ppermute | solution.py:633
  143.0 9.3 %collective-permute-start.22 = (bf16[256,128]{1,0:T(8,128)(2,1)S(1)}, bf16[256,128]{1,0:T(8,128)(2,1)S(1)}, u32[]{:S(2)}, u32[]{:S(2)}) collective-permute-start(bf16[256,128]{1,0:T(8,128)(2,1)S(1)} %get-tuple-element.54), channel_id=1, source_target_pairs={{0,20},{4,16},{8,28},{12,24},{16,4},{20,0},{24,12},{28,8},{1,21},{... | collective-permute-start | bytes 196616 | tf_op jit(solution)/shard_map/ppermute | solution.py:633
  146.9 5.4 %collective-permute-start.23 = (bf16[256,128]{1,0:T(8,128)(2,1)S(1)}, bf16[256,128]{1,0:T(8,128)(2,1)S(1)}, u32[]{:S(2)}, u32[]{:S(2)}) collective-permute-start(bf16[256,128]{1,0:T(8,128)(2,1)S(1)} %get-tuple-element.55), channel_id=1, source_target_pairs={{0,8},{4,12},{8,0},{12,4},{16,24},{20,28},{24,16},{28,20},{1,9},{5... | collective-permute-start | bytes 196616 | tf_op jit(solution)/shard_map/ppermute | solution.py:633
  146.9 6.2 %collective-permute-start.24 = (bf16[256,128]{1,0:T(8,128)(2,1)S(1)}, bf16[256,128]{1,0:T(8,128)(2,1)S(1)}, u32[]{:S(2)}, u32[]{:S(2)}) collective-permute-start(bf16[256,128]{1,0:T(8,128)(2,1)S(1)} %get-tuple-element.56), channel_id=1, source_target_pairs={{0,12},{4,8},{8,4},{12,0},{16,28},{20,24},{24,20},{28,16},{1,13},{... | collective-permute-start | bytes 196616 | tf_op jit(solution)/shard_map/ppermute | solution.py:633
  148.9 4.8 %collective-permute-start.25 = (bf16[256,128]{1,0:T(8,128)(2,1)S(1)}, bf16[256,128]{1,0:T(8,128)(2,1)S(1)}, u32[]{:S(2)}, u32[]{:S(2)}) collective-permute-start(bf16[256,128]{1,0:T(8,128)(2,1)S(1)} %get-tuple-element.57), channel_id=1, source_target_pairs={{0,4},{4,0},{8,12},{12,8},{16,20},{20,16},{24,28},{28,24},{1,5},{5... | collective-permute-start | bytes 196616 | tf_op jit(solution)/shard_map/ppermute | solution.py:633
  154.6 2.0 %collective-permute-start.27 = (bf16[256,1024]{1,0:T(8,128)(2,1)S(1)}, bf16[256,1024]{1,0:T(8,128)(2,1)S(1)}, u32[]{:S(2)}, u32[]{:S(2)}) collective-permute-start(bf16[256,1024]{1,0:T(8,128)(2,1)S(1)} %get-tuple-element.60), channel_id=1, source_target_pairs={{0,1},{1,0},{2,3},{3,2},{4,5},{5,4},{6,7},{7,6},{8,9},{9,8},{10,11... | collective-permute-start | bytes 1572872 | tf_op jit(solution)/shard_map/ppermute | solution.py:633
  155.4 2.9 %collective-permute-start.26 = (bf16[256,1024]{1,0:T(8,128)(2,1)S(1)}, bf16[256,1024]{1,0:T(8,128)(2,1)S(1)}, u32[]{:S(2)}, u32[]{:S(2)}) collective-permute-start(bf16[256,1024]{1,0:T(8,128)(2,1)S(1)} %emit.5), channel_id=1, source_target_pairs={{0,1},{1,0},{2,3},{3,2},{4,5},{5,4},{6,7},{7,6},{8,9},{9,8},{10,11... | collective-permute-start | bytes 1572872 | tf_op jit(solution)/shard_map/ppermute | solution.py:633
  157.3 14.0 %collective-permute-start.28 = (bf16[256,1024]{1,0:T(8,128)(2,1)S(1)}, bf16[256,1024]{1,0:T(8,128)(2,1)S(1)}, u32[]{:S(2)}, u32[]{:S(2)}) collective-permute-start(bf16[256,1024]{1,0:T(8,128)(2,1)S(1)} %emit.7), channel_id=1, source_target_pairs={{0,2},{1,3},{2,0},{3,1},{4,6},{5,7},{6,4},{7,5},{8,10},{9,11},{10,... | collective-permute-start | bytes 1572872 | tf_op jit(solution)/shard_map/ppermute | solution.py:633
  (8 other events, 82.3 us)

commit v8 on v7

--- a/solution.py
+++ b/solution.py
@@ -164,11 +164,11 @@
     )
 
 
-def halve_kernel(tokens, filters, weight, ours, theirs, *refs, plan):
+def halve_kernel(tokens, filters, weight, theirs, *refs, plan):
     pieces, sems = refs[:-1], refs[-1]
     place = lax.axis_index("seq")
     depth, side = place // 2, place % 2
-    rows, half = ours.shape
+    rows, half = tokens.shape[0], theirs.shape[1]
     part = half // 4
     copies = []
 
@@ -178,7 +178,6 @@
             pltpu.make_async_copy(source.at[:, columns], target, sems.at[len(copies)])
         )
 
-    copy(tokens, side, half, ours)
     copy(tokens, 1 - side, half, theirs.at[pl.ds(0, rows), :])
     for i in range(4):
         target = theirs.at[pl.ds(rows, filters.shape[0]), pl.ds(i * part, part)]
@@ -204,18 +203,38 @@
     return pl.pallas_call(
         functools.partial(halve_kernel, plan=plan),
         out_shape=(
-            jax.ShapeDtypeStruct((rows, half), tokens.dtype),
             jax.ShapeDtypeStruct((rows + filters.shape[0], half), tokens.dtype),
         )
         + pieces,
         in_specs=[pl.BlockSpec(memory_space=pl.ANY)] * 3,
-        out_specs=(vmem,) * (2 + len(plan)),
+        out_specs=(vmem,) * (1 + len(plan)),
         scratch_shapes=[
-            pltpu.SemaphoreType.DMA((6 + sum(len(names) for _, names in plan),))
+            pltpu.SemaphoreType.DMA((5 + sum(len(names) for _, names in plan),))
         ],
         compiler_params=pltpu.CompilerParams(vmem_limit_bytes=60 * 2**20),
         name="halve",
     )(tokens, filters, weight)
+
+
+def own_half_kernel(tokens, ours, sem):
+    half = ours.shape[1]
+    start = pl.multiple_of(lax.axis_index("seq") % 2 * half, half)
+    copy = pltpu.make_async_copy(tokens.at[:, pl.ds(start, half)], ours, sem)
+    copy.start()
+    copy.wait()
+
+
+def own_half(tokens, after):
+    rows, half = tokens.shape[0], tokens.shape[1] // 2
+    return pl.pallas_call(
+        lambda *refs: own_half_kernel(refs[0], refs[-2], refs[-1]),
+        out_shape=jax.ShapeDtypeStruct((rows, half), tokens.dtype),
+        in_specs=[pl.BlockSpec(memory_space=pl.ANY)] * (1 + len(after)),
+        out_specs=pl.BlockSpec(memory_space=pltpu.VMEM),
+        scratch_shapes=[pltpu.SemaphoreType.DMA],
+        compiler_params=pltpu.CompilerParams(vmem_limit_bytes=8 * 2**20),
+        name="own_half",
+    )(tokens, *after)
 
 
 def cut_kernel(weight, filters, filter_beside, *refs, plan, after):
@@ -644,9 +663,10 @@
     lags = tokens.shape[0]
     rows = in_weight.shape[0]
 
-    ours, theirs, cut1_2, cut_1 = halve(
+    theirs, cut1_2, cut_1 = halve(
         tokens, long_filter, weight, [(2, (1,)), (1, (1, 2))]
     )
+    ours = own_half(tokens, [theirs])
     beside = swap(theirs, "seq", seq, 1)
     w1_2, w_1 = swap(cut1_2, "seq", seq, 4), swap(cut_1, "seq", seq, 2)
     whole = [(0, 0, lags), (1, 0, lags)]

time: 172 us -> 172 us (level)
  waiting for transfers between devices: 104 us -> 102 us
  transfers between devices with their start and end apart: 29 -> 29, of which waited for: 18 -> 17; matrix products, arithmetic and copies ran while one was open for 0% -> 0% of each run, Pallas kernels for 13% -> 13%
where the time goes in v8:
time: 172 us; the launch traced here: 171 us
  waiting for transfers between devices  102 us (59%)
  starting transfers between devices  41 us (24%)
  Pallas kernels  25.7 us (15%)
    ppermute x29, waiting for transfers between devices, swap(): return lax.ppermute(value, axis, [(i, i ^ turn) for i in range(count)])  102 us
    ppermute x29, starting transfers between devices, swap(): return lax.ppermute(value, axis, [(i, i ^ turn) for i in range(count)])  41 us
    pallas_call x1, Pallas kernels, mix(): pl.pallas_call(functools.partial(mix_kernel, after=len(after)), out_shape...  7.95 us
    pallas_call x3, Pallas kernels, project(): pl.pallas_call(functools.partial(project_kernel, lows=lows, after=len(aft...  7.46 us
  transfers between devices with their start and end apart: 29, of which 17 were waited for; matrix products, arithmetic and copies ran while one was open for 0% of the time, Pallas kernels for 13%

profile of v8, /device:TPU:0, one launch (start us, length us, event | category | flops | bytes accessed | tf_op | source)
XLA Modules:
  0.0 171.4 jit_solution(3178965050414265613)
XLA Ops:
  0.0 2.6 %halve.1 = (bf16[512,512]{1,0:T(8,128)(2,1)}, bf16[512,256]{1,0:T(8,128)(2,1)}, bf16[1024,256]{1,0:T(8,128)(2,1)}) custom-call(bf16[256,1024]{1,0:T(8,128)(2,1)} %refs_0_.1, bf16[256,1024]{1,0:T(8,128)(2,1)} %filters.3, bf16[3,512,1024]{2,1,0:T(8,128)(2,1)} %bitcast.2), custom_call_target="tpu_custom_call" | custom-call | tf_op jit(solution)/shard_map/halve/pallas_call | solution.py:203
  2.6 3.0 %collective-permute-start = (bf16[512,512]{1,0:T(8,128)(2,1)}, bf16[512,512]{1,0:T(8,128)(2,1)S(1)}, u32[]{:S(2)}, u32[]{:S(2)}) collective-permute-start(bf16[512,512]{1,0:T(8,128)(2,1)} %get-tuple-element.32.refs_1_), channel_id=1, source_target_pairs={{0,4},{4,0},{8,12},{12,8},{16,20},{20,16},{24,28},{28,24},{1,5},{5... | collective-permute-start | bytes 1572872 | tf_op jit(solution)/shard_map/ppermute | solution.py:652
  5.6 2.6 %collective-permute-start.1 = (bf16[512,256]{1,0:T(8,128)(2,1)}, bf16[512,256]{1,0:T(8,128)(2,1)S(1)}, u32[]{:S(2)}, u32[]{:S(2)}) collective-permute-start(bf16[512,256]{1,0:T(8,128)(2,1)} %get-tuple-element.33), channel_id=1, source_target_pairs={{0,16},{4,20},{8,24},{12,28},{16,0},{20,4},{24,8},{28,12},{1,17},{... | collective-permute-start | bytes 786440 | tf_op jit(solution)/shard_map/ppermute | solution.py:652
  8.2 1.6 collective-permute-start.6
  10.9 9.3 %collective-permute-done.1.refs_2_.refs_11_ = bf16[512,256]{1,0:T(8,128)(2,1)S(1)} collective-permute-done((bf16[512,256]{1,0:T(8,128)(2,1)}, bf16[512,256]{1,0:T(8,128)(2,1)S(1)}, u32[]{:S(2)}, u32[]{:S(2)}) %collective-permute-start.1) | collective-permute-done | bytes 262176 | tf_op jit(solution)/shard_map/ppermute | solution.py:652
  20.3 1.6 collective-permute-start.5
  22.2 3.7 %collective-permute-start.2 = (bf16[512,512]{1,0:T(8,128)(2,1)S(1)}, bf16[512,512]{1,0:T(8,128)(2,1)S(1)}, u32[]{:S(2)}, u32[]{:S(2)}) collective-permute-start(bf16[512,512]{1,0:T(8,128)(2,1)S(1)} %join.4.refs_0_), channel_id=1, source_target_pairs={{0,8},{4,12},{8,0},{12,4},{16,24},{20,28},{24,16},{28,20},{1,9},{5... | collective-permute-start | bytes 1572872 | tf_op jit(solution)/shard_map/ppermute | solution.py:652
  26.6 4.1 %collective-permute-done.6.refs_4_.refs_10_ = bf16[1024,256]{1,0:T(8,128)(2,1)S(1)} collective-permute-done((bf16[1024,256]{1,0:T(8,128)(2,1)}, bf16[1024,256]{1,0:T(8,128)(2,1)S(1)}, u32[]{:S(2)}, u32[]{:S(2)}) %collective-permute-start.6) | collective-permute-done | bytes 524320 | tf_op jit(solution)/shard_map/ppermute | solution.py:652
  30.7 2.4 %collective-permute-done.5.refs_2_.refs_1_.refs_4_ = bf16[512,512]{1,0:T(8,128)(2,1)S(1)} collective-permute-done((bf16[512,512]{1,0:T(8,128)(2,1)S(1)}, bf16[512,512]{1,0:T(8,128)(2,1)S(1)}, u32[]{:S(2)}, u32[]{:S(2)}) %collective-permute-start.5) | collective-permute-done | bytes 524320 | tf_op jit(solution)/shard_map/ppermute | solution.py:652
  33.1 13.5 %collective-permute-done.3.refs_0_.refs_2_ = bf16[512,512]{1,0:T(8,128)(2,1)S(1)} collective-permute-done((bf16[512,512]{1,0:T(8,128)(2,1)S(1)}, bf16[512,512]{1,0:T(8,128)(2,1)S(1)}, u32[]{:S(2)}, u32[]{:S(2)}) %collective-permute-start.3) | collective-permute-done | bytes 524320 | tf_op jit(solution)/shard_map/ppermute | solution.py:652
  46.6 1.9 %collective-permute-done.2.refs_1_.refs_2_ = bf16[512,512]{1,0:T(8,128)(2,1)S(1)} collective-permute-done((bf16[512,512]{1,0:T(8,128)(2,1)S(1)}, bf16[512,512]{1,0:T(8,128)(2,1)S(1)}, u32[]{:S(2)}, u32[]{:S(2)}) %collective-permute-start.2) | collective-permute-done | bytes 524320 | tf_op jit(solution)/shard_map/ppermute | solution.py:652
  48.6 1.6 collective-permute-start.7
  50.2 1.5 collective-permute-start.4
  53.0 11.0 %collective-permute-done.4.refs_2_.refs_3_ = bf16[512,512]{1,0:T(8,128)(2,1)S(1)} collective-permute-done((bf16[512,512]{1,0:T(8,128)(2,1)S(1)}, bf16[512,512]{1,0:T(8,128)(2,1)S(1)}, u32[]{:S(2)}, u32[]{:S(2)}) %collective-permute-start.4) | collective-permute-done | bytes 524320 | tf_op jit(solution)/shard_map/ppermute | solution.py:652
  64.5 2.4 %collective-permute-start.10 = (bf16[512,256]{1,0:T(8,128)(2,1)S(1)}, bf16[512,256]{1,0:T(8,128)(2,1)S(1)}, u32[]{:S(2)}, u32[]{:S(2)}) collective-permute-start(bf16[512,256]{1,0:T(8,128)(2,1)S(1)} %get-tuple-element.36), channel_id=1, source_target_pairs={{0,16},{4,20},{8,24},{12,28},{16,0},{20,4},{24,8},{28,12},{1,17},{... | collective-permute-start | bytes 786440 | tf_op jit(solution)/shard_map/ppermute | solution.py:652
  66.9 24.5 %collective-permute-done.10.refs_5_.refs_11_ = bf16[512,256]{1,0:T(8,128)(2,1)S(1)} collective-permute-done((bf16[512,256]{1,0:T(8,128)(2,1)S(1)}, bf16[512,256]{1,0:T(8,128)(2,1)S(1)}, u32[]{:S(2)}, u32[]{:S(2)}) %collective-permute-start.10) | collective-permute-done | bytes 262176 | tf_op jit(solution)/shard_map/ppermute | solution.py:652
  92.3 2.4 %collective-permute-start.17 = (bf16[512,256]{1,0:T(8,128)(2,1)S(1)}, bf16[512,256]{1,0:T(8,128)(2,1)S(1)}, u32[]{:S(2)}, u32[]{:S(2)}) collective-permute-start(bf16[512,256]{1,0:T(8,128)(2,1)S(1)} %get-tuple-element.44), channel_id=1, source_target_pairs={{0,24},{4,28},{8,16},{12,20},{16,8},{20,12},{24,0},{28,4},{1,25},{... | collective-permute-start | bytes 786440 | tf_op jit(solution)/shard_map/ppermute | solution.py:652
  94.7 2.0 %collective-permute-start.16 = (bf16[768,256]{1,0:T(8,128)(2,1)S(1)}, bf16[768,256]{1,0:T(8,128)(2,1)S(1)}, u32[]{:S(2)}, u32[]{:S(2)}) collective-permute-start(bf16[768,256]{1,0:T(8,128)(2,1)S(1)} %get-tuple-element.43), channel_id=1, source_target_pairs={{0,16},{4,20},{8,24},{12,28},{16,0},{20,4},{24,8},{28,12},{1,17},{... | collective-permute-start | bytes 1179656 | tf_op jit(solution)/shard_map/ppermute | solution.py:652
  96.7 2.0 %collective-permute-done.12.refs_8_ = bf16[2048,512]{1,0:T(8,128)(2,1)S(1)} collective-permute-done((bf16[2048,512]{1,0:T(8,128)(2,1)S(1)}, bf16[2048,512]{1,0:T(8,128)(2,1)S(1)}, u32[]{:S(2)}, u32[]{:S(2)}) %collective-permute-start.12) | collective-permute-done | bytes 2097184 | tf_op jit(solution)/shard_map/ppermute | solution.py:652
  98.8 2.5 %project.3 = (f32[2048,128]{1,0:T(8,128)S(1)}, bf16[2048,128]{1,0:T(8,128)(2,1)S(1)}) custom-call(bf16[512,512]{1,0:T(8,128)(2,1)S(1)} %join.4.refs_0_, bf16[512,512]{1,0:T(8,128)(2,1)S(1)} %collective-permute-done.2.refs_1_.refs_2_, bf16[512,512]{1,0:T(8,128)(2,1)S(1)} %collective-permute-done.3.refs_0_.refs_2_, ...), custom_call_target="tpu_custom_call" | custom-call | flops 4294967296 | bytes 8388608 | tf_op jit(solution)/shard_map/project/pallas_call | solution.py:356
  101.9 2.5 %project.4 = (f32[2048,128]{1,0:T(8,128)S(1)}, bf16[2048,128]{1,0:T(8,128)(2,1)S(1)}) custom-call(bf16[512,512]{1,0:T(8,128)(2,1)S(1)} %join.4.refs_0_, bf16[512,512]{1,0:T(8,128)(2,1)S(1)} %collective-permute-done.2.refs_1_.refs_2_, bf16[512,512]{1,0:T(8,128)(2,1)S(1)} %collective-permute-done.3.refs_0_.refs_2_, ...), custom_call_target="tpu_custom_call" | custom-call | flops 4294967296 | bytes 8388608 | tf_op jit(solution)/shard_map/project/pallas_call | solution.py:356
  104.4 1.6 collective-permute-start.14
  106.0 10.7 %collective-permute-done.15.refs_1_.refs_10_ = bf16[768,256]{1,0:T(8,128)(2,1)S(1)} collective-permute-done((bf16[768,256]{1,0:T(8,128)(2,1)S(1)}, bf16[768,256]{1,0:T(8,128)(2,1)S(1)}, u32[]{:S(2)}, u32[]{:S(2)}) %collective-permute-start.15) | collective-permute-done | bytes 393248 | tf_op jit(solution)/shard_map/ppermute | solution.py:652
  116.7 5.5 %collective-permute-done.16.refs_2_.refs_11_ = bf16[768,256]{1,0:T(8,128)(2,1)S(1)} collective-permute-done((bf16[768,256]{1,0:T(8,128)(2,1)S(1)}, bf16[768,256]{1,0:T(8,128)(2,1)S(1)}, u32[]{:S(2)}, u32[]{:S(2)}) %collective-permute-start.16) | collective-permute-done | bytes 393248 | tf_op jit(solution)/shard_map/ppermute | solution.py:652
  122.1 2.5 %project.5 = (f32[2048,128]{1,0:T(8,128)S(1)}, bf16[2048,128]{1,0:T(8,128)(2,1)S(1)}) custom-call(bf16[512,512]{1,0:T(8,128)(2,1)S(1)} %join.4.refs_0_, bf16[512,512]{1,0:T(8,128)(2,1)S(1)} %collective-permute-done.2.refs_1_.refs_2_, bf16[512,512]{1,0:T(8,128)(2,1)S(1)} %collective-permute-done.3.refs_0_.refs_2_, ...), custom_call_target="tpu_custom_call" | custom-call | flops 4294967296 | bytes 8388608 | tf_op jit(solution)/shard_map/project/pallas_call | solution.py:356
  125.3 3.0 %spectrum.1.freq_ref = f32[4224,128]{1,0:T(8,128)S(1)} custom-call(bf16[80,32]{1,0:T(8,128)(2,1)S(1)} %copy-done.7, bf16[33,128,128]{2,1,0:T(8,128)(2,1)S(1)} %copy-done.1, bf16[1792,256]{1,0:T(8,128)(2,1)S(1)} %get-tuple-element.37.refs_9_.refs_0_, bf16[768,256]{1,0:T(8,128)(2,1)S(1)} %collective-permute-done.15.refs_1_.refs_10_, ...), custom_call_target="tpu_custom_call" | custom-call | flops 67108864 | bytes 1048576 | tf_op jit(solution)/shard_map/spectrum/pallas_call | solution.py:444
  128.4 7.9 %mix.1 = (f32[2048,128]{1,0:T(8,128)S(1)}, bf16[1024,4096]{1,0:T(8,128)(2,1)S(1)}) custom-call(f32[2048,128]{1,0:T(8,128)S(1)} %get-tuple-element.38.own1, bf16[2048,128]{1,0:T(8,128)(2,1)S(1)} %collective-permute-done.13.recv1, f32[2048,128]{1,0:T(8,128)S(1)} %get-tuple-element.40.own2, bf16[2048,128]{1,0:T(8,128)(2,1)S(1)} %collective-permute-done.14.recv2, ...), custom_call_target="tpu_custom_call" | custom-call | flops 201326592 | bytes 6291456 | tf_op jit(solution)/shard_map/mix/pallas_call | solution.py:546
  138.2 2.4 %collective-permute-start.19 = (bf16[256,128]{1,0:T(8,128)(2,1)S(1)}, bf16[256,128]{1,0:T(8,128)(2,1)S(1)}, u32[]{:S(2)}, u32[]{:S(2)}) collective-permute-start(bf16[256,128]{1,0:T(8,128)(2,1)S(1)} %get-tuple-element.49), channel_id=1, source_target_pairs={{0,24},{4,28},{8,16},{12,20},{16,8},{20,12},{24,0},{28,4},{1,25},{... | collective-permute-start | bytes 196616 | tf_op jit(solution)/shard_map/ppermute | solution.py:652
  142.1 3.8 %collective-permute-start.22 = (bf16[256,128]{1,0:T(8,128)(2,1)S(1)}, bf16[256,128]{1,0:T(8,128)(2,1)S(1)}, u32[]{:S(2)}, u32[]{:S(2)}) collective-permute-start(bf16[256,128]{1,0:T(8,128)(2,1)S(1)} %get-tuple-element.52), channel_id=1, source_target_pairs={{0,20},{4,16},{8,28},{12,24},{16,4},{20,0},{24,12},{28,8},{1,21},{... | collective-permute-start | bytes 196616 | tf_op jit(solution)/shard_map/ppermute | solution.py:652
  146.0 2.0 %collective-permute-start.24 = (bf16[256,128]{1,0:T(8,128)(2,1)S(1)}, bf16[256,128]{1,0:T(8,128)(2,1)S(1)}, u32[]{:S(2)}, u32[]{:S(2)}) collective-permute-start(bf16[256,128]{1,0:T(8,128)(2,1)S(1)} %get-tuple-element.54), channel_id=1, source_target_pairs={{0,12},{4,8},{8,4},{12,0},{16,28},{20,24},{24,20},{28,16},{1,13},{... | collective-permute-start | bytes 196616 | tf_op jit(solution)/shard_map/ppermute | solution.py:652
  149.6 1.8 %collective-permute-done.22.refs_3_ = bf16[256,128]{1,0:T(8,128)(2,1)S(1)} collective-permute-done((bf16[256,128]{1,0:T(8,128)(2,1)S(1)}, bf16[256,128]{1,0:T(8,128)(2,1)S(1)}, u32[]{:S(2)}, u32[]{:S(2)}) %collective-permute-start.22) | collective-permute-done | bytes 65568 | tf_op jit(solution)/shard_map/ppermute | solution.py:652
  158.5 11.9 %collective-permute-done.28 = bf16[256,1024]{1,0:T(8,128)(2,1)S(1)} collective-permute-done((bf16[256,1024]{1,0:T(8,128)(2,1)S(1)}, bf16[256,1024]{1,0:T(8,128)(2,1)S(1)}, u32[]{:S(2)}, u32[]{:S(2)}) %collective-permute-start.28) | collective-permute-done | bytes 524320 | tf_op jit(solution)/shard_map/ppermute | solution.py:652
  (69 shorter events, 19.3 us)
Async XLA Ops:
  0.0 25.9 %copy-start = (bf16[512,3,1024]{2,0,1:T(8,128)(2,1)S(1)}, bf16[512,3,1024]{2,0,1:T(8,128)(2,1)}, u32[]{:S(2)}) copy-start(bf16[512,3,1024]{2,0,1:T(8,128)(2,1)} %param.11) | copy-start | bytes 9437188
  2.6 17.6 %collective-permute-start = (bf16[512,512]{1,0:T(8,128)(2,1)}, bf16[512,512]{1,0:T(8,128)(2,1)S(1)}, u32[]{:S(2)}, u32[]{:S(2)}) collective-permute-start(bf16[512,512]{1,0:T(8,128)(2,1)} %get-tuple-element.32.refs_1_), channel_id=1, source_target_pairs={{0,4},{4,0},{8,12},{12,8},{16,20},{20,16},{24,28},{28,24},{1,5},{5... | collective-permute-start | bytes 1572872 | tf_op jit(solution)/shard_map/ppermute | solution.py:652
  5.6 14.6 %collective-permute-start.1 = (bf16[512,256]{1,0:T(8,128)(2,1)}, bf16[512,256]{1,0:T(8,128)(2,1)S(1)}, u32[]{:S(2)}, u32[]{:S(2)}) collective-permute-start(bf16[512,256]{1,0:T(8,128)(2,1)} %get-tuple-element.33), channel_id=1, source_target_pairs={{0,16},{4,20},{8,24},{12,28},{16,0},{20,4},{24,8},{28,12},{1,17},{... | collective-permute-start | bytes 786440 | tf_op jit(solution)/shard_map/ppermute | solution.py:652
  8.2 22.5 %collective-permute-start.6 = (bf16[1024,256]{1,0:T(8,128)(2,1)}, bf16[1024,256]{1,0:T(8,128)(2,1)S(1)}, u32[]{:S(2)}, u32[]{:S(2)}) collective-permute-start(bf16[1024,256]{1,0:T(8,128)(2,1)} %get-tuple-element.35), channel_id=1, source_target_pairs={{0,8},{4,12},{8,0},{12,4},{16,24},{20,28},{24,16},{28,20},{1,9},{5... | collective-permute-start | bytes 1572872 | tf_op jit(solution)/shard_map/ppermute | solution.py:652
  20.3 12.8 %collective-permute-start.5 = (bf16[512,512]{1,0:T(8,128)(2,1)S(1)}, bf16[512,512]{1,0:T(8,128)(2,1)S(1)}, u32[]{:S(2)}, u32[]{:S(2)}) collective-permute-start(bf16[512,512]{1,0:T(8,128)(2,1)S(1)} %join.4.refs_0_), channel_id=1, source_target_pairs={{0,2},{1,3},{2,0},{3,1},{4,6},{5,7},{6,4},{7,5},{8,10},{9,11},{10,... | collective-permute-start | bytes 1572872 | tf_op jit(solution)/shard_map/ppermute | solution.py:652
  21.9 24.7 %collective-permute-start.3 = (bf16[512,512]{1,0:T(8,128)(2,1)S(1)}, bf16[512,512]{1,0:T(8,128)(2,1)S(1)}, u32[]{:S(2)}, u32[]{:S(2)}) collective-permute-start(bf16[512,512]{1,0:T(8,128)(2,1)S(1)} %join.4.refs_0_), channel_id=1, source_target_pairs={{0,16},{4,20},{8,24},{12,28},{16,0},{20,4},{24,8},{28,12},{1,17},{... | collective-permute-start | bytes 1572872 | tf_op jit(solution)/shard_map/ppermute | solution.py:652
  22.2 26.3 %collective-permute-start.2 = (bf16[512,512]{1,0:T(8,128)(2,1)S(1)}, bf16[512,512]{1,0:T(8,128)(2,1)S(1)}, u32[]{:S(2)}, u32[]{:S(2)}) collective-permute-start(bf16[512,512]{1,0:T(8,128)(2,1)S(1)} %join.4.refs_0_), channel_id=1, source_target_pairs={{0,8},{4,12},{8,0},{12,4},{16,24},{20,28},{24,16},{28,20},{1,9},{5... | collective-permute-start | bytes 1572872 | tf_op jit(solution)/shard_map/ppermute | solution.py:652
  48.6 42.8 %collective-permute-start.7 = (bf16[1024,512]{1,0:T(8,128)(2,1)S(1)}, bf16[1024,512]{1,0:T(8,128)(2,1)S(1)}, u32[]{:S(2)}, u32[]{:S(2)}) collective-permute-start(bf16[1024,512]{1,0:T(8,128)(2,1)S(1)} %join.5), channel_id=1, source_target_pairs={{0,2},{1,3},{2,0},{3,1},{4,6},{5,7},{6,4},{7,5},{8,10},{9,11},{10,... | collective-permute-start | bytes 3145736 | tf_op jit(solution)/shard_map/ppermute | solution.py:652
  50.2 13.9 %collective-permute-start.4 = (bf16[512,512]{1,0:T(8,128)(2,1)S(1)}, bf16[512,512]{1,0:T(8,128)(2,1)S(1)}, u32[]{:S(2)}, u32[]{:S(2)}) collective-permute-start(bf16[512,512]{1,0:T(8,128)(2,1)S(1)} %collective-permute-done.3.refs_0_.refs_2_), channel_id=1, source_target_pairs={{0,8},{4,12},{8,0},{12,4},{16,24},{20,28},{24,16},{28,20},{1,9},{5... | collective-permute-start | bytes 1572872 | tf_op jit(solution)/shard_map/ppermute | solution.py:652
  51.7 39.7 %collective-permute-start.9 = (bf16[1280,256]{1,0:T(8,128)(2,1)S(1)}, bf16[1280,256]{1,0:T(8,128)(2,1)S(1)}, u32[]{:S(2)}, u32[]{:S(2)}) collective-permute-start(bf16[1280,256]{1,0:T(8,128)(2,1)S(1)} %get-tuple-element.34.refs_3_), channel_id=1, source_target_pairs={{0,24},{4,28},{8,16},{12,20},{16,8},{20,12},{24,0},{28,4},{1,25},{... | collective-permute-start | bytes 1966088 | tf_op jit(solution)/shard_map/ppermute | solution.py:652
  64.0 27.6 %collective-permute-start.8 = (bf16[512,512]{1,0:T(8,128)(2,1)S(1)}, bf16[512,512]{1,0:T(8,128)(2,1)S(1)}, u32[]{:S(2)}, u32[]{:S(2)}) collective-permute-start(bf16[512,512]{1,0:T(8,128)(2,1)S(1)} %collective-permute-done.4.refs_2_.refs_3_), channel_id=1, source_target_pairs={{0,2},{1,3},{2,0},{3,1},{4,6},{5,7},{6,4},{7,5},{8,10},{9,11},{10,... | collective-permute-start | bytes 1572872 | tf_op jit(solution)/shard_map/ppermute | solution.py:652
  64.5 26.8 %collective-permute-start.10 = (bf16[512,256]{1,0:T(8,128)(2,1)S(1)}, bf16[512,256]{1,0:T(8,128)(2,1)S(1)}, u32[]{:S(2)}, u32[]{:S(2)}) collective-permute-start(bf16[512,256]{1,0:T(8,128)(2,1)S(1)} %get-tuple-element.36), channel_id=1, source_target_pairs={{0,16},{4,20},{8,24},{12,28},{16,0},{20,4},{24,8},{28,12},{1,17},{... | collective-permute-start | bytes 786440 | tf_op jit(solution)/shard_map/ppermute | solution.py:652
  91.5 5.2 %collective-permute-start.11 = (bf16[2048,512]{1,0:T(8,128)(2,1)S(1)}, bf16[2048,512]{1,0:T(8,128)(2,1)S(1)}, u32[]{:S(2)}, u32[]{:S(2)}) collective-permute-start(bf16[2048,512]{1,0:T(8,128)(2,1)S(1)} %join.6), channel_id=1, source_target_pairs={{0,1},{1,0},{2,3},{3,2},{4,5},{5,4},{6,7},{7,6},{8,9},{9,8},{10,11... | collective-permute-start | bytes 6291464 | tf_op jit(solution)/shard_map/ppermute | solution.py:652
  91.8 7.0 %collective-permute-start.12 = (bf16[2048,512]{1,0:T(8,128)(2,1)S(1)}, bf16[2048,512]{1,0:T(8,128)(2,1)S(1)}, u32[]{:S(2)}, u32[]{:S(2)}) collective-permute-start(bf16[2048,512]{1,0:T(8,128)(2,1)S(1)} %join.7), channel_id=1, source_target_pairs={{0,1},{1,0},{2,3},{3,2},{4,5},{5,4},{6,7},{7,6},{8,9},{9,8},{10,11... | collective-permute-start | bytes 6291464 | tf_op jit(solution)/shard_map/ppermute | solution.py:652
  92.3 13.6 %collective-permute-start.17 = (bf16[512,256]{1,0:T(8,128)(2,1)S(1)}, bf16[512,256]{1,0:T(8,128)(2,1)S(1)}, u32[]{:S(2)}, u32[]{:S(2)}) collective-permute-start(bf16[512,256]{1,0:T(8,128)(2,1)S(1)} %get-tuple-element.44), channel_id=1, source_target_pairs={{0,24},{4,28},{8,16},{12,20},{16,8},{20,12},{24,0},{28,4},{1,25},{... | collective-permute-start | bytes 786440 | tf_op jit(solution)/shard_map/ppermute | solution.py:652
  94.7 22.0 %collective-permute-start.15 = (bf16[768,256]{1,0:T(8,128)(2,1)S(1)}, bf16[768,256]{1,0:T(8,128)(2,1)S(1)}, u32[]{:S(2)}, u32[]{:S(2)}) collective-permute-start(bf16[768,256]{1,0:T(8,128)(2,1)S(1)} %get-tuple-element.42), channel_id=1, source_target_pairs={{0,8},{4,12},{8,0},{12,4},{16,24},{20,28},{24,16},{28,20},{1,9},{5... | collective-permute-start | bytes 1179656 | tf_op jit(solution)/shard_map/ppermute | solution.py:652
  94.7 27.4 %collective-permute-start.16 = (bf16[768,256]{1,0:T(8,128)(2,1)S(1)}, bf16[768,256]{1,0:T(8,128)(2,1)S(1)}, u32[]{:S(2)}, u32[]{:S(2)}) collective-permute-start(bf16[768,256]{1,0:T(8,128)(2,1)S(1)} %get-tuple-element.43), channel_id=1, source_target_pairs={{0,16},{4,20},{8,24},{12,28},{16,0},{20,4},{24,8},{28,12},{1,17},{... | collective-permute-start | bytes 1179656 | tf_op jit(solution)/shard_map/ppermute | solution.py:652
  101.3 27.1 %collective-permute-start.13 = (bf16[2048,128]{1,0:T(8,128)(2,1)S(1)}, bf16[2048,128]{1,0:T(8,128)(2,1)S(1)}, u32[]{:S(2)}, u32[]{:S(2)}) collective-permute-start(bf16[2048,128]{1,0:T(8,128)(2,1)S(1)} %get-tuple-element.39), channel_id=1, source_target_pairs={{0,4},{4,0},{8,12},{12,8},{16,20},{20,16},{24,28},{28,24},{1,5},{5... | collective-permute-start | bytes 1572872 | tf_op jit(solution)/shard_map/ppermute | solution.py:652
  104.3 24.0 %slice-start = ((s8[8388608]{0:T(1024)(128)(4,1)}), s8[4194304]{0:T(1024)(128)(4,1)S(1)}, s32[]{:S(2)}) async-start(s8[8388608]{0:T(1024)(128)(4,1)} %bitcast.4), calls=%async_computation | async-start | bytes 8388608
  104.4 24.0 %slice-start.1 = ((s8[8388608]{0:T(1024)(128)(4,1)}), s8[4194304]{0:T(1024)(128)(4,1)S(1)}, s32[]{:S(2)}) async-start(s8[8388608]{0:T(1024)(128)(4,1)} %bitcast.4), calls=%async_computation.1 | async-start | bytes 8388608
  104.4 23.9 %collective-permute-start.14 = (bf16[2048,128]{1,0:T(8,128)(2,1)S(1)}, bf16[2048,128]{1,0:T(8,128)(2,1)S(1)}, u32[]{:S(2)}, u32[]{:S(2)}) collective-permute-start(bf16[2048,128]{1,0:T(8,128)(2,1)S(1)} %get-tuple-element.41.refs_4_), channel_id=1, source_target_pairs={{0,4},{4,0},{8,12},{12,8},{16,20},{20,16},{24,28},{28,24},{1,5},{5... | collective-permute-start | bytes 1572872 | tf_op jit(solution)/shard_map/ppermute | solution.py:652
  124.7 13.1 %collective-permute-start.18 = (bf16[2048,128]{1,0:T(8,128)(2,1)S(1)}, bf16[2048,128]{1,0:T(8,128)(2,1)S(1)}, u32[]{:S(2)}, u32[]{:S(2)}) collective-permute-start(bf16[2048,128]{1,0:T(8,128)(2,1)S(1)} %get-tuple-element.45.refs_0_), channel_id=1, source_target_pairs={{0,4},{4,0},{8,12},{12,8},{16,20},{20,16},{24,28},{28,24},{1,5},{5... | collective-permute-start | bytes 1572872 | tf_op jit(solution)/shard_map/ppermute | solution.py:652
  138.2 7.7 %collective-permute-start.19 = (bf16[256,128]{1,0:T(8,128)(2,1)S(1)}, bf16[256,128]{1,0:T(8,128)(2,1)S(1)}, u32[]{:S(2)}, u32[]{:S(2)}) collective-permute-start(bf16[256,128]{1,0:T(8,128)(2,1)S(1)} %get-tuple-element.49), channel_id=1, source_target_pairs={{0,24},{4,28},{8,16},{12,20},{16,8},{20,12},{24,0},{28,4},{1,25},{... | collective-permute-start | bytes 196616 | tf_op jit(solution)/shard_map/ppermute | solution.py:652
  140.7 7.4 %collective-permute-start.20 = (bf16[256,128]{1,0:T(8,128)(2,1)S(1)}, bf16[256,128]{1,0:T(8,128)(2,1)S(1)}, u32[]{:S(2)}, u32[]{:S(2)}) collective-permute-start(bf16[256,128]{1,0:T(8,128)(2,1)S(1)} %get-tuple-element.50), channel_id=1, source_target_pairs={{0,28},{4,24},{8,20},{12,16},{16,12},{20,8},{24,4},{28,0},{1,29},{... | collective-permute-start | bytes 196616 | tf_op jit(solution)/shard_map/ppermute | solution.py:652
  142.1 7.4 %collective-permute-start.21 = (bf16[256,128]{1,0:T(8,128)(2,1)S(1)}, bf16[256,128]{1,0:T(8,128)(2,1)S(1)}, u32[]{:S(2)}, u32[]{:S(2)}) collective-permute-start(bf16[256,128]{1,0:T(8,128)(2,1)S(1)} %get-tuple-element.51), channel_id=1, source_target_pairs={{0,16},{4,20},{8,24},{12,28},{16,0},{20,4},{24,8},{28,12},{1,17},{... | collective-permute-start | bytes 196616 | tf_op jit(solution)/shard_map/ppermute | solution.py:652
  142.1 9.3 %collective-permute-start.22 = (bf16[256,128]{1,0:T(8,128)(2,1)S(1)}, bf16[256,128]{1,0:T(8,128)(2,1)S(1)}, u32[]{:S(2)}, u32[]{:S(2)}) collective-permute-start(bf16[256,128]{1,0:T(8,128)(2,1)S(1)} %get-tuple-element.52), channel_id=1, source_target_pairs={{0,20},{4,16},{8,28},{12,24},{16,4},{20,0},{24,12},{28,8},{1,21},{... | collective-permute-start | bytes 196616 | tf_op jit(solution)/shard_map/ppermute | solution.py:652
  146.0 5.4 %collective-permute-start.23 = (bf16[256,128]{1,0:T(8,128)(2,1)S(1)}, bf16[256,128]{1,0:T(8,128)(2,1)S(1)}, u32[]{:S(2)}, u32[]{:S(2)}) collective-permute-start(bf16[256,128]{1,0:T(8,128)(2,1)S(1)} %get-tuple-element.53), channel_id=1, source_target_pairs={{0,8},{4,12},{8,0},{12,4},{16,24},{20,28},{24,16},{28,20},{1,9},{5... | collective-permute-start | bytes 196616 | tf_op jit(solution)/shard_map/ppermute | solution.py:652
  146.0 6.2 %collective-permute-start.24 = (bf16[256,128]{1,0:T(8,128)(2,1)S(1)}, bf16[256,128]{1,0:T(8,128)(2,1)S(1)}, u32[]{:S(2)}, u32[]{:S(2)}) collective-permute-start(bf16[256,128]{1,0:T(8,128)(2,1)S(1)} %get-tuple-element.54), channel_id=1, source_target_pairs={{0,12},{4,8},{8,4},{12,0},{16,28},{20,24},{24,20},{28,16},{1,13},{... | collective-permute-start | bytes 196616 | tf_op jit(solution)/shard_map/ppermute | solution.py:652
  148.0 4.8 %collective-permute-start.25 = (bf16[256,128]{1,0:T(8,128)(2,1)S(1)}, bf16[256,128]{1,0:T(8,128)(2,1)S(1)}, u32[]{:S(2)}, u32[]{:S(2)}) collective-permute-start(bf16[256,128]{1,0:T(8,128)(2,1)S(1)} %get-tuple-element.55), channel_id=1, source_target_pairs={{0,4},{4,0},{8,12},{12,8},{16,20},{20,16},{24,28},{28,24},{1,5},{5... | collective-permute-start | bytes 196616 | tf_op jit(solution)/shard_map/ppermute | solution.py:652
  153.7 2.0 %collective-permute-start.27 = (bf16[256,1024]{1,0:T(8,128)(2,1)S(1)}, bf16[256,1024]{1,0:T(8,128)(2,1)S(1)}, u32[]{:S(2)}, u32[]{:S(2)}) collective-permute-start(bf16[256,1024]{1,0:T(8,128)(2,1)S(1)} %get-tuple-element.58), channel_id=1, source_target_pairs={{0,1},{1,0},{2,3},{3,2},{4,5},{5,4},{6,7},{7,6},{8,9},{9,8},{10,11... | collective-permute-start | bytes 1572872 | tf_op jit(solution)/shard_map/ppermute | solution.py:652
  154.5 3.3 %collective-permute-start.26 = (bf16[256,1024]{1,0:T(8,128)(2,1)S(1)}, bf16[256,1024]{1,0:T(8,128)(2,1)S(1)}, u32[]{:S(2)}, u32[]{:S(2)}) collective-permute-start(bf16[256,1024]{1,0:T(8,128)(2,1)S(1)} %emit.5), channel_id=1, source_target_pairs={{0,1},{1,0},{2,3},{3,2},{4,5},{5,4},{6,7},{7,6},{8,9},{9,8},{10,11... | collective-permute-start | bytes 1572872 | tf_op jit(solution)/shard_map/ppermute | solution.py:652
  156.4 14.0 %collective-permute-start.28 = (bf16[256,1024]{1,0:T(8,128)(2,1)S(1)}, bf16[256,1024]{1,0:T(8,128)(2,1)S(1)}, u32[]{:S(2)}, u32[]{:S(2)}) collective-permute-start(bf16[256,1024]{1,0:T(8,128)(2,1)S(1)} %emit.7), channel_id=1, source_target_pairs={{0,2},{1,3},{2,0},{3,1},{4,6},{5,7},{6,4},{7,5},{8,10},{9,11},{10,... | collective-permute-start | bytes 1572872 | tf_op jit(solution)/shard_map/ppermute | solution.py:652
  (9 other events, 90.9 us)

commit v9 on v8

--- a/solution.py
+++ b/solution.py
@@ -373,6 +373,76 @@
     )(*line, *across, *cores, *parts, *after)
 
 
+def project_part_kernel(*refs, lows, far):
+    line, across, cores, parts = refs[:4], refs[4:7], refs[7:9], refs[9:11]
+    weights = refs[-1]
+    place, chan = lax.axis_index("seq"), lax.axis_index("chan")
+    depth, side = place // 2, place % 2
+    rows = line[0].shape[1]
+    turned = jnp.bitwise_xor(depth, chan)
+    for i in range(2):
+        slot = jnp.bitwise_xor(turned % 2, i)
+        start = pl.multiple_of(slot * rows, rows)
+        weights[pl.ds(start, rows), :] = parts[i][lows[i] : lows[i] + rows, :]
+    block = line[0].shape[0] // 2
+    half = weights.shape[1] // 2
+
+    def run(second):
+        for step in range(4):
+            low = 4 * block * (step % 2)
+            both = cores[step // 2]
+            if second:
+                beside = across[(0, 1, 1, 2)[step]]
+                at = 2 * block if step == 1 else 0
+                first = beside[at : at + 2 * block, :]
+                low += 2 * block
+            else:
+                first = line[step][...]
+            joined = jnp.concatenate([first, both[low : low + 2 * block, :]], 1)
+            total = jnp.dot(joined, weights[...], preferred_element_type=jnp.float32)
+            rows_here = slice(2 * step * block, 2 * (step + 1) * block)
+            if not far:
+                refs[11][rows_here, :] = total
+                continue
+            total = total + refs[11][rows_here, :]
+            left, right = total[:, :half], total[:, half:]
+            own = jnp.where(side == 0, left, right)
+            send = jnp.where(side == 0, right, left).astype(jnp.bfloat16)
+            for pair in range(2):
+                start = pl.multiple_of(jnp.bitwise_xor(place, 2 * step + pair) * block, block)
+                refs[12][pl.ds(start, block), :] = own[pair * block : (pair + 1) * block]
+                refs[13][pl.ds(start, block), :] = send[pair * block : (pair + 1) * block]
+
+    pair_of = turned // 2
+    pl.when(pair_of == (1 if far else 0))(lambda: run(False))
+    pl.when(pair_of == (0 if far else 1))(lambda: run(True))
+
+
+def project_part(line, across, cores, parts, lows, length, begun):
+    depth, width = line[0].shape[1], parts[0].shape[1]
+    vmem = pl.BlockSpec(memory_space=pltpu.VMEM)
+    shapes = (jax.ShapeDtypeStruct((length, width), jnp.float32),)
+    if begun:
+        shapes = (
+            jax.ShapeDtypeStruct((length, width // 2), jnp.float32),
+            jax.ShapeDtypeStruct((length, width // 2), jnp.bfloat16),
+        )
+    return pl.pallas_call(
+        functools.partial(project_part_kernel, lows=lows, far=len(begun) > 0),
+        out_shape=shapes,
+        in_specs=[vmem] * (11 + len(begun)),
+        out_specs=(vmem,) * len(shapes),
+        scratch_shapes=[pltpu.VMEM((2 * depth, width), jnp.bfloat16)],
+        compiler_params=pltpu.CompilerParams(vmem_limit_bytes=12 * 2**20),
+        cost_estimate=pl.CostEstimate(
+            flops=2 * length * 2 * depth * width,
+            bytes_accessed=2 * length * 2 * depth,
+            transcendentals=0,
+        ),
+        name="project_part",
+    )(*line, *across, *cores, *parts, *begun)
+
+
 def smooth_into(padded, own_ref, recv_ref, taps, branch, store):
     length = own_ref.shape[0]
     tap_count = taps.shape[1]
@@ -409,7 +479,7 @@
 
 
 def unroll_of(rows):
-    return 11 if rows % 11 == 0 else 1
+    return rows
 
 
 def spectrum_kernel(ahead, middle, *refs, lows):
@@ -607,7 +677,7 @@
     out_ref = refs[len(order) + added]
     place, chan = lax.axis_index("seq"), lax.axis_index("chan")
     columns = out_ref.shape[1]
-    tile = 256
+    tile = columns // 2
     if len(order) == 1:
         joined = parts[0]
     else:
@@ -714,8 +784,8 @@
     freq = spectrum(
         tables, [w_0, w0_1, w0_2, w_3], (3 * rows, rows, rows, 2 * rows), length, [send2]
     )
-    parts0 = [w_0, w0_1, w0_2, w0_3]
-    own0, send0 = project(*shared, parts0, (2 * rows, 0, 0, 0), length, [])
+    begun = project_part(*shared, [w_0, w0_1], (2 * rows, 0), length, [])
+    own0, send0 = project_part(*shared, [w0_2, w0_3], (0, 0), length, begun)
     recv0 = swap(send0, "seq", seq, 1)
     mixed, held = mix(
         own1,

time: 172 us -> 171 us (level)
  starting transfers between devices: 41 us -> 42.9 us
    pallas_call x0 -> x2, Pallas kernels: none -> 2.89 us  [project_part(): pl.pallas_call(functools.partial(project_part_kernel, lows=lows, far=len(...]
    pallas_call x3 -> x2, Pallas kernels: 7.46 us -> 4.97 us  [project(): pl.pallas_call(functools.partial(project_kernel, lows=lows, after=len(aft...]
    ppermute x29, starting transfers between devices: 41 us -> 42.9 us  [swap(): return lax.ppermute(value, axis, [(i, i ^ turn) for i in range(count)])]
  transfers between devices with their start and end apart: 29 -> 29, of which waited for: 17 -> 19; matrix products, arithmetic and copies ran while one was open for 0% -> 0% of each run, Pallas kernels for 13% -> 12%
where the time goes in v9:
time: 171 us
  waiting for transfers between devices  101 us (59%)
  starting transfers between devices  42.9 us (25%)
  Pallas kernels  24.4 us (14%)
    ppermute x29, waiting for transfers between devices, swap(): return lax.ppermute(value, axis, [(i, i ^ turn) for i in range(count)])  101 us
    ppermute x29, starting transfers between devices, swap(): return lax.ppermute(value, axis, [(i, i ^ turn) for i in range(count)])  42.9 us
    pallas_call x1, Pallas kernels, mix(): pl.pallas_call(functools.partial(mix_kernel, after=len(after)), out_shape...  7 us
    pallas_call x2, Pallas kernels, project(): pl.pallas_call(functools.partial(project_kernel, lows=lows, after=len(aft...  4.97 us
  transfers between devices with their start and end apart: 29, of which 19 were waited for; matrix products, arithmetic and copies ran while one was open for 0% of the time, Pallas kernels for 12%

profile of v9, /device:TPU:0, one launch (start us, length us, event | category | flops | bytes accessed | tf_op | source)
XLA Modules:
  0.0 171.0 jit_solution(18157890795288981751)
XLA Ops:
  0.0 2.6 %halve.1 = (bf16[512,512]{1,0:T(8,128)(2,1)}, bf16[512,256]{1,0:T(8,128)(2,1)}, bf16[1024,256]{1,0:T(8,128)(2,1)}) custom-call(bf16[256,1024]{1,0:T(8,128)(2,1)} %refs_0_.1, bf16[256,1024]{1,0:T(8,128)(2,1)} %filters.3, bf16[3,512,1024]{2,1,0:T(8,128)(2,1)} %bitcast.2), custom_call_target="tpu_custom_call" | custom-call | tf_op jit(solution)/shard_map/halve/pallas_call | solution.py:203
  2.6 3.0 %collective-permute-start = (bf16[512,512]{1,0:T(8,128)(2,1)}, bf16[512,512]{1,0:T(8,128)(2,1)S(1)}, u32[]{:S(2)}, u32[]{:S(2)}) collective-permute-start(bf16[512,512]{1,0:T(8,128)(2,1)} %get-tuple-element.32.refs_1_), channel_id=1, source_target_pairs={{0,4},{4,0},{8,12},{12,8},{16,20},{20,16},{24,28},{28,24},{1,5},{5... | collective-permute-start | bytes 1572872 | tf_op jit(solution)/shard_map/ppermute | solution.py:722
  5.6 2.6 %collective-permute-start.1 = (bf16[512,256]{1,0:T(8,128)(2,1)}, bf16[512,256]{1,0:T(8,128)(2,1)S(1)}, u32[]{:S(2)}, u32[]{:S(2)}) collective-permute-start(bf16[512,256]{1,0:T(8,128)(2,1)} %get-tuple-element.33), channel_id=1, source_target_pairs={{0,16},{4,20},{8,24},{12,28},{16,0},{20,4},{24,8},{28,12},{1,17},{... | collective-permute-start | bytes 786440 | tf_op jit(solution)/shard_map/ppermute | solution.py:722
  8.2 1.6 collective-permute-start.6
  10.9 9.3 %collective-permute-done.1.refs_2_.refs_11_ = bf16[512,256]{1,0:T(8,128)(2,1)S(1)} collective-permute-done((bf16[512,256]{1,0:T(8,128)(2,1)}, bf16[512,256]{1,0:T(8,128)(2,1)S(1)}, u32[]{:S(2)}, u32[]{:S(2)}) %collective-permute-start.1) | collective-permute-done | bytes 262176 | tf_op jit(solution)/shard_map/ppermute | solution.py:722
  20.7 3.7 %collective-permute-start.2 = (bf16[512,512]{1,0:T(8,128)(2,1)S(1)}, bf16[512,512]{1,0:T(8,128)(2,1)S(1)}, u32[]{:S(2)}, u32[]{:S(2)}) collective-permute-start(bf16[512,512]{1,0:T(8,128)(2,1)S(1)} %join.4.refs_0_), channel_id=1, source_target_pairs={{0,8},{4,12},{8,0},{12,4},{16,24},{20,28},{24,16},{28,20},{1,9},{5... | collective-permute-start | bytes 1572872 | tf_op jit(solution)/shard_map/ppermute | solution.py:722
  26.6 5.3 %collective-permute-done.6.refs_4_.refs_10_ = bf16[1024,256]{1,0:T(8,128)(2,1)S(1)} collective-permute-done((bf16[1024,256]{1,0:T(8,128)(2,1)}, bf16[1024,256]{1,0:T(8,128)(2,1)S(1)}, u32[]{:S(2)}, u32[]{:S(2)}) %collective-permute-start.6) | collective-permute-done | bytes 524320 | tf_op jit(solution)/shard_map/ppermute | solution.py:722
  32.0 13.4 %collective-permute-done.3.refs_0_.refs_2_ = bf16[512,512]{1,0:T(8,128)(2,1)S(1)} collective-permute-done((bf16[512,512]{1,0:T(8,128)(2,1)S(1)}, bf16[512,512]{1,0:T(8,128)(2,1)S(1)}, u32[]{:S(2)}, u32[]{:S(2)}) %collective-permute-start.3) | collective-permute-done | bytes 524320 | tf_op jit(solution)/shard_map/ppermute | solution.py:722
  45.4 3.2 %collective-permute-done.2.refs_1_.refs_2_ = bf16[512,512]{1,0:T(8,128)(2,1)S(1)} collective-permute-done((bf16[512,512]{1,0:T(8,128)(2,1)S(1)}, bf16[512,512]{1,0:T(8,128)(2,1)S(1)}, u32[]{:S(2)}, u32[]{:S(2)}) %collective-permute-start.2) | collective-permute-done | bytes 524320 | tf_op jit(solution)/shard_map/ppermute | solution.py:722
  48.6 1.6 collective-permute-start.7
  53.0 11.0 %collective-permute-done.4.refs_2_.refs_3_ = bf16[512,512]{1,0:T(8,128)(2,1)S(1)} collective-permute-done((bf16[512,512]{1,0:T(8,128)(2,1)S(1)}, bf16[512,512]{1,0:T(8,128)(2,1)S(1)}, u32[]{:S(2)}, u32[]{:S(2)}) %collective-permute-start.4) | collective-permute-done | bytes 524320 | tf_op jit(solution)/shard_map/ppermute | solution.py:722
  64.6 2.4 %collective-permute-start.10 = (bf16[512,256]{1,0:T(8,128)(2,1)S(1)}, bf16[512,256]{1,0:T(8,128)(2,1)S(1)}, u32[]{:S(2)}, u32[]{:S(2)}) collective-permute-start(bf16[512,256]{1,0:T(8,128)(2,1)S(1)} %get-tuple-element.36), channel_id=1, source_target_pairs={{0,16},{4,20},{8,24},{12,28},{16,0},{20,4},{24,8},{28,12},{1,17},{... | collective-permute-start | bytes 786440 | tf_op jit(solution)/shard_map/ppermute | solution.py:722
  66.9 7.8 %collective-permute-done.7.refs_3_.refs_1_.refs_5_ = bf16[1024,512]{1,0:T(8,128)(2,1)S(1)} collective-permute-done((bf16[1024,512]{1,0:T(8,128)(2,1)S(1)}, bf16[1024,512]{1,0:T(8,128)(2,1)S(1)}, u32[]{:S(2)}, u32[]{:S(2)}) %collective-permute-start.7) | collective-permute-done | bytes 1048608 | tf_op jit(solution)/shard_map/ppermute | solution.py:722
  74.8 8.6 %collective-permute-done.8.refs_3_.refs_6_ = bf16[512,512]{1,0:T(8,128)(2,1)S(1)} collective-permute-done((bf16[512,512]{1,0:T(8,128)(2,1)S(1)}, bf16[512,512]{1,0:T(8,128)(2,1)S(1)}, u32[]{:S(2)}, u32[]{:S(2)}) %collective-permute-start.8) | collective-permute-done | bytes 524320 | tf_op jit(solution)/shard_map/ppermute | solution.py:722
  83.5 7.9 %collective-permute-done.10.refs_5_.refs_11_ = bf16[512,256]{1,0:T(8,128)(2,1)S(1)} collective-permute-done((bf16[512,256]{1,0:T(8,128)(2,1)S(1)}, bf16[512,256]{1,0:T(8,128)(2,1)S(1)}, u32[]{:S(2)}, u32[]{:S(2)}) %collective-permute-start.10) | collective-permute-done | bytes 262176 | tf_op jit(solution)/shard_map/ppermute | solution.py:722
  91.7 2.8 %collective-permute-start.16 = (bf16[768,256]{1,0:T(8,128)(2,1)S(1)}, bf16[768,256]{1,0:T(8,128)(2,1)S(1)}, u32[]{:S(2)}, u32[]{:S(2)}) collective-permute-start(bf16[768,256]{1,0:T(8,128)(2,1)S(1)} %get-tuple-element.43), channel_id=1, source_target_pairs={{0,16},{4,20},{8,24},{12,28},{16,0},{20,4},{24,8},{28,12},{1,17},{... | collective-permute-start | bytes 1179656 | tf_op jit(solution)/shard_map/ppermute | solution.py:722
  94.5 1.6 collective-permute-start.17
  96.1 2.5 %project.3 = (f32[2048,128]{1,0:T(8,128)S(1)}, bf16[2048,128]{1,0:T(8,128)(2,1)S(1)}) custom-call(bf16[512,512]{1,0:T(8,128)(2,1)S(1)} %join.4.refs_0_, bf16[512,512]{1,0:T(8,128)(2,1)S(1)} %collective-permute-done.2.refs_1_.refs_2_, bf16[512,512]{1,0:T(8,128)(2,1)S(1)} %collective-permute-done.3.refs_0_.refs_2_, ...), custom_call_target="tpu_custom_call" | custom-call | flops 4294967296 | bytes 8388608 | tf_op jit(solution)/shard_map/project/pallas_call | solution.py:356
  99.2 2.5 %project.2 = (f32[2048,128]{1,0:T(8,128)S(1)}, bf16[2048,128]{1,0:T(8,128)(2,1)S(1)}) custom-call(bf16[512,512]{1,0:T(8,128)(2,1)S(1)} %join.4.refs_0_, bf16[512,512]{1,0:T(8,128)(2,1)S(1)} %collective-permute-done.2.refs_1_.refs_2_, bf16[512,512]{1,0:T(8,128)(2,1)S(1)} %collective-permute-done.3.refs_0_.refs_2_, ...), custom_call_target="tpu_custom_call" | custom-call | flops 4294967296 | bytes 8388608 | tf_op jit(solution)/shard_map/project/pallas_call | solution.py:356
  101.7 1.6 collective-permute-start.13
  103.2 7.9 %collective-permute-done.15.refs_1_.refs_10_ = bf16[768,256]{1,0:T(8,128)(2,1)S(1)} collective-permute-done((bf16[768,256]{1,0:T(8,128)(2,1)S(1)}, bf16[768,256]{1,0:T(8,128)(2,1)S(1)}, u32[]{:S(2)}, u32[]{:S(2)}) %collective-permute-start.15) | collective-permute-done | bytes 393248 | tf_op jit(solution)/shard_map/ppermute | solution.py:722
  112.5 5.3 %collective-permute-done.17.refs_10_ = bf16[512,256]{1,0:T(8,128)(2,1)S(1)} collective-permute-done((bf16[512,256]{1,0:T(8,128)(2,1)S(1)}, bf16[512,256]{1,0:T(8,128)(2,1)S(1)}, u32[]{:S(2)}, u32[]{:S(2)}) %collective-permute-start.17) | collective-permute-done | bytes 262176 | tf_op jit(solution)/shard_map/ppermute | solution.py:722
  118.7 1.6 project_part.3
  120.9 2.5 %spectrum.1.freq_ref = f32[4224,128]{1,0:T(8,128)S(1)} custom-call(bf16[80,32]{1,0:T(8,128)(2,1)S(1)} %copy-done.7, bf16[33,128,128]{2,1,0:T(8,128)(2,1)S(1)} %copy-done.1, bf16[1792,256]{1,0:T(8,128)(2,1)S(1)} %get-tuple-element.37.refs_9_.refs_0_, bf16[768,256]{1,0:T(8,128)(2,1)S(1)} %collective-permute-done.15.refs_1_.refs_10_, ...), custom_call_target="tpu_custom_call" | custom-call | flops 67108864 | bytes 1048576 | tf_op jit(solution)/shard_map/spectrum/pallas_call | solution.py:514
  124.7 7.0 %mix.1 = (f32[2048,128]{1,0:T(8,128)S(1)}, bf16[1024,4096]{1,0:T(8,128)(2,1)S(1)}) custom-call(f32[2048,128]{1,0:T(8,128)S(1)} %get-tuple-element.38.own1, bf16[2048,128]{1,0:T(8,128)(2,1)S(1)} %collective-permute-done.13.recv1, f32[2048,128]{1,0:T(8,128)S(1)} %get-tuple-element.40.own2, bf16[2048,128]{1,0:T(8,128)(2,1)S(1)} %collective-permute-done.14.recv2, ...), custom_call_target="tpu_custom_call" | custom-call | flops 201326592 | bytes 6291456 | tf_op jit(solution)/shard_map/mix/pallas_call | solution.py:616
  131.7 3.0 %collective-permute-done.18.recv0 = bf16[2048,128]{1,0:T(8,128)(2,1)S(1)} collective-permute-done((bf16[2048,128]{1,0:T(8,128)(2,1)S(1)}, bf16[2048,128]{1,0:T(8,128)(2,1)S(1)}, u32[]{:S(2)}, u32[]{:S(2)}) %collective-permute-start.18) | collective-permute-done | bytes 524320 | tf_op jit(solution)/shard_map/ppermute | solution.py:722
  135.2 2.3 %collective-permute-start.19 = (bf16[256,128]{1,0:T(8,128)(2,1)S(1)}, bf16[256,128]{1,0:T(8,128)(2,1)S(1)}, u32[]{:S(2)}, u32[]{:S(2)}) collective-permute-start(bf16[256,128]{1,0:T(8,128)(2,1)S(1)} %get-tuple-element.49), channel_id=1, source_target_pairs={{0,24},{4,28},{8,16},{12,20},{16,8},{20,12},{24,0},{28,4},{1,25},{... | collective-permute-start | bytes 196616 | tf_op jit(solution)/shard_map/ppermute | solution.py:722
  137.5 1.6 collective-permute-start.20
  139.1 3.6 %collective-permute-start.21 = (bf16[256,128]{1,0:T(8,128)(2,1)S(1)}, bf16[256,128]{1,0:T(8,128)(2,1)S(1)}, u32[]{:S(2)}, u32[]{:S(2)}) collective-permute-start(bf16[256,128]{1,0:T(8,128)(2,1)S(1)} %get-tuple-element.51), channel_id=1, source_target_pairs={{0,16},{4,20},{8,24},{12,28},{16,0},{20,4},{24,8},{28,12},{1,17},{... | collective-permute-start | bytes 196616 | tf_op jit(solution)/shard_map/ppermute | solution.py:722
  143.6 2.1 %collective-permute-start.23 = (bf16[256,128]{1,0:T(8,128)(2,1)S(1)}, bf16[256,128]{1,0:T(8,128)(2,1)S(1)}, u32[]{:S(2)}, u32[]{:S(2)}) collective-permute-start(bf16[256,128]{1,0:T(8,128)(2,1)S(1)} %get-tuple-element.53), channel_id=1, source_target_pairs={{0,8},{4,12},{8,0},{12,4},{16,24},{20,28},{24,16},{28,20},{1,9},{5... | collective-permute-start | bytes 196616 | tf_op jit(solution)/shard_map/ppermute | solution.py:722
  147.0 2.5 %collective-permute-start.25 = (bf16[256,128]{1,0:T(8,128)(2,1)S(1)}, bf16[256,128]{1,0:T(8,128)(2,1)S(1)}, u32[]{:S(2)}, u32[]{:S(2)}) collective-permute-start(bf16[256,128]{1,0:T(8,128)(2,1)S(1)} %get-tuple-element.55), channel_id=1, source_target_pairs={{0,4},{4,0},{8,12},{12,8},{16,20},{20,16},{24,28},{28,24},{1,5},{5... | collective-permute-start | bytes 196616 | tf_op jit(solution)/shard_map/ppermute | solution.py:722
  157.3 12.7 %collective-permute-done.28 = bf16[256,1024]{1,0:T(8,128)(2,1)S(1)} collective-permute-done((bf16[256,1024]{1,0:T(8,128)(2,1)S(1)}, bf16[256,1024]{1,0:T(8,128)(2,1)S(1)}, u32[]{:S(2)}, u32[]{:S(2)}) %collective-permute-start.28) | collective-permute-done | bytes 524320 | tf_op jit(solution)/shard_map/ppermute | solution.py:722
  (70 shorter events, 23.8 us)
Async XLA Ops:
  0.0 25.9 %copy-start = (bf16[512,3,1024]{2,0,1:T(8,128)(2,1)S(1)}, bf16[512,3,1024]{2,0,1:T(8,128)(2,1)}, u32[]{:S(2)}) copy-start(bf16[512,3,1024]{2,0,1:T(8,128)(2,1)} %param.11) | copy-start | bytes 9437188
  2.6 23.3 %copy-start.2 = (bf16[256,1024]{1,0:T(8,128)(2,1)S(1)}, bf16[256,1024]{1,0:T(8,128)(2,1)}, u32[]{:S(2)}) copy-start(bf16[256,1024]{1,0:T(8,128)(2,1)} %filters.3) | copy-start | bytes 1572868
  2.6 17.6 %collective-permute-start = (bf16[512,512]{1,0:T(8,128)(2,1)}, bf16[512,512]{1,0:T(8,128)(2,1)S(1)}, u32[]{:S(2)}, u32[]{:S(2)}) collective-permute-start(bf16[512,512]{1,0:T(8,128)(2,1)} %get-tuple-element.32.refs_1_), channel_id=1, source_target_pairs={{0,4},{4,0},{8,12},{12,8},{16,20},{20,16},{24,28},{28,24},{1,5},{5... | collective-permute-start | bytes 1572872 | tf_op jit(solution)/shard_map/ppermute | solution.py:722
  5.6 14.6 %collective-permute-start.1 = (bf16[512,256]{1,0:T(8,128)(2,1)}, bf16[512,256]{1,0:T(8,128)(2,1)S(1)}, u32[]{:S(2)}, u32[]{:S(2)}) collective-permute-start(bf16[512,256]{1,0:T(8,128)(2,1)} %get-tuple-element.33), channel_id=1, source_target_pairs={{0,16},{4,20},{8,24},{12,28},{16,0},{20,4},{24,8},{28,12},{1,17},{... | collective-permute-start | bytes 786440 | tf_op jit(solution)/shard_map/ppermute | solution.py:722
  8.2 23.7 %collective-permute-start.6 = (bf16[1024,256]{1,0:T(8,128)(2,1)}, bf16[1024,256]{1,0:T(8,128)(2,1)S(1)}, u32[]{:S(2)}, u32[]{:S(2)}) collective-permute-start(bf16[1024,256]{1,0:T(8,128)(2,1)} %get-tuple-element.35), channel_id=1, source_target_pairs={{0,8},{4,12},{8,0},{12,4},{16,24},{20,28},{24,16},{28,20},{1,9},{5... | collective-permute-start | bytes 1572872 | tf_op jit(solution)/shard_map/ppermute | solution.py:722
  20.3 25.1 %collective-permute-start.3 = (bf16[512,512]{1,0:T(8,128)(2,1)S(1)}, bf16[512,512]{1,0:T(8,128)(2,1)S(1)}, u32[]{:S(2)}, u32[]{:S(2)}) collective-permute-start(bf16[512,512]{1,0:T(8,128)(2,1)S(1)} %join.4.refs_0_), channel_id=1, source_target_pairs={{0,16},{4,20},{8,24},{12,28},{16,0},{20,4},{24,8},{28,12},{1,17},{... | collective-permute-start | bytes 1572872 | tf_op jit(solution)/shard_map/ppermute | solution.py:722
  20.7 27.8 %collective-permute-start.2 = (bf16[512,512]{1,0:T(8,128)(2,1)S(1)}, bf16[512,512]{1,0:T(8,128)(2,1)S(1)}, u32[]{:S(2)}, u32[]{:S(2)}) collective-permute-start(bf16[512,512]{1,0:T(8,128)(2,1)S(1)} %join.4.refs_0_), channel_id=1, source_target_pairs={{0,8},{4,12},{8,0},{12,4},{16,24},{20,28},{24,16},{28,20},{1,9},{5... | collective-permute-start | bytes 1572872 | tf_op jit(solution)/shard_map/ppermute | solution.py:722
  24.4 24.1 %collective-permute-start.5 = (bf16[512,512]{1,0:T(8,128)(2,1)S(1)}, bf16[512,512]{1,0:T(8,128)(2,1)S(1)}, u32[]{:S(2)}, u32[]{:S(2)}) collective-permute-start(bf16[512,512]{1,0:T(8,128)(2,1)S(1)} %join.4.refs_0_), channel_id=1, source_target_pairs={{0,2},{1,3},{2,0},{3,1},{4,6},{5,7},{6,4},{7,5},{8,10},{9,11},{10,... | collective-permute-start | bytes 1572872 | tf_op jit(solution)/shard_map/ppermute | solution.py:722
  48.6 26.2 %collective-permute-start.7 = (bf16[1024,512]{1,0:T(8,128)(2,1)S(1)}, bf16[1024,512]{1,0:T(8,128)(2,1)S(1)}, u32[]{:S(2)}, u32[]{:S(2)}) collective-permute-start(bf16[1024,512]{1,0:T(8,128)(2,1)S(1)} %join.5), channel_id=1, source_target_pairs={{0,2},{1,3},{2,0},{3,1},{4,6},{5,7},{6,4},{7,5},{8,10},{9,11},{10,... | collective-permute-start | bytes 3145736 | tf_op jit(solution)/shard_map/ppermute | solution.py:722
  50.2 13.9 %collective-permute-start.4 = (bf16[512,512]{1,0:T(8,128)(2,1)S(1)}, bf16[512,512]{1,0:T(8,128)(2,1)S(1)}, u32[]{:S(2)}, u32[]{:S(2)}) collective-permute-start(bf16[512,512]{1,0:T(8,128)(2,1)S(1)} %collective-permute-done.3.refs_0_.refs_2_), channel_id=1, source_target_pairs={{0,8},{4,12},{8,0},{12,4},{16,24},{20,28},{24,16},{28,20},{1,9},{5... | collective-permute-start | bytes 1572872 | tf_op jit(solution)/shard_map/ppermute | solution.py:722
  51.7 39.7 %collective-permute-start.9 = (bf16[1280,256]{1,0:T(8,128)(2,1)S(1)}, bf16[1280,256]{1,0:T(8,128)(2,1)S(1)}, u32[]{:S(2)}, u32[]{:S(2)}) collective-permute-start(bf16[1280,256]{1,0:T(8,128)(2,1)S(1)} %get-tuple-element.34.refs_3_), channel_id=1, source_target_pairs={{0,24},{4,28},{8,16},{12,20},{16,8},{20,12},{24,0},{28,4},{1,25},{... | collective-permute-start | bytes 1966088 | tf_op jit(solution)/shard_map/ppermute | solution.py:722
  64.0 19.3 %collective-permute-start.8 = (bf16[512,512]{1,0:T(8,128)(2,1)S(1)}, bf16[512,512]{1,0:T(8,128)(2,1)S(1)}, u32[]{:S(2)}, u32[]{:S(2)}) collective-permute-start(bf16[512,512]{1,0:T(8,128)(2,1)S(1)} %collective-permute-done.4.refs_2_.refs_3_), channel_id=1, source_target_pairs={{0,2},{1,3},{2,0},{3,1},{4,6},{5,7},{6,4},{7,5},{8,10},{9,11},{10,... | collective-permute-start | bytes 1572872 | tf_op jit(solution)/shard_map/ppermute | solution.py:722
  64.6 26.8 %collective-permute-start.10 = (bf16[512,256]{1,0:T(8,128)(2,1)S(1)}, bf16[512,256]{1,0:T(8,128)(2,1)S(1)}, u32[]{:S(2)}, u32[]{:S(2)}) collective-permute-start(bf16[512,256]{1,0:T(8,128)(2,1)S(1)} %get-tuple-element.36), channel_id=1, source_target_pairs={{0,16},{4,20},{8,24},{12,28},{16,0},{20,4},{24,8},{28,12},{1,17},{... | collective-permute-start | bytes 786440 | tf_op jit(solution)/shard_map/ppermute | solution.py:722
  83.5 12.6 %collective-permute-start.12 = (bf16[2048,512]{1,0:T(8,128)(2,1)S(1)}, bf16[2048,512]{1,0:T(8,128)(2,1)S(1)}, u32[]{:S(2)}, u32[]{:S(2)}) collective-permute-start(bf16[2048,512]{1,0:T(8,128)(2,1)S(1)} %join.7), channel_id=1, source_target_pairs={{0,1},{1,0},{2,3},{3,2},{4,5},{5,4},{6,7},{7,6},{8,9},{9,8},{10,11... | collective-permute-start | bytes 6291464 | tf_op jit(solution)/shard_map/ppermute | solution.py:722
  91.5 4.5 %collective-permute-start.11 = (bf16[2048,512]{1,0:T(8,128)(2,1)S(1)}, bf16[2048,512]{1,0:T(8,128)(2,1)S(1)}, u32[]{:S(2)}, u32[]{:S(2)}) collective-permute-start(bf16[2048,512]{1,0:T(8,128)(2,1)S(1)} %join.6), channel_id=1, source_target_pairs={{0,1},{1,0},{2,3},{3,2},{4,5},{5,4},{6,7},{7,6},{8,9},{9,8},{10,11... | collective-permute-start | bytes 6291464 | tf_op jit(solution)/shard_map/ppermute | solution.py:722
  91.6 19.5 %collective-permute-start.15 = (bf16[768,256]{1,0:T(8,128)(2,1)S(1)}, bf16[768,256]{1,0:T(8,128)(2,1)S(1)}, u32[]{:S(2)}, u32[]{:S(2)}) collective-permute-start(bf16[768,256]{1,0:T(8,128)(2,1)S(1)} %get-tuple-element.42), channel_id=1, source_target_pairs={{0,8},{4,12},{8,0},{12,4},{16,24},{20,28},{24,16},{28,20},{1,9},{5... | collective-permute-start | bytes 1179656 | tf_op jit(solution)/shard_map/ppermute | solution.py:722
  91.7 27.0 %collective-permute-start.16 = (bf16[768,256]{1,0:T(8,128)(2,1)S(1)}, bf16[768,256]{1,0:T(8,128)(2,1)S(1)}, u32[]{:S(2)}, u32[]{:S(2)}) collective-permute-start(bf16[768,256]{1,0:T(8,128)(2,1)S(1)} %get-tuple-element.43), channel_id=1, source_target_pairs={{0,16},{4,20},{8,24},{12,28},{16,0},{20,4},{24,8},{28,12},{1,17},{... | collective-permute-start | bytes 1179656 | tf_op jit(solution)/shard_map/ppermute | solution.py:722
  94.5 23.3 %collective-permute-start.17 = (bf16[512,256]{1,0:T(8,128)(2,1)S(1)}, bf16[512,256]{1,0:T(8,128)(2,1)S(1)}, u32[]{:S(2)}, u32[]{:S(2)}) collective-permute-start(bf16[512,256]{1,0:T(8,128)(2,1)S(1)} %get-tuple-element.44), channel_id=1, source_target_pairs={{0,24},{4,28},{8,16},{12,20},{16,8},{20,12},{24,0},{28,4},{1,25},{... | collective-permute-start | bytes 786440 | tf_op jit(solution)/shard_map/ppermute | solution.py:722
  98.6 24.8 %collective-permute-start.14 = (bf16[2048,128]{1,0:T(8,128)(2,1)S(1)}, bf16[2048,128]{1,0:T(8,128)(2,1)S(1)}, u32[]{:S(2)}, u32[]{:S(2)}) collective-permute-start(bf16[2048,128]{1,0:T(8,128)(2,1)S(1)} %get-tuple-element.41.refs_4_), channel_id=1, source_target_pairs={{0,4},{4,0},{8,12},{12,8},{16,20},{20,16},{24,28},{28,24},{1,5},{5... | collective-permute-start | bytes 1572872 | tf_op jit(solution)/shard_map/ppermute | solution.py:722
  101.7 23.0 %collective-permute-start.13 = (bf16[2048,128]{1,0:T(8,128)(2,1)S(1)}, bf16[2048,128]{1,0:T(8,128)(2,1)S(1)}, u32[]{:S(2)}, u32[]{:S(2)}) collective-permute-start(bf16[2048,128]{1,0:T(8,128)(2,1)S(1)} %get-tuple-element.39), channel_id=1, source_target_pairs={{0,4},{4,0},{8,12},{12,8},{16,20},{20,16},{24,28},{28,24},{1,5},{5... | collective-permute-start | bytes 1572872 | tf_op jit(solution)/shard_map/ppermute | solution.py:722
  111.1 13.6 %slice-start = ((s8[8388608]{0:T(1024)(128)(4,1)}), s8[4194304]{0:T(1024)(128)(4,1)S(1)}, s32[]{:S(2)}) async-start(s8[8388608]{0:T(1024)(128)(4,1)} %bitcast.4), calls=%async_computation | async-start | bytes 8388608
  120.3 14.4 %collective-permute-start.18 = (bf16[2048,128]{1,0:T(8,128)(2,1)S(1)}, bf16[2048,128]{1,0:T(8,128)(2,1)S(1)}, u32[]{:S(2)}, u32[]{:S(2)}) collective-permute-start(bf16[2048,128]{1,0:T(8,128)(2,1)S(1)} %get-tuple-element.45.refs_0_), channel_id=1, source_target_pairs={{0,4},{4,0},{8,12},{12,8},{16,20},{20,16},{24,28},{28,24},{1,5},{5... | collective-permute-start | bytes 1572872 | tf_op jit(solution)/shard_map/ppermute | solution.py:722
  135.2 10.6 %collective-permute-start.19 = (bf16[256,128]{1,0:T(8,128)(2,1)S(1)}, bf16[256,128]{1,0:T(8,128)(2,1)S(1)}, u32[]{:S(2)}, u32[]{:S(2)}) collective-permute-start(bf16[256,128]{1,0:T(8,128)(2,1)S(1)} %get-tuple-element.49), channel_id=1, source_target_pairs={{0,24},{4,28},{8,16},{12,20},{16,8},{20,12},{24,0},{28,4},{1,25},{... | collective-permute-start | bytes 196616 | tf_op jit(solution)/shard_map/ppermute | solution.py:722
  137.5 9.5 %collective-permute-start.20 = (bf16[256,128]{1,0:T(8,128)(2,1)S(1)}, bf16[256,128]{1,0:T(8,128)(2,1)S(1)}, u32[]{:S(2)}, u32[]{:S(2)}) collective-permute-start(bf16[256,128]{1,0:T(8,128)(2,1)S(1)} %get-tuple-element.50), channel_id=1, source_target_pairs={{0,28},{4,24},{8,20},{12,16},{16,12},{20,8},{24,4},{28,0},{1,29},{... | collective-permute-start | bytes 196616 | tf_op jit(solution)/shard_map/ppermute | solution.py:722
  139.1 11.4 %collective-permute-start.21 = (bf16[256,128]{1,0:T(8,128)(2,1)S(1)}, bf16[256,128]{1,0:T(8,128)(2,1)S(1)}, u32[]{:S(2)}, u32[]{:S(2)}) collective-permute-start(bf16[256,128]{1,0:T(8,128)(2,1)S(1)} %get-tuple-element.51), channel_id=1, source_target_pairs={{0,16},{4,20},{8,24},{12,28},{16,0},{20,4},{24,8},{28,12},{1,17},{... | collective-permute-start | bytes 196616 | tf_op jit(solution)/shard_map/ppermute | solution.py:722
  142.7 8.5 %collective-permute-start.22 = (bf16[256,128]{1,0:T(8,128)(2,1)S(1)}, bf16[256,128]{1,0:T(8,128)(2,1)S(1)}, u32[]{:S(2)}, u32[]{:S(2)}) collective-permute-start(bf16[256,128]{1,0:T(8,128)(2,1)S(1)} %get-tuple-element.52), channel_id=1, source_target_pairs={{0,20},{4,16},{8,28},{12,24},{16,4},{20,0},{24,12},{28,8},{1,21},{... | collective-permute-start | bytes 196616 | tf_op jit(solution)/shard_map/ppermute | solution.py:722
  143.6 7.6 %collective-permute-start.23 = (bf16[256,128]{1,0:T(8,128)(2,1)S(1)}, bf16[256,128]{1,0:T(8,128)(2,1)S(1)}, u32[]{:S(2)}, u32[]{:S(2)}) collective-permute-start(bf16[256,128]{1,0:T(8,128)(2,1)S(1)} %get-tuple-element.53), channel_id=1, source_target_pairs={{0,8},{4,12},{8,0},{12,4},{16,24},{20,28},{24,16},{28,20},{1,9},{5... | collective-permute-start | bytes 196616 | tf_op jit(solution)/shard_map/ppermute | solution.py:722
  145.7 6.1 %collective-permute-start.24 = (bf16[256,128]{1,0:T(8,128)(2,1)S(1)}, bf16[256,128]{1,0:T(8,128)(2,1)S(1)}, u32[]{:S(2)}, u32[]{:S(2)}) collective-permute-start(bf16[256,128]{1,0:T(8,128)(2,1)S(1)} %get-tuple-element.54), channel_id=1, source_target_pairs={{0,12},{4,8},{8,4},{12,0},{16,28},{20,24},{24,20},{28,16},{1,13},{... | collective-permute-start | bytes 196616 | tf_op jit(solution)/shard_map/ppermute | solution.py:722
  147.0 5.5 %collective-permute-start.25 = (bf16[256,128]{1,0:T(8,128)(2,1)S(1)}, bf16[256,128]{1,0:T(8,128)(2,1)S(1)}, u32[]{:S(2)}, u32[]{:S(2)}) collective-permute-start(bf16[256,128]{1,0:T(8,128)(2,1)S(1)} %get-tuple-element.55), channel_id=1, source_target_pairs={{0,4},{4,0},{8,12},{12,8},{16,20},{20,16},{24,28},{28,24},{1,5},{5... | collective-permute-start | bytes 196616 | tf_op jit(solution)/shard_map/ppermute | solution.py:722
  153.3 2.0 %collective-permute-start.27 = (bf16[256,1024]{1,0:T(8,128)(2,1)S(1)}, bf16[256,1024]{1,0:T(8,128)(2,1)S(1)}, u32[]{:S(2)}, u32[]{:S(2)}) collective-permute-start(bf16[256,1024]{1,0:T(8,128)(2,1)S(1)} %get-tuple-element.58), channel_id=1, source_target_pairs={{0,1},{1,0},{2,3},{3,2},{4,5},{5,4},{6,7},{7,6},{8,9},{9,8},{10,11... | collective-permute-start | bytes 1572872 | tf_op jit(solution)/shard_map/ppermute | solution.py:722
  154.1 2.5 %collective-permute-start.26 = (bf16[256,1024]{1,0:T(8,128)(2,1)S(1)}, bf16[256,1024]{1,0:T(8,128)(2,1)S(1)}, u32[]{:S(2)}, u32[]{:S(2)}) collective-permute-start(bf16[256,1024]{1,0:T(8,128)(2,1)S(1)} %emit.5), channel_id=1, source_target_pairs={{0,1},{1,0},{2,3},{3,2},{4,5},{5,4},{6,7},{7,6},{8,9},{9,8},{10,11... | collective-permute-start | bytes 1572872 | tf_op jit(solution)/shard_map/ppermute | solution.py:722
  156.0 14.0 %collective-permute-start.28 = (bf16[256,1024]{1,0:T(8,128)(2,1)S(1)}, bf16[256,1024]{1,0:T(8,128)(2,1)S(1)}, u32[]{:S(2)}, u32[]{:S(2)}) collective-permute-start(bf16[256,1024]{1,0:T(8,128)(2,1)S(1)} %emit.7), channel_id=1, source_target_pairs={{0,2},{1,3},{2,0},{3,1},{4,6},{5,7},{6,4},{7,5},{8,10},{9,11},{10,... | collective-permute-start | bytes 1572872 | tf_op jit(solution)/shard_map/ppermute | solution.py:722
  (9 other events, 57.7 us)
